TPU v7x, 32 devices: a whole 2x2x4 slice. The times are simulated.
32 devices in a mesh: section: 2 (over core), ctx: 4 (over z), heads: 4 (over y, x).
Axes of the slice: x: 2, y: 2, z: 4, core: 2. Of those that a mesh axis runs over, the one named last changes fastest.
Arguments:
- boundary: bfloat16 [2, 2, 1024, 768], P('section', None, 'ctx'), may hold values from -6 to 6
- norm_first: bfloat16 [2, 768], P('section'), may hold values from 0.5 to 1.5
- qkv_weight: bfloat16 [2, 3, 768, 768], P('section', None, None, 'heads'), may hold values from -0.21875 to 0.21875
- position_bias: float32 [2, 32, 12], P('section', None, 'heads'), may hold values from -4 to 4
- out_weight: bfloat16 [2, 768, 768], P('section', 'heads'), may hold values from -0.875 to 0.875
- norm_second: bfloat16 [2, 768], P('section'), may hold values from 0.5 to 1.5
- router: bfloat16 [2, 768, 4], P('section'), may hold values from -0.15625 to 0.15625
- expert_up: bfloat16 [2, 4, 768, 3072], P('section', 'ctx', None, 'heads'), may hold values from -0.21875 to 0.21875
- expert_down: bfloat16 [2, 4, 3072, 768], P('section', 'ctx', 'heads'), may hold values from -0.15625 to 0.15625
- routes: int32 [2, 2, 1024, 2], P('section', None, 'ctx'), may hold values from 0 to 3, all different within a row; in each aligned block of 256 rows (0 to 255, 256 to 511, ..., all dimensions but the last counted through in order) at most 160 rows name the same one
Outputs:
- boundary_out: float32 [2, 2, 1024, 768], P('section', None, 'ctx')
- grad_norm_first: float32 [2, 768], P('section', 'ctx')
- grad_qkv_weight: float32 [2, 3, 768, 768], P('section', None, 'ctx', 'heads')
- grad_position_bias: float32 [2, 32, 12], P('section', 'ctx', 'heads')
- grad_out_weight: float32 [2, 768, 768], P('section', 'heads', 'ctx')
- grad_norm_second: float32 [2, 768], P('section', 'ctx')
- grad_router: float32 [2, 768, 4], P('section', 'ctx')
- grad_expert_up: float32 [2, 4, 768, 3072], P('section', 'ctx', None, 'heads')
- grad_expert_down: float32 [2, 4, 3072, 768], P('section', 'ctx', 'heads')
Inputs may be any that keep to these rules, and one draw needn't show every extreme that they name: `routes`: each token's two experts differ and every expert is named somewhere. Among the 256 rows of one index of ctx, for one layer and micro-batch, no expert is named more than 160 times, and in some of these blocks one expert is named exactly 160 times.
All inputs are finite; a program needn't handle non-finite values.
Results may differ from a plain program's by a relative error of at most 0.04.
Values may be sent and summed in bfloat16 or wider, within the bound.
No kernel may reach another device: no remote copies, remote signals or barrier semaphores. Data moves between devices by JAX's collectives and lax.ppermute only.
A program may use at most 256 MiB of HBM per device.

v0:
```python
import math

import jax
import jax.numpy as jnp
from jax import lax
from jax.sharding import PartitionSpec as P

HD = 64
BUCKETS = 32
REACH = 128


EPSILON = 1e-06
NEGATIVE = -1e30
HIGHEST = lax.Precision.HIGHEST


def shifted(array, axis, by):
    devices = lax.axis_size(axis)
    pairs = [(i, i + by) for i in range(devices) if 0 <= i + by < devices]
    return lax.ppermute(array, axis, pairs)


def bucket_of(distance, buckets, reach_max):
    exact_span = buckets // 2
    result = jnp.minimum(distance, exact_span)
    for edge_rank in range(1, buckets - exact_span):
        threshold = int(
            math.ceil(exact_span * (reach_max / exact_span) ** (edge_rank / (buckets - exact_span)))
        )
        result = result + (distance >= threshold).astype(jnp.int32)
    return result


def rms_norm(values, gain_row):
    scale_rows = lax.rsqrt(jnp.mean(values * values, axis=-1, keepdims=True) + EPSILON)
    return values * scale_rows * gain_row


def gelu_tanh(values):
    return jax.nn.gelu(values, approximate=True)


def heads_total(values):
    return lax.psum(values.astype(jnp.bfloat16), "heads").astype(jnp.float32)


def rows_total(values):
    return lax.psum(values.astype(jnp.bfloat16), "heads").astype(jnp.float32)


def send_back(values):
    return lax.all_to_all(values, "ctx", split_axis=0, concat_axis=0, tiled=True)


def back_send(values):
    return lax.all_to_all(values, "ctx", split_axis=0, concat_axis=0, tiled=True)


def dispatch_rows(values, handler):
    return handler(lax.all_to_all(values, "ctx", split_axis=0, concat_axis=0, tiled=True))


def share_dense(gradients):
    return (
        lax.psum_scatter(
            gradients[0].astype(jnp.bfloat16), "ctx", scatter_dimension=1, tiled=True
        ).astype(jnp.float32),
        lax.psum_scatter(
            gradients[1].astype(jnp.bfloat16), "ctx", scatter_dimension=1, tiled=True
        ).astype(jnp.float32),
        lax.psum_scatter(
            gradients[2].astype(jnp.bfloat16), "ctx", scatter_dimension=0, tiled=True
        ).astype(jnp.float32),
        lax.psum_scatter(
            gradients[3].astype(jnp.bfloat16), "ctx", scatter_dimension=0, tiled=True
        ).astype(jnp.float32),
        lax.psum_scatter(
            gradients[4].astype(jnp.bfloat16), "ctx", scatter_dimension=0, tiled=True
        ).astype(jnp.float32),
        lax.psum_scatter(
            gradients[5].astype(jnp.bfloat16), "ctx", scatter_dimension=0, tiled=True
        ).astype(jnp.float32),
    )


def dealt_start(device, part, n_ctx, half):
    return jnp.where(part == 0, device, 2 * n_ctx - 1 - device) * half


def index_positions(indices, row_count, n_ctx):
    half = row_count // 2
    device = indices // row_count
    local = indices % row_count
    return dealt_start(device, local // half, n_ctx, half) + local % half


def shard_info(device, row_count, n_ctx):
    half = row_count // 2
    starts = jnp.stack([dealt_start(device, 0, n_ctx, half), dealt_start(device, 1, n_ctx, half)])
    places = index_positions(device * row_count + lax.iota(jnp.int32, row_count), row_count, n_ctx)
    return (places, starts, half)


def piece_info(piece_start, piece_rows, row_count, n_ctx):
    tile_span = math.gcd(piece_rows, row_count // 2)
    starts = index_positions(
        piece_start + tile_span * lax.iota(jnp.int32, piece_rows // tile_span), row_count, n_ctx
    )
    places = index_positions(piece_start + lax.iota(jnp.int32, piece_rows), row_count, n_ctx)
    return (places, starts, tile_span)


def diagonal_spread(coeffs, row_span, col_span):
    length = row_span + col_span
    flipped = jnp.roll(coeffs[:, ::-1], -row_span, axis=1)
    tiled_rows = jnp.tile(flipped, (1, row_span))[:, : row_span * (length - 1)]
    return tiled_rows.reshape(coeffs.shape[0], row_span, length - 1)[:, :, :col_span]


def diagonal_sums(score_grid):
    head_count, row_span, col_span = score_grid.shape
    length = row_span + col_span
    padded = jnp.pad(score_grid, ((0, 0), (0, 0), (0, length - 1 - col_span)))
    flat_rows = jnp.pad(
        padded.reshape(head_count, row_span * (length - 1)), ((0, 0), (0, row_span))
    )
    folded = jnp.sum(flat_rows.reshape(head_count, row_span, length), axis=1)
    return jnp.roll(folded, row_span, axis=1)[:, ::-1]


def tile_onehot(query_starts, query_span, key_starts, key_span):
    offsets = (
        query_starts[:, None, None]
        - key_starts[None, :, None]
        - (key_span - 1)
        + lax.iota(jnp.int32, query_span + key_span)[None, None, :]
    )
    buckets = bucket_of(jnp.maximum(offsets, 0), BUCKETS, REACH)
    return (buckets[..., None] == lax.iota(jnp.int32, BUCKETS)).astype(jnp.float32)


def tile_bias(hot_table, bias_table, query_span, key_span):
    coeffs = jnp.einsum("nmlb,bh->nmhl", hot_table, bias_table, precision=HIGHEST)
    spread = jax.vmap(
        jax.vmap(lambda coeff_rows: diagonal_spread(coeff_rows, query_span, key_span))
    )(coeffs)
    query_tiles, key_tiles, head_count = (spread.shape[0], spread.shape[1], spread.shape[2])
    return spread.transpose(2, 0, 3, 1, 4).reshape(
        head_count, query_tiles * query_span, key_tiles * key_span
    )


def tile_table_grad(dscores, hot_table, query_span, key_span):
    head_count, row_total, col_total = dscores.shape
    query_tiles = row_total // query_span
    key_tiles = col_total // key_span
    tiles = dscores.reshape(head_count, query_tiles, query_span, key_tiles, key_span).transpose(
        1, 3, 0, 2, 4
    )
    sums = jax.vmap(jax.vmap(diagonal_sums))(tiles)
    return jnp.einsum("nmhl,nmlb->bh", sums, hot_table, precision=HIGHEST)


def bias_grid(bias_table, row_count, n_ctx):
    query_info = shard_info(lax.axis_index("ctx"), row_count, n_ctx)
    key_info = piece_info(0, row_count * n_ctx, row_count, n_ctx)
    half = row_count // 2
    hot_table = tile_onehot(query_info[1], half, key_info[1], half)
    grid = tile_bias(hot_table, bias_table, half, half)
    visible = query_info[0][:, None] >= key_info[0][None, :]
    return (jnp.where(visible[None], grid, NEGATIVE), hot_table)


def grid_scores(queries, key_block, grid, first_key):
    grid_block = lax.dynamic_slice_in_dim(grid, first_key, key_block.shape[0], 2)
    raw_scores = (
        jnp.einsum("qhe,khe->hqk", queries, key_block, preferred_element_type=jnp.float32) * 0.125
    )
    return raw_scores + grid_block


def attend_forward(queries, key_rows, value_rows, grid):
    row_count, head_count = (queries.shape[0], queries.shape[1])
    block_total = key_rows.shape[0] // row_count

    def block_at(block_index):
        first_key = block_index * row_count
        key_block = lax.dynamic_slice_in_dim(key_rows, first_key, row_count, 0)
        value_block = lax.dynamic_slice_in_dim(value_rows, first_key, row_count, 0)
        return (grid_scores(queries, key_block, grid, first_key), value_block)

    def stats_step(block_index, running):
        row_max, row_mass = running
        scores, _ = block_at(block_index)
        new_max = jnp.maximum(row_max, jnp.max(scores, axis=2))
        row_mass = row_mass * jnp.exp(row_max - new_max) + jnp.sum(
            jnp.exp(scores - new_max[:, :, None]), axis=2
        )
        return (new_max, row_mass)

    begin = (
        jnp.full((head_count, row_count), NEGATIVE, jnp.float32),
        jnp.zeros((head_count, row_count), jnp.float32),
    )
    row_max, row_mass = lax.fori_loop(0, block_total, stats_step, begin)
    logsum = row_max + jnp.log(row_mass)

    def value_step(block_index, running):
        scores, value_block = block_at(block_index)
        prob_rows = jnp.exp(scores - logsum[:, :, None]).astype(jnp.bfloat16)
        return running + jnp.einsum(
            "hqk,khe->qhe", prob_rows, value_block, preferred_element_type=jnp.float32
        )

    totals = lax.fori_loop(0, block_total, value_step, jnp.zeros(queries.shape, jnp.float32))
    return (totals, logsum)


def query_side(queries, key_rows, value_rows, dout_heads, logsum, row_delta, grid, dscore_total):
    row_count = queries.shape[0]
    block_total = key_rows.shape[0] // row_count

    def grad_step(block_index, running):
        first_key = block_index * row_count
        key_block = lax.dynamic_slice_in_dim(key_rows, first_key, row_count, 0)
        value_block = lax.dynamic_slice_in_dim(value_rows, first_key, row_count, 0)
        scores = grid_scores(queries, key_block, grid, first_key)
        prob_rows = jnp.exp(scores - logsum[:, :, None])
        dprobs = jnp.einsum(
            "qhe,khe->hqk", dout_heads, value_block, preferred_element_type=jnp.float32
        )
        dscores = (prob_rows * (dprobs - row_delta[:, :, None])).astype(jnp.bfloat16)
        dquery = (
            running[0]
            + jnp.einsum("hqk,khe->qhe", dscores, key_block, preferred_element_type=jnp.float32)
            * 0.125
        )
        old_block = lax.dynamic_slice_in_dim(running[1], first_key, row_count, 2)
        dscore_next = lax.dynamic_update_slice_in_dim(
            running[1], old_block + dscores.astype(jnp.float32), first_key, 2
        )
        next_state = (dquery, dscore_next)
        dkey_block = (
            jnp.einsum("hqk,qhe->khe", dscores, queries, preferred_element_type=jnp.float32) * 0.125
        )
        dvalue_block = jnp.einsum(
            "hqk,qhe->khe",
            prob_rows.astype(jnp.bfloat16),
            dout_heads,
            preferred_element_type=jnp.float32,
        )
        next_state = next_state + (
            lax.dynamic_update_slice_in_dim(running[2], dkey_block, first_key, 0),
            lax.dynamic_update_slice_in_dim(running[3], dvalue_block, first_key, 0),
        )
        return next_state

    begin = (jnp.zeros(queries.shape, jnp.float32), dscore_total)
    begin = begin + (
        jnp.zeros(key_rows.shape, jnp.float32),
        jnp.zeros(value_rows.shape, jnp.float32),
    )
    return lax.fori_loop(0, block_total, grad_step, begin)


def expert_apply(arrived, up_w, down_w):
    pre_act = jnp.einsum("sxnd,xdf->sxnf", arrived, up_w, preferred_element_type=jnp.float32)
    hidden = gelu_tanh(pre_act).astype(jnp.bfloat16)
    partial_out = jnp.einsum("sxnf,xfd->sxnd", hidden, down_w, preferred_element_type=jnp.float32)
    return (pre_act, hidden, partial_out)


def layer_forward(inputs, routes_now, params, grid):
    gain_first, qkv_w, bias_table, out_w, gain_second, router_w, up_w, down_w = params
    row_count, width_model = inputs.shape
    head_count = qkv_w.shape[-1] // HD
    normed = rms_norm(inputs, gain_first).astype(jnp.bfloat16)
    projected = jnp.einsum("td,cdf->ctf", normed, qkv_w, preferred_element_type=jnp.float32).astype(
        jnp.bfloat16
    )
    key_all, value_all = (
        lax.all_gather(projected[1], "ctx", axis=0, tiled=True),
        lax.all_gather(projected[2], "ctx", axis=0, tiled=True),
    )
    queries = projected[0].reshape(row_count, head_count, HD)
    key_rows = key_all.reshape(-1, head_count, HD)
    value_rows = value_all.reshape(-1, head_count, HD)
    totals, logsum = attend_forward(queries, key_rows, value_rows, grid)
    head_mix = totals.astype(jnp.bfloat16).reshape(row_count, head_count * HD)
    attended = heads_total(jnp.dot(head_mix, out_w, preferred_element_type=jnp.float32))
    middle = inputs + attended
    expert_in = rms_norm(middle, gain_second).astype(jnp.bfloat16)
    logits = jnp.dot(expert_in, router_w, preferred_element_type=jnp.float32)
    experts_count = router_w.shape[1]
    local_experts = up_w.shape[0]
    capacity = 5 * row_count // (2 * experts_count)
    pair_experts = routes_now.reshape(-1)
    route_hot = (pair_experts[:, None] == lax.iota(jnp.int32, experts_count)[None, :]).astype(
        jnp.int32
    )
    slot_rank = jnp.sum(route_hot * (jnp.cumsum(route_hot, axis=0) - 1), axis=1)
    position = pair_experts * capacity + slot_rank
    chosen = jnp.sum(
        logits[:, None, :] * route_hot.reshape(row_count, 2, experts_count).astype(jnp.float32),
        axis=2,
    )
    gate_values = jax.nn.softmax(chosen, axis=1)
    outgoing = (
        jnp.zeros((experts_count * capacity, width_model), jnp.bfloat16)
        .at[position]
        .set(jnp.repeat(expert_in, 2, axis=0))
    )
    outgoing = outgoing.reshape(
        experts_count // local_experts, local_experts, capacity, width_model
    )

    def expert_forward(arrived):
        pre_act, hidden, partial_out = expert_apply(arrived, up_w, down_w)
        return (send_back(rows_total(partial_out).astype(jnp.bfloat16)), pre_act, hidden, arrived)

    returned, pre_act, hidden, received = dispatch_rows(outgoing, expert_forward)
    picked = returned.reshape(experts_count * capacity, width_model)[position].reshape(
        row_count, 2, width_model
    )
    output = middle + jnp.sum(gate_values[:, :, None] * picked.astype(jnp.float32), axis=1)
    kept_state = (
        inputs,
        normed,
        middle,
        expert_in,
        projected,
        key_rows,
        value_rows,
        totals,
        head_mix,
        logsum,
        route_hot,
        position,
        gate_values,
        picked,
        pre_act,
        hidden,
        received,
    )
    return (output, kept_state)


def layer_backward_input(upstream, kept_state, params, grid, dscore_total):
    gain_first, qkv_w, bias_table, out_w, gain_second, router_w, up_w, down_w = params
    (
        inputs,
        normed,
        middle,
        expert_in,
        projected,
        key_rows,
        value_rows,
        totals,
        head_mix,
        logsum,
        route_hot,
        position,
        gate_values,
        picked,
        pre_act,
        hidden,
        received,
    ) = kept_state
    row_count, width_model = inputs.shape
    head_count = qkv_w.shape[-1] // HD
    experts_count = router_w.shape[1]
    local_experts = up_w.shape[0]
    capacity = 5 * row_count // (2 * experts_count)
    dgates = jnp.sum(upstream[:, None, :] * picked.astype(jnp.float32), axis=2)
    dchosen = gate_values * (dgates - jnp.sum(gate_values * dgates, axis=1, keepdims=True))
    dlogits = jnp.sum(
        dchosen[:, :, None] * route_hot.reshape(row_count, 2, experts_count).astype(jnp.float32),
        axis=1,
    )
    dpairs = (
        (gate_values[:, :, None] * upstream[:, None, :])
        .astype(jnp.bfloat16)
        .reshape(2 * row_count, width_model)
    )
    outgoing = (
        jnp.zeros((experts_count * capacity, width_model), jnp.bfloat16).at[position].set(dpairs)
    )
    outgoing = outgoing.reshape(
        experts_count // local_experts, local_experts, capacity, width_model
    )
    incoming = back_send(outgoing)
    dhidden = jnp.einsum("sxnd,xfd->sxnf", incoming, down_w, preferred_element_type=jnp.float32)
    gelu_back = jax.vjp(gelu_tanh, pre_act)[1]
    dpre_act = gelu_back(dhidden)[0].astype(jnp.bfloat16)
    dreceived = jnp.einsum("sxnf,xdf->sxnd", dpre_act, up_w, preferred_element_type=jnp.float32)
    dreturned = send_back(rows_total(dreceived).astype(jnp.bfloat16))
    dexpert_in = jnp.sum(
        dreturned.reshape(experts_count * capacity, width_model)[position]
        .astype(jnp.float32)
        .reshape(row_count, 2, width_model),
        axis=1,
    )
    dexpert_in = dexpert_in + jnp.dot(dlogits, router_w.astype(jnp.float32).T, precision=HIGHEST)
    norm_back = jax.vjp(rms_norm, middle, gain_second)[1]
    dmiddle_part, grad_gain_second = norm_back(dexpert_in)
    dmiddle = upstream + dmiddle_part
    dattended = dmiddle.astype(jnp.bfloat16)
    dhead_mix = jnp.dot(dattended, out_w.T, preferred_element_type=jnp.float32).astype(jnp.bfloat16)
    dout_heads = dhead_mix.reshape(row_count, head_count, HD)
    row_delta = jnp.sum(dout_heads.astype(jnp.float32) * totals, axis=2).T
    queries = projected[0].reshape(row_count, head_count, HD)
    dquery, dscore_total, dkey_all, dvalue_all = query_side(
        queries, key_rows, value_rows, dout_heads, logsum, row_delta, grid, dscore_total
    )
    dkey_rows, dvalue_rows = (
        lax.psum_scatter(
            dkey_all.reshape(-1, head_count * HD).astype(jnp.bfloat16),
            "ctx",
            scatter_dimension=0,
            tiled=True,
        ).astype(jnp.float32),
        lax.psum_scatter(
            dvalue_all.reshape(-1, head_count * HD).astype(jnp.bfloat16),
            "ctx",
            scatter_dimension=0,
            tiled=True,
        ).astype(jnp.float32),
    )
    dprojected = jnp.stack(
        [
            dquery.reshape(row_count, head_count * HD).astype(jnp.bfloat16),
            dkey_rows.astype(jnp.bfloat16),
            dvalue_rows.astype(jnp.bfloat16),
        ]
    )
    dnormed = heads_total(
        jnp.einsum("ctf,cdf->td", dprojected, qkv_w, preferred_element_type=jnp.float32)
    )
    norm_back_first = jax.vjp(rms_norm, inputs, gain_first)[1]
    dinput_part, grad_gain_first = norm_back_first(dnormed)
    dinput = dmiddle + dinput_part
    small_grads = (grad_gain_first, grad_gain_second)
    weight_state = (
        normed,
        dprojected,
        head_mix,
        dattended,
        expert_in,
        dlogits,
        received,
        dpre_act,
        hidden,
        incoming,
    )
    return (dinput, small_grads, weight_state, dscore_total)


def layer_backward_weights(weight_state):
    (
        normed,
        dprojected,
        head_mix,
        dattended,
        expert_in,
        dlogits,
        received,
        dpre_act,
        hidden,
        incoming,
    ) = weight_state
    grad_qkv = jnp.einsum("td,ctf->cdf", normed, dprojected, preferred_element_type=jnp.float32)
    grad_out = jnp.dot(head_mix.T, dattended, preferred_element_type=jnp.float32)
    grad_router = jnp.dot(expert_in.astype(jnp.float32).T, dlogits, precision=HIGHEST)
    grad_down = jnp.einsum("sxnf,sxnd->xfd", hidden, incoming, preferred_element_type=jnp.float32)
    grad_up = jnp.einsum("sxnd,sxnf->xdf", received, dpre_act, preferred_element_type=jnp.float32)
    return (grad_qkv, grad_out, grad_router, (grad_up, grad_down))


def body(
    boundary,
    norm_first,
    qkv_weight,
    position_bias,
    out_weight,
    norm_second,
    router,
    expert_up,
    expert_down,
    routes,
):
    section_index = lax.axis_index("section")
    params = (
        norm_first[0].astype(jnp.float32),
        qkv_weight[0],
        position_bias[0],
        out_weight[0],
        norm_second[0].astype(jnp.float32),
        router[0],
        expert_up[0],
        expert_down[0],
    )
    micro_count = boundary.shape[1]
    row_count = boundary.shape[2]
    n_ctx = lax.axis_size("ctx")
    half = row_count // 2
    grid, hot_table = bias_grid(position_bias[0], row_count, n_ctx)
    received = jnp.zeros(boundary.shape[2:], jnp.bfloat16)
    saved_list = []
    forward_outs = []
    for tick_index in range(micro_count + 1):
        micro_index = jnp.clip(tick_index - section_index, 0, micro_count - 1)
        routes_now = lax.dynamic_index_in_dim(routes[0], micro_index, 0, keepdims=False)
        first_input = boundary[0, min(tick_index, micro_count - 1)].astype(jnp.float32)
        inputs = jnp.where(section_index == 0, first_input, received.astype(jnp.float32))
        output, kept_state = layer_forward(inputs, routes_now, params, grid)
        saved_list.append(kept_state)
        forward_outs.append(output)
        if tick_index < micro_count:
            received = shifted(output.astype(jnp.bfloat16), "section", 1)
    back_received = jnp.zeros(boundary.shape[2:], jnp.bfloat16)
    dscore_total = jnp.zeros(grid.shape, jnp.float32)
    dense_total = None
    expert_total = None
    input_grads = []
    for tick_index in range(micro_count + 1):
        kept_state = jax.tree.map(
            lambda first_tree, second_tree: jnp.where(section_index == 0, first_tree, second_tree),
            saved_list[max(tick_index - 1, 0)],
            saved_list[min(tick_index + 1, micro_count)],
        )
        live_scale = 1.0 if tick_index < micro_count else 0.0
        cotangent = boundary[0, min(tick_index, micro_count - 1)].astype(jnp.float32) * live_scale
        upstream = jnp.where(section_index == 1, cotangent, back_received.astype(jnp.float32))
        dinput, small_grads, weight_state, dscore_total = layer_backward_input(
            upstream, kept_state, params, grid, dscore_total
        )
        if tick_index < micro_count:
            back_received = shifted(dinput.astype(jnp.bfloat16), "section", -1)
        grad_qkv, grad_out, grad_router, expert_grads = layer_backward_weights(weight_state)
        if tick_index == micro_count:
            grad_table = tile_table_grad(dscore_total, hot_table, half, half)
        else:
            grad_table = jnp.zeros((BUCKETS, grid.shape[0]), jnp.float32)
        dense_grads = (grad_qkv, grad_out, grad_table, grad_router, small_grads[0], small_grads[1])
        if dense_total is None:
            dense_total = dense_grads
            expert_total = expert_grads
        else:
            dense_total = jax.tree.map(jnp.add, dense_total, dense_grads)
            expert_total = jax.tree.map(jnp.add, expert_total, expert_grads)
        input_grads.append(dinput)
    dense_total = share_dense(dense_total)
    boundary_out = jnp.stack(
        [
            jnp.where(section_index == 1, forward_outs[micro_slot + 1], input_grads[micro_slot + 1])
            for micro_slot in range(micro_count)
        ]
    )[None]
    return (
        boundary_out,
        dense_total[4][None],
        dense_total[0][None],
        dense_total[2][None],
        dense_total[1][None],
        dense_total[5][None],
        dense_total[3][None],
        expert_total[0][None],
        expert_total[1][None],
    )


def solution(mesh):
    placed = (
        P("section", None, "ctx", None),
        P("section", None),
        P("section", None, None, "heads"),
        P("section", None, "heads"),
        P("section", "heads", None),
        P("section", None),
        P("section", None, None),
        P("section", "ctx", None, "heads"),
        P("section", "ctx", "heads", None),
        P("section", None, "ctx", None),
    )
    return jax.shard_map(
        body,
        mesh=mesh,
        in_specs=placed,
        out_specs=(
            P("section", None, "ctx", None),
            P("section", "ctx"),
            P("section", None, "ctx", "heads"),
            P("section", "ctx", "heads"),
            P("section", "heads", "ctx"),
            P("section", "ctx"),
            P("section", "ctx", None),
            P("section", "ctx", None, "heads"),
            P("section", "ctx", "heads", None),
        ),
        check_vma=False,
    )
```

profile of v0, /device:TPU:0, one launch (start us, length us, event | category | flops | bytes accessed | tf_op | source)
XLA Modules:
  0.0 1516.5 jit_solution(13822387483817768294)
XLA Ops:
  11.2 16.2 %all-gather = bf16[1,1024,192]{1,2,0:T(8,128)(2,1)S(1)} all-gather(bf16[1,256,192]{1,2,0:T(8,128)(2,1)S(1)} %get-tuple-element.2306), channel_id=2, replica_groups=mesh['section'=2,'ctx'=4,'heads'=4] {'ctx'}, dimensions={1}, use_global_device_ids=true | all-gather | bytes 491520 | tf_op jit(solution)/shard_map/all_gather | solution.py:284
  27.4 15.4 %all-gather.1 = bf16[1,1024,192]{1,2,0:T(8,128)(2,1)S(1)} all-gather(bf16[1,256,192]{1,2,0:T(8,128)(2,1)S(1)} %get-tuple-element.2305), channel_id=3, replica_groups=mesh['section'=2,'ctx'=4,'heads'=4] {'ctx'}, dimensions={1}, use_global_device_ids=true | all-gather | bytes 491520 | tf_op jit(solution)/shard_map/all_gather | solution.py:283
  46.8 7.2 tile.10
  54.0 5.8 slice.137
  59.8 12.7 reshape.1677
  78.1 4.6 reshape.1678
  90.7 6.7 while.150
  97.4 6.8 while.151
  113.8 36.6 %all-reduce.19.cloned.1.call-done = bf16[256,768]{1,0:T(8,128)(2,1)} async-done(((bf16[256,768]{1,0:T(8,128)(2,1)}), bf16[256,768]{1,0:T(8,128)(2,1)}) %all-reduce.19.cloned.1.call-update) | async-done | bytes 393232 | tf_op jit(solution)/shard_map/psum | solution.py:45
  158.7 28.4 %all_to_all.60 = bf16[4,1,160,768]{3,2,1,0:T(8,128)(2,1)S(1)} all-to-all(bf16[4,1,160,768]{3,2,1,0:T(8,128)(2,1)S(1)} %bitcast.982), channel_id=1, replica_groups=mesh['section'=2,'ctx'=4,'heads'=4] {'ctx'}, dimensions={0} | all-to-all | bytes 1966080 | tf_op jit(solution)/shard_map/all_to_all | solution.py:61
  192.6 49.8 %all-reduce.21.cloned.1.call-done = bf16[4,1,160,768]{3,2,0,1:T(8,128)(2,1)} async-done(((bf16[4,1,160,768]{3,2,0,1:T(8,128)(2,1)}), bf16[4,1,160,768]{3,2,0,1:T(8,128)(2,1)}) %all-reduce.21.cloned.1.call-update) | async-done | bytes 983056 | tf_op jit(solution)/shard_map/psum | solution.py:49
  242.4 4.6 all-to-all-start.1
  249.6 21.7 %all-to-all-done.1 = bf16[4,1,160,768]{3,2,1,0:T(8,128)(2,1)S(1)} async-done(((bf16[4,1,160,768]{3,2,1,0:T(8,128)(2,1)}), bf16[4,1,160,768]{3,2,1,0:T(8,128)(2,1)S(1)}, u32[]{:S(2)}, u32[]{:S(2)}) %all-to-all-start.1) | async-done | bytes 983072 | tf_op jit(solution)/shard_map/all_to_all | solution.py:53
  288.0 15.7 %all-gather.2 = bf16[1,1024,192]{1,2,0:T(8,128)(2,1)} all-gather(bf16[1,256,192]{1,2,0:T(8,128)(2,1)S(1)} %get-tuple-element.2303), channel_id=4, replica_groups=mesh['section'=2,'ctx'=4,'heads'=4] {'ctx'}, dimensions={1}, use_global_device_ids=true | all-gather | bytes 491520 | tf_op jit(solution)/shard_map/all_gather | solution.py:284
  303.7 15.9 %all-gather.3 = bf16[1,1024,192]{1,2,0:T(8,128)(2,1)} all-gather(bf16[1,256,192]{1,2,0:T(8,128)(2,1)S(1)} %get-tuple-element.2302), channel_id=5, replica_groups=mesh['section'=2,'ctx'=4,'heads'=4] {'ctx'}, dimensions={1}, use_global_device_ids=true | all-gather | bytes 491520 | tf_op jit(solution)/shard_map/all_gather | solution.py:283
  319.7 11.2 while.152
  332.2 9.7 while.153
  343.9 42.4 %all-reduce.23.cloned.1.call-done = bf16[256,768]{1,0:T(8,128)(2,1)} async-done(((bf16[256,768]{1,0:T(8,128)(2,1)}), bf16[256,768]{1,0:T(8,128)(2,1)}) %all-reduce.23.cloned.1.call-update) | async-done | bytes 393232 | tf_op jit(solution)/shard_map/psum | solution.py:45
  395.5 4.8 all-to-all-start.2
  406.4 4.6 scatter_custom_fusion.2
  411.0 13.2 all-to-all-done.2
  433.9 17.6 %all-to-all-done.4 = bf16[4,1,160,768]{3,2,1,0:T(8,128)(2,1)S(1)} async-done(((bf16[4,1,160,768]{3,2,1,0:T(8,128)(2,1)}), bf16[4,1,160,768]{3,2,1,0:T(8,128)(2,1)S(1)}, u32[]{:S(2)}, u32[]{:S(2)}) %all-to-all-start.4) | async-done | bytes 983072 | tf_op jit(solution)/shard_map/all_to_all | solution.py:57
  458.8 65.9 %all-reduce.37.cloned.1.call-done = (bf16[4,1,160,768]{3,2,0,1:T(8,128)(2,1)}, bf16[4,1,160,768]{3,2,0,1:T(8,128)(2,1)}) async-done(((bf16[4,1,160,768]{3,2,0,1:T(8,128)(2,1)}, bf16[4,1,160,768]{3,2,0,1:T(8,128)(2,1)}), (bf16[4,1,160,768]{3,2,0,1:T(8,128)(2,1)}, bf16[4,1,160,768]{3,2,0,1:T(8,128)(2,1)})) %all-reduce.37.cloned.1.call-update) | async-done | bytes 1966096 | tf_op jit(solution)/shard_map/psum | solution.py:49
  524.7 29.0 %all_to_all.61 = bf16[4,1,160,768]{3,2,1,0:T(8,128)(2,1)} all-to-all(bf16[4,1,160,768]{3,2,1,0:T(8,128)(2,1)} %bitcast.1009), channel_id=1, replica_groups=mesh['section'=2,'ctx'=4,'heads'=4] {'ctx'}, dimensions={0} | all-to-all | bytes 1966080 | tf_op jit(solution)/shard_map/all_to_all | solution.py:53
  561.2 4.4 gather_fusion.2
  568.5 12.5 all-to-all-done.3
  603.2 27.6 %while.154 = (s32[]{:T(128)}, f32[256,3,64]{0,2,1:T(8,128)S(1)}, f32[3,256,1024]{1,2,0:T(8,128)}, bf16[1024,3,64]{0,2,1:T(8,128)(2,1)}, bf16[1024,3,64]{0,2,1:T(...) while((s32[]{:T(128)}, f32[256,3,64]{0,2,1:T(8,128)S(1)}, ...), condition=%wide.region_46.47_spmd.clone, body=%wide.region_45.46_spmd.clone.sunk | while | flops 127795200 | bytes 7381217 | solution.py:264
  642.3 7.4 reduce-scatter.19.cloned.1.call-done
  649.7 21.7 %reduce-scatter.17.cloned.1.call-done = bf16[256,192]{0,1:T(8,128)(2,1)} async-done(((bf16[1024,192]{0,1:T(8,128)(2,1)}), bf16[256,192]{0,1:T(8,128)(2,1)}) %reduce-scatter.17.cloned.1.call-update) | async-done | bytes 98320 | tf_op jit(solution)/shard_map/reduce_scatter | solution.py:417
  675.3 42.0 %all-reduce.25.cloned.1.call-done = bf16[256,768]{1,0:T(8,128)(2,1)} async-done(((bf16[256,768]{1,0:T(8,128)(2,1)}), bf16[256,768]{1,0:T(8,128)(2,1)}) %all-reduce.25.cloned.1.call-update) | async-done | bytes 393232 | tf_op jit(solution)/shard_map/psum | solution.py:45
  724.1 15.2 all-gather.4
  739.3 16.2 %all-gather.5 = bf16[1,1024,192]{1,2,0:T(8,128)(2,1)} all-gather(bf16[1,256,192]{1,2,0:T(8,128)(2,1)S(1)} %get-tuple-element.2297), channel_id=7, replica_groups=mesh['section'=2,'ctx'=4,'heads'=4] {'ctx'}, dimensions={1}, use_global_device_ids=true | all-gather | bytes 491520 | tf_op jit(solution)/shard_map/all_gather | solution.py:283
  755.5 11.4 while.155
  768.2 9.9 while.156
  781.6 42.8 %all-reduce.27.cloned.1.call-done = bf16[256,768]{1,0:T(8,128)(2,1)} async-done(((bf16[256,768]{1,0:T(8,128)(2,1)}), bf16[256,768]{1,0:T(8,128)(2,1)}) %all-reduce.27.cloned.1.call-update) | async-done | bytes 393232 | tf_op jit(solution)/shard_map/psum | solution.py:45
  838.0 4.6 all-to-all-start.7
  848.7 4.6 scatter_custom_fusion.3
  853.3 13.3 all-to-all-done.7
  876.2 17.7 %all-to-all-done.6 = bf16[4,1,160,768]{3,2,1,0:T(8,128)(2,1)S(1)} async-done(((bf16[4,1,160,768]{3,2,1,0:T(8,128)(2,1)}), bf16[4,1,160,768]{3,2,1,0:T(8,128)(2,1)S(1)}, u32[]{:S(2)}, u32[]{:S(2)}) %all-to-all-start.6) | async-done | bytes 983072 | tf_op jit(solution)/shard_map/all_to_all | solution.py:57
  901.3 65.9 %all-reduce.35.cloned.1.call-done = (bf16[4,1,160,768]{3,2,0,1:T(8,128)(2,1)}, bf16[4,1,160,768]{3,2,0,1:T(8,128)(2,1)}) async-done(((bf16[4,1,160,768]{3,2,0,1:T(8,128)(2,1)}, bf16[4,1,160,768]{3,2,0,1:T(8,128)(2,1)}), (bf16[4,1,160,768]{3,2,0,1:T(8,128)(2,1)}, bf16[4,1,160,768]{3,2,0,1:T(8,128)(2,1)})) %all-reduce.35.cloned.1.call-update) | async-done | bytes 1966096 | tf_op jit(solution)/shard_map/psum | solution.py:49
  967.2 29.2 %all_to_all.62 = bf16[4,1,160,768]{3,2,1,0:T(8,128)(2,1)} all-to-all(bf16[4,1,160,768]{3,2,1,0:T(8,128)(2,1)} %bitcast.1010), channel_id=1, replica_groups=mesh['section'=2,'ctx'=4,'heads'=4] {'ctx'}, dimensions={0} | all-to-all | bytes 1966080 | tf_op jit(solution)/shard_map/all_to_all | solution.py:53
  1011.8 11.8 all-to-all-done.9
  1050.1 30.5 %while.157 = (s32[]{:T(128)}, f32[256,3,64]{0,2,1:T(8,128)}, f32[3,256,1024]{1,2,0:T(8,128)}, bf16[1024,3,64]{0,2,1:T(8,128)(2,1)}, bf16[1024,3,64]{0,2,1:T(8,12...) while((s32[]{:T(128)}, f32[256,3,64]{0,2,1:T(8,128)}, ...), condition=%wide.region_79.80_spmd.clone, body=%wide.region_78.79_spmd.clone.sunk | while | flops 127795200 | bytes 7381217 | solution.py:264
  1082.4 17.1 %reduce-scatter.23.cloned.1.call-done = bf16[256,192]{0,1:T(8,128)(2,1)} async-done(((bf16[1024,192]{0,1:T(8,128)(2,1)}), bf16[256,192]{0,1:T(8,128)(2,1)}) %reduce-scatter.23.cloned.1.call-update) | async-done | bytes 98320 | tf_op jit(solution)/shard_map/reduce_scatter | solution.py:423
  1099.5 21.8 %reduce-scatter.21.cloned.1.call-done = bf16[256,192]{0,1:T(8,128)(2,1)} async-done(((bf16[1024,192]{0,1:T(8,128)(2,1)}), bf16[256,192]{0,1:T(8,128)(2,1)}) %reduce-scatter.21.cloned.1.call-update) | async-done | bytes 98320 | tf_op jit(solution)/shard_map/reduce_scatter | solution.py:417
  1126.5 40.7 %all-reduce.29.cloned.1.call-done = bf16[256,768]{1,0:T(8,128)(2,1)} async-done(((bf16[256,768]{1,0:T(8,128)(2,1)}), bf16[256,768]{1,0:T(8,128)(2,1)}) %all-reduce.29.cloned.1.call-update) | async-done | bytes 393232 | tf_op jit(solution)/shard_map/psum | solution.py:45
  1189.3 4.6 scatter_custom_fusion.5
  1193.9 4.6 all-to-all-start.10
  1198.7 4.5 fusion.218
  1208.5 15.3 %all-to-all-done.10 = bf16[4,1,160,768]{3,2,1,0:T(8,128)(2,1)} async-done(((bf16[4,1,160,768]{3,2,1,0:T(8,128)(2,1)}), bf16[4,1,160,768]{3,2,1,0:T(8,128)(2,1)}, u32[]{:S(2)}, u32[]{:S(2)}) %all-to-all-start.10) | async-done | bytes 983072 | tf_op jit(solution)/shard_map/all_to_all | solution.py:57
  1238.6 42.3 %all-reduce.31.cloned.1.call-done = bf16[4,1,160,768]{3,2,0,1:T(8,128)(2,1)} async-done(((bf16[4,1,160,768]{3,2,0,1:T(8,128)(2,1)}), bf16[4,1,160,768]{3,2,0,1:T(8,128)(2,1)}) %all-reduce.31.cloned.1.call-update) | async-done | bytes 983056 | tf_op jit(solution)/shard_map/psum | solution.py:49
  1280.9 4.6 all-to-all-start.11
  1299.6 17.0 %reduce-scatter.33.cloned.1.call-done = bf16[192,4]{1,0:T(8,128)(2,1)} async-done(((bf16[768,4]{1,0:T(8,128)(2,1)}), bf16[192,4]{1,0:T(8,128)(2,1)}) %reduce-scatter.33.cloned.1.call-update) | async-done | bytes 1552
  1333.3 27.9 %while.158 = (s32[]{:T(128)}, f32[256,3,64]{0,2,1:T(8,128)}, f32[3,256,1024]{1,2,0:T(8,128)}, bf16[1024,3,64]{0,2,1:T(8,128)(2,1)}, bf16[1024,3,64]{0,2,1:T(8,12...) while((s32[]{:T(128)}, f32[256,3,64]{0,2,1:T(8,128)}, ...), condition=%wide.region_96.97_spmd.clone, body=%wide.region_95.96_spmd.clone.sunk | while | flops 127795200 | bytes 8954137 | solution.py:264
  1361.8 7.2 fusion.123
  1369.3 5.6 fusion.124
  1375.6 5.2 reshape.1721
  1380.8 5.7 copy.346
  1386.5 5.4 pad.8
  1391.9 8.1 reshape.1722
  1403.3 4.6 copy.382
  1436.3 42.2 %all-reduce.33.cloned.1.call-done = bf16[256,768]{1,0:T(8,128)(2,1)} async-done(((bf16[256,768]{1,0:T(8,128)(2,1)}), bf16[256,768]{1,0:T(8,128)(2,1)}) %all-reduce.33.cloned.1.call-update) | async-done | bytes 393232 | tf_op jit(solution)/shard_map/psum | solution.py:45
  1481.0 12.8 all-reduce.7
  1501.0 6.0 reduce-scatter.29.cloned.1.call-done
  (844 shorter events, 500.9 us)
Async XLA Ops:
  7.2 183.1 %copy-start = (bf16[1,1,768,768]{3,2,1,0:T(8,128)(2,1)S(1)}, bf16[1,1,768,768]{3,2,1,0:T(8,128)(2,1)}, u32[]{:S(2)}) copy-start(bf16[1,1,768,768]{3,2,1,0:T(8,128)(2,1)} %param.36) | copy-start | bytes 3538948
  7.2 143.2 %all-reduce.19.cloned.1.call-start = ((), (), s32[]{:S(2)}) async-start(), calls=%async_computation.21 | async-start | bytes 786432 | tf_op jit(solution)/shard_map/psum | solution.py:45
  8.1 276.9 %copy-start.89 = (f32[768]{0:T(1024)}, f32[768]{0:T(1024)S(1)}, u32[]{:S(2)}) copy-start(f32[768]{0:T(1024)S(1)} %convert_reduce_fusion.1) | copy-start | bytes 9220
  104.2 47.4 %copy-start.27 = (bf16[1024,3,64]{0,2,1:T(8,128)(2,1)}, bf16[1024,3,64]{0,2,1:T(8,128)(2,1)S(1)}, u32[]{:S(2)}) copy-start(bf16[1024,3,64]{0,2,1:T(8,128)(2,1)S(1)} %get-tuple-element.3184) | copy-start | bytes 1179652
  104.2 47.4 %copy-start.47 = (bf16[1024,3,64]{0,2,1:T(8,128)(2,1)}, bf16[1024,3,64]{0,2,1:T(8,128)(2,1)S(1)}, u32[]{:S(2)}) copy-start(bf16[1024,3,64]{0,2,1:T(8,128)(2,1)S(1)} %get-tuple-element.3191) | copy-start | bytes 1179652
  104.2 495.3 %copy-start.19 = (f32[256,3,64]{0,2,1:T(8,128)}, f32[256,3,64]{0,2,1:T(8,128)S(1)}, u32[]{:S(2)}) copy-start(f32[256,3,64]{0,2,1:T(8,128)S(1)} %get-tuple-element.1319) | copy-start | bytes 589828
  104.3 46.1 %copy-start.1 = (bf16[1,2,256,768]{3,2,1,0:T(8,128)(2,1)S(1)}, bf16[1,2,256,768]{3,2,1,0:T(8,128)(2,1)}, u32[]{:S(2)}) copy-start(bf16[1,2,256,768]{3,2,1,0:T(8,128)(2,1)} %param.28) | copy-start | bytes 2359300
  104.3 47.3 %copy-start.77 = (bf16[256,3,64]{0,2,1:T(8,128)(2,1)}, bf16[256,3,64]{0,2,1:T(8,128)(2,1)S(1)}, u32[]{:S(2)}) copy-start(bf16[256,3,64]{0,2,1:T(8,128)(2,1)S(1)} %convert_element_type.730) | copy-start | bytes 294916
  105.4 137.0 %all-reduce.21.cloned.1.call-start = ((), (), s32[]{:S(2)}) async-start(), calls=%async_computation.22 | async-start | bytes 1966080 | tf_op jit(solution)/shard_map/psum | solution.py:49
  105.7 142.9 %copy-start.114 = (s32[1,1,256,2]{2,3,1,0:T(2,128)}, s32[1,1,256,2]{2,3,1,0:T(2,128)S(1)}, u32[]{:S(2)}) copy-start(s32[1,1,256,2]{2,3,1,0:T(2,128)S(1)} %get-tuple-element.2318) | copy-start | bytes 6148
  192.5 54.9 %copy-start.92 = (bf16[1,768,4]{1,2,0:T(4,128)(2,1)S(1)}, bf16[1,768,4]{1,2,0:T(4,128)(2,1)}, u32[]{:S(2)}) copy-start(bf16[1,768,4]{1,2,0:T(4,128)(2,1)} %param.34) | copy-start | bytes 18436
  242.4 28.9 %all-to-all-start.1 = ((bf16[4,1,160,768]{3,2,1,0:T(8,128)(2,1)}), bf16[4,1,160,768]{3,2,1,0:T(8,128)(2,1)S(1)}, u32[]{:S(2)}, u32[]{:S(2)}) async-start(bf16[4,1,160,768]{3,2,1,0:T(8,128)(2,1)} %bitcast.1008), calls=%async_computation.1 | async-start | bytes 1966080 | tf_op jit(solution)/shard_map/all_to_all | solution.py:53
  247.0 139.3 %all-reduce.23.cloned.1.call-start = ((), (), s32[]{:S(2)}) async-start(), calls=%async_computation.23 | async-start | bytes 786432 | tf_op jit(solution)/shard_map/psum | solution.py:45
  281.3 2.8 collective-permute-start
  284.2 102.1 %copy-start.4 = (bf16[256,768]{1,0:T(8,128)(2,1)}, bf16[256,768]{1,0:T(8,128)(2,1)S(1)}, u32[]{:S(2)}) copy-start(bf16[256,768]{1,0:T(8,128)(2,1)S(1)} %collective-permute-done) | copy-start | bytes 1179652
  332.2 54.1 %copy-start.41 = (bf16[256,768]{1,0:T(8,128)(2,1)S(1)}, bf16[256,768]{1,0:T(8,128)(2,1)}, u32[]{:S(2)}) copy-start(bf16[256,768]{1,0:T(8,128)(2,1)} %all-reduce.19.cloned.1.call-done) | copy-start | bytes 1179652
  341.9 46.6 %copy-start.98 = (f32[3,256]{1,0:T(4,128)}, f32[3,256]{1,0:T(4,128)S(1)}, u32[]{:S(2)}) copy-start(f32[3,256]{1,0:T(4,128)S(1)} %get-tuple-element.3266) | copy-start | bytes 9220
  342.8 45.7 %copy-start.79 = (bf16[256,3,64]{0,2,1:T(8,128)(2,1)}, bf16[256,3,64]{0,2,1:T(8,128)(2,1)S(1)}, u32[]{:S(2)}) copy-start(bf16[256,3,64]{0,2,1:T(8,128)(2,1)S(1)} %convert_element_type.749) | copy-start | bytes 294916
  395.5 28.8 %all-to-all-start.2 = ((bf16[4,1,160,768]{3,2,1,0:T(8,128)(2,1)}), bf16[4,1,160,768]{3,2,1,0:T(8,128)(2,1)}, u32[]{:S(2)}, u32[]{:S(2)}) async-start(bf16[4,1,160,768]{3,2,1,0:T(8,128)(2,1)} %bitcast.981), calls=%async_computation.2 | async-start | bytes 1966080 | tf_op jit(solution)/shard_map/all_to_all | solution.py:61
  424.2 27.3 %all-to-all-start.4 = ((bf16[4,1,160,768]{3,2,1,0:T(8,128)(2,1)}), bf16[4,1,160,768]{3,2,1,0:T(8,128)(2,1)S(1)}, u32[]{:S(2)}, u32[]{:S(2)}) async-start(bf16[4,1,160,768]{3,2,1,0:T(8,128)(2,1)} %bitcast.70), calls=%async_computation.4 | async-start | bytes 1966080 | tf_op jit(solution)/shard_map/all_to_all | solution.py:57
  427.7 97.0 %all-reduce.37.cloned.1.call-start = ((), (), s32[]{:S(2)}) async-start(), calls=%async_computation.39 | async-start | bytes 3932160 | tf_op jit(solution)/shard_map/psum | solution.py:49
  553.8 27.3 %all-to-all-start.3 = ((bf16[4,1,160,768]{3,2,1,0:T(8,128)(2,1)}), bf16[4,1,160,768]{3,2,1,0:T(8,128)(2,1)S(1)}, u32[]{:S(2)}, u32[]{:S(2)}) async-start(bf16[4,1,160,768]{3,2,1,0:T(8,128)(2,1)} %bitcast.1007), calls=%async_computation.3 | async-start | bytes 1966080 | tf_op jit(solution)/shard_map/all_to_all | solution.py:53
  557.3 92.4 %reduce-scatter.19.cloned.1.call-start = ((), (), s32[]{:S(2)}) async-start(), calls=%async_computation.25 | async-start | bytes 491520 | tf_op jit(solution)/shard_map/reduce_scatter | solution.py:423
  630.8 40.6 %reduce-scatter.17.cloned.1.call-start = ((), (), s32[]{:S(2)}) async-start(), calls=%async_computation.24 | async-start | bytes 491520 | tf_op jit(solution)/shard_map/reduce_scatter | solution.py:417
  631.4 85.9 %all-reduce.25.cloned.1.call-start = ((), (), s32[]{:S(2)}) async-start(), calls=%async_computation.26 | async-start | bytes 786432 | tf_op jit(solution)/shard_map/psum | solution.py:45
  640.1 77.1 %copy-start.5 = (bf16[256,768]{1,0:T(8,128)(2,1)S(1)}, bf16[256,768]{1,0:T(8,128)(2,1)}, u32[]{:S(2)}) copy-start(bf16[256,768]{1,0:T(8,128)(2,1)} %copy-done.4) | copy-start | bytes 1179652
  640.1 77.1 %copy-start.90 = (f32[768]{0:T(1024)S(1)}, f32[768]{0:T(1024)}, u32[]{:S(2)}) copy-start(f32[768]{0:T(1024)} %copy-done.89) | copy-start | bytes 9220
  640.1 35.2 %collective-permute-start.2 = (bf16[256,768]{1,0:T(8,128)(2,1)}, bf16[256,768]{1,0:T(8,128)(2,1)S(1)}, u32[]{:S(2)}, u32[]{:S(2)}) collective-permute-start(bf16[256,768]{1,0:T(8,128)(2,1)} %get-tuple-element.2258), channel_id=1, source_target_pairs={{0,16},{1,17},{2,18},{3,19},{4,20},{5,21},{6,22},{7,23},{8,24},{9,... | collective-permute-start | bytes 1179656 | tf_op jit(solution)/shard_map/ppermute | solution.py:21
  674.0 150.4 %all-reduce.27.cloned.1.call-start = ((), (), s32[]{:S(2)}) async-start(), calls=%async_computation.27 | async-start | bytes 786432 | tf_op jit(solution)/shard_map/psum | solution.py:45
  675.3 46.7 %copy-start.42 = (bf16[256,768]{1,0:T(8,128)(2,1)}, bf16[256,768]{1,0:T(8,128)(2,1)S(1)}, u32[]{:S(2)}) copy-start(bf16[256,768]{1,0:T(8,128)(2,1)S(1)} %collective-permute-done.2) | copy-start | bytes 1179652
  768.2 56.2 %copy-start.43 = (bf16[256,768]{1,0:T(8,128)(2,1)S(1)}, bf16[256,768]{1,0:T(8,128)(2,1)}, u32[]{:S(2)}) copy-start(bf16[256,768]{1,0:T(8,128)(2,1)} %copy-done.42) | copy-start | bytes 1179652
  778.1 48.9 %copy-start.96 = (f32[3,256]{1,0:T(4,128)}, f32[3,256]{1,0:T(4,128)S(1)}, u32[]{:S(2)}) copy-start(f32[3,256]{1,0:T(4,128)S(1)} %get-tuple-element.3265) | copy-start | bytes 9220
  779.1 48.0 %copy-start.74 = (bf16[256,3,64]{0,2,1:T(8,128)(2,1)}, bf16[256,3,64]{0,2,1:T(8,128)(2,1)S(1)}, u32[]{:S(2)}) copy-start(bf16[256,3,64]{0,2,1:T(8,128)(2,1)S(1)} %convert_element_type.793) | copy-start | bytes 294916
  780.1 47.0 %collective-permute-start.1 = (bf16[256,768]{1,0:T(8,128)(2,1)}, bf16[256,768]{1,0:T(8,128)(2,1)}, u32[]{:S(2)}, u32[]{:S(2)}) collective-permute-start(bf16[256,768]{1,0:T(8,128)(2,1)} %get-tuple-element.2286), channel_id=1, source_target_pairs={{16,0},{17,1},{18,2},{19,3},{20,4},{21,5},{22,6},{23,7},{24,8},{25... | collective-permute-start | bytes 1179656 | tf_op jit(solution)/shard_map/ppermute | solution.py:21
  829.5 174.3 %copy-start.148 = (f32[256]{0:T(256)}, f32[256]{0:T(256)S(1)}, u32[]{:S(2)}) copy-start(f32[256]{0:T(256)S(1)} %get-tuple-element.2252) | copy-start | bytes 3076
  838.0 28.6 %all-to-all-start.7 = ((bf16[4,1,160,768]{3,2,1,0:T(8,128)(2,1)}), bf16[4,1,160,768]{3,2,1,0:T(8,128)(2,1)}, u32[]{:S(2)}, u32[]{:S(2)}) async-start(bf16[4,1,160,768]{3,2,1,0:T(8,128)(2,1)} %bitcast.980), calls=%async_computation.9 | async-start | bytes 1966080 | tf_op jit(solution)/shard_map/all_to_all | solution.py:61
  866.6 27.3 %all-to-all-start.6 = ((bf16[4,1,160,768]{3,2,1,0:T(8,128)(2,1)}), bf16[4,1,160,768]{3,2,1,0:T(8,128)(2,1)S(1)}, u32[]{:S(2)}, u32[]{:S(2)}) async-start(bf16[4,1,160,768]{3,2,1,0:T(8,128)(2,1)} %bitcast.104), calls=%async_computation.8 | async-start | bytes 1966080 | tf_op jit(solution)/shard_map/all_to_all | solution.py:57
  870.2 97.0 %all-reduce.35.cloned.1.call-start = ((), (), s32[]{:S(2)}) async-start(), calls=%async_computation.38 | async-start | bytes 3932160 | tf_op jit(solution)/shard_map/psum | solution.py:49
  996.3 27.3 %all-to-all-start.9 = ((bf16[4,1,160,768]{3,2,1,0:T(8,128)(2,1)}), bf16[4,1,160,768]{3,2,1,0:T(8,128)(2,1)S(1)}, u32[]{:S(2)}, u32[]{:S(2)}) async-start(bf16[4,1,160,768]{3,2,1,0:T(8,128)(2,1)} %bitcast.1006), calls=%async_computation.11 | async-start | bytes 1966080 | tf_op jit(solution)/shard_map/all_to_all | solution.py:53
  999.8 99.7 %reduce-scatter.23.cloned.1.call-start = ((), (), s32[]{:S(2)}) async-start(), calls=%async_computation.29 | async-start | bytes 491520 | tf_op jit(solution)/shard_map/reduce_scatter | solution.py:423
  1080.6 45.3 %copy-start.151 = (s32[512,1]{0,1:T(1,128)S(1)}, s32[512,1]{0,1:T(1,128)}, u32[]{:S(2)}) copy-start(s32[512,1]{0,1:T(1,128)} %get-tuple-element.2311) | copy-start | bytes 6148
  1080.6 45.9 %copy-start.143 = (f32[256]{0:T(256)S(1)}, f32[256]{0:T(256)}, u32[]{:S(2)}) copy-start(f32[256]{0:T(256)} %get-tuple-element.2250) | copy-start | bytes 3076
  1080.6 86.6 %copy-start.91 = (f32[768]{0:T(1024)S(1)}, f32[768]{0:T(1024)}, u32[]{:S(2)}) copy-start(f32[768]{0:T(1024)} %copy-done.89) | copy-start | bytes 9220
  1080.6 40.7 %reduce-scatter.21.cloned.1.call-start = ((), (), s32[]{:S(2)}) async-start(), calls=%async_computation.28 | async-start | bytes 491520 | tf_op jit(solution)/shard_map/reduce_scatter | solution.py:417
  1081.4 85.8 %all-reduce.29.cloned.1.call-start = ((), (), s32[]{:S(2)}) async-start(), calls=%async_computation.30 | async-start | bytes 786432 | tf_op jit(solution)/shard_map/psum | solution.py:45
  1082.3 87.0 %copy-start.103 = (bf16[256,3,64]{0,2,1:T(8,128)(2,1)}, bf16[256,3,64]{0,2,1:T(8,128)(2,1)S(1)}, u32[]{:S(2)}) copy-start(bf16[256,3,64]{0,2,1:T(8,128)(2,1)S(1)} %convert_element_type.818) | copy-start | bytes 294916
  1121.3 48.1 %copy-start.13 = (f32[256,768]{1,0:T(8,128)S(1)}, f32[256,768]{1,0:T(8,128)}, u32[]{:S(2)}) copy-start(f32[256,768]{1,0:T(8,128)} %copy-done.12) | copy-start | bytes 2359300
  1172.0 8.1 collective-permute-start.3
  1193.9 29.9 %all-to-all-start.10 = ((bf16[4,1,160,768]{3,2,1,0:T(8,128)(2,1)}), bf16[4,1,160,768]{3,2,1,0:T(8,128)(2,1)}, u32[]{:S(2)}, u32[]{:S(2)}) async-start(bf16[4,1,160,768]{3,2,1,0:T(8,128)(2,1)} %bitcast.142), calls=%async_computation.14 | async-start | bytes 1966080 | tf_op jit(solution)/shard_map/all_to_all | solution.py:57
  1198.5 82.4 %all-reduce.31.cloned.1.call-start = ((), (), s32[]{:S(2)}) async-start(), calls=%async_computation.31 | async-start | bytes 1966080 | tf_op jit(solution)/shard_map/psum | solution.py:49
  1238.6 46.9 %copy-start.116 = (f32[768,4]{0,1:T(4,128)S(1)}, f32[768,4]{0,1:T(4,128)}, u32[]{:S(2)}) copy-start(f32[768,4]{0,1:T(4,128)} %fusion.311) | copy-start | bytes 36868
  1238.6 46.9 %copy-start.119 = (f32[256,4]{0,1:T(4,128)S(1)}, f32[256,4]{0,1:T(4,128)}, u32[]{:S(2)}) copy-start(f32[256,4]{0,1:T(4,128)} %fusion.375) | copy-start | bytes 12292
  1280.9 36.5 %all-to-all-start.11 = ((bf16[4,1,160,768]{3,2,1,0:T(8,128)(2,1)}), bf16[4,1,160,768]{3,2,1,0:T(8,128)(2,1)S(1)}, u32[]{:S(2)}, u32[]{:S(2)}) async-start(bf16[4,1,160,768]{3,2,1,0:T(8,128)(2,1)} %bitcast.1005), calls=%async_computation.15 | async-start | bytes 1966080 | tf_op jit(solution)/shard_map/all_to_all | solution.py:53
  1285.5 31.1 %reduce-scatter.33.cloned.1.call-start = ((), (), s32[]{:S(2)}) async-start(), calls=%async_computation.37 | async-start | bytes 245760
  1296.6 119.6 %reduce-scatter.27.cloned.1.call-start = ((), (), s32[]{:S(2)}) async-start(), calls=%async_computation.33 | async-start | bytes 491520 | tf_op jit(solution)/shard_map/reduce_scatter | solution.py:423
  1361.1 55.0 %reduce-scatter.25.cloned.1.call-start = ((), (), s32[]{:S(2)}) async-start(), calls=%async_computation.32 | async-start | bytes 491520 | tf_op jit(solution)/shard_map/reduce_scatter | solution.py:417
  1369.0 64.0 %reduce-scatter.31.cloned.1.call-start = ((), (), s32[]{:S(2)}) async-start(), calls=%async_computation.36 | async-start | bytes 491520
  1413.2 65.2 %all-reduce.33.cloned.1.call-start = ((), (), s32[]{:S(2)}) async-start(), calls=%async_computation.34 | async-start | bytes 786432 | tf_op jit(solution)/shard_map/psum | solution.py:45
  1418.8 88.2 %reduce-scatter.29.cloned.1.call-start = ((), (), s32[]{:S(2)}) async-start(), calls=%async_computation.35 | async-start | bytes 1228800
  1427.5 50.9 %copy-start.6 = (bf16[256,768]{1,0:T(8,128)(2,1)S(1)}, bf16[256,768]{1,0:T(8,128)(2,1)}, u32[]{:S(2)}) copy-start(bf16[256,768]{1,0:T(8,128)(2,1)} %copy-done.4) | copy-start | bytes 1179652
  1427.5 50.9 %copy-start.44 = (bf16[256,768]{1,0:T(8,128)(2,1)S(1)}, bf16[256,768]{1,0:T(8,128)(2,1)}, u32[]{:S(2)}) copy-start(bf16[256,768]{1,0:T(8,128)(2,1)} %copy-done.42) | copy-start | bytes 1179652
  1431.7 48.7 %copy-start.132 = (f32[768]{0:T(1024)S(1)}, f32[768]{0:T(1024)}, u32[]{:S(2)}) copy-start(f32[768]{0:T(1024)} %get-tuple-element.2078) | copy-start | bytes 9220
  1433.0 47.4 %copy-start.134 = (f32[768]{0:T(1024)S(1)}, f32[768]{0:T(1024)}, u32[]{:S(2)}) copy-start(f32[768]{0:T(1024)} %get-tuple-element.2080) | copy-start | bytes 9220
  1433.0 64.1 %copy-start.141 = (f32[256]{0:T(256)S(1)}, f32[256]{0:T(256)}, u32[]{:S(2)}) copy-start(f32[256]{0:T(256)} %get-tuple-element.2082) | copy-start | bytes 3076
  (154 other events, 960.2 us)
Sparse Core Ops, SparseCore 0:
  105.5 44.8 all-reduce.18
  192.7 49.6 all-reduce.20
  344.1 42.1 all-reduce.22
  459.0 65.7 all-reduce.36
  630.9 18.7 reduce-scatter.18
  652.5 18.8 reduce-scatter.16
  674.9 42.3 all-reduce.24
  780.3 44.0 all-reduce.26
  901.4 65.7 all-reduce.34
  1080.7 18.7 reduce-scatter.22
  1102.5 18.8 reduce-scatter.20
  1124.7 42.3 all-reduce.28
  1231.1 49.7 all-reduce.30
  1296.7 19.8 reduce-scatter.32
  1361.3 19.0 reduce-scatter.26
  1382.6 18.8 reduce-scatter.24
  1413.3 19.0 reduce-scatter.30
  1436.1 42.2 all-reduce.32
  1480.8 26.1 reduce-scatter.28
where the time goes:
time: 1530 us; the launch traced here: 1520 us
  waiting for transfers between devices  688 us (45%)
  matrix products  230 us (15%)
  local copies, waits for them, and re-layouts  200 us (13%)
  blocking collectives  194 us (13%)
  other arithmetic  140 us (9%)
  starting transfers between devices  45.9 us (3%)
  between operations  18 us (1%)
    psum x6, waiting for transfers between devices, heads_total(): return lax.psum(values.astype(jnp.bfloat16), 'heads').astype(jnp.float32)  247 us
    psum x4, waiting for transfers between devices, rows_total(): return lax.psum(values.astype(jnp.bfloat16), 'heads').astype(jnp.float32)  224 us
    all_to_all x2, blocking collectives, send_back(): lax.all_to_all(values, 'ctx', split_axis=0, concat_axis=0, tiled=True)  58.2 us
    all_to_all x3, waiting for transfers between devices, back_send(): lax.all_to_all(values, 'ctx', split_axis=0, concat_axis=0, tiled=True)  50.6 us
    all_gather x3, blocking collectives, layer_forward(): lax.all_gather(projected[1], 'ctx', axis=0, tiled=True)  47.6 us
    all_gather x3, blocking collectives, layer_forward(): lax.all_gather(projected[2], 'ctx', axis=0, tiled=True)  47.1 us
    all_to_all x4, waiting for transfers between devices, send_back(): lax.all_to_all(values, 'ctx', split_axis=0, concat_axis=0, tiled=True)  46 us
    reduce_scatter x3, waiting for transfers between devices, layer_backward_input(): lax.psum_scatter(dkey_all.reshape(-1, head_count * HD).astype(jnp.bfloat1...  43.5 us
  transfers between devices with their start and end apart: 32, of which 25 were waited for; matrix products, arithmetic and copies ran while one was open for 13% of the time, Pallas kernels for 0%

commit v1 on v0

v1 whole, which is shorter than its diff:
```python
import math

import jax
import jax.numpy as jnp
from jax import lax
from jax.experimental import pallas as pl
from jax.experimental.pallas import tpu as pltpu
from jax.sharding import PartitionSpec as P

HD = 64
BUCKETS = 32
REACH = 128
EPSILON = 1e-06
NEGATIVE = -1e30
F32 = jnp.float32
BF16 = jnp.bfloat16
LANES = 128
VMEM_BYTES = 40 * 1024 * 1024
ROOT_2_PI = math.sqrt(2.0 / math.pi)


def kernel_call(body, outs, args, scratch=(), flops=0):
    def spec(a):
        scalar = a.ndim == 1 and a.dtype == jnp.int32
        return pl.BlockSpec(memory_space=pltpu.SMEM if scalar else pltpu.VMEM)

    size = sum(math.prod(a.shape) * a.dtype.itemsize for a in list(args) + list(outs))
    return pl.pallas_call(
        body,
        out_shape=outs,
        in_specs=[spec(a) for a in args],
        out_specs=[pl.BlockSpec(memory_space=pltpu.VMEM)] * len(outs),
        scratch_shapes=list(scratch),
        compiler_params=pltpu.CompilerParams(vmem_limit_bytes=VMEM_BYTES),
        cost_estimate=pl.CostEstimate(flops=flops, bytes_accessed=size, transcendentals=0),
    )(*args)


def like(*shape, dtype=BF16):
    return jax.ShapeDtypeStruct(shape, dtype)


def dot(a, b, contract=((1,), (0,))):
    return lax.dot_general(a, b, (contract, ((), ())), preferred_element_type=F32)


def dot_nt(a, b):
    return dot(a, b, ((1,), (1,)))


def dot_tn(a, b):
    return dot(a, b, ((0,), (0,)))


def swap(array, axis, by=1):
    devices = lax.axis_size(axis)
    return lax.ppermute(array, axis, [(i, i ^ by) for i in range(devices)])


def one_way(array, source):
    return lax.ppermute(array, "section", [(source, 1 - source)])


def exchange(chunks, axis):
    return [chunks[0]] + [swap(chunks[r], axis, r) for r in range(1, len(chunks))]


def gather_rows(array, axis):
    return lax.all_gather(array, axis, axis=0, tiled=True)


def project_rows(x, gain, w_ref, normed_ref, q_ref, kv_ref):
    width = q_ref.shape[1]
    scale = lax.rsqrt(jnp.mean(x * x, axis=-1, keepdims=True) + EPSILON)
    normed = (x * scale * gain).astype(BF16)
    normed_ref[...] = normed
    q_ref[...] = dot(normed, w_ref[0]).astype(BF16)
    kv_ref[:, :width] = dot(normed, w_ref[1]).astype(BF16)
    kv_ref[:, width:] = dot(normed, w_ref[2]).astype(BF16)


def project(x, gain, qkv):
    rows, model = x.shape
    width = qkv.shape[2]

    def body(x_ref, gain_ref, w_ref, *outs):
        project_rows(x_ref[...].astype(F32), gain_ref[...], w_ref, *outs)

    return kernel_call(
        body,
        [like(rows, model), like(rows, width), like(rows, 2 * width)],
        [x, gain, qkv],
        flops=6 * rows * model * width,
    )


def score_rows(q, keys, table_ref, scores_ref, head, query_block, n_ctx):
    half = q.shape[0]
    raw = dot_nt(q, keys)
    for key_tile in range(2 * n_ctx):
        owner = key_tile // 2
        key_block = owner if key_tile % 2 == 0 else 2 * n_ctx - 1 - owner
        pick = jnp.clip(query_block - key_block, -1, 2) + 1
        span = slice(key_tile * half, (key_tile + 1) * half)
        scores_ref[:, span] = raw[:, span] * 0.125 + table_ref[head, pick]


def attend(place, q, kv_all, table, n_ctx):
    rows, width = q.shape
    half, heads, keys = rows // 2, width // HD, kv_all.shape[0]

    def body(place_ref, q_ref, kv_ref, table_ref, mix_ref, lse_ref, scores_ref):
        mine = place_ref[0]
        for head in range(heads):
            cols = slice(head * HD, (head + 1) * HD)
            key_rows = kv_ref[:, cols]
            value_rows = kv_ref[:, width + head * HD : width + (head + 1) * HD]
            for part in range(2):
                span = slice(part * half, (part + 1) * half)
                block = mine if part == 0 else 2 * n_ctx - 1 - mine
                score_rows(q_ref[span, cols], key_rows, table_ref, scores_ref, head, block, n_ctx)
                scores = scores_ref[...]
                top = jnp.max(scores, axis=1, keepdims=True)
                mass = jnp.exp(scores - top)
                total = jnp.sum(mass, axis=1, keepdims=True)
                out = dot(mass.astype(BF16), value_rows) / total
                mix_ref[span, cols] = out.astype(BF16)
                lse_ref[span, head : head + 1] = top + jnp.log(total)

    return kernel_call(
        body,
        [like(rows, width), like(rows, heads, dtype=F32)],
        [place, q, kv_all, table],
        [pltpu.VMEM((half, keys), F32)],
        flops=4 * rows * keys * width,
    )


def attend_back(place, q, kv_all, table, lse, dmix, n_ctx):
    rows, width = q.shape
    half, heads, keys = rows // 2, width // HD, kv_all.shape[0]

    def body(place_ref, q_ref, kv_ref, table_ref, lse_ref, dmix_ref, dq_ref, dtable_ref, *rest):
        chunk_refs, (scores_ref, total_ref) = rest[:n_ctx], rest[n_ctx:]
        mine = place_ref[0]
        dtable_ref[...] = jnp.zeros(dtable_ref.shape, F32)
        for head in range(heads):
            cols = slice(head * HD, (head + 1) * HD)
            value_cols = slice(width + head * HD, width + (head + 1) * HD)
            key_rows = kv_ref[:, cols]
            value_rows = kv_ref[:, value_cols]
            for part in range(2):
                span = slice(part * half, (part + 1) * half)
                block = mine if part == 0 else 2 * n_ctx - 1 - mine
                q = q_ref[span, cols]
                dmix = dmix_ref[span, cols]
                score_rows(q, key_rows, table_ref, scores_ref, head, block, n_ctx)
                probs = jnp.exp(scores_ref[...] - lse_ref[span, head : head + 1])
                dprobs = dot_nt(dmix, value_rows)
                delta = jnp.sum(probs * dprobs, axis=1, keepdims=True)
                dscores = (probs * (dprobs - delta)).astype(BF16)
                dq_ref[span, cols] = (dot(dscores, key_rows) * 0.125).astype(BF16)
                dkeys = dot_tn(dscores, q) * 0.125
                dvalues = dot_tn(probs.astype(BF16), dmix)
                if part == 0:
                    total_ref[:, cols] = dkeys
                    total_ref[:, value_cols] = dvalues
                else:
                    total_ref[:, cols] += dkeys
                    total_ref[:, value_cols] += dvalues
                for key_tile in range(2 * n_ctx):
                    owner = key_tile // 2
                    key_block = owner if key_tile % 2 == 0 else 2 * n_ctx - 1 - owner
                    pick = jnp.clip(block - key_block, -1, 2) + 1
                    tile = dscores[:, key_tile * half : (key_tile + 1) * half]
                    dtable_ref[head, pick] += tile.astype(F32)
        for r in range(n_ctx):
            first = pl.multiple_of((mine ^ r) * rows, rows)
            chunk_refs[r][...] = total_ref[pl.ds(first, rows), :].astype(BF16)

    outs = kernel_call(
        body,
        [like(rows, width), like(*table.shape, dtype=F32)] + [like(rows, 2 * width)] * n_ctx,
        [place, q, kv_all, table, lse, dmix],
        [pltpu.VMEM((half, keys), F32), pltpu.VMEM((keys, 2 * width), F32)],
        flops=10 * rows * keys * width,
    )
    return outs[0], outs[1], outs[2:]


def slot_picks(slots_ref, first, count):
    ids = first + lax.broadcasted_iota(jnp.int32, (count, slots_ref.shape[1]), 0)
    hit = (ids == slots_ref[0:1, :]) | (ids == slots_ref[1:2, :])
    return jnp.where(hit, 1.0, 0.0).astype(BF16)


def token_picks(slots_ref, count):
    ids = lax.broadcasted_iota(jnp.int32, (slots_ref.shape[0], count), 1)
    hit = (ids == slots_ref[:, 0:1]) | (ids == slots_ref[:, 1:2])
    return jnp.where(hit, 1.0, 0.0).astype(BF16)


def dispatch_into(rows, place_ref, slots_ref, chunk_refs):
    per = chunk_refs[0].shape[0]
    first = place_ref[1] * (per * len(chunk_refs))
    for r, chunk_ref in enumerate(chunk_refs):
        picks = slot_picks(slots_ref, first + r * per, per)
        chunk_ref[...] = dot(picks, rows).astype(BF16)


def dispatch(place, rows, slots, n_ctx, per):
    model = rows.shape[1]

    def body(place_ref, rows_ref, slots_ref, *chunk_refs):
        dispatch_into(rows_ref[...], place_ref, slots_ref, chunk_refs)

    return kernel_call(body, [like(per, model)] * n_ctx, [place, rows, slots])


def finish_attention(place, mixes, out_w, x, gain, slots, n_ctx, per):
    rows, model = x.shape
    n_heads, width = len(mixes), mixes[0].shape[1]

    def body(place_ref, *refs):
        mix_refs, refs = refs[:n_heads], refs[n_heads:]
        w_ref, x_ref, gain_ref, slots_ref, middle_ref = refs[:5]
        chunk_refs, mixed_ref = refs[5:-1], refs[-1]
        for r in range(n_heads):
            mixed_ref[place_ref[1] ^ r] = mix_refs[r][...]
        middle = x_ref[...].astype(F32)
        attended = dot(mixed_ref[0], w_ref[:width, :])
        for h in range(1, n_heads):
            attended += dot(mixed_ref[h], w_ref[h * width : (h + 1) * width, :])
        middle = middle + attended
        middle_ref[...] = middle
        scale = lax.rsqrt(jnp.mean(middle * middle, axis=-1, keepdims=True) + EPSILON)
        expert_in = (middle * scale * gain_ref[...]).astype(BF16)
        dispatch_into(expert_in, place_ref, slots_ref, chunk_refs)

    outs = kernel_call(
        body,
        [like(rows, model, dtype=F32)] + [like(per, model)] * n_ctx,
        [place, *mixes, out_w, x, gain, slots],
        [pltpu.VMEM((n_heads, rows, width), BF16)],
        flops=2 * rows * model * model + 2 * rows * model * per * n_ctx,
    )
    return outs[0], outs[1:]


def gelu_parts(v):
    inner = jnp.tanh(ROOT_2_PI * (v + 0.044715 * v * v * v))
    return inner, 0.5 * v * (1.0 + inner)


def experts(place, arrived, up, down, router, other, n_heads):
    slots, model = arrived.shape
    per, hidden_width = slots // n_heads, up.shape[1]

    def body(place_ref, in_ref, up_ref, down_ref, router_ref, other_ref, *refs):
        chunk_refs, (pre_ref, hidden_ref, margin_ref) = refs[:n_heads], refs[n_heads:]
        for r in range(n_heads):
            span = pl.ds(pl.multiple_of((place_ref[1] ^ r) * per, per), per)
            rows = in_ref[span, :]
            logits = dot(rows, router_ref[...])
            lane = lax.broadcasted_iota(jnp.int32, logits.shape, 1)
            signs = jnp.where(lane == place_ref[0], 1.0, 0.0) - jnp.where(
                lane == other_ref[span, :], 1.0, 0.0
            )
            margin = jnp.sum(logits * signs, axis=1, keepdims=True)
            margin_ref[span, :] = margin
            gate = 1.0 / (1.0 + jnp.exp(-margin))
            pre_act = dot(rows, up_ref[...])
            pre_ref[span, :] = pre_act
            hidden = gelu_parts(pre_act)[1].astype(BF16)
            hidden_ref[span, :] = hidden
            chunk_refs[r][...] = (gate * dot(hidden, down_ref[...])).astype(BF16)

    outs = kernel_call(
        body,
        [like(per, model)] * n_heads
        + [
            like(slots, hidden_width, dtype=F32),
            like(slots, hidden_width),
            like(slots, 1, dtype=F32),
        ],
        [place, arrived, up, down, router, other],
        flops=4 * slots * model * hidden_width,
    )
    return outs[:n_heads], outs[n_heads:]


def experts_back(place, dout_rows, kept, up, down, router, other, n_heads):
    pre_act, hidden, margin = kept
    slots, model = dout_rows.shape
    per, hidden_width = slots // n_heads, up.shape[1]

    def body(place_ref, dout_ref, pre_ref, hidden_ref, margin_ref, up_ref, down_ref, router_ref, other_ref, *refs):
        chunk_refs, (dpre_ref, dslots_ref, dlogits_ref) = refs[:n_heads], refs[n_heads:]
        for r in range(n_heads):
            span = pl.ds(pl.multiple_of((place_ref[1] ^ r) * per, per), per)
            dout = dout_ref[span, :]
            dhidden = dot_nt(dout, down_ref[...])
            margin = margin_ref[span, :]
            gate = 1.0 / (1.0 + jnp.exp(-margin))
            other_gate = 1.0 / (1.0 + jnp.exp(margin))
            dgate = jnp.sum(dhidden * hidden_ref[span, :].astype(F32), axis=1, keepdims=True)
            v = pre_ref[span, :]
            inner, _ = gelu_parts(v)
            slope = 0.5 * (1.0 + inner) + 0.5 * v * (1.0 - inner * inner) * ROOT_2_PI * (
                1.0 + 3.0 * 0.044715 * v * v
            )
            dpre = (gate * dhidden * slope).astype(BF16)
            dpre_ref[span, :] = dpre
            dslots_ref[span, :] = (gate * dout.astype(F32)).astype(BF16)
            lane = lax.broadcasted_iota(jnp.int32, (per, LANES), 1)
            signs = jnp.where(lane == place_ref[0], 1.0, 0.0) - jnp.where(
                lane == other_ref[span, :], 1.0, 0.0
            )
            dlogits = (gate * other_gate * dgate * signs).astype(BF16)
            dlogits_ref[span, :] = dlogits
            chunk_refs[r][...] = (
                dot_nt(dpre, up_ref[...]) + dot_nt(dlogits, router_ref[...])
            ).astype(BF16)

    outs = kernel_call(
        body,
        [like(per, model)] * n_heads
        + [like(slots, hidden_width), like(slots, model), like(slots, LANES)],
        [place, dout_rows, pre_act, hidden, margin, up, down, router, other],
        flops=4 * slots * model * hidden_width,
    )
    return outs[:n_heads], outs[n_heads:]


def combine(middle, returned, tokens):
    rows, model = middle.shape

    def body(middle_ref, returned_ref, tokens_ref, out_ref):
        picks = token_picks(tokens_ref, returned_ref.shape[0])
        out_ref[...] = middle_ref[...] + dot(picks, returned_ref[...])

    return kernel_call(
        body,
        [like(rows, model, dtype=F32)],
        [middle, returned, tokens],
        flops=2 * rows * model * returned.shape[0],
    )[0]


def combine_project(middle, returned, tokens, gain, qkv):
    rows, model = middle.shape
    width = qkv.shape[2]

    def body(middle_ref, returned_ref, tokens_ref, gain_ref, w_ref, passed_ref, *outs):
        picks = token_picks(tokens_ref, returned_ref.shape[0])
        passed = (middle_ref[...] + dot(picks, returned_ref[...])).astype(BF16)
        passed_ref[...] = passed
        project_rows(passed.astype(F32), gain_ref[...], w_ref, *outs)

    return kernel_call(
        body,
        [like(rows, model), like(rows, model), like(rows, width), like(rows, 2 * width)],
        [middle, returned, tokens, gain, qkv],
        flops=2 * rows * model * returned.shape[0] + 6 * rows * model * width,
    )


def norm_back(values, gain, upstream):
    scale = lax.rsqrt(jnp.mean(values * values, axis=-1, keepdims=True) + EPSILON)
    unit = values * scale
    scaled = upstream * gain
    dvalues = scale * (scaled - unit * jnp.mean(unit * scaled, axis=-1, keepdims=True))
    return dvalues, jnp.sum(upstream * unit, axis=0, keepdims=True)


def middle_back(returned, tokens, middle, gain, dout, out_w):
    rows, model = middle.shape
    width = out_w.shape[0]

    def body(returned_ref, tokens_ref, middle_ref, gain_ref, dout_ref, w_ref, dmiddle_ref, datt_ref, dmix_ref, dgain_ref):
        picks = token_picks(tokens_ref, returned_ref.shape[0])
        dexpert_in = dot(picks, returned_ref[...])
        part, dgain = norm_back(middle_ref[...], gain_ref[...], dexpert_in)
        dgain_ref[...] = dgain
        dmiddle = dout_ref[...].astype(F32) + part
        dmiddle_ref[...] = dmiddle
        datt = dmiddle.astype(BF16)
        datt_ref[...] = datt
        dmix_ref[...] = dot_nt(datt, w_ref[...]).astype(BF16)

    return kernel_call(
        body,
        [
            like(rows, model, dtype=F32),
            like(rows, model),
            like(rows, width),
            like(1, model, dtype=F32),
        ],
        [returned, tokens, middle, gain, dout, out_w],
        flops=2 * rows * model * (returned.shape[0] + width),
    )


def project_back(place, dq, dkv_parts, qkv, n_heads):
    rows, width = dq.shape
    model, n_parts = qkv.shape[1], len(dkv_parts)
    share = rows // n_heads

    def body(place_ref, dq_ref, *refs):
        part_refs, refs = refs[:n_parts], refs[n_parts:]
        w_ref, dkv_ref = refs[:2]
        chunk_refs, total_ref = refs[2:-1], refs[-1]
        dkv = part_refs[0][...].astype(F32)
        for ref in part_refs[1:]:
            dkv += ref[...].astype(F32)
        dkv = dkv.astype(BF16)
        dkv_ref[...] = dkv
        total_ref[...] = (
            dot_nt(dq_ref[...], w_ref[0])
            + dot_nt(dkv[:, :width], w_ref[1])
            + dot_nt(dkv[:, width:], w_ref[2])
        )
        for r in range(n_heads):
            first = pl.multiple_of((place_ref[1] ^ r) * share, share)
            chunk_refs[r][...] = total_ref[pl.ds(first, share), :].astype(BF16)

    outs = kernel_call(
        body,
        [like(rows, 2 * width)] + [like(share, model)] * n_heads,
        [place, dq, *dkv_parts, qkv],
        [pltpu.VMEM((rows, model), F32)],
        flops=6 * rows * model * width,
    )
    return outs[0], outs[1:]


def input_back(place, dnormed_parts, x, gain, dmiddle, slots=None, n_ctx=0, per=0):
    rows, model = x.shape
    n_heads, share = len(dnormed_parts), dnormed_parts[0].shape[0]

    def body(place_ref, *refs):
        part_refs, refs = refs[:n_heads], refs[n_heads:]
        x_ref, gain_ref, dmiddle_ref = refs[:3]
        refs = refs[3:] if slots is None else refs[4:]
        dx_ref, dgain_ref = refs[:2]
        chunk_refs, dnormed_ref = refs[2:-1], refs[-1]
        for r in range(n_heads):
            first = pl.multiple_of((place_ref[1] ^ r) * share, share)
            dnormed_ref[pl.ds(first, share), :] = part_refs[r][...].astype(F32)
        part, dgain = norm_back(x_ref[...].astype(F32), gain_ref[...], dnormed_ref[...])
        dgain_ref[...] = dgain
        dx = (dmiddle_ref[...] + part).astype(dx_ref.dtype)
        dx_ref[...] = dx
        if chunk_refs:
            dispatch_into(dx, place_ref, refs_slots[0], chunk_refs)

    refs_slots = []

    def wrapped(place_ref, *refs):
        if slots is not None:
            refs_slots[:] = [refs[n_heads + 3]]
        body(place_ref, *refs)

    outs = kernel_call(
        wrapped,
        [like(rows, model, dtype=F32 if slots is None else BF16), like(1, model, dtype=F32)]
        + [like(per, model)] * n_ctx,
        [place, *dnormed_parts, x, gain, dmiddle] + ([] if slots is None else [slots]),
        [pltpu.VMEM((rows, model), F32)],
    )
    return outs[0], outs[1], outs[2:]


def table_back(dtable, buckets):
    heads, half = dtable.shape[0], dtable.shape[3]

    def body(dtable_ref, buckets_ref, out_ref):
        held = buckets_ref[...]
        for bucket in range(BUCKETS):
            hit = held == bucket
            for head in range(heads):
                kept = jnp.where(hit, dtable_ref[head, 1:], 0.0)
                out_ref[bucket * heads + head : bucket * heads + head + 1, :] = jnp.sum(
                    jnp.sum(kept, axis=0), axis=0, keepdims=True
                )

    return kernel_call(body, [like(BUCKETS * heads, half, dtype=F32)], [dtable, buckets])[0]


def bucket_of(distance):
    exact_span = BUCKETS // 2
    result = jnp.minimum(distance, exact_span)
    for rank in range(1, BUCKETS - exact_span):
        edge = int(
            math.ceil(exact_span * (REACH / exact_span) ** (rank / (BUCKETS - exact_span)))
        )
        result = result + (distance >= edge).astype(jnp.int32)
    return result


def tile_buckets(half):
    row = lax.broadcasted_iota(jnp.int32, (half, half), 0)
    col = lax.broadcasted_iota(jnp.int32, (half, half), 1)
    same = jnp.where(row >= col, bucket_of(jnp.maximum(row - col, 0)), -1)
    return jnp.stack([same, bucket_of(half + row - col), bucket_of(2 * half + row - col)])


def bias_table(buckets, bias):
    half = buckets.shape[1]
    value = jnp.full((bias.shape[1],) + buckets.shape, NEGATIVE, F32)
    for bucket in range(BUCKETS):
        value = jnp.where(buckets[None] == bucket, bias[bucket][:, None, None, None], value)
    hidden = jnp.full((bias.shape[1], 1, half, half), NEGATIVE, F32)
    return jnp.concatenate([hidden, value], axis=1)


def slot_ids(routes, n_experts, per, n_heads, ctx_index):
    rows = routes.shape[0]
    pairs = routes.reshape(-1)
    hot = (pairs[:, None] == lax.iota(jnp.int32, n_experts)[None, :]).astype(BF16)
    order = lax.iota(jnp.int32, 2 * rows)
    before = (order[:, None] > order[None, :]).astype(BF16)
    rank = jnp.sum(dot(before, hot) * hot.astype(F32), axis=1).astype(jnp.int32)
    slot = (rank // per) * (per * n_experts) + (pairs ^ ctx_index) * per + rank % per
    return slot.reshape(rows, 2)


def return_rows(chunks, n_ctx):
    parts = exchange(chunks, "heads")
    total = parts[0].astype(F32)
    for part in parts[1:]:
        total = total + part.astype(F32)
    total = total.astype(BF16)
    per = total.shape[0] // n_ctx
    back = exchange([total[r * per : (r + 1) * per] for r in range(n_ctx)], "ctx")
    return gather_rows(jnp.concatenate(back, axis=0), "heads")


def send_rows(chunks):
    return gather_rows(jnp.concatenate(exchange(chunks, "ctx"), axis=0), "heads")


def body(
    boundary,
    norm_first,
    qkv_weight,
    position_bias,
    out_weight,
    norm_second,
    router,
    expert_up,
    expert_down,
    routes,
):
    section = lax.axis_index("section")
    ctx_index = lax.axis_index("ctx")
    heads_index = lax.axis_index("heads")
    n_ctx, n_heads = lax.axis_size("ctx"), lax.axis_size("heads")
    first = section == 0
    place = jnp.stack([ctx_index, heads_index]).astype(jnp.int32)
    rows, model = boundary.shape[2:]
    half = rows // 2
    n_experts = router.shape[2]
    per = 5 * rows // (2 * n_experts) // n_heads

    def both(own):
        other = swap(own, "section")
        return jnp.where(first, own, other), jnp.where(first, other, own)

    given = swap(jnp.where(first, boundary[0, 1], boundary[0, 0]), "section")
    x0 = jnp.where(first, boundary[0, 0], given)
    cotangent = jnp.where(first, given, boundary[0, 1])
    gains_first = [g.astype(F32) for g in both(norm_first)]
    qkv = both(qkv_weight[0])
    tables = both(position_bias[0])
    own_routes = jnp.where(first, routes[0, 0], routes[0, 1])
    got_routes = swap(jnp.where(first, routes[0, 1], routes[0, 0]), "section")
    layer_routes = (
        jnp.where(first, own_routes, got_routes),
        jnp.where(first, got_routes, own_routes),
    )
    gains_second = [g.astype(F32) for g in both(norm_second)]
    out_full = both(gather_rows(out_weight[0], "heads"))
    out_own = both(out_weight[0])
    router_wide = both(jnp.pad(router[0], ((0, 0), (0, LANES - n_experts))))
    up = both(expert_up[0, 0])
    down = both(expert_down[0, 0])

    tokens = [slot_ids(r, n_experts, per, n_heads, ctx_index) for r in layer_routes]
    slots = [t.T for t in tokens]
    quarter = n_ctx * per
    here = heads_index * quarter + lax.iota(jnp.int32, quarter)
    others = []
    for t, r in zip(tokens, layer_routes):
        hit = here[:, None, None] == t[None]
        others.append(jnp.sum(jnp.where(hit, r[:, ::-1][None], 0), axis=(1, 2)))
    others = jnp.stack(others).astype(F32).reshape(2, n_ctx, per)
    others = jnp.stack(exchange([others[:, r] for r in range(n_ctx)], "ctx"))
    others = lax.all_gather(others, "heads")
    others = [others[:, :, layer].reshape(-1, 1).astype(jnp.int32) for layer in range(2)]
    buckets = tile_buckets(half)
    biases = [bias_table(buckets, t) for t in tables]

    def forward(layer, x, normed, q, kv):
        kv_all = gather_rows(kv, "ctx")
        mix, lse = attend(place, q, kv_all, biases[layer], n_ctx)
        mixes = exchange([mix] * n_heads, "heads")
        middle, chunks = finish_attention(
            place, mixes, out_full[layer], x, gains_second[layer], slots[layer], n_ctx, per
        )
        arrived = send_rows(chunks)
        partial, kept = experts(
            place, arrived, up[layer], down[layer], router_wide[layer], others[layer], n_heads
        )
        state = (x, normed, q, kv_all, lse, mix, middle, arrived, kept)
        return state, partial

    def backward(layer, state, dout, dout_rows):
        x, normed, q, kv_all, lse, mix, middle, arrived, kept = state
        chunks, (dpre, dslots, dlogits) = experts_back(
            place,
            dout_rows,
            kept,
            up[layer],
            down[layer],
            router_wide[layer],
            others[layer],
            n_heads,
        )
        dreturned = return_rows(chunks, n_ctx)
        grad_up = dot_tn(arrived, dpre)
        grad_down = dot_tn(kept[1], dslots)
        grad_router = dot_tn(arrived, dlogits)[:, :n_experts]
        dmiddle, datt, dmix, dgain_second = middle_back(
            dreturned, tokens[layer], middle, gains_second[layer], dout, out_own[layer]
        )
        grad_out = dot_tn(datt, mix)
        dq, dtable, dkv = attend_back(place, q, kv_all, biases[layer], lse, dmix, n_ctx)
        dkv_parts = exchange(dkv, "ctx")
        lanes = table_back(dtable, buckets)
        grad_bias = jnp.sum(lanes, axis=1).reshape(BUCKETS, -1)
        dkv_sum, chunks = project_back(place, dq, dkv_parts, qkv[layer], n_heads)
        parts = exchange(chunks, "heads")
        total = parts[0].astype(F32)
        for part in parts[1:]:
            total = total + part.astype(F32)
        dnormed_parts = exchange([total.astype(BF16)] * n_heads, "heads")
        grad_qkv = dot_tn(normed, jnp.concatenate([dq, dkv_sum], axis=1))
        if layer == 1:
            dx, dgain_first, sent = input_back(
                place, dnormed_parts, x, gains_first[layer], dmiddle, slots[0], n_ctx, per
            )
        else:
            dx, dgain_first, sent = input_back(
                place, dnormed_parts, x, gains_first[layer], dmiddle
            )
        dense = jnp.concatenate([grad_qkv, grad_out], axis=1)
        small = (dgain_first[0], dgain_second[0], grad_bias, grad_router)
        return dx, sent, dense, small, (grad_up, grad_down)

    dout_rows1 = send_rows(dispatch(place, cotangent, slots[1], n_ctx, per))
    normed, q, kv = project(x0, gains_first[0], qkv[0])
    state0, partial = forward(0, x0, normed, q, kv)
    returned = return_rows(partial, n_ctx)
    x1, normed, q, kv = combine_project(
        state0[6], returned, tokens[0], gains_first[1], qkv[1]
    )
    state1, partial = forward(1, x1, normed, q, kv)
    returned1 = return_rows(partial, n_ctx)
    out = combine(state1[6], returned1, tokens[1])
    dx1, sent, dense1, small1, expert1 = backward(1, state1, cotangent, dout_rows1)
    dx0, _, dense0, small0, expert0 = backward(0, state0, dx1, send_rows(sent))

    def settle(layer0, layer1):
        got = jnp.where(
            first,
            one_way(layer0.astype(BF16), 1).astype(F32),
            one_way(layer1.astype(BF16), 0).astype(F32),
        )
        return jnp.where(first, layer0, layer1) + got

    grad_up, grad_down = (settle(a, b) for a, b in zip(expert0, expert1))
    dense = settle(dense0, dense1)
    gain_first_sum, gain_second_sum, bias_sum, router_sum = (
        settle(a, b) for a, b in zip(small0, small1)
    )
    dense = lax.psum_scatter(
        dense.astype(BF16), "ctx", scatter_dimension=0, tiled=True
    ).astype(F32)
    width = qkv_weight.shape[3]
    grad_qkv = jnp.stack([dense[:, i * width : (i + 1) * width] for i in range(3)])
    grad_out = dense[:, 3 * width :].T

    def share(array):
        return lax.psum_scatter(array, "ctx", scatter_dimension=0, tiled=True)

    router_sum = lax.psum(router_sum, "heads")
    got_out = one_way(out, 0)
    got_dx = one_way(dx0, 1)
    boundary_out = jnp.stack([jnp.where(first, dx0, got_out), jnp.where(first, got_dx, out)])
    return (
        boundary_out[None],
        share(gain_first_sum)[None],
        grad_qkv[None],
        share(bias_sum)[None],
        grad_out[None],
        share(gain_second_sum)[None],
        share(router_sum)[None],
        grad_up[None, None],
        grad_down[None, None],
    )


def solution(mesh):
    placed = (
        P("section", None, "ctx", None),
        P("section", None),
        P("section", None, None, "heads"),
        P("section", None, "heads"),
        P("section", "heads", None),
        P("section", None),
        P("section", None, None),
        P("section", "ctx", None, "heads"),
        P("section", "ctx", "heads", None),
        P("section", None, "ctx", None),
    )
    return jax.shard_map(
        body,
        mesh=mesh,
        in_specs=placed,
        out_specs=(
            P("section", None, "ctx", None),
            P("section", "ctx"),
            P("section", None, "ctx", "heads"),
            P("section", "ctx", "heads"),
            P("section", "heads", "ctx"),
            P("section", "ctx"),
            P("section", "ctx", None),
            P("section", "ctx", None, "heads"),
            P("section", "ctx", "heads", None),
        ),
        check_vma=False,
    )
```

time: 1530 us -> 513 us (0.34)
  waiting for transfers between devices: 688 us -> 47.9 us
  matrix products: 230 us -> 16.3 us
  local copies, waits for them, and re-layouts: 200 us -> 29.4 us
  other arithmetic: 140 us -> 47.5 us
  starting transfers between devices: 45.9 us -> 119 us
  Pallas kernels: 0 us -> 51 us
  blocking collectives: 194 us -> 175 us
    psum x10 -> x0, waiting for transfers between devices: 471 us -> none  [the longest x6 247 us: heads_total(): return lax.psum(values.astype(jnp.bfloat16), 'heads').astype(jnp.float32)]
    dot_general x128 -> x12, matrix products: 226 us -> 16.3 us  [dot(): lax.dot_general(a, b, (contract, ((), ())), preferred_element_type=F32)]
    all_to_all x9 -> x0, waiting for transfers between devices: 123 us -> none  [the longest x3 50.6 us: back_send(): lax.all_to_all(values, 'ctx', split_axis=0, concat_axis=0, tiled=True)]
    ppermute x4 -> x90, starting transfers between devices: 5.88 us -> 119 us  [the longest x74 89.3 us: swap(): return lax.ppermute(array, axis, [(i, i ^ by) for i in range(devices)])]
    all_to_all x3 -> x0, blocking collectives: 86.6 us -> none  [the longest x2 58.2 us: send_back(): lax.all_to_all(values, 'ctx', split_axis=0, concat_axis=0, tiled=True)]
    reduce_scatter x6 -> x1, waiting for transfers between devices: 68.1 us -> 0.01 us  [body(): lax.psum_scatter(dense.astype(BF16), 'ctx', scatter_dimension=0, tiled=True)]
    reduce_sum x52 -> x3, other arithmetic: 59.6 us -> 0.97 us  [the longest x2 0.73 us: backward(): grad_bias = jnp.sum(lanes, axis=1).reshape(BUCKETS, -1)]
    all_gather x6 -> x11, blocking collectives: 94.7 us -> 147 us  [the longest x10 139 us: gather_rows(): return lax.all_gather(array, axis, axis=0, tiled=True)]
  transfers between devices with their start and end apart: 32 -> 93, of which waited for: 25 -> 27; matrix products, arithmetic and copies ran while one was open for 13% -> 16% of each run, Pallas kernels for 0% -> 8%
where the time goes in v1:
time: 513 us; the launch traced here: 504 us
  blocking collectives  175 us (34%)
  starting transfers between devices  119 us (23%)
  Pallas kernels  51 us (10%)
  waiting for transfers between devices  47.9 us (9%)
  other arithmetic  47.5 us (9%)
  local copies, waits for them, and re-layouts  29.4 us (6%)
  between operations  18.2 us (4%)
  matrix products  16.3 us (3%)
    all_gather x10, blocking collectives, gather_rows(): return lax.all_gather(array, axis, axis=0, tiled=True)  139 us
    ppermute x74, starting transfers between devices, swap(): return lax.ppermute(array, axis, [(i, i ^ by) for i in range(devices)])  89.3 us
    pallas_call x22, Pallas kernels, kernel_call(): pl.pallas_call(body, out_shape=outs, in_specs=[spec(a) for a in args], ou...  51 us
    ppermute x74, waiting for transfers between devices, swap(): return lax.ppermute(array, axis, [(i, i ^ by) for i in range(devices)])  43.2 us
    ppermute x16, starting transfers between devices, one_way(): return lax.ppermute(array, 'section', [(source, 1 - source)])  29.6 us
    unnamed x1, blocking collectives  18.6 us
    unnamed x338, local copies, waits for them, and re-layouts  16.5 us
    dot_general x12, matrix products, dot(): lax.dot_general(a, b, (contract, ((), ())), preferred_element_type=F32)  16.3 us
  transfers between devices with their start and end apart: 93, of which 27 were waited for; matrix products, arithmetic and copies ran while one was open for 16% of the time, Pallas kernels for 8%

profile of v1, /device:TPU:0, one launch (start us, length us, event | category | flops | bytes accessed | tf_op | source)
XLA Modules:
  0.0 504.4 jit_solution(9445539189950858731)
XLA Ops:
  10.8 2.3 copy.87
  28.6 5.1 %collective-permute-start.18 = (f32[2,40]{1,0:T(2,128)S(1)}, f32[2,40]{1,0:T(2,128)S(1)}, u32[]{:S(2)}, u32[]{:S(2)}) collective-permute-start(f32[2,40]{1,0:T(2,128)S(1)} %get-tuple-element.371), channel_id=1, source_target_pairs={{0,12},{4,8},{8,4},{12,0},{1,13},{5,9},{9,5},{13,1},{2,14},{6,10},... | collective-permute-start | bytes 968 | tf_op jit(solution)/shard_map/ppermute | solution.py:57
  35.3 3.0 collective-permute-done.17
  38.8 8.2 %all-gather.1 = f32[16,2,40]{2,1,0:T(2,128)S(1)} all-gather(f32[4,2,40]{2,1,0:T(2,128)S(1)} %pad_maximum_fusion.10), channel_id=3, replica_groups=mesh['section'=2,'ctx'=4,'heads'=4] {'heads'}, dimensions={0}, use_global_device_ids=true | all-gather | bytes 6400 | tf_op jit(solution)/shard_map/all_gather | solution.py:599
  49.2 2.0 bitcast_select_fusion.2
  51.2 2.3 copy.89
  56.7 17.9 %all_gather.39.kv_ref = bf16[1024,384]{1,0:T(8,128)(2,1)S(1)} all-gather(bf16[256,384]{1,0:T(8,128)(2,1)S(1)} %get-tuple-element.101), channel_id=1, replica_groups=mesh['section'=2,'ctx'=4,'heads'=4] {'ctx'}, dimensions={0}, use_global_device_ids=true | all-gather | bytes 983040 | tf_op jit(solution)/shard_map/all_gather | solution.py:69
  74.7 2.9 shard_map.170
  79.7 2.4 broadcast_select_fusion.1
  83.7 2.4 broadcast_select_fusion.2
  86.1 2.0 collective-permute-done.6.refs_3_
  89.9 2.3 collective-permute-start.12
  92.2 2.2 collective-permute-start.10
  94.3 2.5 broadcast_select_fusion
  97.3 12.1 %all_gather.41.in_ref = bf16[640,768]{1,0:T(8,128)(2,1)S(1)} all-gather(bf16[160,768]{1,0:T(8,128)(2,1)S(1)} %pad_maximum_fusion.2), channel_id=1, replica_groups=mesh['section'=2,'ctx'=4,'heads'=4] {'heads'}, dimensions={0}, use_global_device_ids=true | all-gather | bytes 1228800 | tf_op jit(solution)/shard_map/all_gather | solution.py:69
  109.8 3.7 shard_map.172
  117.5 2.7 select_select_fusion
  125.2 2.2 collective-permute-start.24
  132.4 2.2 collective-permute-start.27
  134.6 2.3 collective-permute-start.25
  136.9 11.6 %all_gather.44.returned_ref = bf16[640,768]{1,0:T(8,128)(2,1)S(1)} all-gather(bf16[160,768]{1,0:T(8,128)(2,1)S(1)} %pad_maximum_fusion.3), channel_id=1, replica_groups=mesh['section'=2,'ctx'=4,'heads'=4] {'heads'}, dimensions={0}, use_global_device_ids=true | all-gather | bytes 1228800 | tf_op jit(solution)/shard_map/all_gather | solution.py:69
  149.9 16.2 %all_gather.45.kv_ref = bf16[1024,384]{1,0:T(8,128)(2,1)S(1)} all-gather(bf16[256,384]{1,0:T(8,128)(2,1)S(1)} %get-tuple-element.114), channel_id=1, replica_groups=mesh['section'=2,'ctx'=4,'heads'=4] {'ctx'}, dimensions={0}, use_global_device_ids=true | all-gather | bytes 983040 | tf_op jit(solution)/shard_map/all_gather | solution.py:69
  166.1 2.9 shard_map.174
  174.8 3.7 collective-permute-done.30.refs_3_
  181.8 2.9 collective-permute-start.31
  184.8 10.9 %all_gather.46.dout_ref = bf16[640,768]{1,0:T(8,128)(2,1)S(1)} all-gather(bf16[160,768]{1,0:T(8,128)(2,1)S(1)} %pad_maximum_fusion.4), channel_id=1, replica_groups=mesh['section'=2,'ctx'=4,'heads'=4] {'heads'}, dimensions={0}, use_global_device_ids=true | all-gather | bytes 1228800 | tf_op jit(solution)/shard_map/all_gather | solution.py:69
  195.8 19.1 %all_gather.47.in_ref = bf16[640,768]{1,0:T(8,128)(2,1)S(1)} all-gather(bf16[160,768]{1,0:T(8,128)(2,1)S(1)} %pad_maximum_fusion.5), channel_id=1, replica_groups=mesh['section'=2,'ctx'=4,'heads'=4] {'heads'}, dimensions={0}, use_global_device_ids=true | all-gather | bytes 1228800 | tf_op jit(solution)/shard_map/all_gather | solution.py:69
  214.9 3.0 shard_map.177
  217.9 5.1 %shard_map.178 = (bf16[160,768]{1,0:T(8,128)(2,1)S(1)}, bf16[160,768]{1,0:T(8,128)(2,1)S(1)}, bf16[160,768]{1,0:T(8,128)(2,1)S(1)}, bf16[160,768]{1,0:T(8,128)(2...) custom-call(s32[2]{0:T(128)S(1)} %pad_add_fusion.1.place_ref, ...), custom_call_target="tpu_custom_call" | custom-call | flops 1509949440 | bytes 9606152 | tf_op jit(solution)/shard_map/pallas_call | solution.py:28
  229.7 2.9 fusion.89
  232.6 2.9 fusion.91
  247.8 16.1 %all_gather.48.returned_ref = bf16[640,768]{1,0:T(8,128)(2,1)S(1)} all-gather(bf16[160,768]{1,0:T(8,128)(2,1)S(1)} %pad_maximum_fusion.6), channel_id=1, replica_groups=mesh['section'=2,'ctx'=4,'heads'=4] {'heads'}, dimensions={0}, use_global_device_ids=true | all-gather | bytes 1228800 | tf_op jit(solution)/shard_map/all_gather | solution.py:69
  266.0 5.5 %shard_map.180 = (bf16[256,192]{1,0:T(8,128)(2,1)S(1)}, f32[3,4,128,128]{3,2,1,0:T(8,128)S(1)}, bf16[256,384]{1,0:T(8,128)(2,1)S(1)}, bf16[256,384]{1,0:T(8,128)...) custom-call(s32[2]{0:T(128)S(1)} %pad_add_fusion.1.place_ref, bf16[256,192]{1,0:T(8,128)(2,1)S(1)} %get-tuple-element.113.q_ref, ...), custom_call_target="tpu_custom_call" | custom-call | flops 503316480 | bytes 3443720 | tf_op jit(solution)/shard_map/pallas_call | solution.py:28
  271.4 3.8 collective-permute-start.41
  275.3 2.4 collective-permute-start.43
  277.8 10.4 %all_gather.51.returned_ref = bf16[640,768]{1,0:T(8,128)(2,1)S(1)} all-gather(bf16[160,768]{1,0:T(8,128)(2,1)S(1)} %pad_maximum_fusion.9), channel_id=1, replica_groups=mesh['section'=2,'ctx'=4,'heads'=4] {'heads'}, dimensions={0}, use_global_device_ids=true | all-gather | bytes 1228800 | tf_op jit(solution)/shard_map/all_gather | solution.py:69
  294.1 2.0 shard_map.181
  297.6 2.0 collective-permute-start.45
  309.3 2.4 collective-permute-start.79
  313.5 2.1 collective-permute-start.52
  315.6 3.3 collective-permute-start.51
  319.6 2.9 collective-permute-done.51
  323.2 12.5 %all_gather.49.dout_ref = bf16[640,768]{1,0:T(8,128)(2,1)S(1)} all-gather(bf16[160,768]{1,0:T(8,128)(2,1)S(1)} %pad_maximum_fusion.7), channel_id=1, replica_groups=mesh['section'=2,'ctx'=4,'heads'=4] {'heads'}, dimensions={0}, use_global_device_ids=true | all-gather | bytes 1228800 | tf_op jit(solution)/shard_map/all_gather | solution.py:69
  335.8 5.1 %shard_map.183 = (bf16[160,768]{1,0:T(8,128)(2,1)S(1)}, bf16[160,768]{1,0:T(8,128)(2,1)S(1)}, bf16[160,768]{1,0:T(8,128)(2,1)S(1)}, bf16[160,768]{1,0:T(8,128)(2...) custom-call(s32[2]{0:T(128)S(1)} %pad_add_fusion.1.place_ref, ...), custom_call_target="tpu_custom_call" | custom-call | flops 1509949440 | bytes 9606152 | tf_op jit(solution)/shard_map/pallas_call | solution.py:28
  344.4 3.0 fusion.90
  353.0 2.3 collective-permute-start.56
  359.1 11.6 %all_gather.50.returned_ref = bf16[640,768]{1,0:T(8,128)(2,1)S(1)} all-gather(bf16[160,768]{1,0:T(8,128)(2,1)S(1)} %pad_maximum_fusion.8), channel_id=1, replica_groups=mesh['section'=2,'ctx'=4,'heads'=4] {'heads'}, dimensions={0}, use_global_device_ids=true | all-gather | bytes 1228800 | tf_op jit(solution)/shard_map/all_gather | solution.py:69
  375.9 4.8 shard_map.185
  381.7 2.0 collective-permute-start.60
  383.7 2.2 collective-permute-start.61
  386.2 4.2 collective-permute-done.59.refs_1_
  390.4 7.4 %collective-permute-done.60.refs_2_ = bf16[256,384]{1,0:T(8,128)(2,1)S(1)} collective-permute-done((bf16[256,384]{1,0:T(8,128)(2,1)S(1)}, bf16[256,384]{1,0:T(8,128)(2,1)S(1)}, u32[]{:S(2)}, u32[]{:S(2)}) %collective-permute-start.60) | collective-permute-done | bytes 196640 | tf_op jit(solution)/shard_map/ppermute | solution.py:57
  402.7 2.9 fusion.92
  406.8 9.8 %psum.8 = f32[192,4]{0,1:T(4,128)} all-reduce(f32[192,4]{0,1:T(4,128)S(1)} %copy.125), channel_id=1, replica_groups=mesh['section'=2,'ctx'=4,'heads'=4] {'heads'}, use_global_device_ids=true, to_apply=%region_10.11 | all-reduce | flops 768 | bytes 6144 | tf_op jit(solution)/shard_map/psum | solution.py:697
  419.0 2.0 collective-permute-start.81
  426.1 3.0 collective-permute-done.64
  429.1 3.0 collective-permute-start.87
  432.1 2.2 collective-permute-start.74
  439.9 4.8 add_convert_fusion
  449.6 5.0 collective-permute-start.89
  459.7 3.9 collective-permute-done.76
  464.8 18.6 %all-reduce.6 = (f32[768]{0:T(1024)S(1)}, f32[32,3]{0,1:T(4,128)S(1)}, f32[768]{0:T(1024)S(1)}) all-reduce(f32[768]{0:T(1024)S(1)} %select_add_fusion.2, f32[32,3]{0,1:T(4,128)S(1)} %select_add_fusion.3, f32[768]{0:T(1024)S(1)} %select_add_fusion.1), channel_id=4, replica_groups=mesh['section'=2,'ctx'=4,'heads'=4] {'ctx'}, use_global_device_ids=true, to_apply=%region_4.5.clone | all-reduce | flops 1632 | bytes 13056
  485.4 4.4 add_bitcast_fusion.1
  489.8 3.5 add_bitcast_fusion
  (629 shorter events, 151.4 us)
Async XLA Ops:
  7.2 41.5 %all-gather.4.cloned.1.call-start = ((), (), s32[]{:S(2)}) async-start(), calls=%async_computation.3 | async-start | bytes 1474560 | tf_op jit(solution)/shard_map/all_gather | solution.py:69
  9.2 39.6 %collective-permute-start = (bf16[256,768]{1,0:T(8,128)(2,1)}, bf16[256,768]{1,0:T(8,128)(2,1)}, u32[]{:S(2)}, u32[]{:S(2)}) collective-permute-start(bf16[256,768]{1,0:T(8,128)(2,1)} %bitcast_select_fusion.3), channel_id=1, source_target_pairs={{0,16},{16,0},{1,17},{17,1},{2,18},{18,2},{3,19},{19,3},{4,20},{20... | collective-permute-start | bytes 1179656 | tf_op jit(solution)/shard_map/ppermute | solution.py:57
  9.6 15.7 %collective-permute-start.1 = (bf16[1,768]{1,0:T(2,128)(2,1)S(1)}, bf16[1,768]{1,0:T(2,128)(2,1)S(1)}, u32[]{:S(2)}, u32[]{:S(2)}) collective-permute-start(bf16[1,768]{1,0:T(2,128)(2,1)S(1)} %copy-done.150), channel_id=1, source_target_pairs={{0,16},{16,0},{1,17},{17,1},{2,18},{18,2},{3,19},{19,3},{4,20},{20... | collective-permute-start | bytes 4616 | tf_op jit(solution)/shard_map/ppermute | solution.py:57
  9.7 41.5 %collective-permute-start.2 = (bf16[3,768,192]{1,2,0:T(8,128)(2,1)}, bf16[3,768,192]{1,2,0:T(8,128)(2,1)}, u32[]{:S(2)}, u32[]{:S(2)}) collective-permute-start(bf16[3,768,192]{1,2,0:T(8,128)(2,1)} %bitcast.5), channel_id=1, source_target_pairs={{0,16},{16,0},{1,17},{17,1},{2,18},{18,2},{3,19},{19,3},{4,20},{20... | collective-permute-start | bytes 2654216 | tf_op jit(solution)/shard_map/ppermute | solution.py:57
  10.1 9.9 %collective-permute-start.3 = (f32[32,3]{0,1:T(4,128)S(1)}, f32[32,3]{0,1:T(4,128)S(1)}, u32[]{:S(2)}, u32[]{:S(2)}) collective-permute-start(f32[32,3]{0,1:T(4,128)S(1)} %bitcast.115), channel_id=1, source_target_pairs={{0,16},{16,0},{1,17},{17,1},{2,18},{18,2},{3,19},{19,3},{4,20},{20... | collective-permute-start | bytes 1160 | tf_op jit(solution)/shard_map/ppermute | solution.py:57
  10.2 395.4 %reduce-scatter.8.cloned.1.call-start = ((), (), s32[]{:S(2)}) async-start(), calls=%async_computation.4 | async-start | bytes 491520
  10.3 15.0 %collective-permute-start.8 = (bf16[1,768]{1,0:T(2,128)(2,1)S(1)}, bf16[1,768]{1,0:T(2,128)(2,1)S(1)}, u32[]{:S(2)}, u32[]{:S(2)}) collective-permute-start(bf16[1,768]{1,0:T(2,128)(2,1)S(1)} %copy-done.151), channel_id=1, source_target_pairs={{0,16},{16,0},{1,17},{17,1},{2,18},{18,2},{3,19},{19,3},{4,20},{20... | collective-permute-start | bytes 4616 | tf_op jit(solution)/shard_map/ppermute | solution.py:57
  35.3 43.9 %collective-permute-start.13 = (bf16[768,768]{1,0:T(8,128)(2,1)}, bf16[768,768]{1,0:T(8,128)(2,1)}, u32[]{:S(2)}, u32[]{:S(2)}) collective-permute-start(bf16[768,768]{1,0:T(8,128)(2,1)} %bitcast.108), channel_id=1, source_target_pairs={{0,16},{16,0},{1,17},{17,1},{2,18},{18,2},{3,19},{19,3},{4,20},{20... | collective-permute-start | bytes 3538952 | tf_op jit(solution)/shard_map/ppermute | solution.py:57
  38.3 56.1 %collective-permute-start.14 = (bf16[768,768]{1,0:T(8,128)(2,1)}, bf16[768,768]{1,0:T(8,128)(2,1)}, u32[]{:S(2)}, u32[]{:S(2)}) collective-permute-start(bf16[768,768]{1,0:T(8,128)(2,1)} %bitcast.109), channel_id=1, source_target_pairs={{0,16},{16,0},{1,17},{17,1},{2,18},{18,2},{3,19},{19,3},{4,20},{20... | collective-permute-start | bytes 3538952 | tf_op jit(solution)/shard_map/ppermute | solution.py:57
  38.3 9.6 %collective-permute-start.15 = (bf16[768,128]{1,0:T(8,128)(2,1)S(1)}, bf16[768,128]{1,0:T(8,128)(2,1)S(1)}, u32[]{:S(2)}, u32[]{:S(2)}) collective-permute-start(bf16[768,128]{1,0:T(8,128)(2,1)S(1)} %copy-done.145), channel_id=1, source_target_pairs={{0,16},{16,0},{1,17},{17,1},{2,18},{18,2},{3,19},{19,3},{4,20},{20... | collective-permute-start | bytes 589832 | tf_op jit(solution)/shard_map/ppermute | solution.py:57
  47.9 81.8 %collective-permute-start.40 = (bf16[192,768]{1,0:T(8,128)(2,1)}, bf16[192,768]{1,0:T(8,128)(2,1)}, u32[]{:S(2)}, u32[]{:S(2)}) collective-permute-start(bf16[192,768]{1,0:T(8,128)(2,1)} %bitcast.22), channel_id=1, source_target_pairs={{0,16},{16,0},{1,17},{17,1},{2,18},{18,2},{3,19},{19,3},{4,20},{20... | collective-permute-start | bytes 884744 | tf_op jit(solution)/shard_map/ppermute | solution.py:57
  48.7 33.4 %collective-permute-start.7 = (bf16[768,768]{1,0:T(8,128)(2,1)}, bf16[768,768]{1,0:T(8,128)(2,1)}, u32[]{:S(2)}, u32[]{:S(2)}) collective-permute-start(bf16[768,768]{1,0:T(8,128)(2,1)} %bitcast.110), channel_id=1, source_target_pairs={{0,16},{16,0},{1,17},{17,1},{2,18},{18,2},{3,19},{19,3},{4,20},{20... | collective-permute-start | bytes 3538952 | tf_op jit(solution)/shard_map/ppermute | solution.py:57
  77.6 8.5 %collective-permute-start.4 = (bf16[256,192]{1,0:T(8,128)(2,1)S(1)}, bf16[256,192]{1,0:T(8,128)(2,1)S(1)}, u32[]{:S(2)}, u32[]{:S(2)}) collective-permute-start(bf16[256,192]{1,0:T(8,128)(2,1)S(1)} %get-tuple-element.103.refs_0_), channel_id=1, source_target_pairs={{0,1},{1,0},{2,3},{3,2},{4,5},{5,4},{6,7},{7,6},{8,9},{9,8},{10,11... | collective-permute-start | bytes 294920 | tf_op jit(solution)/shard_map/ppermute | solution.py:57
  79.2 7.0 %collective-permute-start.5 = (bf16[256,192]{1,0:T(8,128)(2,1)S(1)}, bf16[256,192]{1,0:T(8,128)(2,1)S(1)}, u32[]{:S(2)}, u32[]{:S(2)}) collective-permute-start(bf16[256,192]{1,0:T(8,128)(2,1)S(1)} %get-tuple-element.103.refs_0_), channel_id=1, source_target_pairs={{0,2},{1,3},{2,0},{3,1},{4,6},{5,7},{6,4},{7,5},{8,10},{9,11},{10,... | collective-permute-start | bytes 294920 | tf_op jit(solution)/shard_map/ppermute | solution.py:57
  89.9 6.9 %collective-permute-start.12 = (bf16[40,768]{1,0:T(8,128)(2,1)S(1)}, bf16[40,768]{1,0:T(8,128)(2,1)S(1)}, u32[]{:S(2)}, u32[]{:S(2)}) collective-permute-start(bf16[40,768]{1,0:T(8,128)(2,1)S(1)} %get-tuple-element.108), channel_id=1, source_target_pairs={{0,12},{4,8},{8,4},{12,0},{1,13},{5,9},{9,5},{13,1},{2,14},{6,10},... | collective-permute-start | bytes 184328 | tf_op jit(solution)/shard_map/ppermute | solution.py:57
  113.6 9.5 %collective-permute-start.21 = (bf16[160,768]{1,0:T(8,128)(2,1)}, bf16[160,768]{1,0:T(8,128)(2,1)}, u32[]{:S(2)}, u32[]{:S(2)}) collective-permute-start(bf16[160,768]{1,0:T(8,128)(2,1)} %get-tuple-element.112), channel_id=1, source_target_pairs={{0,3},{1,2},{2,1},{3,0},{4,7},{5,6},{6,5},{7,4},{8,11},{9,10},{10,... | collective-permute-start | bytes 737288 | tf_op jit(solution)/shard_map/ppermute | solution.py:57
  115.1 8.6 %collective-permute-start.20 = (bf16[160,768]{1,0:T(8,128)(2,1)}, bf16[160,768]{1,0:T(8,128)(2,1)}, u32[]{:S(2)}, u32[]{:S(2)}) collective-permute-start(bf16[160,768]{1,0:T(8,128)(2,1)} %get-tuple-element.111), channel_id=1, source_target_pairs={{0,2},{1,3},{2,0},{3,1},{4,6},{5,7},{6,4},{7,5},{8,10},{9,11},{10,... | collective-permute-start | bytes 737288 | tf_op jit(solution)/shard_map/ppermute | solution.py:57
  116.3 7.4 %collective-permute-start.19 = (bf16[160,768]{1,0:T(8,128)(2,1)}, bf16[160,768]{1,0:T(8,128)(2,1)}, u32[]{:S(2)}, u32[]{:S(2)}) collective-permute-start(bf16[160,768]{1,0:T(8,128)(2,1)} %get-tuple-element.110), channel_id=1, source_target_pairs={{0,1},{1,0},{2,3},{3,2},{4,5},{5,4},{6,7},{7,6},{8,9},{9,8},{10,11... | collective-permute-start | bytes 737288 | tf_op jit(solution)/shard_map/ppermute | solution.py:57
  125.2 9.4 %collective-permute-start.24 = (bf16[40,768]{1,0:T(8,128)(2,1)S(1)}, bf16[40,768]{1,0:T(8,128)(2,1)S(1)}, u32[]{:S(2)}, u32[]{:S(2)}) collective-permute-start(bf16[40,768]{1,0:T(8,128)(2,1)S(1)} %get-tuple-element.329), channel_id=1, source_target_pairs={{0,12},{4,8},{8,4},{12,0},{1,13},{5,9},{9,5},{13,1},{2,14},{6,10},... | collective-permute-start | bytes 184328 | tf_op jit(solution)/shard_map/ppermute | solution.py:57
  127.4 9.5 %collective-permute-start.23 = (bf16[40,768]{1,0:T(8,128)(2,1)S(1)}, bf16[40,768]{1,0:T(8,128)(2,1)S(1)}, u32[]{:S(2)}, u32[]{:S(2)}) collective-permute-start(bf16[40,768]{1,0:T(8,128)(2,1)S(1)} %get-tuple-element.330), channel_id=1, source_target_pairs={{0,8},{4,12},{8,0},{12,4},{1,9},{5,13},{9,1},{13,5},{2,10},{6,14},... | collective-permute-start | bytes 184328 | tf_op jit(solution)/shard_map/ppermute | solution.py:57
  127.7 9.1 %collective-permute-start.22 = (bf16[40,768]{1,0:T(8,128)(2,1)S(1)}, bf16[40,768]{1,0:T(8,128)(2,1)S(1)}, u32[]{:S(2)}, u32[]{:S(2)}) collective-permute-start(bf16[40,768]{1,0:T(8,128)(2,1)S(1)} %get-tuple-element.331), channel_id=1, source_target_pairs={{0,4},{4,0},{8,12},{12,8},{1,5},{5,1},{9,13},{13,9},{2,6},{6,2},{1... | collective-permute-start | bytes 184328 | tf_op jit(solution)/shard_map/ppermute | solution.py:57
  132.4 38.8 %collective-permute-start.27 = (bf16[40,768]{1,0:T(8,128)(2,1)S(1)}, bf16[40,768]{1,0:T(8,128)(2,1)S(1)}, u32[]{:S(2)}, u32[]{:S(2)}) collective-permute-start(bf16[40,768]{1,0:T(8,128)(2,1)S(1)} %get-tuple-element.119), channel_id=1, source_target_pairs={{0,12},{4,8},{8,4},{12,0},{1,13},{5,9},{9,5},{13,1},{2,14},{6,10},... | collective-permute-start | bytes 184328 | tf_op jit(solution)/shard_map/ppermute | solution.py:57
  134.6 38.1 %collective-permute-start.26 = (bf16[40,768]{1,0:T(8,128)(2,1)S(1)}, bf16[40,768]{1,0:T(8,128)(2,1)S(1)}, u32[]{:S(2)}, u32[]{:S(2)}) collective-permute-start(bf16[40,768]{1,0:T(8,128)(2,1)S(1)} %get-tuple-element.118), channel_id=1, source_target_pairs={{0,8},{4,12},{8,0},{12,4},{1,9},{5,13},{9,1},{13,5},{2,10},{6,14},... | collective-permute-start | bytes 184328 | tf_op jit(solution)/shard_map/ppermute | solution.py:57
  134.6 38.1 %collective-permute-start.25 = (bf16[40,768]{1,0:T(8,128)(2,1)S(1)}, bf16[40,768]{1,0:T(8,128)(2,1)S(1)}, u32[]{:S(2)}, u32[]{:S(2)}) collective-permute-start(bf16[40,768]{1,0:T(8,128)(2,1)S(1)} %get-tuple-element.117), channel_id=1, source_target_pairs={{0,4},{4,0},{8,12},{12,8},{1,5},{5,1},{9,13},{13,9},{2,6},{6,2},{1... | collective-permute-start | bytes 184328 | tf_op jit(solution)/shard_map/ppermute | solution.py:57
  171.2 7.3 %collective-permute-start.30 = (bf16[256,192]{1,0:T(8,128)(2,1)S(1)}, bf16[256,192]{1,0:T(8,128)(2,1)S(1)}, u32[]{:S(2)}, u32[]{:S(2)}) collective-permute-start(bf16[256,192]{1,0:T(8,128)(2,1)S(1)} %get-tuple-element.120.refs_0_), channel_id=1, source_target_pairs={{0,3},{1,2},{2,1},{3,0},{4,7},{5,6},{6,5},{7,4},{8,11},{9,10},{10,... | collective-permute-start | bytes 294920 | tf_op jit(solution)/shard_map/ppermute | solution.py:57
  180.2 15.5 %collective-permute-start.33 = (bf16[40,768]{1,0:T(8,128)(2,1)S(1)}, bf16[40,768]{1,0:T(8,128)(2,1)S(1)}, u32[]{:S(2)}, u32[]{:S(2)}) collective-permute-start(bf16[40,768]{1,0:T(8,128)(2,1)S(1)} %get-tuple-element.125), channel_id=1, source_target_pairs={{0,12},{4,8},{8,4},{12,0},{1,13},{5,9},{9,5},{13,1},{2,14},{6,10},... | collective-permute-start | bytes 184328 | tf_op jit(solution)/shard_map/ppermute | solution.py:57
  181.8 13.9 %collective-permute-start.32 = (bf16[40,768]{1,0:T(8,128)(2,1)S(1)}, bf16[40,768]{1,0:T(8,128)(2,1)S(1)}, u32[]{:S(2)}, u32[]{:S(2)}) collective-permute-start(bf16[40,768]{1,0:T(8,128)(2,1)S(1)} %get-tuple-element.124), channel_id=1, source_target_pairs={{0,8},{4,12},{8,0},{12,4},{1,9},{5,13},{9,1},{13,5},{2,10},{6,14},... | collective-permute-start | bytes 184328 | tf_op jit(solution)/shard_map/ppermute | solution.py:57
  181.8 13.9 %collective-permute-start.31 = (bf16[40,768]{1,0:T(8,128)(2,1)S(1)}, bf16[40,768]{1,0:T(8,128)(2,1)S(1)}, u32[]{:S(2)}, u32[]{:S(2)}) collective-permute-start(bf16[40,768]{1,0:T(8,128)(2,1)S(1)} %get-tuple-element.123), channel_id=1, source_target_pairs={{0,4},{4,0},{8,12},{12,8},{1,5},{5,1},{9,13},{13,9},{2,6},{6,2},{1... | collective-permute-start | bytes 184328 | tf_op jit(solution)/shard_map/ppermute | solution.py:57
  223.0 13.4 %collective-permute-start.36 = (bf16[160,768]{1,0:T(8,128)(2,1)S(1)}, bf16[160,768]{1,0:T(8,128)(2,1)S(1)}, u32[]{:S(2)}, u32[]{:S(2)}) collective-permute-start(bf16[160,768]{1,0:T(8,128)(2,1)S(1)} %get-tuple-element.132), channel_id=1, source_target_pairs={{0,3},{1,2},{2,1},{3,0},{4,7},{5,6},{6,5},{7,4},{8,11},{9,10},{10,... | collective-permute-start | bytes 737288 | tf_op jit(solution)/shard_map/ppermute | solution.py:57
  224.5 12.2 %collective-permute-start.35 = (bf16[160,768]{1,0:T(8,128)(2,1)S(1)}, bf16[160,768]{1,0:T(8,128)(2,1)S(1)}, u32[]{:S(2)}, u32[]{:S(2)}) collective-permute-start(bf16[160,768]{1,0:T(8,128)(2,1)S(1)} %get-tuple-element.131), channel_id=1, source_target_pairs={{0,2},{1,3},{2,0},{3,1},{4,6},{5,7},{6,4},{7,5},{8,10},{9,11},{10,... | collective-permute-start | bytes 737288 | tf_op jit(solution)/shard_map/ppermute | solution.py:57
  226.2 12.4 %collective-permute-start.34 = (bf16[160,768]{1,0:T(8,128)(2,1)S(1)}, bf16[160,768]{1,0:T(8,128)(2,1)S(1)}, u32[]{:S(2)}, u32[]{:S(2)}) collective-permute-start(bf16[160,768]{1,0:T(8,128)(2,1)S(1)} %get-tuple-element.130), channel_id=1, source_target_pairs={{0,1},{1,0},{2,3},{3,2},{4,5},{5,4},{6,7},{7,6},{8,9},{9,8},{10,11... | collective-permute-start | bytes 737288 | tf_op jit(solution)/shard_map/ppermute | solution.py:57
  226.5 13.7 %collective-permute-start.70 = (bf16[160,768]{1,0:T(8,128)(2,1)S(1)}, bf16[160,768]{1,0:T(8,128)(2,1)S(1)}, u32[]{:S(2)}, u32[]{:S(2)}) collective-permute-start(bf16[160,768]{1,0:T(8,128)(2,1)S(1)} %get-tuple-element.172), channel_id=1, source_target_pairs={{0,3},{1,2},{2,1},{3,0},{4,7},{5,6},{6,5},{7,4},{8,11},{9,10},{10,... | collective-permute-start | bytes 737288 | tf_op jit(solution)/shard_map/ppermute | solution.py:57
  228.0 13.4 %collective-permute-start.69 = (bf16[160,768]{1,0:T(8,128)(2,1)S(1)}, bf16[160,768]{1,0:T(8,128)(2,1)S(1)}, u32[]{:S(2)}, u32[]{:S(2)}) collective-permute-start(bf16[160,768]{1,0:T(8,128)(2,1)S(1)} %get-tuple-element.171), channel_id=1, source_target_pairs={{0,2},{1,3},{2,0},{3,1},{4,6},{5,7},{6,4},{7,5},{8,10},{9,11},{10,... | collective-permute-start | bytes 737288 | tf_op jit(solution)/shard_map/ppermute | solution.py:57
  236.7 116.3 %collective-permute-start.85 = (bf16[768,4]{0,1:T(4,128)(2,1)S(1)}, bf16[768,4]{0,1:T(4,128)(2,1)}, u32[]{:S(2)}, u32[]{:S(2)}) collective-permute-start(bf16[768,4]{0,1:T(4,128)(2,1)S(1)} %get-tuple-element.385), channel_id=1, source_target_pairs={{0,16},{1,17},{2,18},{3,19},{4,20},{5,21},{6,22},{7,23},{8,24},{9,... | collective-permute-start | bytes 18440 | tf_op jit(solution)/shard_map/ppermute | solution.py:61
  243.4 31.9 %collective-permute-start.73 = (bf16[40,768]{1,0:T(8,128)(2,1)S(1)}, bf16[40,768]{1,0:T(8,128)(2,1)S(1)}, u32[]{:S(2)}, u32[]{:S(2)}) collective-permute-start(bf16[40,768]{1,0:T(8,128)(2,1)S(1)} %get-tuple-element.317), channel_id=1, source_target_pairs={{0,12},{4,8},{8,4},{12,0},{1,13},{5,9},{9,5},{13,1},{2,14},{6,10},... | collective-permute-start | bytes 184328 | tf_op jit(solution)/shard_map/ppermute | solution.py:57
  245.5 29.8 %collective-permute-start.72 = (bf16[40,768]{1,0:T(8,128)(2,1)S(1)}, bf16[40,768]{1,0:T(8,128)(2,1)S(1)}, u32[]{:S(2)}, u32[]{:S(2)}) collective-permute-start(bf16[40,768]{1,0:T(8,128)(2,1)S(1)} %get-tuple-element.318), channel_id=1, source_target_pairs={{0,8},{4,12},{8,0},{12,4},{1,9},{5,13},{9,1},{13,5},{2,10},{6,14},... | collective-permute-start | bytes 184328 | tf_op jit(solution)/shard_map/ppermute | solution.py:57
  246.8 31.0 %collective-permute-start.71 = (bf16[40,768]{1,0:T(8,128)(2,1)S(1)}, bf16[40,768]{1,0:T(8,128)(2,1)S(1)}, u32[]{:S(2)}, u32[]{:S(2)}) collective-permute-start(bf16[40,768]{1,0:T(8,128)(2,1)S(1)} %get-tuple-element.319), channel_id=1, source_target_pairs={{0,4},{4,0},{8,12},{12,8},{1,5},{5,1},{9,13},{13,9},{2,6},{6,2},{1... | collective-permute-start | bytes 184328 | tf_op jit(solution)/shard_map/ppermute | solution.py:57
  271.4 22.6 %collective-permute-start.41 = (bf16[256,384]{1,0:T(8,128)(2,1)}, bf16[256,384]{1,0:T(8,128)(2,1)}, u32[]{:S(2)}, u32[]{:S(2)}) collective-permute-start(bf16[256,384]{1,0:T(8,128)(2,1)} %get-tuple-element.137), channel_id=1, source_target_pairs={{0,4},{4,0},{8,12},{12,8},{1,5},{5,1},{9,13},{13,9},{2,6},{6,2},{1... | collective-permute-start | bytes 589832 | tf_op jit(solution)/shard_map/ppermute | solution.py:57
  275.3 18.8 %collective-permute-start.42 = (bf16[256,384]{1,0:T(8,128)(2,1)}, bf16[256,384]{1,0:T(8,128)(2,1)}, u32[]{:S(2)}, u32[]{:S(2)}) collective-permute-start(bf16[256,384]{1,0:T(8,128)(2,1)} %get-tuple-element.138), channel_id=1, source_target_pairs={{0,8},{4,12},{8,0},{12,4},{1,9},{5,13},{9,1},{13,5},{2,10},{6,14},... | collective-permute-start | bytes 589832 | tf_op jit(solution)/shard_map/ppermute | solution.py:57
  275.3 18.8 %collective-permute-start.43 = (bf16[256,384]{1,0:T(8,128)(2,1)}, bf16[256,384]{1,0:T(8,128)(2,1)}, u32[]{:S(2)}, u32[]{:S(2)}) collective-permute-start(bf16[256,384]{1,0:T(8,128)(2,1)} %get-tuple-element.139), channel_id=1, source_target_pairs={{0,12},{4,8},{8,4},{12,0},{1,13},{5,9},{9,5},{13,1},{2,14},{6,10},... | collective-permute-start | bytes 589832 | tf_op jit(solution)/shard_map/ppermute | solution.py:57
  304.5 7.2 %collective-permute-start.47 = (bf16[64,768]{1,0:T(8,128)(2,1)S(1)}, bf16[64,768]{1,0:T(8,128)(2,1)S(1)}, u32[]{:S(2)}, u32[]{:S(2)}) collective-permute-start(bf16[64,768]{1,0:T(8,128)(2,1)S(1)} %add_convert_fusion.6.refs_0_), channel_id=1, source_target_pairs={{0,1},{1,0},{2,3},{3,2},{4,5},{5,4},{6,7},{7,6},{8,9},{9,8},{10,11... | collective-permute-start | bytes 294920 | tf_op jit(solution)/shard_map/ppermute | solution.py:57
  304.9 6.9 %collective-permute-start.48 = (bf16[64,768]{1,0:T(8,128)(2,1)S(1)}, bf16[64,768]{1,0:T(8,128)(2,1)S(1)}, u32[]{:S(2)}, u32[]{:S(2)}) collective-permute-start(bf16[64,768]{1,0:T(8,128)(2,1)S(1)} %add_convert_fusion.6.refs_0_), channel_id=1, source_target_pairs={{0,2},{1,3},{2,0},{3,1},{4,6},{5,7},{6,4},{7,5},{8,10},{9,11},{10,... | collective-permute-start | bytes 294920 | tf_op jit(solution)/shard_map/ppermute | solution.py:57
  309.3 128.4 %collective-permute-start.79 = (bf16[768,768]{1,0:T(8,128)(2,1)}, bf16[768,768]{1,0:T(8,128)(2,1)}, u32[]{:S(2)}, u32[]{:S(2)}) collective-permute-start(bf16[768,768]{1,0:T(8,128)(2,1)} %fusion), channel_id=1, source_target_pairs={{0,16},{1,17},{2,18},{3,19},{4,20},{5,21},{6,22},{7,23},{8,24},{9,... | collective-permute-start | bytes 3538952 | tf_op jit(solution)/shard_map/ppermute | solution.py:61
  340.8 7.3 %collective-permute-start.55 = (bf16[160,768]{1,0:T(8,128)(2,1)S(1)}, bf16[160,768]{1,0:T(8,128)(2,1)S(1)}, u32[]{:S(2)}, u32[]{:S(2)}) collective-permute-start(bf16[160,768]{1,0:T(8,128)(2,1)S(1)} %get-tuple-element.155), channel_id=1, source_target_pairs={{0,3},{1,2},{2,1},{3,0},{4,7},{5,6},{6,5},{7,4},{8,11},{9,10},{10,... | collective-permute-start | bytes 737288 | tf_op jit(solution)/shard_map/ppermute | solution.py:57
  342.4 8.3 %collective-permute-start.54 = (bf16[160,768]{1,0:T(8,128)(2,1)S(1)}, bf16[160,768]{1,0:T(8,128)(2,1)S(1)}, u32[]{:S(2)}, u32[]{:S(2)}) collective-permute-start(bf16[160,768]{1,0:T(8,128)(2,1)S(1)} %get-tuple-element.154), channel_id=1, source_target_pairs={{0,2},{1,3},{2,0},{3,1},{4,6},{5,7},{6,4},{7,5},{8,10},{9,11},{10,... | collective-permute-start | bytes 737288 | tf_op jit(solution)/shard_map/ppermute | solution.py:57
  342.5 8.1 %collective-permute-start.53 = (bf16[160,768]{1,0:T(8,128)(2,1)S(1)}, bf16[160,768]{1,0:T(8,128)(2,1)S(1)}, u32[]{:S(2)}, u32[]{:S(2)}) collective-permute-start(bf16[160,768]{1,0:T(8,128)(2,1)S(1)} %get-tuple-element.153), channel_id=1, source_target_pairs={{0,1},{1,0},{2,3},{3,2},{4,5},{5,4},{6,7},{7,6},{8,9},{9,8},{10,11... | collective-permute-start | bytes 737288 | tf_op jit(solution)/shard_map/ppermute | solution.py:57
  348.1 7.1 %collective-permute-start.84 = (bf16[768,4]{0,1:T(4,128)(2,1)S(1)}, bf16[768,4]{0,1:T(4,128)(2,1)S(1)}, u32[]{:S(2)}, u32[]{:S(2)}) collective-permute-start(bf16[768,4]{0,1:T(4,128)(2,1)S(1)} %get-tuple-element.387), channel_id=1, source_target_pairs={{16,0},{17,1},{18,2},{19,3},{20,4},{21,5},{22,6},{23,7},{24,8},{25... | collective-permute-start | bytes 18440 | tf_op jit(solution)/shard_map/ppermute | solution.py:61
  351.8 7.3 %collective-permute-start.57 = (bf16[40,768]{1,0:T(8,128)(2,1)S(1)}, bf16[40,768]{1,0:T(8,128)(2,1)S(1)}, u32[]{:S(2)}, u32[]{:S(2)}) collective-permute-start(bf16[40,768]{1,0:T(8,128)(2,1)S(1)} %get-tuple-element.322), channel_id=1, source_target_pairs={{0,8},{4,12},{8,0},{12,4},{1,9},{5,13},{9,1},{13,5},{2,10},{6,14},... | collective-permute-start | bytes 184328 | tf_op jit(solution)/shard_map/ppermute | solution.py:57
  356.9 137.7 %reduce-scatter.6.cloned.1.call-start = ((), (), s32[]{:S(2)}) async-start(), calls=%async_computation.2 | async-start | bytes 1474560 | tf_op jit(solution)/shard_map/reduce_scatter | solution.py:687
  381.5 8.9 %collective-permute-start.59 = (bf16[256,384]{1,0:T(8,128)(2,1)S(1)}, bf16[256,384]{1,0:T(8,128)(2,1)S(1)}, u32[]{:S(2)}, u32[]{:S(2)}) collective-permute-start(bf16[256,384]{1,0:T(8,128)(2,1)S(1)} %get-tuple-element.160), channel_id=1, source_target_pairs={{0,4},{4,0},{8,12},{12,8},{1,5},{5,1},{9,13},{13,9},{2,6},{6,2},{1... | collective-permute-start | bytes 589832 | tf_op jit(solution)/shard_map/ppermute | solution.py:57
  381.7 16.1 %collective-permute-start.60 = (bf16[256,384]{1,0:T(8,128)(2,1)S(1)}, bf16[256,384]{1,0:T(8,128)(2,1)S(1)}, u32[]{:S(2)}, u32[]{:S(2)}) collective-permute-start(bf16[256,384]{1,0:T(8,128)(2,1)S(1)} %get-tuple-element.161), channel_id=1, source_target_pairs={{0,8},{4,12},{8,0},{12,4},{1,9},{5,13},{9,1},{13,5},{2,10},{6,14},... | collective-permute-start | bytes 589832 | tf_op jit(solution)/shard_map/ppermute | solution.py:57
  383.7 14.1 %collective-permute-start.61 = (bf16[256,384]{1,0:T(8,128)(2,1)S(1)}, bf16[256,384]{1,0:T(8,128)(2,1)S(1)}, u32[]{:S(2)}, u32[]{:S(2)}) collective-permute-start(bf16[256,384]{1,0:T(8,128)(2,1)S(1)} %get-tuple-element.162), channel_id=1, source_target_pairs={{0,12},{4,8},{8,4},{12,0},{1,13},{5,9},{9,5},{13,1},{2,14},{6,10},... | collective-permute-start | bytes 589832 | tf_op jit(solution)/shard_map/ppermute | solution.py:57
  401.4 37.9 %collective-permute-start.78 = (bf16[768,768]{1,0:T(8,128)(2,1)}, bf16[768,768]{1,0:T(8,128)(2,1)}, u32[]{:S(2)}, u32[]{:S(2)}) collective-permute-start(bf16[768,768]{1,0:T(8,128)(2,1)} %fusion.1), channel_id=1, source_target_pairs={{16,0},{17,1},{18,2},{19,3},{20,4},{21,5},{22,6},{23,7},{24,8},{25... | collective-permute-start | bytes 3538952 | tf_op jit(solution)/shard_map/ppermute | solution.py:61
  424.1 8.1 %collective-permute-start.63 = (bf16[64,768]{1,0:T(8,128)(2,1)S(1)}, bf16[64,768]{1,0:T(8,128)(2,1)S(1)}, u32[]{:S(2)}, u32[]{:S(2)}) collective-permute-start(bf16[64,768]{1,0:T(8,128)(2,1)S(1)} %copy-done.67), channel_id=1, source_target_pairs={{0,2},{1,3},{2,0},{3,1},{4,6},{5,7},{6,4},{7,5},{8,10},{9,11},{10,... | collective-permute-start | bytes 294920 | tf_op jit(solution)/shard_map/ppermute | solution.py:57
  424.7 9.6 %collective-permute-start.62 = (bf16[64,768]{1,0:T(8,128)(2,1)S(1)}, bf16[64,768]{1,0:T(8,128)(2,1)S(1)}, u32[]{:S(2)}, u32[]{:S(2)}) collective-permute-start(bf16[64,768]{1,0:T(8,128)(2,1)S(1)} %get-tuple-element.164), channel_id=1, source_target_pairs={{0,1},{1,0},{2,3},{3,2},{4,5},{5,4},{6,7},{7,6},{8,9},{9,8},{10,11... | collective-permute-start | bytes 294920 | tf_op jit(solution)/shard_map/ppermute | solution.py:57
  429.1 56.2 %collective-permute-start.87 = (bf16[768,768]{1,0:T(8,128)(2,1)}, bf16[768,768]{1,0:T(8,128)(2,1)}, u32[]{:S(2)}, u32[]{:S(2)}) collective-permute-start(bf16[768,768]{1,0:T(8,128)(2,1)} %get-tuple-element.389), channel_id=1, source_target_pairs={{0,16},{1,17},{2,18},{3,19},{4,20},{5,21},{6,22},{7,23},{8,24},{9,... | collective-permute-start | bytes 3538952 | tf_op jit(solution)/shard_map/ppermute | solution.py:61
  432.1 24.8 %collective-permute-start.74 = (f32[256,768]{1,0:T(8,128)S(1)}, f32[256,768]{1,0:T(8,128)}, u32[]{:S(2)}, u32[]{:S(2)}) collective-permute-start(f32[256,768]{1,0:T(8,128)S(1)} %copy-done.20), channel_id=1, source_target_pairs={{0,16},{1,17},{2,18},{3,19},{4,20},{5,21},{6,22},{7,23},{8,24},{9,... | collective-permute-start | bytes 2359304 | tf_op jit(solution)/shard_map/ppermute | solution.py:61
  436.4 49.0 %collective-permute-start.86 = (bf16[768,768]{1,0:T(8,128)(2,1)}, bf16[768,768]{1,0:T(8,128)(2,1)}, u32[]{:S(2)}, u32[]{:S(2)}) collective-permute-start(bf16[768,768]{1,0:T(8,128)(2,1)} %get-tuple-element.391), channel_id=1, source_target_pairs={{16,0},{17,1},{18,2},{19,3},{20,4},{21,5},{22,6},{23,7},{24,8},{25... | collective-permute-start | bytes 3538952 | tf_op jit(solution)/shard_map/ppermute | solution.py:61
  437.7 7.1 %collective-permute-start.82 = (bf16[768]{0:T(1024)(128)(2,1)S(1)}, bf16[768]{0:T(1024)(128)(2,1)S(1)}, u32[]{:S(2)}, u32[]{:S(2)}) collective-permute-start(bf16[768]{0:T(1024)(128)(2,1)S(1)} %convert_reduce_fusion.1), channel_id=1, source_target_pairs={{16,0},{17,1},{18,2},{19,3},{20,4},{21,5},{22,6},{23,7},{24,8},{25... | collective-permute-start | bytes 4616 | tf_op jit(solution)/shard_map/ppermute | solution.py:61
  439.3 7.0 %collective-permute-start.65 = (bf16[64,768]{1,0:T(8,128)(2,1)S(1)}, bf16[64,768]{1,0:T(8,128)(2,1)S(1)}, u32[]{:S(2)}, u32[]{:S(2)}) collective-permute-start(bf16[64,768]{1,0:T(8,128)(2,1)S(1)} %add_convert_fusion.5.refs_0_), channel_id=1, source_target_pairs={{0,1},{1,0},{2,3},{3,2},{4,5},{5,4},{6,7},{7,6},{8,9},{9,8},{10,11... | collective-permute-start | bytes 294920 | tf_op jit(solution)/shard_map/ppermute | solution.py:57
  446.3 8.3 %collective-permute-start.67 = (bf16[64,768]{1,0:T(8,128)(2,1)S(1)}, bf16[64,768]{1,0:T(8,128)(2,1)S(1)}, u32[]{:S(2)}, u32[]{:S(2)}) collective-permute-start(bf16[64,768]{1,0:T(8,128)(2,1)S(1)} %add_convert_fusion.5.refs_0_), channel_id=1, source_target_pairs={{0,3},{1,2},{2,1},{3,0},{4,7},{5,6},{6,5},{7,4},{8,11},{9,10},{10,... | collective-permute-start | bytes 294920 | tf_op jit(solution)/shard_map/ppermute | solution.py:57
  449.6 40.2 %collective-permute-start.89 = (bf16[768,768]{1,0:T(8,128)(2,1)}, bf16[768,768]{1,0:T(8,128)(2,1)}, u32[]{:S(2)}, u32[]{:S(2)}) collective-permute-start(bf16[768,768]{1,0:T(8,128)(2,1)} %get-tuple-element.393), channel_id=1, source_target_pairs={{0,16},{1,17},{2,18},{3,19},{4,20},{5,21},{6,22},{7,23},{8,24},{9,... | collective-permute-start | bytes 3538952 | tf_op jit(solution)/shard_map/ppermute | solution.py:61
  456.9 32.9 %collective-permute-start.88 = (bf16[768,768]{1,0:T(8,128)(2,1)}, bf16[768,768]{1,0:T(8,128)(2,1)}, u32[]{:S(2)}, u32[]{:S(2)}) collective-permute-start(bf16[768,768]{1,0:T(8,128)(2,1)} %get-tuple-element.395), channel_id=1, source_target_pairs={{16,0},{17,1},{18,2},{19,3},{20,4},{21,5},{22,6},{23,7},{24,8},{25... | collective-permute-start | bytes 3538952 | tf_op jit(solution)/shard_map/ppermute | solution.py:61
  463.5 29.8 %collective-permute-start.75 = (f32[256,768]{1,0:T(8,128)S(1)}, f32[256,768]{1,0:T(8,128)S(1)}, u32[]{:S(2)}, u32[]{:S(2)}) collective-permute-start(f32[256,768]{1,0:T(8,128)S(1)} %get-tuple-element.168), channel_id=1, source_target_pairs={{16,0},{17,1},{18,2},{19,3},{20,4},{21,5},{22,6},{23,7},{24,8},{25... | collective-permute-start | bytes 2359304 | tf_op jit(solution)/shard_map/ppermute | solution.py:61
  (192 other events, 1856.4 us)
Sparse Core Ops, SparseCore 0:
  10.3 30.4 all-gather.3
  357.0 18.2 reduce-scatter.7
  444.9 31.5 reduce-scatter.5

commit v2 on v1

v2 whole, which is shorter than its diff:
```python
import math

import jax
import jax.numpy as jnp
from jax import lax
from jax.experimental import pallas as pl
from jax.experimental.pallas import tpu as pltpu
from jax.sharding import PartitionSpec as P

HD = 64
BUCKETS = 32
REACH = 128
EPSILON = 1e-06
NEGATIVE = -1e30
F32 = jnp.float32
BF16 = jnp.bfloat16
LANES = 128
SPARE_BYTES = 6 * 1024 * 1024
ROOT_2_PI = math.sqrt(2.0 / math.pi)


class Pick:
    def __init__(self, first, second):
        self.arrays, self.shape = (first, second), first.shape
        self.dtype, self.ndim = first.dtype, first.ndim


class Rows:
    def __init__(self, array, layer, width, own=False):
        n_heads = array.shape[0] // (2 * width)
        self.array, self.layer, self.width, self.own = array, layer, width, own
        self.shape = (width if own else n_heads * width,) + array.shape[1:]
        self.dtype, self.ndim, self.n_heads = array.dtype, array.ndim, n_heads


class Held:
    def __init__(self, buffer, wait):
        self.buffer, self.wait, self.here = buffer, wait, False

    def ready(self):
        if not self.here:
            self.wait()
        self.here = True
        return self.buffer


def padded_bytes(array):
    *lead, rows, lanes = (1, 1) + tuple(array.shape)
    return math.prod(lead) * (-(-rows // 16) * 16) * (-(-lanes // LANES) * LANES) * jnp.dtype(array.dtype).itemsize


def kernel_call(body, outs, args, scratch=(), flops=0, after=()):
    picks = [a for a in args if isinstance(a, (Pick, Rows))]
    operands, in_specs = [], []
    for a in args:
        if isinstance(a, (Pick, Rows)):
            arrays = a.arrays if isinstance(a, Pick) else (a.array,)
            operands += arrays
            in_specs += [pl.BlockSpec(memory_space=pltpu.HBM)] * len(arrays)
        else:
            scalar = a.ndim == 1 and a.dtype == jnp.int32
            operands.append(a)
            in_specs.append(pl.BlockSpec(memory_space=pltpu.SMEM if scalar else pltpu.VMEM))
    operands += after
    in_specs += [pl.BlockSpec(memory_space=pl.ANY)] * len(after)
    scratch = list(scratch) + [pltpu.VMEM(p.shape, p.dtype) for p in picks]
    if picks:
        scratch.append(pltpu.SemaphoreType.DMA((len(picks),)))
    n_out, n_own = len(outs), len(scratch) - len(picks) - (1 if picks else 0)

    def hold(a, sources, place_ref, buffer, sem):
        if isinstance(a, Pick):
            for section, src in enumerate(sources):

                @pl.when(place_ref[2] == section)
                def _(src=src):
                    pltpu.make_async_copy(src, buffer, sem).start()

            return Held(buffer, pltpu.make_async_copy(sources[0], buffer, sem).wait)
        copies = []
        for h in range(1 if a.own else a.n_heads):
            block = 2 * (place_ref[1] if a.own else h) + (place_ref[2] ^ a.layer)
            src = sources[0].at[pl.ds(pl.multiple_of(block * a.width, a.width), a.width)]
            dst = buffer.at[pl.ds(h * a.width, a.width)]
            copies.append(pltpu.make_async_copy(src, dst, sem))
            copies[-1].start()

        def wait():
            for copy in copies:
                copy.wait()

        return Held(buffer, wait)

    def wrapped(*refs):
        ins, rest = refs[: len(operands)], refs[len(operands) :]
        buffers = list(rest[n_out + n_own :])
        given, at, number = [], 0, 0
        for a in args:
            if not isinstance(a, (Pick, Rows)):
                given.append(ins[at])
                at += 1
                continue
            count = 2 if isinstance(a, Pick) else 1
            sem = buffers[-1].at[number]
            given.append(hold(a, ins[at : at + count], ins[0], buffers[number], sem))
            at, number = at + count, number + 1
        body(*given, *rest[: n_out + n_own])

    size = sum(math.prod(a.shape) * a.dtype.itemsize for a in list(args) + list(outs))
    held = sum(map(padded_bytes, list(args) + list(outs)))
    held += sum(padded_bytes(s) for s in scratch[: n_own])
    return pl.pallas_call(
        wrapped,
        out_shape=outs,
        in_specs=in_specs,
        out_specs=[pl.BlockSpec(memory_space=pltpu.VMEM)] * n_out,
        scratch_shapes=scratch,
        compiler_params=pltpu.CompilerParams(vmem_limit_bytes=held + SPARE_BYTES),
        cost_estimate=pl.CostEstimate(flops=flops, bytes_accessed=size, transcendentals=0),
    )(*operands)


def like(*shape, dtype=BF16):
    return jax.ShapeDtypeStruct(shape, dtype)


def dot(a, b, contract=((1,), (0,))):
    return lax.dot_general(a, b, (contract, ((), ())), preferred_element_type=F32)


def dot_nt(a, b):
    return dot(a, b, ((1,), (1,)))


def dot_tn(a, b):
    return dot(a, b, ((0,), (0,)))


def swap(array, axis, by=1):
    devices = lax.axis_size(axis)
    return lax.ppermute(array, axis, [(i, i ^ by) for i in range(devices)])


def one_way(array, source):
    return lax.ppermute(array, "section", [(source, 1 - source)])


def exchange(chunks, axis):
    return [chunks[0]] + [swap(chunks[r], axis, r) for r in range(1, len(chunks))]


def gather_rows(array, axis):
    return lax.all_gather(array, axis, axis=0, tiled=True)


def project_rows(x, gain, w, normed_ref, q_ref, kv_ref):
    width = q_ref.shape[1]
    scale = lax.rsqrt(jnp.mean(x * x, axis=-1, keepdims=True) + EPSILON)
    normed = (x * scale * gain).astype(BF16)
    normed_ref[...] = normed
    w_ref = w.ready()
    kv_ref[:, :width] = dot(normed, w_ref[1]).astype(BF16)
    kv_ref[:, width:] = dot(normed, w_ref[2]).astype(BF16)
    q_ref[...] = dot(normed, w_ref[0]).astype(BF16)


def either(place_ref, first, second):
    return jnp.where(place_ref[2] == 0, first, second)


def begin(place, own, given, gain_own, gain_other, qkv):
    _, rows, model = own.shape
    width = qkv.shape[2]

    def body(place_ref, own_ref, given_ref, gain_ref, other_ref, w, x_ref, cotangent_ref, *outs):
        x = either(place_ref, own_ref[0], given_ref[...])
        x_ref[...] = x
        cotangent_ref[...] = either(place_ref, given_ref[...], own_ref[1])
        gain = either(place_ref, gain_ref[...].astype(F32), other_ref[...].astype(F32))
        project_rows(x.astype(F32), gain, w, *outs)

    return kernel_call(
        body,
        [like(rows, model)] * 3 + [like(rows, width), like(rows, 2 * width)],
        [place, own, given, gain_own, gain_other, qkv],
        flops=6 * rows * model * width,
    )


def tile_pick(block, key_tile, mine, ordered, n_ctx):
    owner = key_tile // 2 if ordered else mine ^ (key_tile // 2)
    key_block = owner if key_tile % 2 == 0 else 2 * n_ctx - 1 - owner
    return jnp.clip(block - key_block, -1, 2) + 1


def query_parts(mine, half, n_ctx):
    return [
        (slice(0, half), mine),
        (slice(half, 2 * half), 2 * n_ctx - 1 - mine),
    ]


def load_keys(kv_refs, kv_ref):
    rows = kv_refs[0].shape[0]
    for r, ref in enumerate(kv_refs):
        kv_ref[r * rows : (r + 1) * rows, :] = ref[...]


def attend(place, q, kv_parts, table, n_ctx):
    rows, width = q.shape
    half, heads, keys = rows // 2, width // HD, rows * n_ctx
    ordered, count = len(kv_parts) == 1, len(kv_parts)

    def body(place_ref, q_ref, *refs):
        kv_refs, (table_ref, mix_ref, lse_ref, scores_ref, kv_ref) = refs[:count], refs[count:]
        mine = place_ref[0]
        load_keys(kv_refs, kv_ref)
        for head in range(heads):
            cols = slice(head * HD, (head + 1) * HD)
            key_rows = kv_ref[:, cols]
            value_rows = kv_ref[:, width + head * HD : width + (head + 1) * HD]
            for part, (span, block) in enumerate(query_parts(mine, half, n_ctx)):
                raw = dot_nt(q_ref[span, cols], key_rows)
                for key_tile in range(2 * n_ctx):
                    pick = tile_pick(block, key_tile, mine, ordered, n_ctx)
                    tile = slice(key_tile * half, (key_tile + 1) * half)
                    scores_ref[part, :, tile] = raw[:, tile] * 0.125 + table_ref[head, pick]
                scores = scores_ref[part]
                top = jnp.max(scores, axis=1, keepdims=True)
                mass = jnp.exp(scores - top)
                total = jnp.sum(mass, axis=1, keepdims=True)
                out = dot(mass.astype(BF16), value_rows) / total
                mix_ref[span, cols] = out.astype(BF16)
                lse_ref[span, head : head + 1] = top + jnp.log(total)

    return kernel_call(
        body,
        [like(rows, width), like(rows, heads, dtype=F32)],
        [place, q, *kv_parts, table],
        [pltpu.VMEM((2, half, keys), F32), pltpu.VMEM((keys, 2 * width), BF16)],
        flops=4 * rows * keys * width,
    )


def attend_back(place, q, kv_parts, table, lse, dmix, n_ctx):
    rows, width = q.shape
    half, heads, keys = rows // 2, width // HD, rows * n_ctx
    ordered, count = len(kv_parts) == 1, len(kv_parts)

    def body(place_ref, q_ref, *refs):
        kv_refs, refs = refs[:count], refs[count:]
        table_ref, lse_ref, dmix_ref, dq_ref, dtable_ref = refs[:5]
        chunk_refs, (scores_ref, total_ref, kv_ref) = refs[5 : 5 + n_ctx], refs[5 + n_ctx :]
        mine = place_ref[0]
        load_keys(kv_refs, kv_ref)
        dtable_ref[...] = jnp.zeros(dtable_ref.shape, F32)
        for head in range(heads):
            cols = slice(head * HD, (head + 1) * HD)
            value_cols = slice(width + head * HD, width + (head + 1) * HD)
            key_rows = kv_ref[:, cols]
            value_rows = kv_ref[:, value_cols]
            for part, (span, block) in enumerate(query_parts(mine, half, n_ctx)):
                q = q_ref[span, cols]
                dmix = dmix_ref[span, cols]
                raw = dot_nt(q, key_rows)
                for key_tile in range(2 * n_ctx):
                    pick = tile_pick(block, key_tile, mine, ordered, n_ctx)
                    tile = slice(key_tile * half, (key_tile + 1) * half)
                    scores_ref[part, :, tile] = raw[:, tile] * 0.125 + table_ref[head, pick]
                probs = jnp.exp(scores_ref[part] - lse_ref[span, head : head + 1])
                dprobs = dot_nt(dmix, value_rows)
                delta = jnp.sum(probs * dprobs, axis=1, keepdims=True)
                dscores = (probs * (dprobs - delta)).astype(BF16)
                dq_ref[span, cols] = (dot(dscores, key_rows) * 0.125).astype(BF16)
                dkeys = dot_tn(dscores, q) * 0.125
                dvalues = dot_tn(probs.astype(BF16), dmix)
                if part == 0:
                    total_ref[:, cols] = dkeys
                    total_ref[:, value_cols] = dvalues
                else:
                    total_ref[:, cols] += dkeys
                    total_ref[:, value_cols] += dvalues
                for key_tile in range(2 * n_ctx):
                    pick = tile_pick(block, key_tile, mine, ordered, n_ctx)
                    tile = dscores[:, key_tile * half : (key_tile + 1) * half]
                    dtable_ref[head, pick] += tile.astype(F32)
        for r in range(n_ctx):
            first = pl.multiple_of((mine ^ r if ordered else r) * rows, rows)
            chunk_refs[r][...] = total_ref[pl.ds(first, rows), :].astype(BF16)

    outs = kernel_call(
        body,
        [like(rows, width), like(*table.shape, dtype=F32)] + [like(rows, 2 * width)] * n_ctx,
        [place, q, *kv_parts, table, lse, dmix],
        [
            pltpu.VMEM((2, half, keys), F32),
            pltpu.VMEM((keys, 2 * width), F32),
            pltpu.VMEM((keys, 2 * width), BF16),
        ],
        flops=10 * rows * keys * width,
    )
    return outs[0], outs[1], outs[2:]


def token_picks(tokens_ref, count, first=0):
    ids = first + lax.broadcasted_iota(jnp.int32, (tokens_ref.shape[0], count), 1)
    hit = (ids == tokens_ref[:, 0:1]) | (ids == tokens_ref[:, 1:2])
    return jnp.where(hit, 1.0, 0.0).astype(BF16)


def dispatch_into(rows, place_ref, tokens_ref, chunk_refs):
    per = chunk_refs[0].shape[0]
    first = place_ref[1] * (per * len(chunk_refs))
    for r, chunk_ref in enumerate(chunk_refs):
        picks = token_picks(tokens_ref, per, first + r * per)
        chunk_ref[...] = dot_tn(picks, rows).astype(BF16)


def dispatch_whole(place, rows, tokens, n_ctx, per, n_heads, after):
    count, model = rows.shape

    def body(place_ref, rows_ref, tokens_ref, *chunk_refs):
        lane = lax.broadcasted_iota(jnp.int32, (count, n_heads * per), 1)
        ids = lane
        for h in range(1, n_heads):
            ids += jnp.where(lane >= h * per, (n_ctx - 1) * per, 0)
        for r, chunk_ref in enumerate(chunk_refs):
            here = ids + r * per
            hit = (here == tokens_ref[:, 0:1]) | (here == tokens_ref[:, 1:2])
            picks = jnp.where(hit, 1.0, 0.0).astype(BF16)
            chunk_ref[...] = dot_tn(picks, rows_ref[...]).astype(BF16)

    return kernel_call(
        body, [like(n_heads * per, model)] * n_ctx, [place, rows, tokens], after=after
    )


def finish_attention(place, mixes, out_w, x, gain, tokens, n_ctx, per):
    rows, model = x.shape
    n_heads, width = len(mixes), mixes[0].shape[1]

    def body(place_ref, *refs):
        mix_refs, refs = refs[:n_heads], refs[n_heads:]
        w_ref, x_ref, gain_ref, tokens_ref, middle_ref = refs[:5]
        chunk_refs, mixed_ref = refs[5:-1], refs[-1]
        for r in range(n_heads):
            mixed_ref[place_ref[1] ^ r] = mix_refs[r][...]
        middle = x_ref[...].astype(F32)
        w_ref = w_ref.ready()
        attended = dot(mixed_ref[0], w_ref[:width, :])
        for h in range(1, n_heads):
            attended += dot(mixed_ref[h], w_ref[h * width : (h + 1) * width, :])
        middle = middle + attended
        middle_ref[...] = middle
        scale = lax.rsqrt(jnp.mean(middle * middle, axis=-1, keepdims=True) + EPSILON)
        expert_in = (middle * scale * gain_ref[...]).astype(BF16)
        dispatch_into(expert_in, place_ref, tokens_ref, chunk_refs)

    outs = kernel_call(
        body,
        [like(rows, model, dtype=F32)] + [like(per, model)] * n_ctx,
        [place, *mixes, out_w, x, gain, tokens],
        [pltpu.VMEM((n_heads, rows, width), BF16)],
        flops=2 * rows * model * model + 2 * rows * model * per * n_ctx,
    )
    return outs[0], outs[1:]


def gelu_parts(v):
    inner = jnp.tanh(ROOT_2_PI * (v + 0.044715 * v * v * v))
    return inner, 0.5 * v * (1.0 + inner)


def route_signs(place_ref, other):
    lane = lax.broadcasted_iota(jnp.int32, (other.shape[0], LANES), 1)
    return jnp.where(lane == place_ref[0], 1.0, 0.0) - jnp.where(lane == other, 1.0, 0.0)


def expert_hidden(place_ref, rows, up_ref, router_ref, other):
    logits = dot(rows, router_ref[...])
    margin = jnp.sum(logits * route_signs(place_ref, other), axis=1, keepdims=True)
    pre_act = dot(rows, up_ref[...])
    return margin, pre_act, gelu_parts(pre_act)[1].astype(BF16)


def sigmoid(v):
    return 1.0 / (1.0 + jnp.exp(-v))


def experts(place, arrived, up, down, router, other, n_heads):
    slots, model = arrived.shape
    per, hidden_width = slots // n_heads, up.shape[1]

    def body(place_ref, in_ref, up, down, router_ref, other_ref, *refs):
        chunk_refs, (pre_ref, hidden_ref, margin_ref) = refs[:n_heads], refs[n_heads:]
        up_ref = up.ready()
        for r in range(n_heads):
            span = pl.ds(pl.multiple_of((place_ref[1] ^ r) * per, per), per)
            margin, pre_act, hidden = expert_hidden(
                place_ref, in_ref[span, :], up_ref, router_ref, other_ref[span, :]
            )
            margin_ref[span, :] = margin
            pre_ref[span, :] = pre_act
            hidden_ref[span, :] = hidden
            out = sigmoid(margin) * dot(hidden, down.ready()[...])
            chunk_refs[r][...] = out.astype(BF16)

    outs = kernel_call(
        body,
        [like(per, model)] * n_heads
        + [
            like(slots, hidden_width, dtype=F32),
            like(slots, hidden_width),
            like(slots, 1, dtype=F32),
        ],
        [place, arrived, up, down, router, other],
        flops=4 * slots * model * hidden_width,
    )
    return outs[:n_heads], outs[n_heads:]


def experts_out(place, hidden, margin, down, n_heads, after):
    slots, model = hidden.shape[0], down.shape[1]
    per = slots // n_heads

    def body(place_ref, hidden_ref, margin_ref, down, *chunk_refs):
        down_ref = down.ready()
        for r in range(n_heads):
            span = pl.ds(pl.multiple_of((place_ref[1] ^ r) * per, per), per)
            out = sigmoid(margin_ref[span, :]) * dot(hidden_ref[span, :], down_ref[...])
            chunk_refs[r][...] = out.astype(BF16)

    return kernel_call(
        body,
        [like(per, model)] * n_heads,
        [place, hidden, margin, down],
        flops=2 * slots * model * hidden.shape[1],
        after=after,
    )


def experts_back(place, dout_rows, kept, arrived, up, down, router, other, n_heads, after=()):
    slots, model = dout_rows.shape
    per, hidden_width = slots // n_heads, up.shape[1]
    taken = [arrived] if kept is None else list(kept)

    def body(place_ref, dout_ref, *refs):
        kept_refs, refs = refs[: len(taken)], refs[len(taken) :]
        up, down, router_ref, other_ref = refs[:4]
        chunk_refs, refs = refs[4 : 4 + n_heads], refs[4 + n_heads :]
        dpre_ref, dslots_ref, dlogits_ref = refs[:3]
        up_ref, down_ref = up.ready(), down.ready()
        for r in range(n_heads):
            span = pl.ds(pl.multiple_of((place_ref[1] ^ r) * per, per), per)
            if kept is None:
                margin, v, hidden = expert_hidden(
                    place_ref, kept_refs[0][span, :], up_ref, router_ref, other_ref[span, :]
                )
                refs[3][span, :] = hidden
                refs[4][span, :] = margin
            else:
                v, hidden, margin = (ref[span, :] for ref in kept_refs)
            dout = dout_ref[span, :]
            dhidden = dot_nt(dout, down_ref[...])
            gate = sigmoid(margin)
            dgate = jnp.sum(dhidden * hidden.astype(F32), axis=1, keepdims=True)
            inner, _ = gelu_parts(v)
            slope = 0.5 * (1.0 + inner) + 0.5 * v * (1.0 - inner * inner) * ROOT_2_PI * (
                1.0 + 3.0 * 0.044715 * v * v
            )
            dpre = (gate * dhidden * slope).astype(BF16)
            dpre_ref[span, :] = dpre
            dslots_ref[span, :] = (gate * dout.astype(F32)).astype(BF16)
            signs = route_signs(place_ref, other_ref[span, :])
            dlogits = (gate * sigmoid(-margin) * dgate * signs).astype(BF16)
            dlogits_ref[span, :] = dlogits
            chunk_refs[r][...] = (
                dot_nt(dpre, up_ref[...]) + dot_nt(dlogits, router_ref[...])
            ).astype(BF16)

    extra = [like(slots, hidden_width), like(slots, 1, dtype=F32)] if kept is None else []
    outs = kernel_call(
        body,
        [like(per, model)] * n_heads
        + [like(slots, hidden_width), like(slots, model), like(slots, LANES)]
        + extra,
        [place, dout_rows, *taken, up, down, router, other],
        flops=4 * slots * model * hidden_width,
        after=after,
    )
    return outs[:n_heads], outs[n_heads:]


def expert_grads(place, pairs, got=None, after=()):
    outs = [like(p[0].shape[1], p[1].shape[1], dtype=BF16 if got is None else F32) for p in pairs]
    picks = [a for pair in pairs for a in pair]

    def body(place_ref, *refs):
        held, refs = refs[: len(picks)], refs[len(picks) :]
        got_refs, out_refs = refs[: len(refs) - len(pairs)], refs[len(refs) - len(pairs) :]
        for i, out_ref in enumerate(out_refs):
            grad = dot_tn(held[2 * i].ready()[...], held[2 * i + 1].ready()[...])
            if got_refs:
                grad += got_refs[i][...].astype(F32)
            out_ref[...] = grad.astype(out_ref.dtype)

    flops = sum(2 * p[0].shape[0] * p[0].shape[1] * p[1].shape[1] for p in pairs)
    return kernel_call(body, outs, [place, *picks, *(got or [])], flops=flops, after=after)


def dense_shares(place, pairs, n_ctx):
    model = pairs[0][0].shape[1]
    widths = [b.shape[1] for _, b in pairs]
    share, width = model // n_ctx, sum(widths)

    def body(place_ref, *refs):
        ins, out_ref, total_ref = refs[: 2 * len(pairs)], refs[-2], refs[-1]
        at = 0
        for i, size in enumerate(widths):
            total_ref[:, at : at + size] = dot_tn(ins[2 * i][...], ins[2 * i + 1][...])
            at += size
        for r in range(n_ctx):
            first = pl.multiple_of((place_ref[0] ^ r) * share, share)
            out_ref[r] = total_ref[pl.ds(first, share), :].astype(BF16)

    rows = pairs[0][0].shape[0]
    return kernel_call(
        body,
        [like(n_ctx, share, width)],
        [place, *(a for pair in pairs for a in pair)],
        [pltpu.VMEM((model, width), F32)],
        flops=2 * rows * model * width,
    )[0]


def add_shares(one, two):
    n_ctx, share, width = one.shape

    def body(one_ref, two_ref, *outs):
        for r, out_ref in enumerate(outs):
            out_ref[...] = (one_ref[r].astype(F32) + two_ref[r].astype(F32)).astype(BF16)

    return kernel_call(body, [like(share, width)] * n_ctx, [one, two])


def sum_shares(parts):
    share, width = parts[0].shape

    def body(*refs):
        refs[-1][...] = tree_sum([ref[...].astype(F32) for ref in refs[:-1]]).astype(BF16)

    return kernel_call(body, [like(share, width)], parts)[0]


def dense_grads(place, parts0, sum1, got1, width):
    share = sum1.shape[0]

    def body(place_ref, *refs):
        part_refs, (sum_ref, got_ref, qkv_ref, out_ref) = refs[:-4], refs[-4:]
        layer0 = tree_sum([ref[...].astype(F32) for ref in part_refs])
        layer1 = sum_ref[...].astype(F32) + got_ref[...].astype(F32)
        total = either(place_ref, layer0, layer1)
        for i, at in enumerate((0, 2, 3)):
            qkv_ref[i] = total[:, at * width : (at + 1) * width]
        out_ref[...] = total[:, width : 2 * width].T

    return kernel_call(
        body,
        [like(3, share, width, dtype=F32), like(width, share, dtype=F32)],
        [place, *parts0, sum1, got1],
    )


def small_pack(place, layers, n_experts, n_heads, after=()):
    model = layers[0][0].shape[1]
    rows = 1 + n_experts + n_heads

    def body(place_ref, *refs):
        out_ref = refs[-1]
        out_ref[...] = jnp.zeros(out_ref.shape, F32)
        for layer in range(2):
            dgain_ref, dlogits_ref, arrived_ref, lanes_ref = refs[4 * layer : 4 * layer + 4]
            at = layer * rows
            out_ref[at : at + 1, :] = dgain_ref[...] * (1.0 / n_heads)
            router = dot_tn(dlogits_ref[...], arrived_ref[...])
            out_ref[at + 1 : at + 1 + n_experts, :] = router[:n_experts]
            count = lanes_ref.shape[0]
            eye = lax.broadcasted_iota(jnp.int32, (count, count), 0) == lax.broadcasted_iota(
                jnp.int32, (count, count), 1
            )
            sums = jnp.sum(lanes_ref[...], axis=1, keepdims=True)
            row = jnp.sum(jnp.where(eye, sums, 0.0), axis=0, keepdims=True)
            for h in range(n_heads):
                spot = at + 1 + n_experts + h
                out_ref[spot : spot + 1, :count] = jnp.where(place_ref[1] == h, row, 0.0)

    return kernel_call(
        body,
        [like(2 * rows, model, dtype=F32)],
        [place, *(a for layer in layers for a in layer)],
        after=after,
    )[0]


def assemble(place, dx, got_out, got_dx, out):
    def body(place_ref, one, two, both_ref):
        both_ref[0] = one.ready()[...]
        both_ref[1] = two.ready()[...]

    picks = [Pick(dx, got_out), Pick(got_dx, out)]
    return kernel_call(body, [like(2, *dx.shape, dtype=F32)], [place, *picks])[0]


def combine(middle, returned, tokens, after):
    rows, model = middle.shape
    share = returned[0].shape[0]

    def body(middle_ref, tokens_ref, *refs):
        total = 0.0
        for r, ref in enumerate(refs[: len(returned)]):
            total += dot(token_picks(tokens_ref, share, r * share), ref[...])
        refs[-1][...] = middle_ref[...] + total

    return kernel_call(
        body,
        [like(rows, model, dtype=F32)],
        [middle, tokens, *returned],
        flops=2 * rows * model * share * len(returned),
        after=after,
    )[0]


def combine_project(place, middle, returned, tokens, gain, qkv):
    rows, model = middle.shape
    width = qkv.shape[2]

    def body(place_ref, middle_ref, returned_ref, tokens_ref, gain_ref, w, passed_ref, *outs):
        picks = token_picks(tokens_ref, returned_ref.shape[0])
        passed = (middle_ref[...] + dot(picks, returned_ref[...])).astype(BF16)
        passed_ref[...] = passed
        project_rows(passed.astype(F32), gain_ref[...], w, *outs)

    return kernel_call(
        body,
        [like(rows, model), like(rows, model), like(rows, width), like(rows, 2 * width)],
        [place, middle, returned, tokens, gain, qkv],
        flops=2 * rows * model * returned.shape[0] + 6 * rows * model * width,
    )


def norm_back(values, gain, upstream):
    scale = lax.rsqrt(jnp.mean(values * values, axis=-1, keepdims=True) + EPSILON)
    unit = values * scale
    scaled = upstream * gain
    dvalues = scale * (scaled - unit * jnp.mean(unit * scaled, axis=-1, keepdims=True))
    return dvalues, jnp.sum(upstream * unit, axis=0, keepdims=True)


def middle_back(place, returned, tokens, middle, gain, dout, out_w, after=()):
    rows, model = middle.shape
    width = out_w.shape[0]

    def body(place_ref, returned_ref, tokens_ref, middle_ref, gain_ref, dout_ref, w, *refs):
        dmiddle_ref, datt_ref, dmix_ref, dgain_ref = refs
        picks = token_picks(tokens_ref, returned_ref.shape[0])
        dexpert_in = dot(picks, returned_ref[...])
        part, dgain = norm_back(middle_ref[...], gain_ref[...], dexpert_in)
        dgain_ref[...] = dgain
        dmiddle = dout_ref[...].astype(F32) + part
        dmiddle_ref[...] = dmiddle
        datt = dmiddle.astype(BF16)
        datt_ref[...] = datt
        dmix_ref[...] = dot_nt(datt, w.ready()[...]).astype(BF16)

    return kernel_call(
        body,
        [
            like(rows, model, dtype=F32),
            like(rows, model),
            like(rows, width),
            like(1, model, dtype=F32),
        ],
        [place, returned, tokens, middle, gain, dout, out_w],
        flops=2 * rows * model * (returned.shape[0] + width),
        after=after,
    )


def project_back(place, dq, dkv_parts, qkv, n_heads, after=()):
    rows, width = dq.shape
    model, n_parts = qkv.shape[1], len(dkv_parts)
    share = rows // n_heads

    def body(place_ref, dq_ref, *refs):
        part_refs, refs = refs[:n_parts], refs[n_parts:]
        w, dkv_ref = refs[:2]
        chunk_refs, total_ref = refs[2:-1], refs[-1]
        dkv = part_refs[0][...].astype(F32)
        for ref in part_refs[1:]:
            dkv += ref[...].astype(F32)
        dkv = dkv.astype(BF16)
        dkv_ref[...] = dkv
        w_ref = w.ready()
        total_ref[...] = (
            dot_nt(dq_ref[...], w_ref[0])
            + dot_nt(dkv[:, :width], w_ref[1])
            + dot_nt(dkv[:, width:], w_ref[2])
        )
        for r in range(n_heads):
            first = pl.multiple_of((place_ref[1] ^ r) * share, share)
            chunk_refs[r][...] = total_ref[pl.ds(first, share), :].astype(BF16)

    outs = kernel_call(
        body,
        [like(rows, 2 * width)] + [like(share, model)] * n_heads,
        [place, dq, *dkv_parts, qkv],
        [pltpu.VMEM((rows, model), F32)],
        flops=6 * rows * model * width,
        after=after,
    )
    return outs[0], outs[1:]


def tree_sum(values):
    while len(values) > 1:
        values = [values[i] + values[i + 1] for i in range(0, len(values), 2)]
    return values[0]


def share_sum(place, parts, x):
    share, model = parts[0].shape

    def body(place_ref, *refs):
        part_refs, (x_ref, total_ref, dgain_ref) = refs[: len(parts)], refs[len(parts) :]
        total = tree_sum([ref[...].astype(F32) for ref in part_refs])
        total_ref[...] = total.astype(BF16)
        first = pl.multiple_of(place_ref[1] * share, share)
        values = x_ref[pl.ds(first, share), :].astype(F32)
        scale = lax.rsqrt(jnp.mean(values * values, axis=-1, keepdims=True) + EPSILON)
        dgain_ref[...] = jnp.sum(total * (values * scale), axis=0, keepdims=True)

    return kernel_call(
        body, [like(share, model), like(1, model, dtype=F32)], [place, *parts, x]
    )


def input_back(place, dnormed_parts, x, gain, dmiddle, tokens=None, n_ctx=0, per=0, after=()):
    rows, model = x.shape
    n_heads, share = len(dnormed_parts), dnormed_parts[0].shape[0]
    given = [x, gain, dmiddle] + ([] if tokens is None else [tokens])

    def body(place_ref, *refs):
        part_refs, refs = refs[:n_heads], refs[n_heads:]
        x_ref, gain_ref, dmiddle_ref = refs[:3]
        dx_ref, chunk_refs, dnormed_ref = refs[len(given)], refs[len(given) + 1 : -1], refs[-1]
        for r in range(n_heads):
            first = pl.multiple_of((place_ref[1] ^ r) * share, share)
            dnormed_ref[pl.ds(first, share), :] = part_refs[r][...].astype(F32)
        part, _ = norm_back(x_ref[...].astype(F32), gain_ref[...], dnormed_ref[...])
        dx = (dmiddle_ref[...] + part).astype(dx_ref.dtype)
        dx_ref[...] = dx
        if tokens is not None:
            dispatch_into(dx, place_ref, refs[3], chunk_refs)

    outs = kernel_call(
        body,
        [like(rows, model, dtype=F32 if tokens is None else BF16)] + [like(per, model)] * n_ctx,
        [place, *dnormed_parts, *given],
        [pltpu.VMEM((rows, model), F32)],
        after=after,
    )
    return outs[0], outs[1:]


def bucket_of(distance):
    exact_span = BUCKETS // 2
    result = jnp.minimum(distance, exact_span)
    for rank in range(1, BUCKETS - exact_span):
        edge = int(
            math.ceil(exact_span * (REACH / exact_span) ** (rank / (BUCKETS - exact_span)))
        )
        result = result + (distance >= edge).astype(jnp.int32)
    return result


def tile_buckets(half):
    row = lax.broadcasted_iota(jnp.int32, (half, half), 0)
    col = lax.broadcasted_iota(jnp.int32, (half, half), 1)
    same = jnp.where(row >= col, bucket_of(jnp.maximum(row - col, 0)), -1)
    return [same, bucket_of(half + row - col), bucket_of(2 * half + row - col)]


def bias_tables(place, own, other, half, after):
    heads = own.shape[1]

    def body(place_ref, bias_refs, *refs):
        buckets = tile_buckets(half)
        for layer, out_ref in enumerate(refs[-2:]):
            for head in range(heads):
                out_ref[head, 0] = jnp.full((half, half), NEGATIVE, F32)
                values = [jnp.full((half, half), NEGATIVE, F32) for _ in buckets[:2]]
                for bucket in range(BUCKETS):
                    value = bias_refs[place_ref[2] ^ layer, bucket, head]
                    values = [
                        jnp.where(b == bucket, value, v) for b, v in zip(buckets, values)
                    ]
                out_ref[head, 1] = values[0]
                out_ref[head, 2] = values[1]
                far = bias_refs[place_ref[2] ^ layer, BUCKETS - 1, head]
                out_ref[head, 3] = jnp.full((half, half), far, F32)

    shape = like(heads, 4, half, half, dtype=F32)
    return pl.pallas_call(
        body,
        out_shape=[shape] * 2,
        in_specs=[pl.BlockSpec(memory_space=pltpu.SMEM)] * 2
        + [pl.BlockSpec(memory_space=pl.ANY)] * len(after),
        out_specs=[pl.BlockSpec(memory_space=pltpu.VMEM)] * 2,
        compiler_params=pltpu.CompilerParams(vmem_limit_bytes=2 * SPARE_BYTES),
    )(place, jnp.stack([own, other]), *after)


def small_weights(place, gains, routers, after):
    model, n_experts = routers[0].shape

    def body(place_ref, *refs):
        ins, outs = refs[:6], refs[-6:]
        for kind in range(2):
            own, other = (ref[...].astype(F32) for ref in ins[2 * kind : 2 * kind + 2])
            outs[2 * kind][...] = either(place_ref, own, other)
            outs[2 * kind + 1][...] = either(place_ref, other, own)
        own, other = (ref[...].astype(F32) for ref in ins[4:6])
        for out_ref, value in zip(
            outs[4:], (either(place_ref, own, other), either(place_ref, other, own))
        ):
            out_ref[...] = jnp.zeros(out_ref.shape, BF16)
            out_ref[:, :n_experts] = value.astype(BF16)

    args = [place, *gains[0], *gains[1], *routers]
    outs = kernel_call(
        body,
        [like(1, model, dtype=F32)] * 4 + [like(model, LANES)] * 2,
        args,
        after=after,
    )
    return outs[0:2], outs[2:4], outs[4:6]


def layer_row(place_ref, pair_ref, layer, k):
    rows = pair_ref.shape[3]
    row = pair_ref[place_ref[2] ^ layer, place_ref[2], k : k + 1, :]
    eye = lax.broadcasted_iota(jnp.int32, (rows, rows), 0) == lax.broadcasted_iota(
        jnp.int32, (rows, rows), 1
    )
    return jnp.sum(jnp.where(eye, row, 0).astype(F32), axis=1, keepdims=True).astype(jnp.int32)


def earlier(rows):
    row = lax.broadcasted_iota(jnp.int32, (rows, rows), 0)
    col = lax.broadcasted_iota(jnp.int32, (rows, rows), 1)
    return jnp.where(row > col, 1.0, 0.0).astype(BF16)


def quarter_of(rank, per, n_heads):
    return sum([(rank >= h * per).astype(jnp.int32) for h in range(1, n_heads)])


def token_slots(place, pair, n_experts, per, n_heads, after):
    rows = pair.shape[3]

    def body(place_ref, pair_ref, *refs):
        outs = refs[-3:]
        for layer in range(2):
            choices = [layer_row(place_ref, pair_ref, layer, k) for k in range(2)]
            lane = lax.broadcasted_iota(jnp.int32, (rows, LANES), 1)
            hots = [jnp.where(lane == choice, 1.0, 0.0) for choice in choices]
            ranks = dot(earlier(rows), (hots[0] + hots[1]).astype(BF16))
            for k in range(2):
                rank = jnp.sum(ranks * hots[k], axis=1, keepdims=True).astype(jnp.int32)
                quarter = quarter_of(rank, per, n_heads)
                inner = (choices[k] ^ place_ref[0]) * per + rank - quarter * per
                outs[layer][:, k : k + 1] = quarter * (n_experts * per) + inner
                if layer == 1:
                    outs[2][:, k : k + 1] = (quarter ^ place_ref[1]) * (n_experts * per) + inner

    return kernel_call(
        body, [like(rows, 2, dtype=jnp.int32)] * 3, [place, pair], after=after
    )


def other_experts(place, pairs, per, n_heads):
    n_ctx, rows = len(pairs), pairs[0].shape[3]

    def body(place_ref, *refs):
        before = earlier(rows)
        lane = lax.broadcasted_iota(jnp.int32, (rows, per), 1)
        for layer, out_ref in enumerate(refs[n_ctx:]):
            for r, pair_ref in enumerate(refs[:n_ctx]):
                one, two = (layer_row(place_ref, pair_ref, layer, k) for k in range(2))
                here = (one == place_ref[0]) | (two == place_ref[0])
                other = jnp.where(one == place_ref[0], two, one).astype(F32)
                other = jnp.broadcast_to(other, (rows, LANES)).astype(BF16)
                wide = jnp.broadcast_to(jnp.where(here, 1.0, 0.0), (rows, LANES)).astype(BF16)
                rank = dot(before, wide)[:, 0:1].astype(jnp.int32)
                rank = jnp.where(here, rank, -1)
                for h in range(n_heads):
                    picks = jnp.where(lane + h * per == rank, 1.0, 0.0).astype(BF16)
                    found = dot_tn(picks, other)[:, 0:1].astype(jnp.int32)
                    at = (h * n_ctx + r) * per
                    out_ref[at : at + per, :] = found

    return kernel_call(
        body, [like(n_heads * n_ctx * per, 1, dtype=jnp.int32)] * 2, [place, *pairs]
    )


def table_back(dtable, after=()):
    heads, half = dtable.shape[0], dtable.shape[3]

    def body(dtable_ref, *refs):
        out_ref, buckets = refs[-1], tile_buckets(half)
        for bucket in range(BUCKETS):
            hits = [held == bucket for held in buckets]
            for head in range(heads):
                kept = jnp.zeros((half, half), F32)
                for tile, hit in enumerate(hits):
                    kept += jnp.where(hit, dtable_ref[head, 1 + tile], 0.0)
                at = bucket * heads + head
                out_ref[at : at + 1, :] = jnp.sum(kept, axis=0, keepdims=True)

    return kernel_call(
        body, [like(BUCKETS * heads, half, dtype=F32)], [dtable], after=after
    )[0]


def heads_sum(chunks):
    return tree_sum([part.astype(F32) for part in exchange(chunks, "heads")]).astype(BF16)


def back_rows(total, n_ctx):
    per = total.shape[0] // n_ctx
    return exchange([total[r * per : (r + 1) * per] for r in range(n_ctx)], "ctx")


def return_rows(chunks, n_ctx):
    return gather_rows(jnp.concatenate(back_rows(heads_sum(chunks), n_ctx), axis=0), "heads")


def exchange_first(chunks):
    n_ctx = len(chunks)
    parts = [chunks[0]]
    for r in range(1, n_ctx):
        pairs = [(i, i ^ r) for i in range(n_ctx)]
        parts.append(lax.ppermute(chunks[r], ("section", "ctx"), pairs))
    return parts


def send_rows(chunks):
    return gather_rows(jnp.concatenate(exchange(chunks, "ctx"), axis=0), "heads")


def body(
    boundary,
    norm_first,
    qkv_weight,
    position_bias,
    out_weight,
    norm_second,
    router,
    expert_up,
    expert_down,
    routes,
):
    section = lax.axis_index("section")
    ctx_index = lax.axis_index("ctx")
    heads_index = lax.axis_index("heads")
    n_ctx, n_heads = lax.axis_size("ctx"), lax.axis_size("heads")
    first = section == 0
    place = jnp.stack([ctx_index, heads_index, section]).astype(jnp.int32)
    rows, model = boundary.shape[2:]
    half = rows // 2
    n_experts, heads = router.shape[2], position_bias.shape[2]
    per = 5 * rows // (2 * n_experts) // n_heads

    def by_layer(own, other):
        return Pick(own, other), Pick(other, own)

    def with_other(own):
        return own, swap(own, "section")

    given = swap(lax.dynamic_index_in_dim(boundary[0], 1 - section, 0, False), "section")
    gain_pairs = with_other(norm_first), with_other(norm_second)
    qkv = by_layer(*with_other(qkv_weight[0]))
    x0, cotangent, normed0, q0, kv0 = begin(place, boundary[0], given, *gain_pairs[0], qkv[0])
    kv_all0 = gather_rows(kv0, "ctx")

    gains_first, gains_second, routers = small_weights(
        place, gain_pairs, with_other(router[0]), [kv0]
    )
    biases = bias_tables(place, *with_other(position_bias[0]), half, [kv0])
    pair = jnp.stack(with_other(routes[0].transpose(0, 2, 1)))
    *tokens, tokens_near = token_slots(place, pair, n_experts, per, n_heads, [kv0])
    others = other_experts(place, exchange([pair] * n_ctx, "ctx"), per, n_heads)
    up = by_layer(*with_other(expert_up[0, 0]))
    down = by_layer(*with_other(expert_down[0, 0]))
    width = out_weight.shape[1]
    out_gathered = gather_rows(jnp.concatenate(with_other(out_weight[0]), axis=0), "heads")
    out_full = [Rows(out_gathered, layer, width) for layer in range(2)]
    out_own = [Rows(out_gathered, layer, width, own=True) for layer in range(2)]

    def before_experts(layer, x, q, kv_all):
        mix, lse = attend(place, q, [kv_all], biases[layer], n_ctx)
        mixes = exchange([mix] * n_heads, "heads")
        middle, chunks = finish_attention(
            place, mixes, out_full[layer], x, gains_second[layer], tokens[layer], n_ctx, per
        )
        return mix, lse, middle, send_rows(chunks)

    def expert_weights(layer):
        return up[layer], down[layer], routers[layer], others[layer]

    mix0, lse0, middle0, arrived0 = before_experts(0, x0, q0, kv_all0)
    chunks, kept0 = experts(place, arrived0, *expert_weights(0), n_heads)
    dout_chunks = dispatch_whole(place, cotangent, tokens[1], n_ctx, per, n_heads, [middle0])
    returned = return_rows(chunks, n_ctx)
    x1, normed1, q1, kv1 = combine_project(
        place, middle0, returned, tokens[0], gains_first[1], qkv[1]
    )

    kv_all1 = gather_rows(kv1, "ctx")
    mix1, lse1, middle1, arrived1 = before_experts(1, x1, q1, kv_all1)
    dout_rows1 = jnp.stack(exchange(dout_chunks, "ctx"))
    dout_rows1 = dout_rows1.reshape(n_ctx, n_heads, per, model).transpose(1, 0, 2, 3)
    dout_rows1 = dout_rows1.reshape(-1, model)
    chunks, (dpre1, dslots1, dlogits1, hidden1, margin1) = experts_back(
        place, dout_rows1, None, arrived1, *expert_weights(1), n_heads
    )
    dmiddle1, datt1, dmix1, dgain_second1 = middle_back(
        place, return_rows(chunks, n_ctx), tokens[1], middle1, gains_second[1], cotangent, out_own[1]
    )
    dq1, dtable1, dkv1 = attend_back(place, q1, [kv_all1], biases[1], lse1, dmix1, n_ctx)
    out_total = heads_sum(experts_out(place, hidden1, margin1, down[1], n_heads, [dq1]))
    dkv_sum1, chunks = project_back(
        place, dq1, exchange(dkv1, "ctx"), qkv[1], n_heads, [out_total]
    )
    total1, dgain_first1 = share_sum(place, exchange(chunks, "heads"), x1)
    lanes1 = table_back(dtable1)
    shares1 = dense_shares(place, [(normed1, dq1), (datt1, mix1), (normed1, dkv_sum1)], n_ctx)
    dx1, sent = input_back(
        place,
        exchange([total1] * n_heads, "heads"),
        x1,
        gains_first[1],
        dmiddle1,
        tokens[0],
        n_ctx,
        per,
        [lanes1, shares1],
    )

    out_back = back_rows(out_total, n_ctx)
    dout_rows0 = send_rows(sent)
    chunks, (dpre0, dslots0, dlogits0) = experts_back(
        place, dout_rows0, kept0, arrived0, *expert_weights(0), n_heads, out_back
    )
    lists = [(arrived0, arrived1), (dpre0, dpre1), (kept0[1], hidden1), (dslots0, dslots1)]
    mine, theirs = [Pick(a, b) for a, b in lists], [Pick(b, a) for a, b in lists]
    sends = expert_grads(place, [theirs[:2], theirs[2:]])
    sum1 = sum_shares(exchange([shares1[r] for r in range(n_ctx)], "ctx"))
    dmiddle0, datt0, dmix0, dgain_second0 = middle_back(
        place,
        return_rows(chunks, n_ctx),
        tokens[0],
        middle0,
        gains_second[0],
        dx1,
        out_own[0],
        [*sends, sum1],
    )
    dq0, dtable0, dkv0 = attend_back(place, q0, [kv_all0], biases[0], lse0, dmix0, n_ctx)
    lanes0 = table_back(dtable0)
    layers = [
        (dgain_second0, dlogits0, arrived0, lanes0),
        (dgain_second1, dlogits1, arrived1, lanes1),
    ]
    pack = small_pack(place, layers, n_experts, n_heads)
    quarter = jnp.concatenate(out_back, axis=0)
    out = combine(
        middle1, exchange([quarter] * n_heads, "heads"), tokens_near, [dq0]
    )
    dkv_sum0, chunks = project_back(
        place, dq0, exchange(dkv0, "ctx"), qkv[0], n_heads, [pack, out]
    )
    total0, dgain_first0 = share_sum(place, exchange(chunks, "heads"), x0)
    shares0 = dense_shares(place, [(normed0, dq0), (datt0, mix0), (normed0, dkv_sum0)], n_ctx)
    gots = [swap(g, "section") for g in sends]
    grad_up, grad_down = expert_grads(place, [mine[:2], mine[2:]], gots, after=[total0])
    (dx0,) = input_back(
        place,
        exchange([total0] * n_heads, "heads"),
        x0,
        gains_first[0],
        dmiddle0,
        after=[grad_up],
    )[:1]

    got1 = one_way(sum1, 0)
    parts0 = exchange_first(add_shares(shares0, one_way(shares0, 1)))
    grad_qkv, grad_out = dense_grads(place, parts0, sum1, got1, width)
    pack = jnp.concatenate([dgain_first0, dgain_first1, pack])
    pack = tree_sum(exchange([pack] * n_heads, "heads"))
    pack = tree_sum(exchange([pack] * n_ctx, "ctx"))
    count = 1 + n_experts + n_heads
    packs = [jnp.concatenate([pack[i : i + 1], pack[2 + i * count :][:count]]) for i in range(2)]
    pack = jnp.where(first, packs[0], packs[1]) + swap(
        jnp.where(first, packs[1], packs[0]), "section"
    )
    share = model // n_ctx
    mine = lax.dynamic_slice_in_dim(pack, ctx_index * share, share, 1)
    bias_share = BUCKETS // n_ctx * heads
    at = (2 + n_experts + heads_index, ctx_index * bias_share)
    grad_bias = lax.dynamic_slice(pack, at, (1, bias_share))
    boundary_out = assemble(place, dx0, one_way(out, 0), one_way(dx0, 1), out)
    return (
        boundary_out[None],
        mine[0][None],
        grad_qkv[None],
        grad_bias.reshape(1, BUCKETS // n_ctx, heads),
        grad_out[None],
        mine[1][None],
        mine[2 : 2 + n_experts].T[None],
        grad_up[None, None],
        grad_down[None, None],
    )


def solution(mesh):
    placed = (
        P("section", None, "ctx", None),
        P("section", None),
        P("section", None, None, "heads"),
        P("section", None, "heads"),
        P("section", "heads", None),
        P("section", None),
        P("section", None, None),
        P("section", "ctx", None, "heads"),
        P("section", "ctx", "heads", None),
        P("section", None, "ctx", None),
    )
    return jax.shard_map(
        body,
        mesh=mesh,
        in_specs=placed,
        out_specs=(
            P("section", None, "ctx", None),
            P("section", "ctx"),
            P("section", None, "ctx", "heads"),
            P("section", "ctx", "heads"),
            P("section", "heads", "ctx"),
            P("section", "ctx"),
            P("section", "ctx", None),
            P("section", "ctx", None, "heads"),
            P("section", "ctx", "heads", None),
        ),
        check_vma=False,
    )
```

time: 513 us -> 483 us (0.942)
  blocking collectives: 175 us -> 120 us
  Pallas kernels: 51 us -> 95.8 us
  other arithmetic: 47.5 us -> 5.44 us
  waiting for transfers between devices: 47.9 us -> 89 us
  matrix products: 16.3 us -> 0 us
    pallas_call x22 -> x37, Pallas kernels: 51 us -> 95.8 us  [the longest x36 93 us: kernel_call(): pl.pallas_call(wrapped, out_shape=outs, in_specs=in_specs, out_specs=[pl....]
    ppermute x74 -> x88, waiting for transfers between devices: 43.2 us -> 87.1 us  [swap(): return lax.ppermute(array, axis, [(i, i ^ by) for i in range(devices)])]
    ppermute x16 -> x4, starting transfers between devices: 29.6 us -> 8.54 us  [one_way(): return lax.ppermute(array, 'section', [(source, 1 - source)])]
    select_n x16 -> x1, other arithmetic: 21.1 us -> 0.64 us  [body(): jnp.where(first, packs[1], packs[0])]
    unnamed x1 -> x0, blocking collectives: 18.6 us -> none
    all_gather x10 -> x8, blocking collectives: 139 us -> 120 us  [gather_rows(): return lax.all_gather(array, axis, axis=0, tiled=True)]
    dot_general x12 -> x0, matrix products: 16.3 us -> none  [dot(): lax.dot_general(a, b, (contract, ((), ())), preferred_element_type=F32)]
    ppermute x74 -> x88, starting transfers between devices: 89.3 us -> 105 us  [swap(): return lax.ppermute(array, axis, [(i, i ^ by) for i in range(devices)])]
  transfers between devices with their start and end apart: 93 -> 96, of which waited for: 27 -> 32; matrix products, arithmetic and copies ran while one was open for 16% -> 2% of each run, Pallas kernels for 8% -> 13%
where the time goes in v2:
time: 483 us; the launch traced here: 477 us
  starting transfers between devices  124 us (26%)
  blocking collectives  120 us (25%)
  Pallas kernels  95.8 us (20%)
  waiting for transfers between devices  89 us (18%)
  local copies, waits for them, and re-layouts  26.8 us (6%)
  between operations  15.7 us (3%)
  other arithmetic  5.44 us (1%)
    all_gather x8, blocking collectives, gather_rows(): return lax.all_gather(array, axis, axis=0, tiled=True)  120 us
    ppermute x88, starting transfers between devices, swap(): return lax.ppermute(array, axis, [(i, i ^ by) for i in range(devices)])  105 us
    pallas_call x36, Pallas kernels, kernel_call(): pl.pallas_call(wrapped, out_shape=outs, in_specs=in_specs, out_specs=[pl....  93 us
    ppermute x88, waiting for transfers between devices, swap(): return lax.ppermute(array, axis, [(i, i ^ by) for i in range(devices)])  87.1 us
    unnamed x143, local copies, waits for them, and re-layouts  20.6 us
    ppermute x3, starting transfers between devices, exchange_first(): parts.append(lax.ppermute(chunks[r], ('section', 'ctx'), pairs))  10.1 us
  transfers between devices with their start and end apart: 96, of which 32 were waited for; matrix products, arithmetic and copies ran while one was open for 2% of the time, Pallas kernels for 13%

profile of v2, /device:TPU:0, one launch (start us, length us, event | category | flops | bytes accessed | tf_op | source)
XLA Modules:
  0.0 477.0 jit_solution(16477693851572696760)
XLA Ops:
  23.1 2.8 shard_map.170
  25.9 21.3 %all_gather.27.refs_2_ = bf16[1024,384]{1,0:T(8,128)(2,1)S(1)} all-gather(bf16[256,384]{1,0:T(8,128)(2,1)S(1)} %get-tuple-element.126.refs_0_.refs_7_.refs_2_), channel_id=1, replica_groups=mesh['section'=2,'ctx'=4,'heads'=4] {'ctx'}, dimensions={0}, use_global_device_ids=true | all-gather | bytes 983040 | tf_op jit(solution)/shard_map/all_gather | solution.py:153
  47.3 3.0 shard_map.171
  61.0 2.4 collective-permute-start.17
  67.0 2.4 shard_map.174
  71.4 2.5 collective-permute-start.11
  73.9 3.7 shard_map.175
  77.7 12.9 %all_gather.29.refs_1_.refs_2_.refs_3_ = bf16[640,768]{1,0:T(8,128)(2,1)S(1)} all-gather(bf16[160,768]{1,0:T(8,128)(2,1)S(1)} %pad_maximum_fusion.2), channel_id=1, replica_groups=mesh['section'=2,'ctx'=4,'heads'=4] {'heads'}, dimensions={0}, use_global_device_ids=true | all-gather | bytes 1228800 | tf_op jit(solution)/shard_map/all_gather | solution.py:153
  90.6 4.5 shard_map.176
  98.7 3.7 collective-permute-done.21
  102.4 2.5 collective-permute-done.20
  105.1 2.2 collective-permute-start.24
  107.4 2.1 collective-permute-start.22
  111.0 2.2 collective-permute-start.27
  113.2 3.0 collective-permute-start.25
  117.5 13.1 %all_gather.30.refs_2_ = bf16[640,768]{1,0:T(8,128)(2,1)S(1)} all-gather(bf16[160,768]{1,0:T(8,128)(2,1)S(1)} %pad_maximum_fusion.3), channel_id=1, replica_groups=mesh['section'=2,'ctx'=4,'heads'=4] {'heads'}, dimensions={0}, use_global_device_ids=true | all-gather | bytes 1228800 | tf_op jit(solution)/shard_map/all_gather | solution.py:153
  130.6 2.2 shard_map.177
  132.9 15.8 %all_gather.31.refs_2_ = bf16[1024,384]{1,0:T(8,128)(2,1)S(1)} all-gather(bf16[256,384]{1,0:T(8,128)(2,1)S(1)} %get-tuple-element.146), channel_id=1, replica_groups=mesh['section'=2,'ctx'=4,'heads'=4] {'ctx'}, dimensions={0}, use_global_device_ids=true | all-gather | bytes 983040 | tf_op jit(solution)/shard_map/all_gather | solution.py:153
  148.7 3.0 shard_map.178
  153.7 2.9 collective-permute-done.28.refs_2_
  158.2 5.5 %collective-permute-done.30.refs_4_ = bf16[256,192]{1,0:T(8,128)(2,1)S(1)} collective-permute-done((bf16[256,192]{1,0:T(8,128)(2,1)S(1)}, bf16[256,192]{1,0:T(8,128)(2,1)S(1)}, u32[]{:S(2)}, u32[]{:S(2)}) %collective-permute-start.30) | collective-permute-done | bytes 98336 | tf_op jit(solution)/shard_map/ppermute | solution.py:141
  163.7 2.4 shard_map.180
  166.1 3.2 collective-permute-start.33
  172.1 2.2 collective-permute-done.32
  174.4 14.1 %all_gather.32.refs_2_.refs_1_.refs_7_ = bf16[640,768]{1,0:T(8,128)(2,1)S(1)} all-gather(bf16[160,768]{1,0:T(8,128)(2,1)S(1)} %pad_maximum_fusion.4), channel_id=1, replica_groups=mesh['section'=2,'ctx'=4,'heads'=4] {'heads'}, dimensions={0}, use_global_device_ids=true | all-gather | bytes 1228800 | tf_op jit(solution)/shard_map/all_gather | solution.py:153
  188.5 8.2 %shard_map.181 = (bf16[160,768]{1,0:T(8,128)(2,1)S(1)}, bf16[160,768]{1,0:T(8,128)(2,1)S(1)}, bf16[160,768]{1,0:T(8,128)(2,1)S(1)}, bf16[160,768]{1,0:T(8,128)(2...) custom-call(s32[3]{0:T(128)S(1)} %pad_add_fusion.1.refs_0_.place_ref, ...), custom_call_target="tpu_custom_call" | custom-call | flops 1509949440 | bytes 8623116 | tf_op jit(solution)/shard_map/pallas_call | solution.py:112
  198.2 2.0 collective-permute-start.35
  200.3 5.4 %collective-permute-done.36 = bf16[160,768]{1,0:T(8,128)(2,1)S(1)} collective-permute-done((bf16[160,768]{1,0:T(8,128)(2,1)S(1)}, bf16[160,768]{1,0:T(8,128)(2,1)S(1)}, u32[]{:S(2)}, u32[]{:S(2)}) %collective-permute-start.36) | collective-permute-done | bytes 245792 | tf_op jit(solution)/shard_map/ppermute | solution.py:141
  205.6 3.1 collective-permute-done.35
  208.9 2.2 collective-permute-start.39
  211.2 2.2 collective-permute-start.37
  216.6 15.8 %all_gather.33.refs_1_ = bf16[640,768]{1,0:T(8,128)(2,1)S(1)} all-gather(bf16[160,768]{1,0:T(8,128)(2,1)S(1)} %pad_maximum_fusion.5), channel_id=1, replica_groups=mesh['section'=2,'ctx'=4,'heads'=4] {'heads'}, dimensions={0}, use_global_device_ids=true | all-gather | bytes 1228800 | tf_op jit(solution)/shard_map/all_gather | solution.py:153
  234.3 4.9 %shard_map.183 = (bf16[256,192]{1,0:T(8,128)(2,1)S(1)}, f32[3,4,128,128]{3,2,1,0:T(8,128)S(1)}, bf16[256,384]{1,0:T(8,128)(2,1)S(1)}, bf16[256,384]{1,0:T(8,128)...) custom-call(s32[3]{0:T(128)S(1)} %pad_add_fusion.1.refs_0_.place_ref, ...), custom_call_target="tpu_custom_call" | custom-call | flops 503316480 | bytes 3443724 | tf_op jit(solution)/shard_map/pallas_call | solution.py:112
  239.2 2.8 shard_map.184
  249.3 2.2 collective-permute-start.42
  251.9 9.9 %collective-permute-done.41.refs_4_ = bf16[256,384]{1,0:T(8,128)(2,1)S(1)} collective-permute-done((bf16[256,384]{1,0:T(8,128)(2,1)S(1)}, bf16[256,384]{1,0:T(8,128)(2,1)S(1)}, u32[]{:S(2)}, u32[]{:S(2)}) %collective-permute-start.41) | collective-permute-done | bytes 196640 | tf_op jit(solution)/shard_map/ppermute | solution.py:141
  269.6 2.6 collective-permute-done.48.refs_4_
  282.2 5.0 %collective-permute-start.53 = (bf16[40,768]{1,0:T(8,128)(2,1)S(1)}, bf16[40,768]{1,0:T(8,128)(2,1)S(1)}, u32[]{:S(2)}, u32[]{:S(2)}) collective-permute-start(bf16[40,768]{1,0:T(8,128)(2,1)S(1)} %get-tuple-element.193), channel_id=1, source_target_pairs={{0,8},{4,12},{8,0},{12,4},{1,9},{5,13},{9,1},{13,5},{2,10},{6,14},... | collective-permute-start | bytes 184328 | tf_op jit(solution)/shard_map/ppermute | solution.py:141
  287.2 2.1 collective-permute-start.55
  289.3 2.4 collective-permute-start.57
  291.8 8.9 %collective-permute-done.53 = bf16[40,768]{1,0:T(8,128)(2,1)S(1)} collective-permute-done((bf16[40,768]{1,0:T(8,128)(2,1)S(1)}, bf16[40,768]{1,0:T(8,128)(2,1)S(1)}, u32[]{:S(2)}, u32[]{:S(2)}) %collective-permute-start.53) | collective-permute-done | bytes 61472 | tf_op jit(solution)/shard_map/ppermute | solution.py:141
  300.7 15.7 %all_gather.34.refs_1_ = bf16[640,768]{1,0:T(8,128)(2,1)S(1)} all-gather(bf16[160,768]{1,0:T(8,128)(2,1)S(1)} %pad_maximum_fusion.6), channel_id=1, replica_groups=mesh['section'=2,'ctx'=4,'heads'=4] {'heads'}, dimensions={0}, use_global_device_ids=true | all-gather | bytes 1228800 | tf_op jit(solution)/shard_map/all_gather | solution.py:153
  316.4 6.8 %shard_map.190 = (bf16[160,768]{1,0:T(8,128)(2,1)S(1)}, bf16[160,768]{1,0:T(8,128)(2,1)S(1)}, bf16[160,768]{1,0:T(8,128)(2,1)S(1)}, bf16[160,768]{1,0:T(8,128)(2...) custom-call(s32[3]{0:T(128)S(1)} %pad_add_fusion.1.refs_0_.place_ref, ...), custom_call_target="tpu_custom_call" | custom-call | flops 1509949440 | bytes 9606156 | tf_op jit(solution)/shard_map/pallas_call | solution.py:112
  328.0 2.4 collective-permute-done.60
  335.4 4.2 collective-permute-done.64.refs_1_
  339.6 5.8 %shard_map.191 = (bf16[768,768]{1,0:T(8,128)(2,1)}, bf16[768,768]{1,0:T(8,128)(2,1)}) custom-call(s32[3]{0:T(128)S(1)} %pad_add_fusion.1.refs_0_.place_ref, bf16[640,768]{1,0:T(8,128)(2,1)S(1)} %all_gather.32.refs_2_.refs_1_.refs_7_, bf16[640,768]{1,0:T(8,128)(2,1)S(1)} %all_gather.29.refs_1_.refs_2_.refs_3_, ...), custom_call_target="tpu_custom_call" | custom-call | flops 1509949440 | bytes 6291468 | tf_op jit(solution)/shard_map/pallas_call | solution.py:112
  345.5 4.3 collective-permute-done.65.refs_2_
  353.5 2.4 collective-permute-done.62
  355.9 11.6 %all_gather.35.refs_1_ = bf16[640,768]{1,0:T(8,128)(2,1)S(1)} all-gather(bf16[160,768]{1,0:T(8,128)(2,1)S(1)} %pad_maximum_fusion.7), channel_id=1, replica_groups=mesh['section'=2,'ctx'=4,'heads'=4] {'heads'}, dimensions={0}, use_global_device_ids=true | all-gather | bytes 1228800 | tf_op jit(solution)/shard_map/all_gather | solution.py:153
  370.3 4.9 %shard_map.194 = (bf16[256,192]{1,0:T(8,128)(2,1)S(1)}, f32[3,4,128,128]{3,2,1,0:T(8,128)S(1)}, bf16[256,384]{1,0:T(8,128)(2,1)S(1)}, bf16[256,384]{1,0:T(8,128)...) custom-call(s32[3]{0:T(128)S(1)} %pad_add_fusion.1.refs_0_.place_ref, ...), custom_call_target="tpu_custom_call" | custom-call | flops 503316480 | bytes 3443724 | tf_op jit(solution)/shard_map/pallas_call | solution.py:112
  375.2 3.0 collective-permute-start.67
  378.2 2.4 collective-permute-start.69
  384.2 4.7 collective-permute-done.68.refs_4_
  395.2 3.2 collective-permute-done.74.refs_3_
  403.4 2.4 shard_map.203.refs_0_
  409.1 2.3 collective-permute-start.88
  416.0 3.9 collective-permute-start.81
  429.6 7.7 %shard_map.200 = (f32[768,768]{1,0:T(8,128)}, f32[768,768]{1,0:T(8,128)}) custom-call(s32[3]{0:T(128)S(1)} %pad_add_fusion.1.refs_0_.place_ref, bf16[640,768]{1,0:T(8,128)(2,1)S(1)} %all_gather.29.refs_1_.refs_2_.refs_3_, bf16[640,768]{1,0:T(8,128)(2,1)S(1)} %copy-done.3, bf16[640,768]{1,0:T(8,128)(2,1)S(1)} %copy-done.17, bf16[640,768]{1,0:T(8,128)(2,1)S(1)} %copy-done.13, ...), custom_call_target="tpu_custom_call" | custom-call | flops 1509949440 | bytes 11010060 | tf_op jit(solution)/shard_map/pallas_call | solution.py:112
  443.1 2.1 collective-permute-start.94
  445.1 2.6 shard_map.204
  447.7 3.6 collective-permute-start.91
  451.4 2.4 collective-permute-start.92
  453.8 4.1 collective-permute-start.93
  467.5 2.1 shard_map.205
  (352 shorter events, 141.3 us)
Async XLA Ops:
  7.2 58.2 %all-gather.2.cloned.1.call-start = ((), (), s32[]{:S(2)}) async-start(), calls=%async_computation | async-start | bytes 2949120 | tf_op jit(solution)/shard_map/all_gather | solution.py:153
  12.4 78.2 %collective-permute-start.14 = (bf16[768,768]{1,0:T(8,128)(2,1)}, bf16[768,768]{1,0:T(8,128)(2,1)}, u32[]{:S(2)}, u32[]{:S(2)}) collective-permute-start(bf16[768,768]{1,0:T(8,128)(2,1)} %bitcast.15.refs_2_.refs_4_.refs_5_), channel_id=1, source_target_pairs={{0,16},{16,0},{1,17},{17,1},{2,18},{18,2},{3,19},{19,3},{4,20},{20... | collective-permute-start | bytes 3538952 | tf_op jit(solution)/shard_map/ppermute | solution.py:141
  12.8 77.8 %collective-permute-start.15 = (bf16[768,768]{1,0:T(8,128)(2,1)}, bf16[768,768]{1,0:T(8,128)(2,1)}, u32[]{:S(2)}, u32[]{:S(2)}) collective-permute-start(bf16[768,768]{1,0:T(8,128)(2,1)} %bitcast.16.refs_4_.refs_6_.refs_7_), channel_id=1, source_target_pairs={{0,16},{16,0},{1,17},{17,1},{2,18},{18,2},{3,19},{19,3},{4,20},{20... | collective-permute-start | bytes 3538952 | tf_op jit(solution)/shard_map/ppermute | solution.py:141
  15.8 36.1 %collective-permute-start.8 = (bf16[1,768]{1,0:T(2,128)(2,1)S(1)}, bf16[1,768]{1,0:T(2,128)(2,1)}, u32[]{:S(2)}, u32[]{:S(2)}) collective-permute-start(bf16[1,768]{1,0:T(2,128)(2,1)S(1)} %copy-done.57), channel_id=1, source_target_pairs={{0,16},{16,0},{1,17},{17,1},{2,18},{18,2},{3,19},{19,3},{4,20},{20... | collective-permute-start | bytes 4616 | tf_op jit(solution)/shard_map/ppermute | solution.py:141
  17.7 37.2 %collective-permute-start.9 = (bf16[768,4]{1,0:T(8,128)(2,1)}, bf16[768,4]{1,0:T(8,128)(2,1)S(1)}, u32[]{:S(2)}, u32[]{:S(2)}) collective-permute-start(bf16[768,4]{1,0:T(8,128)(2,1)} %bitcast.9.refs_5_), channel_id=1, source_target_pairs={{0,16},{16,0},{1,17},{17,1},{2,18},{18,2},{3,19},{19,3},{4,20},{20... | collective-permute-start | bytes 18440 | tf_op jit(solution)/shard_map/ppermute | solution.py:141
  18.6 34.7 %collective-permute-start.10 = (s32[2,2,256]{2,1,0:T(2,128)}, s32[2,2,256]{2,1,0:T(2,128)S(1)}, u32[]{:S(2)}, u32[]{:S(2)}) collective-permute-start(s32[2,2,256]{2,1,0:T(2,128)} %bitcast.69), channel_id=1, source_target_pairs={{0,16},{16,0},{1,17},{17,1},{2,18},{18,2},{3,19},{19,3},{4,20},{20... | collective-permute-start | bytes 12296 | tf_op jit(solution)/shard_map/ppermute | solution.py:141
  51.8 9.1 %collective-permute-start.4 = (bf16[256,192]{1,0:T(8,128)(2,1)S(1)}, bf16[256,192]{1,0:T(8,128)(2,1)S(1)}, u32[]{:S(2)}, u32[]{:S(2)}) collective-permute-start(bf16[256,192]{1,0:T(8,128)(2,1)S(1)} %get-tuple-element.129.refs_1_.refs_4_), channel_id=1, source_target_pairs={{0,1},{1,0},{2,3},{3,2},{4,5},{5,4},{6,7},{7,6},{8,9},{9,8},{10,11... | collective-permute-start | bytes 294920 | tf_op jit(solution)/shard_map/ppermute | solution.py:141
  53.3 7.6 %collective-permute-start.5 = (bf16[256,192]{1,0:T(8,128)(2,1)S(1)}, bf16[256,192]{1,0:T(8,128)(2,1)S(1)}, u32[]{:S(2)}, u32[]{:S(2)}) collective-permute-start(bf16[256,192]{1,0:T(8,128)(2,1)S(1)} %get-tuple-element.129.refs_1_.refs_4_), channel_id=1, source_target_pairs={{0,2},{1,3},{2,0},{3,1},{4,6},{5,7},{6,4},{7,5},{8,10},{9,11},{10,... | collective-permute-start | bytes 294920 | tf_op jit(solution)/shard_map/ppermute | solution.py:141
  54.8 8.5 %collective-permute-start.6 = (bf16[256,192]{1,0:T(8,128)(2,1)S(1)}, bf16[256,192]{1,0:T(8,128)(2,1)S(1)}, u32[]{:S(2)}, u32[]{:S(2)}) collective-permute-start(bf16[256,192]{1,0:T(8,128)(2,1)S(1)} %get-tuple-element.129.refs_1_.refs_4_), channel_id=1, source_target_pairs={{0,3},{1,2},{2,1},{3,0},{4,7},{5,6},{6,5},{7,4},{8,11},{9,10},{10,... | collective-permute-start | bytes 294920 | tf_op jit(solution)/shard_map/ppermute | solution.py:141
  60.9 8.5 %collective-permute-start.16 = (s32[2,2,2,256]{3,2,1,0:T(2,128)S(1)}, s32[2,2,2,256]{3,2,1,0:T(2,128)S(1)}, u32[]{:S(2)}, u32[]{:S(2)}) collective-permute-start(s32[2,2,2,256]{3,2,1,0:T(2,128)S(1)} %pad_add_fusion.refs_1_), channel_id=1, source_target_pairs={{0,4},{4,0},{8,12},{12,8},{1,5},{5,1},{9,13},{13,9},{2,6},{6,2},{1... | collective-permute-start | bytes 24584 | tf_op jit(solution)/shard_map/ppermute | solution.py:141
  61.0 10.4 %collective-permute-start.17 = (s32[2,2,2,256]{3,2,1,0:T(2,128)S(1)}, s32[2,2,2,256]{3,2,1,0:T(2,128)S(1)}, u32[]{:S(2)}, u32[]{:S(2)}) collective-permute-start(s32[2,2,2,256]{3,2,1,0:T(2,128)S(1)} %pad_add_fusion.refs_1_), channel_id=1, source_target_pairs={{0,8},{4,12},{8,0},{12,4},{1,9},{5,13},{9,1},{13,5},{2,10},{6,14},... | collective-permute-start | bytes 24584 | tf_op jit(solution)/shard_map/ppermute | solution.py:141
  63.4 8.0 %collective-permute-start.18 = (s32[2,2,2,256]{3,2,1,0:T(2,128)S(1)}, s32[2,2,2,256]{3,2,1,0:T(2,128)S(1)}, u32[]{:S(2)}, u32[]{:S(2)}) collective-permute-start(s32[2,2,2,256]{3,2,1,0:T(2,128)S(1)} %pad_add_fusion.refs_1_), channel_id=1, source_target_pairs={{0,12},{4,8},{8,4},{12,0},{1,13},{5,9},{9,5},{13,1},{2,14},{6,10},... | collective-permute-start | bytes 24584 | tf_op jit(solution)/shard_map/ppermute | solution.py:141
  69.5 8.2 %collective-permute-start.13 = (bf16[40,768]{1,0:T(8,128)(2,1)S(1)}, bf16[40,768]{1,0:T(8,128)(2,1)S(1)}, u32[]{:S(2)}, u32[]{:S(2)}) collective-permute-start(bf16[40,768]{1,0:T(8,128)(2,1)S(1)} %get-tuple-element.137), channel_id=1, source_target_pairs={{0,12},{4,8},{8,4},{12,0},{1,13},{5,9},{9,5},{13,1},{2,14},{6,10},... | collective-permute-start | bytes 184328 | tf_op jit(solution)/shard_map/ppermute | solution.py:141
  95.1 7.3 %collective-permute-start.21 = (bf16[160,768]{1,0:T(8,128)(2,1)S(1)}, bf16[160,768]{1,0:T(8,128)(2,1)S(1)}, u32[]{:S(2)}, u32[]{:S(2)}) collective-permute-start(bf16[160,768]{1,0:T(8,128)(2,1)S(1)} %get-tuple-element.143), channel_id=1, source_target_pairs={{0,3},{1,2},{2,1},{3,0},{4,7},{5,6},{6,5},{7,4},{8,11},{9,10},{10,... | collective-permute-start | bytes 737288 | tf_op jit(solution)/shard_map/ppermute | solution.py:141
  96.6 8.3 %collective-permute-start.20 = (bf16[160,768]{1,0:T(8,128)(2,1)S(1)}, bf16[160,768]{1,0:T(8,128)(2,1)S(1)}, u32[]{:S(2)}, u32[]{:S(2)}) collective-permute-start(bf16[160,768]{1,0:T(8,128)(2,1)S(1)} %get-tuple-element.142), channel_id=1, source_target_pairs={{0,2},{1,3},{2,0},{3,1},{4,6},{5,7},{6,4},{7,5},{8,10},{9,11},{10,... | collective-permute-start | bytes 737288 | tf_op jit(solution)/shard_map/ppermute | solution.py:141
  97.2 7.7 %collective-permute-start.19 = (bf16[160,768]{1,0:T(8,128)(2,1)S(1)}, bf16[160,768]{1,0:T(8,128)(2,1)S(1)}, u32[]{:S(2)}, u32[]{:S(2)}) collective-permute-start(bf16[160,768]{1,0:T(8,128)(2,1)S(1)} %get-tuple-element.141), channel_id=1, source_target_pairs={{0,1},{1,0},{2,3},{3,2},{4,5},{5,4},{6,7},{7,6},{8,9},{9,8},{10,11... | collective-permute-start | bytes 737288 | tf_op jit(solution)/shard_map/ppermute | solution.py:141
  105.1 8.2 %collective-permute-start.24 = (bf16[40,768]{1,0:T(8,128)(2,1)S(1)}, bf16[40,768]{1,0:T(8,128)(2,1)S(1)}, u32[]{:S(2)}, u32[]{:S(2)}) collective-permute-start(bf16[40,768]{1,0:T(8,128)(2,1)S(1)} %get-tuple-element.294), channel_id=1, source_target_pairs={{0,12},{4,8},{8,4},{12,0},{1,13},{5,9},{9,5},{13,1},{2,14},{6,10},... | collective-permute-start | bytes 184328 | tf_op jit(solution)/shard_map/ppermute | solution.py:141
  107.2 10.3 %collective-permute-start.23 = (bf16[40,768]{1,0:T(8,128)(2,1)S(1)}, bf16[40,768]{1,0:T(8,128)(2,1)S(1)}, u32[]{:S(2)}, u32[]{:S(2)}) collective-permute-start(bf16[40,768]{1,0:T(8,128)(2,1)S(1)} %get-tuple-element.295), channel_id=1, source_target_pairs={{0,8},{4,12},{8,0},{12,4},{1,9},{5,13},{9,1},{13,5},{2,10},{6,14},... | collective-permute-start | bytes 184328 | tf_op jit(solution)/shard_map/ppermute | solution.py:141
  107.4 10.1 %collective-permute-start.22 = (bf16[40,768]{1,0:T(8,128)(2,1)S(1)}, bf16[40,768]{1,0:T(8,128)(2,1)S(1)}, u32[]{:S(2)}, u32[]{:S(2)}) collective-permute-start(bf16[40,768]{1,0:T(8,128)(2,1)S(1)} %get-tuple-element.296), channel_id=1, source_target_pairs={{0,4},{4,0},{8,12},{12,8},{1,5},{5,1},{9,13},{13,9},{2,6},{6,2},{1... | collective-permute-start | bytes 184328 | tf_op jit(solution)/shard_map/ppermute | solution.py:141
  111.0 58.2 %collective-permute-start.27 = (bf16[160,768]{1,0:T(8,128)(2,1)S(1)}, bf16[160,768]{1,0:T(8,128)(2,1)S(1)}, u32[]{:S(2)}, u32[]{:S(2)}) collective-permute-start(bf16[160,768]{1,0:T(8,128)(2,1)S(1)} %get-tuple-element.154), channel_id=1, source_target_pairs={{0,12},{4,8},{8,4},{12,0},{1,13},{5,9},{9,5},{13,1},{2,14},{6,10},... | collective-permute-start | bytes 737288 | tf_op jit(solution)/shard_map/ppermute | solution.py:141
  113.2 57.3 %collective-permute-start.26 = (bf16[160,768]{1,0:T(8,128)(2,1)S(1)}, bf16[160,768]{1,0:T(8,128)(2,1)S(1)}, u32[]{:S(2)}, u32[]{:S(2)}) collective-permute-start(bf16[160,768]{1,0:T(8,128)(2,1)S(1)} %get-tuple-element.153), channel_id=1, source_target_pairs={{0,8},{4,12},{8,0},{12,4},{1,9},{5,13},{9,1},{13,5},{2,10},{6,14},... | collective-permute-start | bytes 737288 | tf_op jit(solution)/shard_map/ppermute | solution.py:141
  113.2 57.3 %collective-permute-start.25 = (bf16[160,768]{1,0:T(8,128)(2,1)S(1)}, bf16[160,768]{1,0:T(8,128)(2,1)S(1)}, u32[]{:S(2)}, u32[]{:S(2)}) collective-permute-start(bf16[160,768]{1,0:T(8,128)(2,1)S(1)} %get-tuple-element.152), channel_id=1, source_target_pairs={{0,4},{4,0},{8,12},{12,8},{1,5},{5,1},{9,13},{13,9},{2,6},{6,2},{1... | collective-permute-start | bytes 737288 | tf_op jit(solution)/shard_map/ppermute | solution.py:141
  196.7 9.0 %collective-permute-start.36 = (bf16[160,768]{1,0:T(8,128)(2,1)S(1)}, bf16[160,768]{1,0:T(8,128)(2,1)S(1)}, u32[]{:S(2)}, u32[]{:S(2)}) collective-permute-start(bf16[160,768]{1,0:T(8,128)(2,1)S(1)} %get-tuple-element.167), channel_id=1, source_target_pairs={{0,3},{1,2},{2,1},{3,0},{4,7},{5,6},{6,5},{7,4},{8,11},{9,10},{10,... | collective-permute-start | bytes 737288 | tf_op jit(solution)/shard_map/ppermute | solution.py:141
  198.2 10.6 %collective-permute-start.35 = (bf16[160,768]{1,0:T(8,128)(2,1)S(1)}, bf16[160,768]{1,0:T(8,128)(2,1)S(1)}, u32[]{:S(2)}, u32[]{:S(2)}) collective-permute-start(bf16[160,768]{1,0:T(8,128)(2,1)S(1)} %get-tuple-element.166), channel_id=1, source_target_pairs={{0,2},{1,3},{2,0},{3,1},{4,6},{5,7},{6,4},{7,5},{8,10},{9,11},{10,... | collective-permute-start | bytes 737288 | tf_op jit(solution)/shard_map/ppermute | solution.py:141
  200.2 8.5 %collective-permute-start.34 = (bf16[160,768]{1,0:T(8,128)(2,1)S(1)}, bf16[160,768]{1,0:T(8,128)(2,1)S(1)}, u32[]{:S(2)}, u32[]{:S(2)}) collective-permute-start(bf16[160,768]{1,0:T(8,128)(2,1)S(1)} %get-tuple-element.165), channel_id=1, source_target_pairs={{0,1},{1,0},{2,3},{3,2},{4,5},{5,4},{6,7},{7,6},{8,9},{9,8},{10,11... | collective-permute-start | bytes 737288 | tf_op jit(solution)/shard_map/ppermute | solution.py:141
  242.0 7.3 %collective-permute-start.45 = (bf16[160,768]{1,0:T(8,128)(2,1)S(1)}, bf16[160,768]{1,0:T(8,128)(2,1)S(1)}, u32[]{:S(2)}, u32[]{:S(2)}) collective-permute-start(bf16[160,768]{1,0:T(8,128)(2,1)S(1)} %get-tuple-element.180), channel_id=1, source_target_pairs={{0,3},{1,2},{2,1},{3,0},{4,7},{5,6},{6,5},{7,4},{8,11},{9,10},{10,... | collective-permute-start | bytes 737288 | tf_op jit(solution)/shard_map/ppermute | solution.py:141
  243.5 8.3 %collective-permute-start.44 = (bf16[160,768]{1,0:T(8,128)(2,1)S(1)}, bf16[160,768]{1,0:T(8,128)(2,1)S(1)}, u32[]{:S(2)}, u32[]{:S(2)}) collective-permute-start(bf16[160,768]{1,0:T(8,128)(2,1)S(1)} %get-tuple-element.179), channel_id=1, source_target_pairs={{0,2},{1,3},{2,0},{3,1},{4,6},{5,7},{6,4},{7,5},{8,10},{9,11},{10,... | collective-permute-start | bytes 737288 | tf_op jit(solution)/shard_map/ppermute | solution.py:141
  244.1 7.7 %collective-permute-start.43 = (bf16[160,768]{1,0:T(8,128)(2,1)S(1)}, bf16[160,768]{1,0:T(8,128)(2,1)S(1)}, u32[]{:S(2)}, u32[]{:S(2)}) collective-permute-start(bf16[160,768]{1,0:T(8,128)(2,1)S(1)} %get-tuple-element.178), channel_id=1, source_target_pairs={{0,1},{1,0},{2,3},{3,2},{4,5},{5,4},{6,7},{7,6},{8,9},{9,8},{10,11... | collective-permute-start | bytes 737288 | tf_op jit(solution)/shard_map/ppermute | solution.py:141
  246.9 15.0 %collective-permute-start.41 = (bf16[256,384]{1,0:T(8,128)(2,1)S(1)}, bf16[256,384]{1,0:T(8,128)(2,1)S(1)}, u32[]{:S(2)}, u32[]{:S(2)}) collective-permute-start(bf16[256,384]{1,0:T(8,128)(2,1)S(1)} %get-tuple-element.173), channel_id=1, source_target_pairs={{0,8},{4,12},{8,0},{12,4},{1,9},{5,13},{9,1},{13,5},{2,10},{6,14},... | collective-permute-start | bytes 589832 | tf_op jit(solution)/shard_map/ppermute | solution.py:141
  249.3 12.6 %collective-permute-start.42 = (bf16[256,384]{1,0:T(8,128)(2,1)S(1)}, bf16[256,384]{1,0:T(8,128)(2,1)S(1)}, u32[]{:S(2)}, u32[]{:S(2)}) collective-permute-start(bf16[256,384]{1,0:T(8,128)(2,1)S(1)} %get-tuple-element.174), channel_id=1, source_target_pairs={{0,12},{4,8},{8,4},{12,0},{1,13},{5,9},{9,5},{13,1},{2,14},{6,10},... | collective-permute-start | bytes 589832 | tf_op jit(solution)/shard_map/ppermute | solution.py:141
  282.1 7.2 %collective-permute-start.54 = (bf16[40,768]{1,0:T(8,128)(2,1)S(1)}, bf16[40,768]{1,0:T(8,128)(2,1)S(1)}, u32[]{:S(2)}, u32[]{:S(2)}) collective-permute-start(bf16[40,768]{1,0:T(8,128)(2,1)S(1)} %get-tuple-element.194), channel_id=1, source_target_pairs={{0,12},{4,8},{8,4},{12,0},{1,13},{5,9},{9,5},{13,1},{2,14},{6,10},... | collective-permute-start | bytes 184328 | tf_op jit(solution)/shard_map/ppermute | solution.py:141
  282.2 18.5 %collective-permute-start.53 = (bf16[40,768]{1,0:T(8,128)(2,1)S(1)}, bf16[40,768]{1,0:T(8,128)(2,1)S(1)}, u32[]{:S(2)}, u32[]{:S(2)}) collective-permute-start(bf16[40,768]{1,0:T(8,128)(2,1)S(1)} %get-tuple-element.193), channel_id=1, source_target_pairs={{0,8},{4,12},{8,0},{12,4},{1,9},{5,13},{9,1},{13,5},{2,10},{6,14},... | collective-permute-start | bytes 184328 | tf_op jit(solution)/shard_map/ppermute | solution.py:141
  287.2 13.5 %collective-permute-start.52 = (bf16[40,768]{1,0:T(8,128)(2,1)S(1)}, bf16[40,768]{1,0:T(8,128)(2,1)S(1)}, u32[]{:S(2)}, u32[]{:S(2)}) collective-permute-start(bf16[40,768]{1,0:T(8,128)(2,1)S(1)} %get-tuple-element.192), channel_id=1, source_target_pairs={{0,4},{4,0},{8,12},{12,8},{1,5},{5,1},{9,13},{13,9},{2,6},{6,2},{1... | collective-permute-start | bytes 184328 | tf_op jit(solution)/shard_map/ppermute | solution.py:141
  287.2 29.1 %collective-permute-start.55 = (bf16[40,768]{1,0:T(8,128)(2,1)S(1)}, bf16[40,768]{1,0:T(8,128)(2,1)S(1)}, u32[]{:S(2)}, u32[]{:S(2)}) collective-permute-start(bf16[40,768]{1,0:T(8,128)(2,1)S(1)} %get-tuple-element.287), channel_id=1, source_target_pairs={{0,4},{4,0},{8,12},{12,8},{1,5},{5,1},{9,13},{13,9},{2,6},{6,2},{1... | collective-permute-start | bytes 184328 | tf_op jit(solution)/shard_map/ppermute | solution.py:141
  289.3 27.0 %collective-permute-start.56 = (bf16[40,768]{1,0:T(8,128)(2,1)S(1)}, bf16[40,768]{1,0:T(8,128)(2,1)S(1)}, u32[]{:S(2)}, u32[]{:S(2)}) collective-permute-start(bf16[40,768]{1,0:T(8,128)(2,1)S(1)} %get-tuple-element.286), channel_id=1, source_target_pairs={{0,8},{4,12},{8,0},{12,4},{1,9},{5,13},{9,1},{13,5},{2,10},{6,14},... | collective-permute-start | bytes 184328 | tf_op jit(solution)/shard_map/ppermute | solution.py:141
  289.3 27.0 %collective-permute-start.57 = (bf16[40,768]{1,0:T(8,128)(2,1)S(1)}, bf16[40,768]{1,0:T(8,128)(2,1)S(1)}, u32[]{:S(2)}, u32[]{:S(2)}) collective-permute-start(bf16[40,768]{1,0:T(8,128)(2,1)S(1)} %get-tuple-element.285), channel_id=1, source_target_pairs={{0,12},{4,8},{8,4},{12,0},{1,13},{5,9},{9,5},{13,1},{2,14},{6,10},... | collective-permute-start | bytes 184328 | tf_op jit(solution)/shard_map/ppermute | solution.py:141
  323.2 7.3 %collective-permute-start.60 = (bf16[160,768]{1,0:T(8,128)(2,1)S(1)}, bf16[160,768]{1,0:T(8,128)(2,1)S(1)}, u32[]{:S(2)}, u32[]{:S(2)}) collective-permute-start(bf16[160,768]{1,0:T(8,128)(2,1)S(1)} %get-tuple-element.201), channel_id=1, source_target_pairs={{0,3},{1,2},{2,1},{3,0},{4,7},{5,6},{6,5},{7,4},{8,11},{9,10},{10,... | collective-permute-start | bytes 737288 | tf_op jit(solution)/shard_map/ppermute | solution.py:141
  324.7 8.3 %collective-permute-start.59 = (bf16[160,768]{1,0:T(8,128)(2,1)S(1)}, bf16[160,768]{1,0:T(8,128)(2,1)S(1)}, u32[]{:S(2)}, u32[]{:S(2)}) collective-permute-start(bf16[160,768]{1,0:T(8,128)(2,1)S(1)} %get-tuple-element.200), channel_id=1, source_target_pairs={{0,2},{1,3},{2,0},{3,1},{4,6},{5,7},{6,4},{7,5},{8,10},{9,11},{10,... | collective-permute-start | bytes 737288 | tf_op jit(solution)/shard_map/ppermute | solution.py:141
  326.8 12.7 %collective-permute-start.64 = (bf16[192,768]{1,0:T(8,128)(2,1)S(1)}, bf16[192,768]{1,0:T(8,128)(2,1)S(1)}, u32[]{:S(2)}, u32[]{:S(2)}) collective-permute-start(bf16[192,768]{1,0:T(8,128)(2,1)S(1)} %get-tuple-element.279), channel_id=1, source_target_pairs={{0,4},{4,0},{8,12},{12,8},{1,5},{5,1},{9,13},{13,9},{2,6},{6,2},{1... | collective-permute-start | bytes 884744 | tf_op jit(solution)/shard_map/ppermute | solution.py:141
  327.6 22.1 %collective-permute-start.65 = (bf16[192,768]{1,0:T(8,128)(2,1)S(1)}, bf16[192,768]{1,0:T(8,128)(2,1)S(1)}, u32[]{:S(2)}, u32[]{:S(2)}) collective-permute-start(bf16[192,768]{1,0:T(8,128)(2,1)S(1)} %get-tuple-element.278), channel_id=1, source_target_pairs={{0,8},{4,12},{8,0},{12,4},{1,9},{5,13},{9,1},{13,5},{2,10},{6,14},... | collective-permute-start | bytes 884744 | tf_op jit(solution)/shard_map/ppermute | solution.py:141
  330.5 20.3 %collective-permute-start.66 = (bf16[192,768]{1,0:T(8,128)(2,1)S(1)}, bf16[192,768]{1,0:T(8,128)(2,1)S(1)}, u32[]{:S(2)}, u32[]{:S(2)}) collective-permute-start(bf16[192,768]{1,0:T(8,128)(2,1)S(1)} %get-tuple-element.277), channel_id=1, source_target_pairs={{0,12},{4,8},{8,4},{12,0},{1,13},{5,9},{9,5},{13,1},{2,14},{6,10},... | collective-permute-start | bytes 884744 | tf_op jit(solution)/shard_map/ppermute | solution.py:141
  333.2 18.8 %collective-permute-start.63 = (bf16[40,768]{1,0:T(8,128)(2,1)S(1)}, bf16[40,768]{1,0:T(8,128)(2,1)S(1)}, u32[]{:S(2)}, u32[]{:S(2)}) collective-permute-start(bf16[40,768]{1,0:T(8,128)(2,1)S(1)} %get-tuple-element.282), channel_id=1, source_target_pairs={{0,12},{4,8},{8,4},{12,0},{1,13},{5,9},{9,5},{13,1},{2,14},{6,10},... | collective-permute-start | bytes 184328 | tf_op jit(solution)/shard_map/ppermute | solution.py:141
  334.5 21.4 %collective-permute-start.62 = (bf16[40,768]{1,0:T(8,128)(2,1)S(1)}, bf16[40,768]{1,0:T(8,128)(2,1)S(1)}, u32[]{:S(2)}, u32[]{:S(2)}) collective-permute-start(bf16[40,768]{1,0:T(8,128)(2,1)S(1)} %get-tuple-element.283), channel_id=1, source_target_pairs={{0,8},{4,12},{8,0},{12,4},{1,9},{5,13},{9,1},{13,5},{2,10},{6,14},... | collective-permute-start | bytes 184328 | tf_op jit(solution)/shard_map/ppermute | solution.py:141
  339.6 16.3 %collective-permute-start.61 = (bf16[40,768]{1,0:T(8,128)(2,1)S(1)}, bf16[40,768]{1,0:T(8,128)(2,1)S(1)}, u32[]{:S(2)}, u32[]{:S(2)}) collective-permute-start(bf16[40,768]{1,0:T(8,128)(2,1)S(1)} %get-tuple-element.284), channel_id=1, source_target_pairs={{0,4},{4,0},{8,12},{12,8},{1,5},{5,1},{9,13},{13,9},{2,6},{6,2},{1... | collective-permute-start | bytes 184328 | tf_op jit(solution)/shard_map/ppermute | solution.py:141
  349.8 28.4 %collective-permute-start.70 = (bf16[160,768]{1,0:T(8,128)(2,1)S(1)}, bf16[160,768]{1,0:T(8,128)(2,1)S(1)}, u32[]{:S(2)}, u32[]{:S(2)}) collective-permute-start(bf16[160,768]{1,0:T(8,128)(2,1)S(1)} %pad_maximum_fusion.8.refs_2_), channel_id=1, source_target_pairs={{0,1},{1,0},{2,3},{3,2},{4,5},{5,4},{6,7},{7,6},{8,9},{9,8},{10,11... | collective-permute-start | bytes 737288 | tf_op jit(solution)/shard_map/ppermute | solution.py:141
  350.8 29.9 %collective-permute-start.71 = (bf16[160,768]{1,0:T(8,128)(2,1)S(1)}, bf16[160,768]{1,0:T(8,128)(2,1)S(1)}, u32[]{:S(2)}, u32[]{:S(2)}) collective-permute-start(bf16[160,768]{1,0:T(8,128)(2,1)S(1)} %pad_maximum_fusion.8.refs_2_), channel_id=1, source_target_pairs={{0,2},{1,3},{2,0},{3,1},{4,6},{5,7},{6,4},{7,5},{8,10},{9,11},{10,... | collective-permute-start | bytes 737288 | tf_op jit(solution)/shard_map/ppermute | solution.py:141
  352.0 28.7 %collective-permute-start.72 = (bf16[160,768]{1,0:T(8,128)(2,1)S(1)}, bf16[160,768]{1,0:T(8,128)(2,1)S(1)}, u32[]{:S(2)}, u32[]{:S(2)}) collective-permute-start(bf16[160,768]{1,0:T(8,128)(2,1)S(1)} %pad_maximum_fusion.8.refs_2_), channel_id=1, source_target_pairs={{0,3},{1,2},{2,1},{3,0},{4,7},{5,6},{6,5},{7,4},{8,11},{9,10},{10,... | collective-permute-start | bytes 737288 | tf_op jit(solution)/shard_map/ppermute | solution.py:141
  375.2 9.0 %collective-permute-start.67 = (bf16[256,384]{1,0:T(8,128)(2,1)S(1)}, bf16[256,384]{1,0:T(8,128)(2,1)S(1)}, u32[]{:S(2)}, u32[]{:S(2)}) collective-permute-start(bf16[256,384]{1,0:T(8,128)(2,1)S(1)} %get-tuple-element.212), channel_id=1, source_target_pairs={{0,4},{4,0},{8,12},{12,8},{1,5},{5,1},{9,13},{13,9},{2,6},{6,2},{1... | collective-permute-start | bytes 589832 | tf_op jit(solution)/shard_map/ppermute | solution.py:141
  378.2 10.8 %collective-permute-start.68 = (bf16[256,384]{1,0:T(8,128)(2,1)S(1)}, bf16[256,384]{1,0:T(8,128)(2,1)S(1)}, u32[]{:S(2)}, u32[]{:S(2)}) collective-permute-start(bf16[256,384]{1,0:T(8,128)(2,1)S(1)} %get-tuple-element.213), channel_id=1, source_target_pairs={{0,8},{4,12},{8,0},{12,4},{1,9},{5,13},{9,1},{13,5},{2,10},{6,14},... | collective-permute-start | bytes 589832 | tf_op jit(solution)/shard_map/ppermute | solution.py:141
  378.2 10.8 %collective-permute-start.69 = (bf16[256,384]{1,0:T(8,128)(2,1)S(1)}, bf16[256,384]{1,0:T(8,128)(2,1)S(1)}, u32[]{:S(2)}, u32[]{:S(2)}) collective-permute-start(bf16[256,384]{1,0:T(8,128)(2,1)S(1)} %get-tuple-element.214), channel_id=1, source_target_pairs={{0,12},{4,8},{8,4},{12,0},{1,13},{5,9},{9,5},{13,1},{2,14},{6,10},... | collective-permute-start | bytes 589832 | tf_op jit(solution)/shard_map/ppermute | solution.py:141
  380.6 40.4 %collective-permute-start.79 = (bf16[768,768]{1,0:T(8,128)(2,1)}, bf16[768,768]{1,0:T(8,128)(2,1)}, u32[]{:S(2)}, u32[]{:S(2)}) collective-permute-start(bf16[768,768]{1,0:T(8,128)(2,1)} %get-tuple-element.207.refs_7_), channel_id=1, source_target_pairs={{0,16},{16,0},{1,17},{17,1},{2,18},{18,2},{3,19},{19,3},{4,20},{20... | collective-permute-start | bytes 3538952 | tf_op jit(solution)/shard_map/ppermute | solution.py:141
  380.7 41.4 %collective-permute-start.80 = (bf16[768,768]{1,0:T(8,128)(2,1)}, bf16[768,768]{1,0:T(8,128)(2,1)}, u32[]{:S(2)}, u32[]{:S(2)}) collective-permute-start(bf16[768,768]{1,0:T(8,128)(2,1)} %get-tuple-element.208.refs_8_), channel_id=1, source_target_pairs={{0,16},{16,0},{1,17},{17,1},{2,18},{18,2},{3,19},{19,3},{4,20},{20... | collective-permute-start | bytes 3538952 | tf_op jit(solution)/shard_map/ppermute | solution.py:141
  405.8 39.3 %collective-permute-start.90 = (bf16[4,192,768]{2,1,0:T(8,128)(2,1)}, bf16[4,192,768]{2,1,0:T(8,128)(2,1)}, u32[]{:S(2)}, u32[]{:S(2)}) collective-permute-start(bf16[4,192,768]{2,1,0:T(8,128)(2,1)} %shard_map.203.refs_0_), channel_id=1, source_target_pairs={{16,0},{17,1},{18,2},{19,3},{20,4},{21,5},{22,6},{23,7},{24,8},{25... | collective-permute-start | bytes 3538952 | tf_op jit(solution)/shard_map/ppermute | solution.py:145
  412.5 7.4 %collective-permute-start.86 = (f32[20,768]{1,0:T(8,128)S(1)}, f32[20,768]{1,0:T(8,128)S(1)}, u32[]{:S(2)}, u32[]{:S(2)}) collective-permute-start(f32[20,768]{1,0:T(8,128)S(1)} %add_add_fusion.1), channel_id=1, source_target_pairs={{0,4},{4,0},{8,12},{12,8},{1,5},{5,1},{9,13},{13,9},{2,6},{6,2},{1... | collective-permute-start | bytes 184328 | tf_op jit(solution)/shard_map/ppermute | solution.py:141
  416.0 37.8 %collective-permute-start.81 = (f32[256,768]{1,0:T(8,128)}, f32[256,768]{1,0:T(8,128)}, u32[]{:S(2)}, u32[]{:S(2)}) collective-permute-start(f32[256,768]{1,0:T(8,128)} %copy-done.8), channel_id=1, source_target_pairs={{0,16},{1,17},{2,18},{3,19},{4,20},{5,21},{6,22},{7,23},{8,24},{9,... | collective-permute-start | bytes 2359304 | tf_op jit(solution)/shard_map/ppermute | solution.py:145
  419.9 17.3 %collective-permute-start.76 = (bf16[64,768]{1,0:T(8,128)(2,1)S(1)}, bf16[64,768]{1,0:T(8,128)(2,1)S(1)}, u32[]{:S(2)}, u32[]{:S(2)}) collective-permute-start(bf16[64,768]{1,0:T(8,128)(2,1)S(1)} %get-tuple-element.225.refs_11_.refs_1_), channel_id=1, source_target_pairs={{0,1},{1,0},{2,3},{3,2},{4,5},{5,4},{6,7},{7,6},{8,9},{9,8},{10,11... | collective-permute-start | bytes 294920 | tf_op jit(solution)/shard_map/ppermute | solution.py:141
  421.0 16.2 %collective-permute-start.77 = (bf16[64,768]{1,0:T(8,128)(2,1)S(1)}, bf16[64,768]{1,0:T(8,128)(2,1)S(1)}, u32[]{:S(2)}, u32[]{:S(2)}) collective-permute-start(bf16[64,768]{1,0:T(8,128)(2,1)S(1)} %get-tuple-element.225.refs_11_.refs_1_), channel_id=1, source_target_pairs={{0,2},{1,3},{2,0},{3,1},{4,6},{5,7},{6,4},{7,5},{8,10},{9,11},{10,... | collective-permute-start | bytes 294920 | tf_op jit(solution)/shard_map/ppermute | solution.py:141
  422.1 15.1 %collective-permute-start.78 = (bf16[64,768]{1,0:T(8,128)(2,1)S(1)}, bf16[64,768]{1,0:T(8,128)(2,1)S(1)}, u32[]{:S(2)}, u32[]{:S(2)}) collective-permute-start(bf16[64,768]{1,0:T(8,128)(2,1)S(1)} %get-tuple-element.225.refs_11_.refs_1_), channel_id=1, source_target_pairs={{0,3},{1,2},{2,1},{3,0},{4,7},{5,6},{6,5},{7,4},{8,11},{9,10},{10,... | collective-permute-start | bytes 294920 | tf_op jit(solution)/shard_map/ppermute | solution.py:141
  439.9 23.8 %collective-permute-start.82 = (f32[256,768]{1,0:T(8,128)S(1)}, f32[256,768]{1,0:T(8,128)S(1)}, u32[]{:S(2)}, u32[]{:S(2)}) collective-permute-start(f32[256,768]{1,0:T(8,128)S(1)} %shard_map.201.refs_1_), channel_id=1, source_target_pairs={{16,0},{17,1},{18,2},{19,3},{20,4},{21,5},{22,6},{23,7},{24,8},{25... | collective-permute-start | bytes 2359304 | tf_op jit(solution)/shard_map/ppermute | solution.py:145
  441.9 9.5 %collective-permute-start.89 = (f32[10,768]{1,0:T(8,128)}, f32[10,768]{1,0:T(8,128)}, u32[]{:S(2)}, u32[]{:S(2)}) collective-permute-start(f32[10,768]{1,0:T(8,128)} %fusion), channel_id=1, source_target_pairs={{0,16},{16,0},{1,17},{17,1},{2,18},{18,2},{3,19},{19,3},{4,20},{20... | collective-permute-start | bytes 92168 | tf_op jit(solution)/shard_map/ppermute | solution.py:141
  443.1 22.5 %collective-permute-start.94 = (bf16[192,768]{1,0:T(8,128)(2,1)S(1)}, bf16[192,768]{1,0:T(8,128)(2,1)S(1)}, u32[]{:S(2)}, u32[]{:S(2)}) collective-permute-start(bf16[192,768]{1,0:T(8,128)(2,1)S(1)} %copy-done.28), channel_id=1, source_target_pairs={{0,16},{1,17},{2,18},{3,19},{4,20},{5,21},{6,22},{7,23},{8,24},{9,... | collective-permute-start | bytes 884744 | tf_op jit(solution)/shard_map/ppermute | solution.py:145
  447.7 17.9 %collective-permute-start.91 = (bf16[192,768]{1,0:T(8,128)(2,1)}, bf16[192,768]{1,0:T(8,128)(2,1)S(1)}, u32[]{:S(2)}, u32[]{:S(2)}) collective-permute-start(bf16[192,768]{1,0:T(8,128)(2,1)} %get-tuple-element.235), channel_id=1, source_target_pairs={{0,4},{4,0},{8,12},{12,8},{1,5},{5,1},{9,13},{13,9},{2,6},{6,2},{1... | collective-permute-start | bytes 884744 | tf_op jit(solution)/shard_map/ppermute | solution.py:954
  451.4 16.1 %collective-permute-start.92 = (bf16[192,768]{1,0:T(8,128)(2,1)}, bf16[192,768]{1,0:T(8,128)(2,1)}, u32[]{:S(2)}, u32[]{:S(2)}) collective-permute-start(bf16[192,768]{1,0:T(8,128)(2,1)} %get-tuple-element.236), channel_id=1, source_target_pairs={{0,8},{4,12},{8,0},{12,4},{1,9},{5,13},{9,1},{13,5},{2,10},{6,14},... | collective-permute-start | bytes 884744 | tf_op jit(solution)/shard_map/ppermute | solution.py:954
  453.8 13.7 %collective-permute-start.93 = (bf16[192,768]{1,0:T(8,128)(2,1)}, bf16[192,768]{1,0:T(8,128)(2,1)}, u32[]{:S(2)}, u32[]{:S(2)}) collective-permute-start(bf16[192,768]{1,0:T(8,128)(2,1)} %get-tuple-element.237), channel_id=1, source_target_pairs={{0,12},{4,8},{8,4},{12,0},{1,13},{5,9},{9,5},{13,1},{2,14},{6,10},... | collective-permute-start | bytes 884744 | tf_op jit(solution)/shard_map/ppermute | solution.py:954
  (101 other events, 1685.2 us)
Sparse Core Ops, SparseCore 0:
  11.1 40.0 all-gather.1

commit v3 on v2

--- a/solution.py
+++ b/solution.py
@@ -16,6 +16,7 @@
 BF16 = jnp.bfloat16
 LANES = 128
 SPARE_BYTES = 6 * 1024 * 1024
+WIDE_BYTES = 48 * 1024 * 1024
 ROOT_2_PI = math.sqrt(2.0 / math.pi)
 
 
@@ -49,7 +50,9 @@
     return math.prod(lead) * (-(-rows // 16) * 16) * (-(-lanes // LANES) * LANES) * jnp.dtype(array.dtype).itemsize
 
 
-def kernel_call(body, outs, args, scratch=(), flops=0, after=()):
+def kernel_call(body, outs, args, scratch=(), flops=0, after=(), grant=0, mark=False):
+    if mark:
+        outs = list(outs) + [like(8, LANES, dtype=F32)]
     picks = [a for a in args if isinstance(a, (Pick, Rows))]
     operands, in_specs = [], []
     for a in args:
@@ -104,7 +107,10 @@
             sem = buffers[-1].at[number]
             given.append(hold(a, ins[at : at + count], ins[0], buffers[number], sem))
             at, number = at + count, number + 1
-        body(*given, *rest[: n_out + n_own])
+        if mark:
+            rest[n_out - 1][...] = jnp.zeros((8, LANES), F32)
+            rest = rest[: n_out - 1] + rest[n_out:]
+        body(*given, *rest[: n_out + n_own - mark])
 
     size = sum(math.prod(a.shape) * a.dtype.itemsize for a in list(args) + list(outs))
     held = sum(map(padded_bytes, list(args) + list(outs)))
@@ -115,7 +121,7 @@
         in_specs=in_specs,
         out_specs=[pl.BlockSpec(memory_space=pltpu.VMEM)] * n_out,
         scratch_shapes=scratch,
-        compiler_params=pltpu.CompilerParams(vmem_limit_bytes=held + SPARE_BYTES),
+        compiler_params=pltpu.CompilerParams(vmem_limit_bytes=max(grant, held + SPARE_BYTES)),
         cost_estimate=pl.CostEstimate(flops=flops, bytes_accessed=size, transcendentals=0),
     )(*operands)
 
@@ -492,113 +498,140 @@
 
 
 def expert_grads(place, pairs, got=None, after=()):
-    outs = [like(p[0].shape[1], p[1].shape[1], dtype=BF16 if got is None else F32) for p in pairs]
+    shapes = [(p[0].shape[1], p[1].shape[1]) for p in pairs]
+    outs = [like(len(pairs), *shapes[0])] if got is None else [like(*x, dtype=F32) for x in shapes]
     picks = [a for pair in pairs for a in pair]
 
     def body(place_ref, *refs):
         held, refs = refs[: len(picks)], refs[len(picks) :]
-        got_refs, out_refs = refs[: len(refs) - len(pairs)], refs[len(refs) - len(pairs) :]
-        for i, out_ref in enumerate(out_refs):
+        for i in range(len(pairs)):
             grad = dot_tn(held[2 * i].ready()[...], held[2 * i + 1].ready()[...])
-            if got_refs:
-                grad += got_refs[i][...].astype(F32)
-            out_ref[...] = grad.astype(out_ref.dtype)
+            if got is None:
+                refs[0][i] = grad.astype(BF16)
+            else:
+                refs[1 + i][...] = grad + refs[0][i].astype(F32)
 
     flops = sum(2 * p[0].shape[0] * p[0].shape[1] * p[1].shape[1] for p in pairs)
-    return kernel_call(body, outs, [place, *picks, *(got or [])], flops=flops, after=after)
-
-
-def dense_shares(place, pairs, n_ctx):
+    args = [place, *picks] + ([] if got is None else [got])
+    return kernel_call(body, outs, args, flops=flops, after=after, grant=WIDE_BYTES, mark=True)
+
+
+def dense_grad(place, pairs, after=()):
     model = pairs[0][0].shape[1]
     widths = [b.shape[1] for _, b in pairs]
-    share, width = model // n_ctx, sum(widths)
+    width = sum(widths)
 
     def body(place_ref, *refs):
-        ins, out_ref, total_ref = refs[: 2 * len(pairs)], refs[-2], refs[-1]
         at = 0
         for i, size in enumerate(widths):
-            total_ref[:, at : at + size] = dot_tn(ins[2 * i][...], ins[2 * i + 1][...])
+            grad = dot_tn(refs[2 * i][...], refs[2 * i + 1][...])
+            refs[-1][:, at : at + size] = grad.astype(BF16)
             at += size
-        for r in range(n_ctx):
-            first = pl.multiple_of((place_ref[0] ^ r) * share, share)
-            out_ref[r] = total_ref[pl.ds(first, share), :].astype(BF16)
 
     rows = pairs[0][0].shape[0]
     return kernel_call(
         body,
-        [like(n_ctx, share, width)],
+        [like(model, width)],
         [place, *(a for pair in pairs for a in pair)],
-        [pltpu.VMEM((model, width), F32)],
         flops=2 * rows * model * width,
-    )[0]
-
-
-def add_shares(one, two):
-    n_ctx, share, width = one.shape
-
-    def body(one_ref, two_ref, *outs):
-        for r, out_ref in enumerate(outs):
-            out_ref[...] = (one_ref[r].astype(F32) + two_ref[r].astype(F32)).astype(BF16)
-
-    return kernel_call(body, [like(share, width)] * n_ctx, [one, two])
-
-
-def sum_shares(parts):
-    share, width = parts[0].shape
-
+        after=after,
+        mark=True,
+    )
+
+
+def small_columns(rows_ref):
+    rows = rows_ref[...]
+    wide = jnp.concatenate([rows, jnp.zeros((LANES - rows.shape[0], rows.shape[1]), F32)])
+    return wide.T
+
+
+def joint_send(place, grad, smalls):
+    model, width = grad.shape
+
+    def body(place_ref, grad, one_ref, two_ref, out_ref):
+        small = either(place_ref, small_columns(two_ref), small_columns(one_ref))
+        out_ref[:, width:] = small.astype(BF16)
+        out_ref[:, :width] = grad.ready()[...]
+
+    return kernel_call(body, [like(model, width + LANES)], [place, grad, *smalls])[0]
+
+
+def joint_sum(place, grad, smalls, got):
+    model, width = grad.shape
+
+    def body(place_ref, grad, one_ref, two_ref, got_ref, out_ref):
+        small = either(place_ref, small_columns(one_ref), small_columns(two_ref))
+        out_ref[:, width:] = (small + got_ref[:, width:].astype(F32)).astype(BF16)
+        total = grad.ready()[...].astype(F32) + got_ref[:, :width].astype(F32)
+        out_ref[:, :width] = total.astype(BF16)
+
+    return kernel_call(body, [like(model, width + LANES)], [place, grad, *smalls, got])[0]
+
+
+def joint_split(total, width, n_experts):
+    share = total.shape[0]
+
+    def body(total_ref, qkv_ref, out_ref, first_ref, second_ref, router_ref, bias_ref):
+        for i, at in enumerate((0, 2, 3)):
+            qkv_ref[i] = total_ref[:, at * width : (at + 1) * width].astype(F32)
+        out_ref[...] = total_ref[:, width : 2 * width].astype(F32).T
+        small = total_ref[:, 4 * width :].astype(F32)
+        router_ref[...] = small[:, 2 : 2 + n_experts]
+        rows = small.T
+        first_ref[...] = rows[0:1]
+        second_ref[...] = rows[1:2]
+        bias_ref[...] = rows[2 + n_experts : 3 + n_experts]
+
+    shapes = [(3, share, width), (width, share)] + [(1, share)] * 2 + [(share, n_experts), (1, share)]
+    return kernel_call(body, [like(*shape, dtype=F32) for shape in shapes], [total])
+
+
+def join_quarter(pieces, after):
     def body(*refs):
-        refs[-1][...] = tree_sum([ref[...].astype(F32) for ref in refs[:-1]]).astype(BF16)
-
-    return kernel_call(body, [like(share, width)], parts)[0]
-
-
-def dense_grads(place, parts0, sum1, got1, width):
-    share = sum1.shape[0]
+        rows = [ref[...].astype(F32) for ref in refs[:-1]]
+        refs[-1][...] = jnp.concatenate(rows).astype(BF16)
+
+    per, model = pieces[0].shape
+    return kernel_call(body, [like(per * len(pieces), model)], pieces, after=after)[0]
+
+
+def router_grads(place, pairs, n_experts):
+    model = pairs[0][1].shape[1]
 
     def body(place_ref, *refs):
-        part_refs, (sum_ref, got_ref, qkv_ref, out_ref) = refs[:-4], refs[-4:]
-        layer0 = tree_sum([ref[...].astype(F32) for ref in part_refs])
-        layer1 = sum_ref[...].astype(F32) + got_ref[...].astype(F32)
-        total = either(place_ref, layer0, layer1)
-        for i, at in enumerate((0, 2, 3)):
-            qkv_ref[i] = total[:, at * width : (at + 1) * width]
-        out_ref[...] = total[:, width : 2 * width].T
+        for layer in range(2):
+            grad = dot_tn(refs[2 * layer][...], refs[2 * layer + 1][...])
+            refs[-1][layer * n_experts : (layer + 1) * n_experts, :] = grad[:n_experts]
+
+    args = [place, *(a for pair in pairs for a in pair)]
+    return kernel_call(body, [like(2 * n_experts, model, dtype=F32)], args)[0]
+
+
+def small_rows(place, layer, dgain_first, dgain_second, router_parts, lanes, n_experts, n_ctx):
+    model, count = dgain_first.shape[1], lanes.shape[0]
+    share, bias_share = model // n_ctx, count // n_ctx
+    rows = -(-(3 + n_experts) // 8) * 8
+
+    def body(place_ref, first_ref, second_ref, lanes_ref, *refs):
+        out_ref = refs[-1]
+        router = tree_sum([ref[...] for ref in refs[:-1]])
+        out_ref[...] = jnp.zeros(out_ref.shape, F32)
+        out_ref[0:1, :] = first_ref[...]
+        out_ref[1:2, :] = second_ref[...]
+        out_ref[2 : 2 + n_experts, :] = router[layer * n_experts : (layer + 1) * n_experts]
+        sums = jnp.sum(lanes_ref[...], axis=1, keepdims=True)
+        value = lax.broadcasted_iota(jnp.int32, (count, model), 0)
+        lane = lax.broadcasted_iota(jnp.int32, (count, model), 1)
+        target = value
+        for c in range(1, n_ctx):
+            target += jnp.where(value >= c * bias_share, share - bias_share, 0)
+        row = jnp.sum(jnp.where(lane == target, sums, 0.0), axis=0, keepdims=True)
+        out_ref[2 + n_experts : 3 + n_experts, :] = row
 
     return kernel_call(
         body,
-        [like(3, share, width, dtype=F32), like(width, share, dtype=F32)],
-        [place, *parts0, sum1, got1],
-    )
-
-
-def small_pack(place, layers, n_experts, n_heads, after=()):
-    model = layers[0][0].shape[1]
-    rows = 1 + n_experts + n_heads
-
-    def body(place_ref, *refs):
-        out_ref = refs[-1]
-        out_ref[...] = jnp.zeros(out_ref.shape, F32)
-        for layer in range(2):
-            dgain_ref, dlogits_ref, arrived_ref, lanes_ref = refs[4 * layer : 4 * layer + 4]
-            at = layer * rows
-            out_ref[at : at + 1, :] = dgain_ref[...] * (1.0 / n_heads)
-            router = dot_tn(dlogits_ref[...], arrived_ref[...])
-            out_ref[at + 1 : at + 1 + n_experts, :] = router[:n_experts]
-            count = lanes_ref.shape[0]
-            eye = lax.broadcasted_iota(jnp.int32, (count, count), 0) == lax.broadcasted_iota(
-                jnp.int32, (count, count), 1
-            )
-            sums = jnp.sum(lanes_ref[...], axis=1, keepdims=True)
-            row = jnp.sum(jnp.where(eye, sums, 0.0), axis=0, keepdims=True)
-            for h in range(n_heads):
-                spot = at + 1 + n_experts + h
-                out_ref[spot : spot + 1, :count] = jnp.where(place_ref[1] == h, row, 0.0)
-
-    return kernel_call(
-        body,
-        [like(2 * rows, model, dtype=F32)],
-        [place, *(a for layer in layers for a in layer)],
-        after=after,
+        [like(rows, model, dtype=F32)],
+        [place, dgain_first, dgain_second, lanes, *router_parts],
     )[0]
 
 
@@ -627,7 +660,8 @@
         [middle, tokens, *returned],
         flops=2 * rows * model * share * len(returned),
         after=after,
-    )[0]
+        mark=True,
+    )
 
 
 def combine_project(place, middle, returned, tokens, gain, qkv):
@@ -727,21 +761,11 @@
     return values[0]
 
 
-def share_sum(place, parts, x):
-    share, model = parts[0].shape
-
-    def body(place_ref, *refs):
-        part_refs, (x_ref, total_ref, dgain_ref) = refs[: len(parts)], refs[len(parts) :]
-        total = tree_sum([ref[...].astype(F32) for ref in part_refs])
-        total_ref[...] = total.astype(BF16)
-        first = pl.multiple_of(place_ref[1] * share, share)
-        values = x_ref[pl.ds(first, share), :].astype(F32)
-        scale = lax.rsqrt(jnp.mean(values * values, axis=-1, keepdims=True) + EPSILON)
-        dgain_ref[...] = jnp.sum(total * (values * scale), axis=0, keepdims=True)
-
-    return kernel_call(
-        body, [like(share, model), like(1, model, dtype=F32)], [place, *parts, x]
-    )
+def share_sum(parts):
+    def body(*refs):
+        refs[-1][...] = tree_sum([ref[...].astype(F32) for ref in refs[:-1]]).astype(BF16)
+
+    return kernel_call(body, [like(*parts[0].shape)], parts)[0]
 
 
 def input_back(place, dnormed_parts, x, gain, dmiddle, tokens=None, n_ctx=0, per=0, after=()):
@@ -752,11 +776,13 @@
     def body(place_ref, *refs):
         part_refs, refs = refs[:n_heads], refs[n_heads:]
         x_ref, gain_ref, dmiddle_ref = refs[:3]
-        dx_ref, chunk_refs, dnormed_ref = refs[len(given)], refs[len(given) + 1 : -1], refs[-1]
+        (dx_ref, dgain_ref), chunk_refs = refs[len(given) :][:2], refs[len(given) + 2 : -1]
+        dnormed_ref = refs[-1]
         for r in range(n_heads):
             first = pl.multiple_of((place_ref[1] ^ r) * share, share)
             dnormed_ref[pl.ds(first, share), :] = part_refs[r][...].astype(F32)
-        part, _ = norm_back(x_ref[...].astype(F32), gain_ref[...], dnormed_ref[...])
+        part, dgain = norm_back(x_ref[...].astype(F32), gain_ref[...], dnormed_ref[...])
+        dgain_ref[...] = dgain
         dx = (dmiddle_ref[...] + part).astype(dx_ref.dtype)
         dx_ref[...] = dx
         if tokens is not None:
@@ -764,12 +790,13 @@
 
     outs = kernel_call(
         body,
-        [like(rows, model, dtype=F32 if tokens is None else BF16)] + [like(per, model)] * n_ctx,
+        [like(rows, model, dtype=F32 if tokens is None else BF16), like(1, model, dtype=F32)]
+        + [like(per, model)] * n_ctx,
         [place, *dnormed_parts, *given],
         [pltpu.VMEM((rows, model), F32)],
         after=after,
     )
-    return outs[0], outs[1:]
+    return outs[0], outs[1], outs[2:]
 
 
 def bucket_of(distance):
@@ -933,26 +960,22 @@
     )[0]
 
 
-def heads_sum(chunks):
-    return tree_sum([part.astype(F32) for part in exchange(chunks, "heads")]).astype(BF16)
-
-
-def back_rows(total, n_ctx):
-    per = total.shape[0] // n_ctx
-    return exchange([total[r * per : (r + 1) * per] for r in range(n_ctx)], "ctx")
-
-
-def return_rows(chunks, n_ctx):
-    return gather_rows(jnp.concatenate(back_rows(heads_sum(chunks), n_ctx), axis=0), "heads")
-
-
-def exchange_first(chunks):
-    n_ctx = len(chunks)
-    parts = [chunks[0]]
-    for r in range(1, n_ctx):
-        pairs = [(i, i ^ r) for i in range(n_ctx)]
-        parts.append(lax.ppermute(chunks[r], ("section", "ctx"), pairs))
-    return parts
+def heads_sum(chunks, n_ctx, after=()):
+    parts = exchange(chunks, "heads")
+    rows, model = parts[0].shape
+    per = rows // n_ctx
+
+    def body(*refs):
+        total = tree_sum([ref[...].astype(F32) for ref in refs[: len(parts)]])
+        for r, out_ref in enumerate(refs[len(parts) :]):
+            out_ref[...] = total[r * per : (r + 1) * per].astype(BF16)
+
+    return kernel_call(body, [like(per, model)] * n_ctx, parts, after=after)
+
+
+def return_rows(chunks, n_ctx, after=()):
+    back = exchange(heads_sum(chunks, n_ctx, after), "ctx")
+    return gather_rows(jnp.concatenate(back, axis=0), "heads")
 
 
 def send_rows(chunks):
@@ -1039,14 +1062,17 @@
         place, return_rows(chunks, n_ctx), tokens[1], middle1, gains_second[1], cotangent, out_own[1]
     )
     dq1, dtable1, dkv1 = attend_back(place, q1, [kv_all1], biases[1], lse1, dmix1, n_ctx)
-    out_total = heads_sum(experts_out(place, hidden1, margin1, down[1], n_heads, [dq1]))
+    out_total = heads_sum(
+        experts_out(place, hidden1, margin1, down[1], n_heads, [dq1]), n_ctx
+    )
     dkv_sum1, chunks = project_back(
-        place, dq1, exchange(dkv1, "ctx"), qkv[1], n_heads, [out_total]
-    )
-    total1, dgain_first1 = share_sum(place, exchange(chunks, "heads"), x1)
+        place, dq1, exchange(dkv1, "ctx"), qkv[1], n_heads, [out_total[0]]
+    )
+    total1 = share_sum(exchange(chunks, "heads"))
     lanes1 = table_back(dtable1)
-    shares1 = dense_shares(place, [(normed1, dq1), (datt1, mix1), (normed1, dkv_sum1)], n_ctx)
-    dx1, sent = input_back(
+    out_back = exchange(out_total, "ctx")
+    dense1, made = dense_grad(place, [(normed1, dq1), (datt1, mix1), (normed1, dkv_sum1)])
+    dx1, dgain_first1, sent = input_back(
         place,
         exchange([total1] * n_heads, "heads"),
         x1,
@@ -1055,80 +1081,78 @@
         tokens[0],
         n_ctx,
         per,
-        [lanes1, shares1],
-    )
-
-    out_back = back_rows(out_total, n_ctx)
+        [lanes1, made, *out_back[1:]],
+    )
+
     dout_rows0 = send_rows(sent)
     chunks, (dpre0, dslots0, dlogits0) = experts_back(
-        place, dout_rows0, kept0, arrived0, *expert_weights(0), n_heads, out_back
+        place, dout_rows0, kept0, arrived0, *expert_weights(0), n_heads
     )
     lists = [(arrived0, arrived1), (dpre0, dpre1), (kept0[1], hidden1), (dslots0, dslots1)]
     mine, theirs = [Pick(a, b) for a, b in lists], [Pick(b, a) for a, b in lists]
-    sends = expert_grads(place, [theirs[:2], theirs[2:]])
-    sum1 = sum_shares(exchange([shares1[r] for r in range(n_ctx)], "ctx"))
+    sends, sends_made = expert_grads(place, [theirs[:2], theirs[2:]])
+    returned = return_rows(chunks, n_ctx, [sends_made])
+    router_part = router_grads(place, [(dlogits0, arrived0), (dlogits1, arrived1)], n_experts)
     dmiddle0, datt0, dmix0, dgain_second0 = middle_back(
         place,
-        return_rows(chunks, n_ctx),
+        returned,
         tokens[0],
         middle0,
         gains_second[0],
         dx1,
         out_own[0],
-        [*sends, sum1],
+        [router_part],
     )
     dq0, dtable0, dkv0 = attend_back(place, q0, [kv_all0], biases[0], lse0, dmix0, n_ctx)
     lanes0 = table_back(dtable0)
-    layers = [
-        (dgain_second0, dlogits0, arrived0, lanes0),
-        (dgain_second1, dlogits1, arrived1, lanes1),
-    ]
-    pack = small_pack(place, layers, n_experts, n_heads)
-    quarter = jnp.concatenate(out_back, axis=0)
-    out = combine(
-        middle1, exchange([quarter] * n_heads, "heads"), tokens_near, [dq0]
-    )
+    router_parts = exchange([router_part] * n_heads, "heads")
+    small1 = small_rows(
+        place, 1, dgain_first1, dgain_second1, router_parts, lanes1, n_experts, n_ctx
+    )
+    quarter = join_quarter(out_back, [dq0])
+    out, out_made = combine(middle1, exchange([quarter] * n_heads, "heads"), tokens_near, [])
     dkv_sum0, chunks = project_back(
-        place, dq0, exchange(dkv0, "ctx"), qkv[0], n_heads, [pack, out]
-    )
-    total0, dgain_first0 = share_sum(place, exchange(chunks, "heads"), x0)
-    shares0 = dense_shares(place, [(normed0, dq0), (datt0, mix0), (normed0, dkv_sum0)], n_ctx)
-    gots = [swap(g, "section") for g in sends]
-    grad_up, grad_down = expert_grads(place, [mine[:2], mine[2:]], gots, after=[total0])
-    (dx0,) = input_back(
+        place, dq0, exchange(dkv0, "ctx"), qkv[0], n_heads, [small1, out_made]
+    )
+    parts = exchange(chunks, "heads")
+    total0 = share_sum(parts)
+    dense0, made = dense_grad(
+        place, [(normed0, dq0), (datt0, mix0), (normed0, dkv_sum0)], parts[1:2]
+    )
+    dx0, dgain_first0, _ = input_back(
         place,
         exchange([total0] * n_heads, "heads"),
         x0,
         gains_first[0],
         dmiddle0,
-        after=[grad_up],
-    )[:1]
-
-    got1 = one_way(sum1, 0)
-    parts0 = exchange_first(add_shares(shares0, one_way(shares0, 1)))
-    grad_qkv, grad_out = dense_grads(place, parts0, sum1, got1, width)
-    pack = jnp.concatenate([dgain_first0, dgain_first1, pack])
-    pack = tree_sum(exchange([pack] * n_heads, "heads"))
-    pack = tree_sum(exchange([pack] * n_ctx, "ctx"))
-    count = 1 + n_experts + n_heads
-    packs = [jnp.concatenate([pack[i : i + 1], pack[2 + i * count :][:count]]) for i in range(2)]
-    pack = jnp.where(first, packs[0], packs[1]) + swap(
-        jnp.where(first, packs[1], packs[0]), "section"
-    )
-    share = model // n_ctx
-    mine = lax.dynamic_slice_in_dim(pack, ctx_index * share, share, 1)
-    bias_share = BUCKETS // n_ctx * heads
-    at = (2 + n_experts + heads_index, ctx_index * bias_share)
-    grad_bias = lax.dynamic_slice(pack, at, (1, bias_share))
-    boundary_out = assemble(place, dx0, one_way(out, 0), one_way(dx0, 1), out)
+        after=[made, lanes0],
+    )
+
+    got_dx = one_way(dx0, 1)
+    small0 = small_rows(
+        place, 0, dgain_first0, dgain_second0, router_parts, lanes0, n_experts, n_ctx
+    )
+    smalls = [small0, small1]
+    got = swap(joint_send(place, Pick(dense1, dense0), smalls), "section")
+    joint = joint_sum(place, Pick(dense0, dense1), smalls, got)
+    joint = lax.psum_scatter(joint, "ctx", scatter_dimension=0, tiled=True)
+    grad_up, grad_down, _ = expert_grads(
+        place, [mine[:2], mine[2:]], swap(sends, "section"), after=[dgain_first0]
+    )
+    grad_qkv, grad_out, grad_first, grad_second, grad_router, grad_bias = joint_split(
+        joint, width, n_experts
+    )
+    bias_share = BUCKETS // n_ctx
+    grad_bias = grad_bias[:, : bias_share * heads].reshape(1, bias_share, heads)
+    boundary_out = assemble(place, dx0, one_way(out, 0), got_dx, out)
     return (
         boundary_out[None],
-        mine[0][None],
+        grad_first,
         grad_qkv[None],
-        grad_bias.reshape(1, BUCKETS // n_ctx, heads),
+        grad_bias,
         grad_out[None],
-        mine[1][None],
-        mine[2 : 2 + n_experts].T[None],
+        grad_second,
+        grad_router[None],
         grad_up[None, None],
         grad_down[None, None],
     )

time: 483 us -> 462 us (0.957)
  starting transfers between devices: 124 us -> 107 us
    ppermute x88 -> x81, waiting for transfers between devices: 87.1 us -> 74.2 us  [swap(): return lax.ppermute(array, axis, [(i, i ^ by) for i in range(devices)])]
    reduce_scatter x0 -> x1, waiting for transfers between devices: none -> 12.3 us  [body(): joint = lax.psum_scatter(joint, 'ctx', scatter_dimension=0, tiled=True)]
    ppermute x3 -> x0, starting transfers between devices: 10.1 us -> none  [exchange_first(): parts.append(lax.ppermute(chunks[r], ('section', 'ctx'), pairs))]
    ppermute x4 -> x2, starting transfers between devices: 8.54 us -> 3.63 us  [one_way(): return lax.ppermute(array, 'section', [(source, 1 - source)])]
    unnamed x143 -> x168, local copies, waits for them, and re-layouts: 20.6 us -> 24.8 us
    ppermute x88 -> x81, starting transfers between devices: 105 us -> 103 us  [swap(): return lax.ppermute(array, axis, [(i, i ^ by) for i in range(devices)])]
    pallas_call x36 -> x43, Pallas kernels: 93 us -> 91.8 us  [kernel_call(): pl.pallas_call(wrapped, out_shape=outs, in_specs=in_specs, out_specs=[pl....]
  transfers between devices with their start and end apart: 96 -> 85, of which waited for: 32 -> 37; matrix products, arithmetic and copies ran while one was open for 2% -> 1% of each run, Pallas kernels for 13% -> 10%
where the time goes in v3:
time: 462 us; the launch traced here: 458 us
  blocking collectives  121 us (26%)
  starting transfers between devices  107 us (23%)
  Pallas kernels  94.6 us (20%)
  waiting for transfers between devices  89.7 us (19%)
  local copies, waits for them, and re-layouts  27.3 us (6%)
  between operations  15.7 us (3%)
    all_gather x8, blocking collectives, gather_rows(): return lax.all_gather(array, axis, axis=0, tiled=True)  121 us
    ppermute x81, starting transfers between devices, swap(): return lax.ppermute(array, axis, [(i, i ^ by) for i in range(devices)])  103 us
    pallas_call x43, Pallas kernels, kernel_call(): pl.pallas_call(wrapped, out_shape=outs, in_specs=in_specs, out_specs=[pl....  91.8 us
    ppermute x81, waiting for transfers between devices, swap(): return lax.ppermute(array, axis, [(i, i ^ by) for i in range(devices)])  74.2 us
    unnamed x168, local copies, waits for them, and re-layouts  24.8 us
    reduce_scatter x1, waiting for transfers between devices, body(): joint = lax.psum_scatter(joint, 'ctx', scatter_dimension=0, tiled=True)  12.3 us
  transfers between devices with their start and end apart: 85, of which 37 were waited for; matrix products, arithmetic and copies ran while one was open for 1% of the time, Pallas kernels for 10%

profile of v3, /device:TPU:0, one launch (start us, length us, event | category | flops | bytes accessed | tf_op | source)
XLA Modules:
  0.0 457.7 jit_solution(15869006619755565336)
XLA Ops:
  17.7 2.1 shard_map.169
  22.1 2.8 shard_map.170
  24.9 21.3 %all_gather.27.refs_2_ = bf16[1024,384]{1,0:T(8,128)(2,1)S(1)} all-gather(bf16[256,384]{1,0:T(8,128)(2,1)S(1)} %get-tuple-element.147.refs_0_.refs_7_.refs_2_), channel_id=1, replica_groups=mesh['section'=2,'ctx'=4,'heads'=4] {'ctx'}, dimensions={0}, use_global_device_ids=true | all-gather | bytes 983040 | tf_op jit(solution)/shard_map/all_gather | solution.py:159
  46.2 3.0 shard_map.171
  50.7 2.4 collective-permute-start.6
  62.8 2.5 collective-permute-start.16
  70.6 2.4 shard_map.174
  73.1 2.4 collective-permute-start.12
  75.5 2.0 collective-permute-start.13
  77.5 3.7 shard_map.175
  81.6 13.2 %all_gather.29.refs_1_.refs_2_ = bf16[640,768]{1,0:T(8,128)(2,1)S(1)} all-gather(bf16[160,768]{1,0:T(8,128)(2,1)S(1)} %pad_maximum_fusion.2), channel_id=1, replica_groups=mesh['section'=2,'ctx'=4,'heads'=4] {'heads'}, dimensions={0}, use_global_device_ids=true | all-gather | bytes 1228800 | tf_op jit(solution)/shard_map/all_gather | solution.py:159
  94.8 4.5 shard_map.176
  102.9 2.7 collective-permute-done.19.refs_1_
  105.6 3.3 collective-permute-done.20.refs_2_
  109.1 2.8 collective-permute-start.23
  115.0 2.8 collective-permute-start.26
  119.7 13.5 %all_gather.30.refs_2_ = bf16[640,768]{1,0:T(8,128)(2,1)S(1)} all-gather(bf16[160,768]{1,0:T(8,128)(2,1)S(1)} %pad_maximum_fusion.3), channel_id=1, replica_groups=mesh['section'=2,'ctx'=4,'heads'=4] {'heads'}, dimensions={0}, use_global_device_ids=true | all-gather | bytes 1228800 | tf_op jit(solution)/shard_map/all_gather | solution.py:159
  133.2 2.2 shard_map.178
  135.4 15.9 %all_gather.31.refs_2_ = bf16[1024,384]{1,0:T(8,128)(2,1)S(1)} all-gather(bf16[256,384]{1,0:T(8,128)(2,1)S(1)} %get-tuple-element.171), channel_id=1, replica_groups=mesh['section'=2,'ctx'=4,'heads'=4] {'ctx'}, dimensions={0}, use_global_device_ids=true | all-gather | bytes 983040 | tf_op jit(solution)/shard_map/all_gather | solution.py:159
  151.3 3.0 shard_map.179
  157.3 3.1 collective-permute-done.30.refs_4_
  161.8 3.5 collective-permute-done.28.refs_2_
  165.3 2.4 shard_map.181
  167.8 2.6 collective-permute-start.32
  173.0 3.5 collective-permute-done.33
  176.5 16.2 %all_gather.32.refs_2_.refs_1_.refs_4_ = bf16[640,768]{1,0:T(8,128)(2,1)S(1)} all-gather(bf16[160,768]{1,0:T(8,128)(2,1)S(1)} %pad_maximum_fusion.4), channel_id=1, replica_groups=mesh['section'=2,'ctx'=4,'heads'=4] {'heads'}, dimensions={0}, use_global_device_ids=true | all-gather | bytes 1228800 | tf_op jit(solution)/shard_map/all_gather | solution.py:159
  192.6 8.0 %shard_map.182 = (bf16[160,768]{1,0:T(8,128)(2,1)S(1)}, bf16[160,768]{1,0:T(8,128)(2,1)S(1)}, bf16[160,768]{1,0:T(8,128)(2,1)S(1)}, bf16[160,768]{1,0:T(8,128)(2...) custom-call(s32[3]{0:T(128)S(1)} %pad_add_fusion.1.refs_0_.place_ref, ...), custom_call_target="tpu_custom_call" | custom-call | flops 1509949440 | bytes 8623116 | tf_op jit(solution)/shard_map/pallas_call | solution.py:118
  205.2 4.0 collective-permute-done.34.refs_1_
  210.8 2.1 collective-permute-done.36.refs_3_
  213.8 2.9 collective-permute-start.38
  218.9 3.8 collective-permute-done.39
  222.7 15.5 %all_gather.33.refs_1_ = bf16[640,768]{1,0:T(8,128)(2,1)S(1)} all-gather(bf16[160,768]{1,0:T(8,128)(2,1)S(1)} %pad_maximum_fusion.5), channel_id=1, replica_groups=mesh['section'=2,'ctx'=4,'heads'=4] {'heads'}, dimensions={0}, use_global_device_ids=true | all-gather | bytes 1228800 | tf_op jit(solution)/shard_map/all_gather | solution.py:159
  238.2 1.8 shard_map.184
  240.1 4.9 %shard_map.185 = (bf16[256,192]{1,0:T(8,128)(2,1)S(1)}, f32[3,4,128,128]{3,2,1,0:T(8,128)S(1)}, bf16[256,384]{1,0:T(8,128)(2,1)S(1)}, bf16[256,384]{1,0:T(8,128)...) custom-call(s32[3]{0:T(128)S(1)} %pad_add_fusion.1.refs_0_.place_ref, ...), custom_call_target="tpu_custom_call" | custom-call | flops 503316480 | bytes 3443724 | tf_op jit(solution)/shard_map/pallas_call | solution.py:118
  245.0 2.8 shard_map.186
  255.7 2.0 collective-permute-done.44.refs_2_
  258.7 4.8 %collective-permute-done.41.refs_4_ = bf16[256,384]{1,0:T(8,128)(2,1)S(1)} collective-permute-done((bf16[256,384]{1,0:T(8,128)(2,1)S(1)}, bf16[256,384]{1,0:T(8,128)(2,1)S(1)}, u32[]{:S(2)}, u32[]{:S(2)}) %collective-permute-start.41) | collective-permute-done | bytes 196640 | tf_op jit(solution)/shard_map/ppermute | solution.py:147
  265.1 1.9 collective-permute-start.47
  268.5 4.0 collective-permute-start.52
  276.2 5.1 %collective-permute-start.53 = (bf16[40,768]{1,0:T(8,128)(2,1)S(1)}, bf16[40,768]{1,0:T(8,128)(2,1)S(1)}, u32[]{:S(2)}, u32[]{:S(2)}) collective-permute-start(bf16[40,768]{1,0:T(8,128)(2,1)S(1)} %get-tuple-element.222), channel_id=1, source_target_pairs={{0,8},{4,12},{8,0},{12,4},{1,9},{5,13},{9,1},{13,5},{2,10},{6,14},... | collective-permute-start | bytes 184328 | tf_op jit(solution)/shard_map/ppermute | solution.py:147
  281.3 2.3 collective-permute-start.54
  289.2 2.9 collective-permute-start.56
  294.4 3.8 collective-permute-done.57
  298.2 13.0 %all_gather.34.refs_1_ = bf16[640,768]{1,0:T(8,128)(2,1)S(1)} all-gather(bf16[160,768]{1,0:T(8,128)(2,1)S(1)} %pad_maximum_fusion.6), channel_id=1, replica_groups=mesh['section'=2,'ctx'=4,'heads'=4] {'heads'}, dimensions={0}, use_global_device_ids=true | all-gather | bytes 1228800 | tf_op jit(solution)/shard_map/all_gather | solution.py:159
  311.2 7.4 %shard_map.193 = (bf16[160,768]{1,0:T(8,128)(2,1)S(1)}, bf16[160,768]{1,0:T(8,128)(2,1)}, bf16[160,768]{1,0:T(8,128)(2,1)}, bf16[160,768]{1,0:T(8,128)(2,1)}, bf...) custom-call(s32[3]{0:T(128)S(1)} %pad_add_fusion.1.refs_0_.place_ref, ...), custom_call_target="tpu_custom_call" | custom-call | flops 1509949440 | bytes 9606156 | tf_op jit(solution)/shard_map/pallas_call | solution.py:118
  323.8 5.9 %shard_map.194 = (bf16[2,768,768]{2,1,0:T(8,128)(2,1)}, f32[8,128]{1,0:T(8,128)S(1)}) custom-call(s32[3]{0:T(128)S(1)} %pad_add_fusion.1.refs_0_.place_ref, bf16[640,768]{1,0:T(8,128)(2,1)S(1)} %all_gather.32.refs_2_.refs_1_.refs_4_, bf16[640,768]{1,0:T(8,128)(2,1)S(1)} %all_gather.29.refs_1_.refs_2_, ...), custom_call_target="tpu_custom_call" | custom-call | flops 1509949440 | bytes 6295564 | tf_op jit(solution)/shard_map/pallas_call | solution.py:118
  329.7 4.1 collective-permute-done.59.refs_2_
  333.9 2.4 collective-permute-start.62
  336.3 2.0 collective-permute-start.63
  340.3 5.1 %collective-permute-done.62 = bf16[40,768]{1,0:T(8,128)(2,1)S(1)} collective-permute-done((bf16[40,768]{1,0:T(8,128)(2,1)S(1)}, bf16[40,768]{1,0:T(8,128)(2,1)S(1)}, u32[]{:S(2)}, u32[]{:S(2)}) %collective-permute-start.62) | collective-permute-done | bytes 61472 | tf_op jit(solution)/shard_map/ppermute | solution.py:147
  345.4 12.5 %all_gather.35.refs_1_ = bf16[640,768]{1,0:T(8,128)(2,1)S(1)} all-gather(bf16[160,768]{1,0:T(8,128)(2,1)S(1)} %pad_maximum_fusion.7), channel_id=1, replica_groups=mesh['section'=2,'ctx'=4,'heads'=4] {'heads'}, dimensions={0}, use_global_device_ids=true | all-gather | bytes 1228800 | tf_op jit(solution)/shard_map/all_gather | solution.py:159
  359.8 4.9 %shard_map.198 = (bf16[256,192]{1,0:T(8,128)(2,1)S(1)}, f32[3,4,128,128]{3,2,1,0:T(8,128)S(1)}, bf16[256,384]{1,0:T(8,128)(2,1)S(1)}, bf16[256,384]{1,0:T(8,128)...) custom-call(s32[3]{0:T(128)S(1)} %pad_add_fusion.1.refs_0_.place_ref, ...), custom_call_target="tpu_custom_call" | custom-call | flops 503316480 | bytes 3443724 | tf_op jit(solution)/shard_map/pallas_call | solution.py:118
  370.9 4.0 collective-permute-done.69.refs_7_
  376.1 1.9 collective-permute-start.64
  378.8 2.5 collective-permute-start.65
  381.2 2.0 collective-permute-start.66
  385.4 4.1 collective-permute-done.65.refs_4_
  409.6 3.1 collective-permute-done.81.refs_5_
  412.7 2.5 shard_map.210
  416.3 2.1 collective-permute-start.79
  420.7 2.4 collective-permute-done.80.refs_3_
  424.2 1.9 shard_map.207
  427.6 7.0 %shard_map.212 = (f32[768,768]{1,0:T(8,128)}, f32[768,768]{1,0:T(8,128)}, f32[8,128]{1,0:T(8,128)}) custom-call(s32[3]{0:T(128)S(1)} %pad_add_fusion.1.refs_0_.place_ref, bf16[640,768]{1,0:T(8,128)(2,1)S(1)} %all_gather.29.refs_1_.refs_2_, bf16[640,768]{1,0:T(8,128)(2,1)S(1)} %copy-done.3, bf16[640,768]{1,0:T(8,128)(2,1)S(1)} %copy-done.14, ...), custom_call_target="tpu_custom_call" | custom-call | flops 1509949440 | bytes 11014156 | tf_op jit(solution)/shard_map/pallas_call | solution.py:118
  434.7 12.3 %reduce-scatter.2.cloned.1.call-done.refs_0_ = bf16[192,896]{1,0:T(8,128)(2,1)} async-done(((bf16[768,896]{1,0:T(8,128)(2,1)}), bf16[192,896]{1,0:T(8,128)(2,1)}) %reduce-scatter.2.cloned.1.call-update) | async-done | bytes 344080 | tf_op jit(solution)/shard_map/reduce_scatter | solution.py:1138
  (344 shorter events, 126.9 us)
Async XLA Ops:
  7.2 58.1 %all-gather.2.cloned.1.call-start = ((), (), s32[]{:S(2)}) async-start(), calls=%async_computation.1 | async-start | bytes 2949120 | tf_op jit(solution)/shard_map/all_gather | solution.py:159
  11.0 436.0 %reduce-scatter.2.cloned.1.call-start = ((), (), s32[]{:S(2)}) async-start(), calls=%async_computation.2 | async-start | bytes 1720320 | tf_op jit(solution)/shard_map/reduce_scatter | solution.py:1138
  12.4 82.4 %collective-permute-start.14 = (bf16[768,768]{1,0:T(8,128)(2,1)}, bf16[768,768]{1,0:T(8,128)(2,1)}, u32[]{:S(2)}, u32[]{:S(2)}) collective-permute-start(bf16[768,768]{1,0:T(8,128)(2,1)} %bitcast.15.refs_2_.refs_4_.refs_5_), channel_id=1, source_target_pairs={{0,16},{16,0},{1,17},{17,1},{2,18},{18,2},{3,19},{19,3},{4,20},{20... | collective-permute-start | bytes 3538952 | tf_op jit(solution)/shard_map/ppermute | solution.py:147
  12.8 82.0 %collective-permute-start.15 = (bf16[768,768]{1,0:T(8,128)(2,1)}, bf16[768,768]{1,0:T(8,128)(2,1)}, u32[]{:S(2)}, u32[]{:S(2)}) collective-permute-start(bf16[768,768]{1,0:T(8,128)(2,1)} %bitcast.16.refs_4_.refs_6_.refs_7_), channel_id=1, source_target_pairs={{0,16},{16,0},{1,17},{17,1},{2,18},{18,2},{3,19},{19,3},{4,20},{20... | collective-permute-start | bytes 3538952 | tf_op jit(solution)/shard_map/ppermute | solution.py:147
  15.3 35.5 %collective-permute-start.8 = (bf16[1,768]{1,0:T(2,128)(2,1)S(1)}, bf16[1,768]{1,0:T(2,128)(2,1)}, u32[]{:S(2)}, u32[]{:S(2)}) collective-permute-start(bf16[1,768]{1,0:T(2,128)(2,1)S(1)} %copy-done.72), channel_id=1, source_target_pairs={{0,16},{16,0},{1,17},{17,1},{2,18},{18,2},{3,19},{19,3},{4,20},{20... | collective-permute-start | bytes 4616 | tf_op jit(solution)/shard_map/ppermute | solution.py:147
  17.2 36.0 %collective-permute-start.10 = (s32[2,2,256]{2,1,0:T(2,128)}, s32[2,2,256]{2,1,0:T(2,128)S(1)}, u32[]{:S(2)}, u32[]{:S(2)}) collective-permute-start(s32[2,2,256]{2,1,0:T(2,128)} %bitcast.60), channel_id=1, source_target_pairs={{0,16},{16,0},{1,17},{17,1},{2,18},{18,2},{3,19},{19,3},{4,20},{20... | collective-permute-start | bytes 12296 | tf_op jit(solution)/shard_map/ppermute | solution.py:147
  17.4 36.3 %collective-permute-start.9 = (bf16[768,4]{1,0:T(8,128)(2,1)S(1)}, bf16[768,4]{1,0:T(8,128)(2,1)S(1)}, u32[]{:S(2)}, u32[]{:S(2)}) collective-permute-start(bf16[768,4]{1,0:T(8,128)(2,1)S(1)} %bitcast.49), channel_id=1, source_target_pairs={{0,16},{16,0},{1,17},{17,1},{2,18},{18,2},{3,19},{19,3},{4,20},{20... | collective-permute-start | bytes 18440 | tf_op jit(solution)/shard_map/ppermute | solution.py:147
  50.7 8.2 %collective-permute-start.6 = (bf16[256,192]{1,0:T(8,128)(2,1)S(1)}, bf16[256,192]{1,0:T(8,128)(2,1)S(1)}, u32[]{:S(2)}, u32[]{:S(2)}) collective-permute-start(bf16[256,192]{1,0:T(8,128)(2,1)S(1)} %get-tuple-element.150.refs_1_.refs_4_), channel_id=1, source_target_pairs={{0,3},{1,2},{2,1},{3,0},{4,7},{5,6},{6,5},{7,4},{8,11},{9,10},{10,... | collective-permute-start | bytes 294920 | tf_op jit(solution)/shard_map/ppermute | solution.py:147
  53.2 8.3 %collective-permute-start.5 = (bf16[256,192]{1,0:T(8,128)(2,1)S(1)}, bf16[256,192]{1,0:T(8,128)(2,1)S(1)}, u32[]{:S(2)}, u32[]{:S(2)}) collective-permute-start(bf16[256,192]{1,0:T(8,128)(2,1)S(1)} %get-tuple-element.150.refs_1_.refs_4_), channel_id=1, source_target_pairs={{0,2},{1,3},{2,0},{3,1},{4,6},{5,7},{6,4},{7,5},{8,10},{9,11},{10,... | collective-permute-start | bytes 294920 | tf_op jit(solution)/shard_map/ppermute | solution.py:147
  53.7 8.4 %collective-permute-start.4 = (bf16[256,192]{1,0:T(8,128)(2,1)S(1)}, bf16[256,192]{1,0:T(8,128)(2,1)S(1)}, u32[]{:S(2)}, u32[]{:S(2)}) collective-permute-start(bf16[256,192]{1,0:T(8,128)(2,1)S(1)} %get-tuple-element.150.refs_1_.refs_4_), channel_id=1, source_target_pairs={{0,1},{1,0},{2,3},{3,2},{4,5},{5,4},{6,7},{7,6},{8,9},{9,8},{10,11... | collective-permute-start | bytes 294920 | tf_op jit(solution)/shard_map/ppermute | solution.py:147
  59.6 13.4 %collective-permute-start.18 = (s32[2,2,2,256]{3,2,1,0:T(2,128)S(1)}, s32[2,2,2,256]{3,2,1,0:T(2,128)S(1)}, u32[]{:S(2)}, u32[]{:S(2)}) collective-permute-start(s32[2,2,2,256]{3,2,1,0:T(2,128)S(1)} %pad_add_fusion.refs_1_), channel_id=1, source_target_pairs={{0,12},{4,8},{8,4},{12,0},{1,13},{5,9},{9,5},{13,1},{2,14},{6,10},... | collective-permute-start | bytes 24584 | tf_op jit(solution)/shard_map/ppermute | solution.py:147
  62.1 11.0 %collective-permute-start.17 = (s32[2,2,2,256]{3,2,1,0:T(2,128)S(1)}, s32[2,2,2,256]{3,2,1,0:T(2,128)S(1)}, u32[]{:S(2)}, u32[]{:S(2)}) collective-permute-start(s32[2,2,2,256]{3,2,1,0:T(2,128)S(1)} %pad_add_fusion.refs_1_), channel_id=1, source_target_pairs={{0,8},{4,12},{8,0},{12,4},{1,9},{5,13},{9,1},{13,5},{2,10},{6,14},... | collective-permute-start | bytes 24584 | tf_op jit(solution)/shard_map/ppermute | solution.py:147
  62.8 12.7 %collective-permute-start.16 = (s32[2,2,2,256]{3,2,1,0:T(2,128)S(1)}, s32[2,2,2,256]{3,2,1,0:T(2,128)S(1)}, u32[]{:S(2)}, u32[]{:S(2)}) collective-permute-start(s32[2,2,2,256]{3,2,1,0:T(2,128)S(1)} %pad_add_fusion.refs_1_), channel_id=1, source_target_pairs={{0,4},{4,0},{8,12},{12,8},{1,5},{5,1},{9,13},{13,9},{2,6},{6,2},{1... | collective-permute-start | bytes 24584 | tf_op jit(solution)/shard_map/ppermute | solution.py:147
  73.0 8.2 %collective-permute-start.11 = (bf16[40,768]{1,0:T(8,128)(2,1)S(1)}, bf16[40,768]{1,0:T(8,128)(2,1)S(1)}, u32[]{:S(2)}, u32[]{:S(2)}) collective-permute-start(bf16[40,768]{1,0:T(8,128)(2,1)S(1)} %get-tuple-element.156), channel_id=1, source_target_pairs={{0,4},{4,0},{8,12},{12,8},{1,5},{5,1},{9,13},{13,9},{2,6},{6,2},{1... | collective-permute-start | bytes 184328 | tf_op jit(solution)/shard_map/ppermute | solution.py:147
  73.1 8.1 %collective-permute-start.12 = (bf16[40,768]{1,0:T(8,128)(2,1)S(1)}, bf16[40,768]{1,0:T(8,128)(2,1)S(1)}, u32[]{:S(2)}, u32[]{:S(2)}) collective-permute-start(bf16[40,768]{1,0:T(8,128)(2,1)S(1)} %get-tuple-element.157), channel_id=1, source_target_pairs={{0,8},{4,12},{8,0},{12,4},{1,9},{5,13},{9,1},{13,5},{2,10},{6,14},... | collective-permute-start | bytes 184328 | tf_op jit(solution)/shard_map/ppermute | solution.py:147
  75.5 6.0 %collective-permute-start.13 = (bf16[40,768]{1,0:T(8,128)(2,1)S(1)}, bf16[40,768]{1,0:T(8,128)(2,1)S(1)}, u32[]{:S(2)}, u32[]{:S(2)}) collective-permute-start(bf16[40,768]{1,0:T(8,128)(2,1)S(1)} %get-tuple-element.158), channel_id=1, source_target_pairs={{0,12},{4,8},{8,4},{12,0},{1,13},{5,9},{9,5},{13,1},{2,14},{6,10},... | collective-permute-start | bytes 184328 | tf_op jit(solution)/shard_map/ppermute | solution.py:147
  99.3 6.3 %collective-permute-start.19 = (bf16[160,768]{1,0:T(8,128)(2,1)S(1)}, bf16[160,768]{1,0:T(8,128)(2,1)S(1)}, u32[]{:S(2)}, u32[]{:S(2)}) collective-permute-start(bf16[160,768]{1,0:T(8,128)(2,1)S(1)} %get-tuple-element.162), channel_id=1, source_target_pairs={{0,1},{1,0},{2,3},{3,2},{4,5},{5,4},{6,7},{7,6},{8,9},{9,8},{10,11... | collective-permute-start | bytes 737288 | tf_op jit(solution)/shard_map/ppermute | solution.py:147
  100.0 8.8 %collective-permute-start.20 = (bf16[160,768]{1,0:T(8,128)(2,1)S(1)}, bf16[160,768]{1,0:T(8,128)(2,1)S(1)}, u32[]{:S(2)}, u32[]{:S(2)}) collective-permute-start(bf16[160,768]{1,0:T(8,128)(2,1)S(1)} %get-tuple-element.163), channel_id=1, source_target_pairs={{0,2},{1,3},{2,0},{3,1},{4,6},{5,7},{6,4},{7,5},{8,10},{9,11},{10,... | collective-permute-start | bytes 737288 | tf_op jit(solution)/shard_map/ppermute | solution.py:147
  101.4 7.4 %collective-permute-start.21 = (bf16[160,768]{1,0:T(8,128)(2,1)S(1)}, bf16[160,768]{1,0:T(8,128)(2,1)S(1)}, u32[]{:S(2)}, u32[]{:S(2)}) collective-permute-start(bf16[160,768]{1,0:T(8,128)(2,1)S(1)} %get-tuple-element.164), channel_id=1, source_target_pairs={{0,3},{1,2},{2,1},{3,0},{4,7},{5,6},{6,5},{7,4},{8,11},{9,10},{10,... | collective-permute-start | bytes 737288 | tf_op jit(solution)/shard_map/ppermute | solution.py:147
  109.0 8.8 %collective-permute-start.22 = (bf16[40,768]{1,0:T(8,128)(2,1)S(1)}, bf16[40,768]{1,0:T(8,128)(2,1)S(1)}, u32[]{:S(2)}, u32[]{:S(2)}) collective-permute-start(bf16[40,768]{1,0:T(8,128)(2,1)S(1)} %get-tuple-element.166), channel_id=1, source_target_pairs={{0,4},{4,0},{8,12},{12,8},{1,5},{5,1},{9,13},{13,9},{2,6},{6,2},{1... | collective-permute-start | bytes 184328 | tf_op jit(solution)/shard_map/ppermute | solution.py:147
  109.1 10.7 %collective-permute-start.23 = (bf16[40,768]{1,0:T(8,128)(2,1)S(1)}, bf16[40,768]{1,0:T(8,128)(2,1)S(1)}, u32[]{:S(2)}, u32[]{:S(2)}) collective-permute-start(bf16[40,768]{1,0:T(8,128)(2,1)S(1)} %get-tuple-element.167), channel_id=1, source_target_pairs={{0,8},{4,12},{8,0},{12,4},{1,9},{5,13},{9,1},{13,5},{2,10},{6,14},... | collective-permute-start | bytes 184328 | tf_op jit(solution)/shard_map/ppermute | solution.py:147
  111.9 7.8 %collective-permute-start.24 = (bf16[40,768]{1,0:T(8,128)(2,1)S(1)}, bf16[40,768]{1,0:T(8,128)(2,1)S(1)}, u32[]{:S(2)}, u32[]{:S(2)}) collective-permute-start(bf16[40,768]{1,0:T(8,128)(2,1)S(1)} %get-tuple-element.168), channel_id=1, source_target_pairs={{0,12},{4,8},{8,4},{12,0},{1,13},{5,9},{9,5},{13,1},{2,14},{6,10},... | collective-permute-start | bytes 184328 | tf_op jit(solution)/shard_map/ppermute | solution.py:147
  114.9 55.5 %collective-permute-start.25 = (bf16[160,768]{1,0:T(8,128)(2,1)S(1)}, bf16[160,768]{1,0:T(8,128)(2,1)S(1)}, u32[]{:S(2)}, u32[]{:S(2)}) collective-permute-start(bf16[160,768]{1,0:T(8,128)(2,1)S(1)} %get-tuple-element.177), channel_id=1, source_target_pairs={{0,4},{4,0},{8,12},{12,8},{1,5},{5,1},{9,13},{13,9},{2,6},{6,2},{1... | collective-permute-start | bytes 737288 | tf_op jit(solution)/shard_map/ppermute | solution.py:147
  115.0 57.1 %collective-permute-start.26 = (bf16[160,768]{1,0:T(8,128)(2,1)S(1)}, bf16[160,768]{1,0:T(8,128)(2,1)S(1)}, u32[]{:S(2)}, u32[]{:S(2)}) collective-permute-start(bf16[160,768]{1,0:T(8,128)(2,1)S(1)} %get-tuple-element.178), channel_id=1, source_target_pairs={{0,8},{4,12},{8,0},{12,4},{1,9},{5,13},{9,1},{13,5},{2,10},{6,14},... | collective-permute-start | bytes 737288 | tf_op jit(solution)/shard_map/ppermute | solution.py:147
  117.8 54.3 %collective-permute-start.27 = (bf16[160,768]{1,0:T(8,128)(2,1)S(1)}, bf16[160,768]{1,0:T(8,128)(2,1)S(1)}, u32[]{:S(2)}, u32[]{:S(2)}) collective-permute-start(bf16[160,768]{1,0:T(8,128)(2,1)S(1)} %get-tuple-element.179), channel_id=1, source_target_pairs={{0,12},{4,8},{8,4},{12,0},{1,13},{5,9},{9,5},{13,1},{2,14},{6,10},... | collective-permute-start | bytes 737288 | tf_op jit(solution)/shard_map/ppermute | solution.py:147
  154.3 6.0 %collective-permute-start.30 = (bf16[256,192]{1,0:T(8,128)(2,1)S(1)}, bf16[256,192]{1,0:T(8,128)(2,1)S(1)}, u32[]{:S(2)}, u32[]{:S(2)}) collective-permute-start(bf16[256,192]{1,0:T(8,128)(2,1)S(1)} %get-tuple-element.180.refs_1_.refs_4_), channel_id=1, source_target_pairs={{0,3},{1,2},{2,1},{3,0},{4,7},{5,6},{6,5},{7,4},{8,11},{9,10},{10,... | collective-permute-start | bytes 294920 | tf_op jit(solution)/shard_map/ppermute | solution.py:147
  155.8 5.9 %collective-permute-start.29 = (bf16[256,192]{1,0:T(8,128)(2,1)S(1)}, bf16[256,192]{1,0:T(8,128)(2,1)S(1)}, u32[]{:S(2)}, u32[]{:S(2)}) collective-permute-start(bf16[256,192]{1,0:T(8,128)(2,1)S(1)} %get-tuple-element.180.refs_1_.refs_4_), channel_id=1, source_target_pairs={{0,2},{1,3},{2,0},{3,1},{4,6},{5,7},{6,4},{7,5},{8,10},{9,11},{10,... | collective-permute-start | bytes 294920 | tf_op jit(solution)/shard_map/ppermute | solution.py:147
  170.4 6.0 %collective-permute-start.33 = (bf16[40,768]{1,0:T(8,128)(2,1)S(1)}, bf16[40,768]{1,0:T(8,128)(2,1)S(1)}, u32[]{:S(2)}, u32[]{:S(2)}) collective-permute-start(bf16[40,768]{1,0:T(8,128)(2,1)S(1)} %get-tuple-element.186), channel_id=1, source_target_pairs={{0,12},{4,8},{8,4},{12,0},{1,13},{5,9},{9,5},{13,1},{2,14},{6,10},... | collective-permute-start | bytes 184328 | tf_op jit(solution)/shard_map/ppermute | solution.py:147
  201.7 7.5 %collective-permute-start.34 = (bf16[160,768]{1,0:T(8,128)(2,1)S(1)}, bf16[160,768]{1,0:T(8,128)(2,1)S(1)}, u32[]{:S(2)}, u32[]{:S(2)}) collective-permute-start(bf16[160,768]{1,0:T(8,128)(2,1)S(1)} %get-tuple-element.190), channel_id=1, source_target_pairs={{0,1},{1,0},{2,3},{3,2},{4,5},{5,4},{6,7},{7,6},{8,9},{9,8},{10,11... | collective-permute-start | bytes 737288 | tf_op jit(solution)/shard_map/ppermute | solution.py:147
  202.1 8.6 %collective-permute-start.35 = (bf16[160,768]{1,0:T(8,128)(2,1)S(1)}, bf16[160,768]{1,0:T(8,128)(2,1)S(1)}, u32[]{:S(2)}, u32[]{:S(2)}) collective-permute-start(bf16[160,768]{1,0:T(8,128)(2,1)S(1)} %get-tuple-element.191), channel_id=1, source_target_pairs={{0,2},{1,3},{2,0},{3,1},{4,6},{5,7},{6,4},{7,5},{8,10},{9,11},{10,... | collective-permute-start | bytes 737288 | tf_op jit(solution)/shard_map/ppermute | solution.py:147
  203.7 9.1 %collective-permute-start.36 = (bf16[160,768]{1,0:T(8,128)(2,1)S(1)}, bf16[160,768]{1,0:T(8,128)(2,1)S(1)}, u32[]{:S(2)}, u32[]{:S(2)}) collective-permute-start(bf16[160,768]{1,0:T(8,128)(2,1)S(1)} %get-tuple-element.192), channel_id=1, source_target_pairs={{0,3},{1,2},{2,1},{3,0},{4,7},{5,6},{6,5},{7,4},{8,11},{9,10},{10,... | collective-permute-start | bytes 737288 | tf_op jit(solution)/shard_map/ppermute | solution.py:147
  216.7 6.0 %collective-permute-start.39 = (bf16[40,768]{1,0:T(8,128)(2,1)S(1)}, bf16[40,768]{1,0:T(8,128)(2,1)S(1)}, u32[]{:S(2)}, u32[]{:S(2)}) collective-permute-start(bf16[40,768]{1,0:T(8,128)(2,1)S(1)} %get-tuple-element.196), channel_id=1, source_target_pairs={{0,12},{4,8},{8,4},{12,0},{1,13},{5,9},{9,5},{13,1},{2,14},{6,10},... | collective-permute-start | bytes 184328 | tf_op jit(solution)/shard_map/ppermute | solution.py:147
  247.8 6.3 %collective-permute-start.43 = (bf16[160,768]{1,0:T(8,128)(2,1)S(1)}, bf16[160,768]{1,0:T(8,128)(2,1)S(1)}, u32[]{:S(2)}, u32[]{:S(2)}) collective-permute-start(bf16[160,768]{1,0:T(8,128)(2,1)S(1)} %get-tuple-element.207), channel_id=1, source_target_pairs={{0,1},{1,0},{2,3},{3,2},{4,5},{5,4},{6,7},{7,6},{8,9},{9,8},{10,11... | collective-permute-start | bytes 737288 | tf_op jit(solution)/shard_map/ppermute | solution.py:147
  248.9 8.8 %collective-permute-start.44 = (bf16[160,768]{1,0:T(8,128)(2,1)S(1)}, bf16[160,768]{1,0:T(8,128)(2,1)S(1)}, u32[]{:S(2)}, u32[]{:S(2)}) collective-permute-start(bf16[160,768]{1,0:T(8,128)(2,1)S(1)} %get-tuple-element.208), channel_id=1, source_target_pairs={{0,2},{1,3},{2,0},{3,1},{4,6},{5,7},{6,4},{7,5},{8,10},{9,11},{10,... | collective-permute-start | bytes 737288 | tf_op jit(solution)/shard_map/ppermute | solution.py:147
  249.9 7.8 %collective-permute-start.45 = (bf16[160,768]{1,0:T(8,128)(2,1)S(1)}, bf16[160,768]{1,0:T(8,128)(2,1)S(1)}, u32[]{:S(2)}, u32[]{:S(2)}) collective-permute-start(bf16[160,768]{1,0:T(8,128)(2,1)S(1)} %get-tuple-element.209), channel_id=1, source_target_pairs={{0,3},{1,2},{2,1},{3,0},{4,7},{5,6},{6,5},{7,4},{8,11},{9,10},{10,... | collective-permute-start | bytes 737288 | tf_op jit(solution)/shard_map/ppermute | solution.py:147
  251.3 7.3 %collective-permute-start.40 = (bf16[256,384]{1,0:T(8,128)(2,1)S(1)}, bf16[256,384]{1,0:T(8,128)(2,1)S(1)}, u32[]{:S(2)}, u32[]{:S(2)}) collective-permute-start(bf16[256,384]{1,0:T(8,128)(2,1)S(1)} %get-tuple-element.201), channel_id=1, source_target_pairs={{0,4},{4,0},{8,12},{12,8},{1,5},{5,1},{9,13},{13,9},{2,6},{6,2},{1... | collective-permute-start | bytes 589832 | tf_op jit(solution)/shard_map/ppermute | solution.py:147
  251.3 12.1 %collective-permute-start.41 = (bf16[256,384]{1,0:T(8,128)(2,1)S(1)}, bf16[256,384]{1,0:T(8,128)(2,1)S(1)}, u32[]{:S(2)}, u32[]{:S(2)}) collective-permute-start(bf16[256,384]{1,0:T(8,128)(2,1)S(1)} %get-tuple-element.202), channel_id=1, source_target_pairs={{0,8},{4,12},{8,0},{12,4},{1,9},{5,13},{9,1},{13,5},{2,10},{6,14},... | collective-permute-start | bytes 589832 | tf_op jit(solution)/shard_map/ppermute | solution.py:147
  254.0 9.4 %collective-permute-start.42 = (bf16[256,384]{1,0:T(8,128)(2,1)S(1)}, bf16[256,384]{1,0:T(8,128)(2,1)S(1)}, u32[]{:S(2)}, u32[]{:S(2)}) collective-permute-start(bf16[256,384]{1,0:T(8,128)(2,1)S(1)} %get-tuple-element.203), channel_id=1, source_target_pairs={{0,12},{4,8},{8,4},{12,0},{1,13},{5,9},{9,5},{13,1},{2,14},{6,10},... | collective-permute-start | bytes 589832 | tf_op jit(solution)/shard_map/ppermute | solution.py:147
  264.9 7.5 %collective-permute-start.46 = (bf16[64,768]{1,0:T(8,128)(2,1)S(1)}, bf16[64,768]{1,0:T(8,128)(2,1)S(1)}, u32[]{:S(2)}, u32[]{:S(2)}) collective-permute-start(bf16[64,768]{1,0:T(8,128)(2,1)S(1)} %get-tuple-element.212), channel_id=1, source_target_pairs={{0,1},{1,0},{2,3},{3,2},{4,5},{5,4},{6,7},{7,6},{8,9},{9,8},{10,11... | collective-permute-start | bytes 294920 | tf_op jit(solution)/shard_map/ppermute | solution.py:147
  265.1 7.3 %collective-permute-start.47 = (bf16[64,768]{1,0:T(8,128)(2,1)S(1)}, bf16[64,768]{1,0:T(8,128)(2,1)S(1)}, u32[]{:S(2)}, u32[]{:S(2)}) collective-permute-start(bf16[64,768]{1,0:T(8,128)(2,1)S(1)} %get-tuple-element.213), channel_id=1, source_target_pairs={{0,2},{1,3},{2,0},{3,1},{4,6},{5,7},{6,4},{7,5},{8,10},{9,11},{10,... | collective-permute-start | bytes 294920 | tf_op jit(solution)/shard_map/ppermute | solution.py:147
  267.0 5.5 %collective-permute-start.48 = (bf16[64,768]{1,0:T(8,128)(2,1)S(1)}, bf16[64,768]{1,0:T(8,128)(2,1)S(1)}, u32[]{:S(2)}, u32[]{:S(2)}) collective-permute-start(bf16[64,768]{1,0:T(8,128)(2,1)S(1)} %get-tuple-element.214), channel_id=1, source_target_pairs={{0,3},{1,2},{2,1},{3,0},{4,7},{5,6},{6,5},{7,4},{8,11},{9,10},{10,... | collective-permute-start | bytes 294920 | tf_op jit(solution)/shard_map/ppermute | solution.py:147
  268.5 12.8 %collective-permute-start.52 = (bf16[40,768]{1,0:T(8,128)(2,1)S(1)}, bf16[40,768]{1,0:T(8,128)(2,1)S(1)}, u32[]{:S(2)}, u32[]{:S(2)}) collective-permute-start(bf16[40,768]{1,0:T(8,128)(2,1)S(1)} %get-tuple-element.221), channel_id=1, source_target_pairs={{0,4},{4,0},{8,12},{12,8},{1,5},{5,1},{9,13},{13,9},{2,6},{6,2},{1... | collective-permute-start | bytes 184328 | tf_op jit(solution)/shard_map/ppermute | solution.py:147
  272.6 14.7 %collective-permute-start.51 = (bf16[64,768]{1,0:T(8,128)(2,1)S(1)}, bf16[64,768]{1,0:T(8,128)(2,1)S(1)}, u32[]{:S(2)}, u32[]{:S(2)}) collective-permute-start(bf16[64,768]{1,0:T(8,128)(2,1)S(1)} %shard_map.189.refs_1_), channel_id=1, source_target_pairs={{0,3},{1,2},{2,1},{3,0},{4,7},{5,6},{6,5},{7,4},{8,11},{9,10},{10,... | collective-permute-start | bytes 294920 | tf_op jit(solution)/shard_map/ppermute | solution.py:147
  274.1 13.2 %collective-permute-start.50 = (bf16[64,768]{1,0:T(8,128)(2,1)S(1)}, bf16[64,768]{1,0:T(8,128)(2,1)S(1)}, u32[]{:S(2)}, u32[]{:S(2)}) collective-permute-start(bf16[64,768]{1,0:T(8,128)(2,1)S(1)} %shard_map.189.refs_1_), channel_id=1, source_target_pairs={{0,2},{1,3},{2,0},{3,1},{4,6},{5,7},{6,4},{7,5},{8,10},{9,11},{10,... | collective-permute-start | bytes 294920 | tf_op jit(solution)/shard_map/ppermute | solution.py:147
  275.1 12.2 %collective-permute-start.49 = (bf16[64,768]{1,0:T(8,128)(2,1)S(1)}, bf16[64,768]{1,0:T(8,128)(2,1)S(1)}, u32[]{:S(2)}, u32[]{:S(2)}) collective-permute-start(bf16[64,768]{1,0:T(8,128)(2,1)S(1)} %shard_map.189.refs_1_), channel_id=1, source_target_pairs={{0,1},{1,0},{2,3},{3,2},{4,5},{5,4},{6,7},{7,6},{8,9},{9,8},{10,11... | collective-permute-start | bytes 294920 | tf_op jit(solution)/shard_map/ppermute | solution.py:147
  276.2 9.9 %collective-permute-start.53 = (bf16[40,768]{1,0:T(8,128)(2,1)S(1)}, bf16[40,768]{1,0:T(8,128)(2,1)S(1)}, u32[]{:S(2)}, u32[]{:S(2)}) collective-permute-start(bf16[40,768]{1,0:T(8,128)(2,1)S(1)} %get-tuple-element.222), channel_id=1, source_target_pairs={{0,8},{4,12},{8,0},{12,4},{1,9},{5,13},{9,1},{13,5},{2,10},{6,14},... | collective-permute-start | bytes 184328 | tf_op jit(solution)/shard_map/ppermute | solution.py:147
  281.3 6.0 %collective-permute-start.54 = (bf16[40,768]{1,0:T(8,128)(2,1)S(1)}, bf16[40,768]{1,0:T(8,128)(2,1)S(1)}, u32[]{:S(2)}, u32[]{:S(2)}) collective-permute-start(bf16[40,768]{1,0:T(8,128)(2,1)S(1)} %get-tuple-element.223), channel_id=1, source_target_pairs={{0,12},{4,8},{8,4},{12,0},{1,13},{5,9},{9,5},{13,1},{2,14},{6,10},... | collective-permute-start | bytes 184328 | tf_op jit(solution)/shard_map/ppermute | solution.py:147
  292.0 6.1 %collective-permute-start.57 = (bf16[40,768]{1,0:T(8,128)(2,1)S(1)}, bf16[40,768]{1,0:T(8,128)(2,1)S(1)}, u32[]{:S(2)}, u32[]{:S(2)}) collective-permute-start(bf16[40,768]{1,0:T(8,128)(2,1)S(1)} %get-tuple-element.227), channel_id=1, source_target_pairs={{0,12},{4,8},{8,4},{12,0},{1,13},{5,9},{9,5},{13,1},{2,14},{6,10},... | collective-permute-start | bytes 184328 | tf_op jit(solution)/shard_map/ppermute | solution.py:147
  320.2 9.4 %collective-permute-start.58 = (bf16[160,768]{1,0:T(8,128)(2,1)}, bf16[160,768]{1,0:T(8,128)(2,1)S(1)}, u32[]{:S(2)}, u32[]{:S(2)}) collective-permute-start(bf16[160,768]{1,0:T(8,128)(2,1)} %get-tuple-element.232), channel_id=1, source_target_pairs={{0,1},{1,0},{2,3},{3,2},{4,5},{5,4},{6,7},{7,6},{8,9},{9,8},{10,11... | collective-permute-start | bytes 737288 | tf_op jit(solution)/shard_map/ppermute | solution.py:147
  321.3 12.5 %collective-permute-start.59 = (bf16[160,768]{1,0:T(8,128)(2,1)}, bf16[160,768]{1,0:T(8,128)(2,1)S(1)}, u32[]{:S(2)}, u32[]{:S(2)}) collective-permute-start(bf16[160,768]{1,0:T(8,128)(2,1)} %get-tuple-element.233), channel_id=1, source_target_pairs={{0,2},{1,3},{2,0},{3,1},{4,6},{5,7},{6,4},{7,5},{8,10},{9,11},{10,... | collective-permute-start | bytes 737288 | tf_op jit(solution)/shard_map/ppermute | solution.py:147
  322.3 11.5 %collective-permute-start.60 = (bf16[160,768]{1,0:T(8,128)(2,1)}, bf16[160,768]{1,0:T(8,128)(2,1)S(1)}, u32[]{:S(2)}, u32[]{:S(2)}) collective-permute-start(bf16[160,768]{1,0:T(8,128)(2,1)} %get-tuple-element.234), channel_id=1, source_target_pairs={{0,3},{1,2},{2,1},{3,0},{4,7},{5,6},{6,5},{7,4},{8,11},{9,10},{10,... | collective-permute-start | bytes 737288 | tf_op jit(solution)/shard_map/ppermute | solution.py:147
  333.9 6.4 %collective-permute-start.61 = (bf16[40,768]{1,0:T(8,128)(2,1)S(1)}, bf16[40,768]{1,0:T(8,128)(2,1)S(1)}, u32[]{:S(2)}, u32[]{:S(2)}) collective-permute-start(bf16[40,768]{1,0:T(8,128)(2,1)S(1)} %get-tuple-element.241), channel_id=1, source_target_pairs={{0,4},{4,0},{8,12},{12,8},{1,5},{5,1},{9,13},{13,9},{2,6},{6,2},{1... | collective-permute-start | bytes 184328 | tf_op jit(solution)/shard_map/ppermute | solution.py:147
  333.9 11.4 %collective-permute-start.62 = (bf16[40,768]{1,0:T(8,128)(2,1)S(1)}, bf16[40,768]{1,0:T(8,128)(2,1)S(1)}, u32[]{:S(2)}, u32[]{:S(2)}) collective-permute-start(bf16[40,768]{1,0:T(8,128)(2,1)S(1)} %get-tuple-element.242), channel_id=1, source_target_pairs={{0,8},{4,12},{8,0},{12,4},{1,9},{5,13},{9,1},{13,5},{2,10},{6,14},... | collective-permute-start | bytes 184328 | tf_op jit(solution)/shard_map/ppermute | solution.py:147
  336.3 9.0 %collective-permute-start.63 = (bf16[40,768]{1,0:T(8,128)(2,1)S(1)}, bf16[40,768]{1,0:T(8,128)(2,1)S(1)}, u32[]{:S(2)}, u32[]{:S(2)}) collective-permute-start(bf16[40,768]{1,0:T(8,128)(2,1)S(1)} %get-tuple-element.243), channel_id=1, source_target_pairs={{0,12},{4,8},{8,4},{12,0},{1,13},{5,9},{9,5},{13,1},{2,14},{6,10},... | collective-permute-start | bytes 184328 | tf_op jit(solution)/shard_map/ppermute | solution.py:147
  364.7 16.5 %collective-permute-start.72 = (bf16[160,768]{1,0:T(8,128)(2,1)S(1)}, bf16[160,768]{1,0:T(8,128)(2,1)S(1)}, u32[]{:S(2)}, u32[]{:S(2)}) collective-permute-start(bf16[160,768]{1,0:T(8,128)(2,1)S(1)} %shard_map.200.refs_2_), channel_id=1, source_target_pairs={{0,3},{1,2},{2,1},{3,0},{4,7},{5,6},{6,5},{7,4},{8,11},{9,10},{10,... | collective-permute-start | bytes 737288 | tf_op jit(solution)/shard_map/ppermute | solution.py:147
  366.3 17.6 %collective-permute-start.71 = (bf16[160,768]{1,0:T(8,128)(2,1)S(1)}, bf16[160,768]{1,0:T(8,128)(2,1)S(1)}, u32[]{:S(2)}, u32[]{:S(2)}) collective-permute-start(bf16[160,768]{1,0:T(8,128)(2,1)S(1)} %shard_map.200.refs_2_), channel_id=1, source_target_pairs={{0,2},{1,3},{2,0},{3,1},{4,6},{5,7},{6,4},{7,5},{8,10},{9,11},{10,... | collective-permute-start | bytes 737288 | tf_op jit(solution)/shard_map/ppermute | solution.py:147
  367.4 16.5 %collective-permute-start.70 = (bf16[160,768]{1,0:T(8,128)(2,1)S(1)}, bf16[160,768]{1,0:T(8,128)(2,1)S(1)}, u32[]{:S(2)}, u32[]{:S(2)}) collective-permute-start(bf16[160,768]{1,0:T(8,128)(2,1)S(1)} %shard_map.200.refs_2_), channel_id=1, source_target_pairs={{0,1},{1,0},{2,3},{3,2},{4,5},{5,4},{6,7},{7,6},{8,9},{9,8},{10,11... | collective-permute-start | bytes 737288 | tf_op jit(solution)/shard_map/ppermute | solution.py:147
  368.3 6.7 %collective-permute-start.69 = (f32[8,768]{1,0:T(8,128)S(1)}, f32[8,768]{1,0:T(8,128)S(1)}, u32[]{:S(2)}, u32[]{:S(2)}) collective-permute-start(f32[8,768]{1,0:T(8,128)S(1)} %shard_map.196.refs_7_.refs_4_), channel_id=1, source_target_pairs={{0,3},{1,2},{2,1},{3,0},{4,7},{5,6},{6,5},{7,4},{8,11},{9,10},{10,... | collective-permute-start | bytes 73736 | tf_op jit(solution)/shard_map/ppermute | solution.py:147
  369.8 6.3 %collective-permute-start.68 = (f32[8,768]{1,0:T(8,128)S(1)}, f32[8,768]{1,0:T(8,128)S(1)}, u32[]{:S(2)}, u32[]{:S(2)}) collective-permute-start(f32[8,768]{1,0:T(8,128)S(1)} %shard_map.196.refs_7_.refs_4_), channel_id=1, source_target_pairs={{0,2},{1,3},{2,0},{3,1},{4,6},{5,7},{6,4},{7,5},{8,10},{9,11},{10,... | collective-permute-start | bytes 73736 | tf_op jit(solution)/shard_map/ppermute | solution.py:147
  376.1 9.3 %collective-permute-start.64 = (bf16[256,384]{1,0:T(8,128)(2,1)S(1)}, bf16[256,384]{1,0:T(8,128)(2,1)S(1)}, u32[]{:S(2)}, u32[]{:S(2)}) collective-permute-start(bf16[256,384]{1,0:T(8,128)(2,1)S(1)} %get-tuple-element.250), channel_id=1, source_target_pairs={{0,4},{4,0},{8,12},{12,8},{1,5},{5,1},{9,13},{13,9},{2,6},{6,2},{1... | collective-permute-start | bytes 589832 | tf_op jit(solution)/shard_map/ppermute | solution.py:147
  378.8 10.8 %collective-permute-start.65 = (bf16[256,384]{1,0:T(8,128)(2,1)S(1)}, bf16[256,384]{1,0:T(8,128)(2,1)S(1)}, u32[]{:S(2)}, u32[]{:S(2)}) collective-permute-start(bf16[256,384]{1,0:T(8,128)(2,1)S(1)} %get-tuple-element.251), channel_id=1, source_target_pairs={{0,8},{4,12},{8,0},{12,4},{1,9},{5,13},{9,1},{13,5},{2,10},{6,14},... | collective-permute-start | bytes 589832 | tf_op jit(solution)/shard_map/ppermute | solution.py:147
  381.2 8.3 %collective-permute-start.66 = (bf16[256,384]{1,0:T(8,128)(2,1)S(1)}, bf16[256,384]{1,0:T(8,128)(2,1)S(1)}, u32[]{:S(2)}, u32[]{:S(2)}) collective-permute-start(bf16[256,384]{1,0:T(8,128)(2,1)S(1)} %get-tuple-element.252), channel_id=1, source_target_pairs={{0,12},{4,8},{8,4},{12,0},{1,13},{5,9},{9,5},{13,1},{2,14},{6,10},... | collective-permute-start | bytes 589832 | tf_op jit(solution)/shard_map/ppermute | solution.py:147
  398.7 6.0 %collective-permute-start.78 = (bf16[64,768]{1,0:T(8,128)(2,1)S(1)}, bf16[64,768]{1,0:T(8,128)(2,1)S(1)}, u32[]{:S(2)}, u32[]{:S(2)}) collective-permute-start(bf16[64,768]{1,0:T(8,128)(2,1)S(1)} %shard_map.203.refs_1_), channel_id=1, source_target_pairs={{0,3},{1,2},{2,1},{3,0},{4,7},{5,6},{6,5},{7,4},{8,11},{9,10},{10,... | collective-permute-start | bytes 294920 | tf_op jit(solution)/shard_map/ppermute | solution.py:147
  415.2 11.0 %collective-permute-start.82 = (bf16[2,768,768]{2,1,0:T(8,128)(2,1)}, bf16[2,768,768]{2,1,0:T(8,128)(2,1)S(1)}, u32[]{:S(2)}, u32[]{:S(2)}) collective-permute-start(bf16[2,768,768]{2,1,0:T(8,128)(2,1)} %get-tuple-element.280), channel_id=1, source_target_pairs={{0,16},{16,0},{1,17},{17,1},{2,18},{18,2},{3,19},{19,3},{4,20},{20... | collective-permute-start | bytes 7077896 | tf_op jit(solution)/shard_map/ppermute | solution.py:147
  (102 other events, 1305.7 us)
Sparse Core Ops, SparseCore 0:
  11.1 40.0 all-gather.1
  415.3 31.6 reduce-scatter.1

commit v4 on v3

--- a/solution.py
+++ b/solution.py
@@ -114,7 +114,7 @@
 
     size = sum(math.prod(a.shape) * a.dtype.itemsize for a in list(args) + list(outs))
     held = sum(map(padded_bytes, list(args) + list(outs)))
-    held += sum(padded_bytes(s) for s in scratch[: n_own])
+    held += sum(padded_bytes(s) for s in scratch[:n_own])
     return pl.pallas_call(
         wrapped,
         out_shape=outs,
@@ -595,7 +595,7 @@
     return kernel_call(body, [like(per * len(pieces), model)], pieces, after=after)[0]
 
 
-def router_grads(place, pairs, n_experts):
+def router_grads(place, pairs, n_experts, after):
     model = pairs[0][1].shape[1]
 
     def body(place_ref, *refs):
@@ -604,7 +604,7 @@
             refs[-1][layer * n_experts : (layer + 1) * n_experts, :] = grad[:n_experts]
 
     args = [place, *(a for pair in pairs for a in pair)]
-    return kernel_call(body, [like(2 * n_experts, model, dtype=F32)], args)[0]
+    return kernel_call(body, [like(2 * n_experts, model, dtype=F32)], args, after=after)[0]
 
 
 def small_rows(place, layer, dgain_first, dgain_second, router_parts, lanes, n_experts, n_ctx):
@@ -817,34 +817,40 @@
     return [same, bucket_of(half + row - col), bucket_of(2 * half + row - col)]
 
 
-def bias_tables(place, own, other, half, after):
-    heads = own.shape[1]
-
-    def body(place_ref, bias_refs, *refs):
-        buckets = tile_buckets(half)
-        for layer, out_ref in enumerate(refs[-2:]):
-            for head in range(heads):
-                out_ref[head, 0] = jnp.full((half, half), NEGATIVE, F32)
-                values = [jnp.full((half, half), NEGATIVE, F32) for _ in buckets[:2]]
+def bias_table(place, own, other, layer, half, after):
+    heads, strip = own.shape[1], 8
+
+    def body(place_ref, own_ref, other_ref, *refs):
+        out_ref = refs[-1]
+
+        def bias(bucket, head):
+            return jnp.where(place_ref[2] == layer, own_ref[bucket, head], other_ref[bucket, head])
+
+        values = [[bias(bucket, head) for head in range(heads)] for bucket in range(BUCKETS)]
+        same, near, _ = tile_buckets(half)
+        for head in range(heads):
+            out_ref[head, 0] = jnp.full((half, half), NEGATIVE, F32)
+            out_ref[head, 3] = jnp.full((half, half), values[-1][head], F32)
+        for at in range(0, half, strip):
+            for kind, held in ((1, same), (2, near)):
+                held = held[at : at + strip]
+                rows = [jnp.full((strip, half), NEGATIVE, F32) for _ in range(heads)]
                 for bucket in range(BUCKETS):
-                    value = bias_refs[place_ref[2] ^ layer, bucket, head]
-                    values = [
-                        jnp.where(b == bucket, value, v) for b, v in zip(buckets, values)
+                    hit = held == bucket
+                    rows = [
+                        jnp.where(hit, values[bucket][head], rows[head]) for head in range(heads)
                     ]
-                out_ref[head, 1] = values[0]
-                out_ref[head, 2] = values[1]
-                far = bias_refs[place_ref[2] ^ layer, BUCKETS - 1, head]
-                out_ref[head, 3] = jnp.full((half, half), far, F32)
-
-    shape = like(heads, 4, half, half, dtype=F32)
+                for head in range(heads):
+                    out_ref[head, kind, at : at + strip] = rows[head]
+
     return pl.pallas_call(
         body,
-        out_shape=[shape] * 2,
-        in_specs=[pl.BlockSpec(memory_space=pltpu.SMEM)] * 2
+        out_shape=like(heads, 4, half, half, dtype=F32),
+        in_specs=[pl.BlockSpec(memory_space=pltpu.SMEM)] * 3
         + [pl.BlockSpec(memory_space=pl.ANY)] * len(after),
-        out_specs=[pl.BlockSpec(memory_space=pltpu.VMEM)] * 2,
+        out_specs=pl.BlockSpec(memory_space=pltpu.VMEM),
         compiler_params=pltpu.CompilerParams(vmem_limit_bytes=2 * SPARE_BYTES),
-    )(place, jnp.stack([own, other]), *after)
+    )(place, own, other, *after)
 
 
 def small_weights(place, gains, routers, after):
@@ -873,9 +879,9 @@
     return outs[0:2], outs[2:4], outs[4:6]
 
 
-def layer_row(place_ref, pair_ref, layer, k):
-    rows = pair_ref.shape[3]
-    row = pair_ref[place_ref[2] ^ layer, place_ref[2], k : k + 1, :]
+def layer_row(place_ref, own, other, layer, k):
+    rows = own.shape[1]
+    row = jnp.where(place_ref[2] == layer, own[k : k + 1], other[k : k + 1])
     eye = lax.broadcasted_iota(jnp.int32, (rows, rows), 0) == lax.broadcasted_iota(
         jnp.int32, (rows, rows), 1
     )
@@ -892,13 +898,16 @@
     return sum([(rank >= h * per).astype(jnp.int32) for h in range(1, n_heads)])
 
 
-def token_slots(place, pair, n_experts, per, n_heads, after):
-    rows = pair.shape[3]
-
-    def body(place_ref, pair_ref, *refs):
-        outs = refs[-3:]
+def token_slots(place, own, other, n_experts, per, n_heads, after):
+    rows = own.shape[2]
+
+    def body(place_ref, own_ref, other_ref, *refs):
+        *outs, pair_ref = refs[-4:]
+        pair_ref[0] = own_ref[...]
+        pair_ref[1] = other_ref[...]
+        own, other = own_ref[place_ref[2]], other_ref[place_ref[2]]
         for layer in range(2):
-            choices = [layer_row(place_ref, pair_ref, layer, k) for k in range(2)]
+            choices = [layer_row(place_ref, own, other, layer, k) for k in range(2)]
             lane = lax.broadcasted_iota(jnp.int32, (rows, LANES), 1)
             hots = [jnp.where(lane == choice, 1.0, 0.0) for choice in choices]
             ranks = dot(earlier(rows), (hots[0] + hots[1]).astype(BF16))
@@ -911,7 +920,10 @@
                     outs[2][:, k : k + 1] = (quarter ^ place_ref[1]) * (n_experts * per) + inner
 
     return kernel_call(
-        body, [like(rows, 2, dtype=jnp.int32)] * 3, [place, pair], after=after
+        body,
+        [like(rows, 2, dtype=jnp.int32)] * 3 + [like(2, *own.shape, dtype=jnp.int32)],
+        [place, own, other],
+        after=after,
     )
 
 
@@ -919,22 +931,26 @@
     n_ctx, rows = len(pairs), pairs[0].shape[3]
 
     def body(place_ref, *refs):
-        before = earlier(rows)
-        lane = lax.broadcasted_iota(jnp.int32, (rows, per), 1)
-        for layer, out_ref in enumerate(refs[n_ctx:]):
-            for r, pair_ref in enumerate(refs[:n_ctx]):
-                one, two = (layer_row(place_ref, pair_ref, layer, k) for k in range(2))
+        lane = lax.broadcasted_iota(jnp.int32, (rows, LANES), 1)
+        slot = lax.broadcasted_iota(jnp.int32, (rows, n_heads * per), 1)
+        found, heres = [], jnp.zeros((rows, LANES), F32)
+        for layer in range(2):
+            for r in range(n_ctx):
+                pair = [refs[r][i, place_ref[2]] for i in range(2)]
+                one, two = (layer_row(place_ref, *pair, layer, k) for k in range(2))
                 here = (one == place_ref[0]) | (two == place_ref[0])
                 other = jnp.where(one == place_ref[0], two, one).astype(F32)
-                other = jnp.broadcast_to(other, (rows, LANES)).astype(BF16)
-                wide = jnp.broadcast_to(jnp.where(here, 1.0, 0.0), (rows, LANES)).astype(BF16)
-                rank = dot(before, wide)[:, 0:1].astype(jnp.int32)
-                rank = jnp.where(here, rank, -1)
-                for h in range(n_heads):
-                    picks = jnp.where(lane + h * per == rank, 1.0, 0.0).astype(BF16)
-                    found = dot_tn(picks, other)[:, 0:1].astype(jnp.int32)
-                    at = (h * n_ctx + r) * per
-                    out_ref[at : at + per, :] = found
+                heres += jnp.where(here & (lane == layer * n_ctx + r), 1.0, 0.0)
+                found.append((here, other))
+        ranks = dot(earlier(rows), heres.astype(BF16)).astype(jnp.int32)
+        for number, (here, other) in enumerate(found):
+            layer, r = number // n_ctx, number % n_ctx
+            picks = jnp.where(here & (slot == ranks[:, number : number + 1]), 1.0, 0.0)
+            other = jnp.broadcast_to(other, (rows, LANES)).astype(BF16)
+            column = dot_tn(picks.astype(BF16), other)[:, 0:1].astype(jnp.int32)
+            for h in range(n_heads):
+                at = (h * n_ctx + r) * per
+                refs[n_ctx + layer][at : at + per, :] = column[h * per : (h + 1) * per]
 
     return kernel_call(
         body, [like(n_heads * n_ctx * per, 1, dtype=jnp.int32)] * 2, [place, *pairs]
@@ -973,8 +989,8 @@
     return kernel_call(body, [like(per, model)] * n_ctx, parts, after=after)
 
 
-def return_rows(chunks, n_ctx, after=()):
-    back = exchange(heads_sum(chunks, n_ctx, after), "ctx")
+def return_rows(chunks, n_ctx):
+    back = exchange(heads_sum(chunks, n_ctx), "ctx")
     return gather_rows(jnp.concatenate(back, axis=0), "heads")
 
 
@@ -1011,38 +1027,43 @@
     def with_other(own):
         return own, swap(own, "section")
 
+    qkv = by_layer(*with_other(qkv_weight[0]))
     given = swap(lax.dynamic_index_in_dim(boundary[0], 1 - section, 0, False), "section")
     gain_pairs = with_other(norm_first), with_other(norm_second)
-    qkv = by_layer(*with_other(qkv_weight[0]))
-    x0, cotangent, normed0, q0, kv0 = begin(place, boundary[0], given, *gain_pairs[0], qkv[0])
+    x0, cotangent, normed0, q0, kv0 = begin(
+        place, boundary[0], given, *gain_pairs[0], qkv[0]
+    )
     kv_all0 = gather_rows(kv0, "ctx")
 
-    gains_first, gains_second, routers = small_weights(
-        place, gain_pairs, with_other(router[0]), [kv0]
-    )
-    biases = bias_tables(place, *with_other(position_bias[0]), half, [kv0])
-    pair = jnp.stack(with_other(routes[0].transpose(0, 2, 1)))
-    *tokens, tokens_near = token_slots(place, pair, n_experts, per, n_heads, [kv0])
-    others = other_experts(place, exchange([pair] * n_ctx, "ctx"), per, n_heads)
+    bias_pair = with_other(position_bias[0])
+    bias0 = bias_table(place, *bias_pair, 0, half, [kv0])
     up = by_layer(*with_other(expert_up[0, 0]))
     down = by_layer(*with_other(expert_down[0, 0]))
     width = out_weight.shape[1]
     out_gathered = gather_rows(jnp.concatenate(with_other(out_weight[0]), axis=0), "heads")
     out_full = [Rows(out_gathered, layer, width) for layer in range(2)]
     out_own = [Rows(out_gathered, layer, width, own=True) for layer in range(2)]
-
-    def before_experts(layer, x, q, kv_all):
-        mix, lse = attend(place, q, [kv_all], biases[layer], n_ctx)
+    mix0, lse0 = attend(place, q0, [kv_all0], bias0, n_ctx)
+    gains_first, gains_second, routers = small_weights(
+        place, gain_pairs, with_other(router[0]), [lse0]
+    )
+    *tokens, tokens_near, pair = token_slots(
+        place, *with_other(routes[0].transpose(0, 2, 1)), n_experts, per, n_heads, [lse0]
+    )
+    pairs = exchange([pair] * n_ctx, "ctx")
+    others = other_experts(place, pairs, per, n_heads)
+
+    def before_experts(layer, x, mix):
         mixes = exchange([mix] * n_heads, "heads")
         middle, chunks = finish_attention(
             place, mixes, out_full[layer], x, gains_second[layer], tokens[layer], n_ctx, per
         )
-        return mix, lse, middle, send_rows(chunks)
+        return middle, send_rows(chunks)
 
     def expert_weights(layer):
         return up[layer], down[layer], routers[layer], others[layer]
 
-    mix0, lse0, middle0, arrived0 = before_experts(0, x0, q0, kv_all0)
+    middle0, arrived0 = before_experts(0, x0, mix0)
     chunks, kept0 = experts(place, arrived0, *expert_weights(0), n_heads)
     dout_chunks = dispatch_whole(place, cotangent, tokens[1], n_ctx, per, n_heads, [middle0])
     returned = return_rows(chunks, n_ctx)
@@ -1051,7 +1072,9 @@
     )
 
     kv_all1 = gather_rows(kv1, "ctx")
-    mix1, lse1, middle1, arrived1 = before_experts(1, x1, q1, kv_all1)
+    bias1 = bias_table(place, *bias_pair, 1, half, [middle0])
+    mix1, lse1 = attend(place, q1, [kv_all1], bias1, n_ctx)
+    middle1, arrived1 = before_experts(1, x1, mix1)
     dout_rows1 = jnp.stack(exchange(dout_chunks, "ctx"))
     dout_rows1 = dout_rows1.reshape(n_ctx, n_heads, per, model).transpose(1, 0, 2, 3)
     dout_rows1 = dout_rows1.reshape(-1, model)
@@ -1061,16 +1084,14 @@
     dmiddle1, datt1, dmix1, dgain_second1 = middle_back(
         place, return_rows(chunks, n_ctx), tokens[1], middle1, gains_second[1], cotangent, out_own[1]
     )
-    dq1, dtable1, dkv1 = attend_back(place, q1, [kv_all1], biases[1], lse1, dmix1, n_ctx)
+    dq1, dtable1, dkv1 = attend_back(place, q1, [kv_all1], bias1, lse1, dmix1, n_ctx)
+    dkv_parts1 = exchange(dkv1, "ctx")
     out_total = heads_sum(
-        experts_out(place, hidden1, margin1, down[1], n_heads, [dq1]), n_ctx
-    )
-    dkv_sum1, chunks = project_back(
-        place, dq1, exchange(dkv1, "ctx"), qkv[1], n_heads, [out_total[0]]
-    )
+        experts_out(place, hidden1, margin1, down[1], n_heads, dkv_parts1[1:2]), n_ctx
+    )
+    dkv_sum1, chunks = project_back(place, dq1, dkv_parts1, qkv[1], n_heads)
     total1 = share_sum(exchange(chunks, "heads"))
     lanes1 = table_back(dtable1)
-    out_back = exchange(out_total, "ctx")
     dense1, made = dense_grad(place, [(normed1, dq1), (datt1, mix1), (normed1, dkv_sum1)])
     dx1, dgain_first1, sent = input_back(
         place,
@@ -1081,18 +1102,25 @@
         tokens[0],
         n_ctx,
         per,
-        [lanes1, made, *out_back[1:]],
+        [lanes1, made],
     )
 
     dout_rows0 = send_rows(sent)
     chunks, (dpre0, dslots0, dlogits0) = experts_back(
-        place, dout_rows0, kept0, arrived0, *expert_weights(0), n_heads
+        place, dout_rows0, kept0, arrived0, *expert_weights(0), n_heads, out_total[:1]
     )
     lists = [(arrived0, arrived1), (dpre0, dpre1), (kept0[1], hidden1), (dslots0, dslots1)]
     mine, theirs = [Pick(a, b) for a, b in lists], [Pick(b, a) for a, b in lists]
     sends, sends_made = expert_grads(place, [theirs[:2], theirs[2:]])
-    returned = return_rows(chunks, n_ctx, [sends_made])
-    router_part = router_grads(place, [(dlogits0, arrived0), (dlogits1, arrived1)], n_experts)
+    back = heads_sum(chunks, n_ctx, [sends_made])
+    returned = gather_rows(jnp.concatenate(exchange(back, "ctx"), axis=0), "heads")
+    router_part = router_grads(
+        place, [(dlogits0, arrived0), (dlogits1, arrived1)], n_experts, back[:1]
+    )
+    router_parts = exchange([router_part] * n_heads, "heads")
+    small1 = small_rows(
+        place, 1, dgain_first1, dgain_second1, router_parts, lanes1, n_experts, n_ctx
+    )
     dmiddle0, datt0, dmix0, dgain_second0 = middle_back(
         place,
         returned,
@@ -1101,27 +1129,20 @@
         gains_second[0],
         dx1,
         out_own[0],
-        [router_part],
-    )
-    dq0, dtable0, dkv0 = attend_back(place, q0, [kv_all0], biases[0], lse0, dmix0, n_ctx)
+        [small1],
+    )
+    dq0, dtable0, dkv0 = attend_back(place, q0, [kv_all0], bias0, lse0, dmix0, n_ctx)
     lanes0 = table_back(dtable0)
-    router_parts = exchange([router_part] * n_heads, "heads")
-    small1 = small_rows(
-        place, 1, dgain_first1, dgain_second1, router_parts, lanes1, n_experts, n_ctx
-    )
-    quarter = join_quarter(out_back, [dq0])
-    out, out_made = combine(middle1, exchange([quarter] * n_heads, "heads"), tokens_near, [])
-    dkv_sum0, chunks = project_back(
-        place, dq0, exchange(dkv0, "ctx"), qkv[0], n_heads, [small1, out_made]
-    )
+    dkv_sum0, chunks = project_back(place, dq0, exchange(dkv0, "ctx"), qkv[0], n_heads)
     parts = exchange(chunks, "heads")
     total0 = share_sum(parts)
     dense0, made = dense_grad(
         place, [(normed0, dq0), (datt0, mix0), (normed0, dkv_sum0)], parts[1:2]
     )
+    near = exchange([total0] * n_heads, "heads")
     dx0, dgain_first0, _ = input_back(
         place,
-        exchange([total0] * n_heads, "heads"),
+        near,
         x0,
         gains_first[0],
         dmiddle0,
@@ -1136,9 +1157,12 @@
     got = swap(joint_send(place, Pick(dense1, dense0), smalls), "section")
     joint = joint_sum(place, Pick(dense0, dense1), smalls, got)
     joint = lax.psum_scatter(joint, "ctx", scatter_dimension=0, tiled=True)
-    grad_up, grad_down, _ = expert_grads(
+    out_back = exchange(out_total, "ctx")
+    quarter = join_quarter(out_back, ())
+    grad_up, grad_down, made = expert_grads(
         place, [mine[:2], mine[2:]], swap(sends, "section"), after=[dgain_first0]
     )
+    out, _ = combine(middle1, exchange([quarter] * n_heads, "heads"), tokens_near, [made])
     grad_qkv, grad_out, grad_first, grad_second, grad_router, grad_bias = joint_split(
         joint, width, n_experts
     )

time: 462 us -> 454 us (0.983)
  the two profiles are of different devices: /device:TPU:0 before, /device:TPU:9 now
where the time goes in v4:
time: 454 us; the launch traced here: 446 us
  starting transfers between devices  117 us (26%)
  blocking collectives  103 us (23%)
  Pallas kernels  93.7 us (21%)
  waiting for transfers between devices  80.6 us (18%)
  local copies, waits for them, and re-layouts  32.7 us (7%)
  between operations  15.6 us (3%)
    ppermute x81, starting transfers between devices, swap(): return lax.ppermute(array, axis, [(i, i ^ by) for i in range(devices)])  109 us
    all_gather x8, blocking collectives, gather_rows(): return lax.all_gather(array, axis, axis=0, tiled=True)  103 us
    pallas_call x43, Pallas kernels, kernel_call(): pl.pallas_call(wrapped, out_shape=outs, in_specs=in_specs, out_specs=[pl....  90 us
    ppermute x81, waiting for transfers between devices, swap(): return lax.ppermute(array, axis, [(i, i ^ by) for i in range(devices)])  77.7 us
    unnamed x170, local copies, waits for them, and re-layouts  30.3 us
  transfers between devices with their start and end apart: 85, of which 37 were waited for; matrix products, arithmetic and copies ran while one was open for 1% of the time, Pallas kernels for 12%

profile of v4, /device:TPU:9, one launch (start us, length us, event | category | flops | bytes accessed | tf_op | source)
XLA Modules:
  0.0 445.8 jit_solution(5571884411376847992)
XLA Ops:
  9.4 1.8 pad_maximum_fusion.1
  16.9 2.1 shard_map.169
  21.7 1.9 shard_map.170.refs_3_
  23.6 17.2 %all_gather.27.refs_2_ = bf16[1024,384]{1,0:T(8,128)(2,1)S(1)} all-gather(bf16[256,384]{1,0:T(8,128)(2,1)S(1)} %get-tuple-element.146.refs_0_), channel_id=1, replica_groups=mesh['section'=2,'ctx'=4,'heads'=4] {'ctx'}, dimensions={0}, use_global_device_ids=true | all-gather | bytes 983040 | tf_op jit(solution)/shard_map/all_gather | solution.py:159
  40.8 3.0 shard_map.171
  57.4 1.7 copy-done
  62.7 2.4 shard_map.174
  65.1 2.3 collective-permute-start.11
  68.7 2.5 shard_map.175
  72.0 10.5 %all_gather.29.refs_1_.refs_2_ = bf16[640,768]{1,0:T(8,128)(2,1)S(1)} all-gather(bf16[160,768]{1,0:T(8,128)(2,1)S(1)} %pad_maximum_fusion.2), channel_id=1, replica_groups=mesh['section'=2,'ctx'=4,'heads'=4] {'heads'}, dimensions={0}, use_global_device_ids=true | all-gather | bytes 1228800 | tf_op jit(solution)/shard_map/all_gather | solution.py:159
  82.5 4.5 %shard_map.176 = (bf16[160,768]{1,0:T(8,128)(2,1)S(1)}, bf16[160,768]{1,0:T(8,128)(2,1)S(1)}, bf16[160,768]{1,0:T(8,128)(2,1)S(1)}, bf16[160,768]{1,0:T(8,128)(2...) custom-call(s32[3]{0:T(128)S(1)} %pad_add_fusion.refs_0_.place_ref, ...), custom_call_target="tpu_custom_call" | custom-call | flops 1509949440 | bytes 7476236 | tf_op jit(solution)/shard_map/pallas_call | solution.py:118
  89.7 2.4 collective-permute-done.19.refs_1_
  92.1 3.8 collective-permute-done.20.refs_2_
  96.0 3.3 collective-permute-start.22
  102.1 2.4 collective-permute-start.25
  104.5 1.9 shard_map.179.refs_3_
  107.7 9.1 %all_gather.30.refs_2_ = bf16[640,768]{1,0:T(8,128)(2,1)S(1)} all-gather(bf16[160,768]{1,0:T(8,128)(2,1)S(1)} %pad_maximum_fusion.3), channel_id=1, replica_groups=mesh['section'=2,'ctx'=4,'heads'=4] {'heads'}, dimensions={0}, use_global_device_ids=true | all-gather | bytes 1228800 | tf_op jit(solution)/shard_map/all_gather | solution.py:159
  116.7 2.2 shard_map.178
  119.0 19.3 %all_gather.31.refs_2_ = bf16[1024,384]{1,0:T(8,128)(2,1)S(1)} all-gather(bf16[256,384]{1,0:T(8,128)(2,1)S(1)} %get-tuple-element.170), channel_id=1, replica_groups=mesh['section'=2,'ctx'=4,'heads'=4] {'ctx'}, dimensions={0}, use_global_device_ids=true | all-gather | bytes 983040 | tf_op jit(solution)/shard_map/all_gather | solution.py:159
  138.3 2.9 shard_map.180
  142.7 2.6 collective-permute-done.28.refs_2_
  146.5 3.5 collective-permute-done.30.refs_4_
  150.1 2.4 shard_map.182
  152.7 1.8 collective-permute-start.32
  158.1 9.0 %all_gather.32.refs_2_.refs_1_.refs_4_ = bf16[640,768]{1,0:T(8,128)(2,1)S(1)} all-gather(bf16[160,768]{1,0:T(8,128)(2,1)S(1)} %pad_maximum_fusion.4), channel_id=1, replica_groups=mesh['section'=2,'ctx'=4,'heads'=4] {'heads'}, dimensions={0}, use_global_device_ids=true | all-gather | bytes 1228800 | tf_op jit(solution)/shard_map/all_gather | solution.py:159
  167.2 8.0 %shard_map.183 = (bf16[160,768]{1,0:T(8,128)(2,1)S(1)}, bf16[160,768]{1,0:T(8,128)(2,1)S(1)}, bf16[160,768]{1,0:T(8,128)(2,1)S(1)}, bf16[160,768]{1,0:T(8,128)(2...) custom-call(s32[3]{0:T(128)S(1)} %pad_add_fusion.refs_0_.place_ref, ...), custom_call_target="tpu_custom_call" | custom-call | flops 1509949440 | bytes 8623116 | tf_op jit(solution)/shard_map/pallas_call | solution.py:118
  178.9 5.2 %collective-permute-done.34.refs_1_ = bf16[160,768]{1,0:T(8,128)(2,1)S(1)} collective-permute-done((bf16[160,768]{1,0:T(8,128)(2,1)S(1)}, bf16[160,768]{1,0:T(8,128)(2,1)S(1)}, u32[]{:S(2)}, u32[]{:S(2)}) %collective-permute-start.34) | collective-permute-done | bytes 245792 | tf_op jit(solution)/shard_map/ppermute | solution.py:147
  184.2 3.3 collective-permute-done.36.refs_3_
  187.6 2.7 collective-permute-start.37
  191.9 2.5 collective-permute-done.38
  195.1 12.5 %all_gather.33.refs_1_ = bf16[640,768]{1,0:T(8,128)(2,1)S(1)} all-gather(bf16[160,768]{1,0:T(8,128)(2,1)S(1)} %pad_maximum_fusion.5), channel_id=1, replica_groups=mesh['section'=2,'ctx'=4,'heads'=4] {'heads'}, dimensions={0}, use_global_device_ids=true | all-gather | bytes 1228800 | tf_op jit(solution)/shard_map/all_gather | solution.py:159
  207.6 1.8 shard_map.185
  209.5 4.9 %shard_map.186 = (bf16[256,192]{1,0:T(8,128)(2,1)S(1)}, f32[3,4,128,128]{3,2,1,0:T(8,128)S(1)}, bf16[256,384]{1,0:T(8,128)(2,1)S(1)}, bf16[256,384]{1,0:T(8,128)...) custom-call(s32[3]{0:T(128)S(1)} %pad_add_fusion.refs_0_.place_ref, ...), custom_call_target="tpu_custom_call" | custom-call | flops 503316480 | bytes 3443724 | tf_op jit(solution)/shard_map/pallas_call | solution.py:118
  215.9 1.9 collective-permute-start.41
  218.0 1.6 collective-permute-done.40.refs_3_.refs_5_
  219.6 5.1 %collective-permute-done.41.refs_4_ = bf16[256,384]{1,0:T(8,128)(2,1)S(1)} collective-permute-done((bf16[256,384]{1,0:T(8,128)(2,1)S(1)}, bf16[256,384]{1,0:T(8,128)(2,1)S(1)}, u32[]{:S(2)}, u32[]{:S(2)}) %collective-permute-start.41) | collective-permute-done | bytes 196640 | tf_op jit(solution)/shard_map/ppermute | solution.py:147
  224.7 3.0 collective-permute-done.42.refs_5_
  227.7 1.6 shard_map.187
  232.1 2.8 shard_map.192
  239.2 2.1 collective-permute-done.46.refs_2_
  246.3 1.7 shard_map.191
  248.8 2.2 collective-permute-start.50
  253.3 2.0 collective-permute-done.51
  255.3 12.6 %all_gather.34.refs_1_ = bf16[640,768]{1,0:T(8,128)(2,1)S(1)} all-gather(bf16[160,768]{1,0:T(8,128)(2,1)S(1)} %pad_maximum_fusion.6), channel_id=1, replica_groups=mesh['section'=2,'ctx'=4,'heads'=4] {'heads'}, dimensions={0}, use_global_device_ids=true | all-gather | bytes 1228800 | tf_op jit(solution)/shard_map/all_gather | solution.py:159
  267.9 7.4 %shard_map.194 = (bf16[160,768]{1,0:T(8,128)(2,1)S(1)}, bf16[160,768]{1,0:T(8,128)(2,1)}, bf16[160,768]{1,0:T(8,128)(2,1)}, bf16[160,768]{1,0:T(8,128)(2,1)}, bf...) custom-call(s32[3]{0:T(128)S(1)} %pad_add_fusion.refs_0_.place_ref, ...), custom_call_target="tpu_custom_call" | custom-call | flops 1509949440 | bytes 9606156 | tf_op jit(solution)/shard_map/pallas_call | solution.py:118
  283.0 6.1 %shard_map.195 = (bf16[2,768,768]{2,1,0:T(8,128)(2,1)}, f32[8,128]{1,0:T(8,128)S(1)}) custom-call(s32[3]{0:T(128)S(1)} %pad_add_fusion.refs_0_.place_ref, bf16[640,768]{1,0:T(8,128)(2,1)S(1)} %all_gather.32.refs_2_.refs_1_.refs_4_, bf16[640,768]{1,0:T(8,128)(2,1)S(1)} %all_gather.29.refs_1_.refs_2_, bf16[640,768]{1,0:T(8,128)(2,1)S(1)} %copy-done.16, ...), custom_call_target="tpu_custom_call" | custom-call | flops 1509949440 | bytes 6295564 | tf_op jit(solution)/shard_map/pallas_call | solution.py:118
  289.3 4.7 %collective-permute-start.58 = (bf16[40,768]{1,0:T(8,128)(2,1)S(1)}, bf16[40,768]{1,0:T(8,128)(2,1)S(1)}, u32[]{:S(2)}, u32[]{:S(2)}) collective-permute-start(bf16[40,768]{1,0:T(8,128)(2,1)S(1)} %get-tuple-element.236), channel_id=1, source_target_pairs={{0,4},{4,0},{8,12},{12,8},{1,5},{5,1},{9,13},{13,9},{2,6},{6,2},{1... | collective-permute-start | bytes 184328 | tf_op jit(solution)/shard_map/ppermute | solution.py:147
  300.3 2.4 collective-permute-done.63.refs_7_
  303.4 13.4 %all_gather.35.refs_1_ = bf16[640,768]{1,0:T(8,128)(2,1)S(1)} all-gather(bf16[160,768]{1,0:T(8,128)(2,1)S(1)} %pad_maximum_fusion.7), channel_id=1, replica_groups=mesh['section'=2,'ctx'=4,'heads'=4] {'heads'}, dimensions={0}, use_global_device_ids=true | all-gather | bytes 1228800 | tf_op jit(solution)/shard_map/all_gather | solution.py:159
  316.8 1.8 shard_map.199
  318.7 4.8 %shard_map.200 = (bf16[256,192]{1,0:T(8,128)(2,1)S(1)}, f32[3,4,128,128]{3,2,1,0:T(8,128)S(1)}, bf16[256,384]{1,0:T(8,128)(2,1)S(1)}, bf16[256,384]{1,0:T(8,128)...) custom-call(s32[3]{0:T(128)S(1)} %pad_add_fusion.refs_0_.place_ref, ...), custom_call_target="tpu_custom_call" | custom-call | flops 503316480 | bytes 3443724 | tf_op jit(solution)/shard_map/pallas_call | solution.py:118
  323.5 3.5 collective-permute-start.64
  328.4 3.1 collective-permute-done.64.refs_3_
  331.5 3.5 collective-permute-done.65.refs_4_
  335.1 3.0 collective-permute-done.66.refs_5_
  342.3 2.1 collective-permute-done.67.refs_1_.refs_7_
  356.4 31.4 %collective-permute-start.82 = (bf16[768,896]{1,0:T(8,128)(2,1)S(1)}, bf16[768,896]{1,0:T(8,128)(2,1)S(1)}, u32[]{:S(2)}, u32[]{:S(2)}) collective-permute-start(bf16[768,896]{1,0:T(8,128)(2,1)S(1)} %shard_map.211), channel_id=1, source_target_pairs={{0,16},{16,0},{1,17},{17,1},{2,18},{18,2},{3,19},{19,3},{4,20},{20... | collective-permute-start | bytes 4128776 | tf_op jit(solution)/shard_map/ppermute | solution.py:147
  387.9 3.9 collective-permute-done.82.refs_5_
  399.7 8.2 %collective-permute-done.75.refs_3_ = bf16[40,768]{1,0:T(8,128)(2,1)S(1)} collective-permute-done((bf16[40,768]{1,0:T(8,128)(2,1)S(1)}, bf16[40,768]{1,0:T(8,128)(2,1)S(1)}, u32[]{:S(2)}, u32[]{:S(2)}) %collective-permute-start.75) | collective-permute-done | bytes 61472 | tf_op jit(solution)/shard_map/ppermute | solution.py:147
  408.5 2.2 collective-permute-start.78
  410.7 6.7 %collective-permute-start.81 = (f32[256,768]{1,0:T(8,128)}, f32[256,768]{1,0:T(8,128)S(1)}, u32[]{:S(2)}, u32[]{:S(2)}) collective-permute-start(f32[256,768]{1,0:T(8,128)} %copy-done.37), channel_id=1, source_target_pairs={{16,0},{17,1},{18,2},{19,3},{20,4},{21,5},{22,6},{23,7},{24,8},{25... | collective-permute-start | bytes 2359304 | tf_op jit(solution)/shard_map/ppermute | solution.py:151
  421.0 7.1 %shard_map.207 = (f32[768,768]{1,0:T(8,128)}, f32[768,768]{1,0:T(8,128)}, f32[8,128]{1,0:T(8,128)S(1)}) custom-call(s32[3]{0:T(128)S(1)} %pad_add_fusion.refs_0_.place_ref, bf16[640,768]{1,0:T(8,128)(2,1)S(1)} %all_gather.29.refs_1_.refs_2_, bf16[640,768]{1,0:T(8,128)(2,1)S(1)} %copy-done.3, bf16[640,768]{1,0:T(8,128)(2,1)S(1)} %copy-done.21, ...), custom_call_target="tpu_custom_call" | custom-call | flops 1509949440 | bytes 11014156 | tf_op jit(solution)/shard_map/pallas_call | solution.py:118
  430.2 2.9 collective-permute-done.80.refs_2_
  433.0 1.9 shard_map.209
  (345 shorter events, 116.2 us)
Async XLA Ops:
  7.2 50.2 %all-gather.2.cloned.1.call-start = ((), (), s32[]{:S(2)}) async-start(), calls=%async_computation.1 | async-start | bytes 2949120 | tf_op jit(solution)/shard_map/all_gather | solution.py:159
  11.3 423.8 %reduce-scatter.2.cloned.1.call-start = ((), (), s32[]{:S(2)}) async-start(), calls=%async_computation.2 | async-start | bytes 1720320 | tf_op jit(solution)/shard_map/reduce_scatter | solution.py:1159
  12.7 69.8 %collective-permute-start.15 = (bf16[768,768]{1,0:T(8,128)(2,1)}, bf16[768,768]{1,0:T(8,128)(2,1)}, u32[]{:S(2)}, u32[]{:S(2)}) collective-permute-start(bf16[768,768]{1,0:T(8,128)(2,1)} %bitcast.14.refs_4_.refs_6_.refs_7_), channel_id=1, source_target_pairs={{0,16},{16,0},{1,17},{17,1},{2,18},{18,2},{3,19},{19,3},{4,20},{20... | collective-permute-start | bytes 3538952 | tf_op jit(solution)/shard_map/ppermute | solution.py:147
  13.0 69.4 %collective-permute-start.14 = (bf16[768,768]{1,0:T(8,128)(2,1)}, bf16[768,768]{1,0:T(8,128)(2,1)}, u32[]{:S(2)}, u32[]{:S(2)}) collective-permute-start(bf16[768,768]{1,0:T(8,128)(2,1)} %bitcast.13.refs_2_.refs_4_.refs_5_), channel_id=1, source_target_pairs={{0,16},{16,0},{1,17},{17,1},{2,18},{18,2},{3,19},{19,3},{4,20},{20... | collective-permute-start | bytes 3538952 | tf_op jit(solution)/shard_map/ppermute | solution.py:147
  14.6 6.7 %collective-permute-start.3 = (f32[32,3]{1,0:T(8,128)S(1)}, f32[32,3]{1,0:T(8,128)S(1)}, u32[]{:S(2)}, u32[]{:S(2)}) collective-permute-start(f32[32,3]{1,0:T(8,128)S(1)} %bitcast.46), channel_id=1, source_target_pairs={{0,16},{16,0},{1,17},{17,1},{2,18},{18,2},{3,19},{19,3},{4,20},{20... | collective-permute-start | bytes 1160 | tf_op jit(solution)/shard_map/ppermute | solution.py:147
  16.3 28.7 %collective-permute-start.10 = (s32[2,2,256]{2,1,0:T(2,128)S(1)}, s32[2,2,256]{2,1,0:T(2,128)S(1)}, u32[]{:S(2)}, u32[]{:S(2)}) collective-permute-start(s32[2,2,256]{2,1,0:T(2,128)S(1)} %bitcast.50), channel_id=1, source_target_pairs={{0,16},{16,0},{1,17},{17,1},{2,18},{18,2},{3,19},{19,3},{4,20},{20... | collective-permute-start | bytes 12296 | tf_op jit(solution)/shard_map/ppermute | solution.py:147
  16.8 29.5 %collective-permute-start.9 = (bf16[768,4]{1,0:T(8,128)(2,1)S(1)}, bf16[768,4]{1,0:T(8,128)(2,1)S(1)}, u32[]{:S(2)}, u32[]{:S(2)}) collective-permute-start(bf16[768,4]{1,0:T(8,128)(2,1)S(1)} %bitcast.43), channel_id=1, source_target_pairs={{0,16},{16,0},{1,17},{17,1},{2,18},{18,2},{3,19},{19,3},{4,20},{20... | collective-permute-start | bytes 18440 | tf_op jit(solution)/shard_map/ppermute | solution.py:147
  21.3 22.5 %collective-permute-start.8 = (bf16[1,768]{1,0:T(2,128)(2,1)S(1)}, bf16[1,768]{1,0:T(2,128)(2,1)S(1)}, u32[]{:S(2)}, u32[]{:S(2)}) collective-permute-start(bf16[1,768]{1,0:T(2,128)(2,1)S(1)} %copy-done.73), channel_id=1, source_target_pairs={{0,16},{16,0},{1,17},{17,1},{2,18},{18,2},{3,19},{19,3},{4,20},{20... | collective-permute-start | bytes 4616 | tf_op jit(solution)/shard_map/ppermute | solution.py:147
  43.8 8.0 %collective-permute-start.4 = (bf16[256,192]{1,0:T(8,128)(2,1)S(1)}, bf16[256,192]{1,0:T(8,128)(2,1)S(1)}, u32[]{:S(2)}, u32[]{:S(2)}) collective-permute-start(bf16[256,192]{1,0:T(8,128)(2,1)S(1)} %get-tuple-element.148.refs_1_.refs_4_), channel_id=1, source_target_pairs={{0,1},{1,0},{2,3},{3,2},{4,5},{5,4},{6,7},{7,6},{8,9},{9,8},{10,11... | collective-permute-start | bytes 294920 | tf_op jit(solution)/shard_map/ppermute | solution.py:147
  45.1 8.3 %collective-permute-start.5 = (bf16[256,192]{1,0:T(8,128)(2,1)S(1)}, bf16[256,192]{1,0:T(8,128)(2,1)S(1)}, u32[]{:S(2)}, u32[]{:S(2)}) collective-permute-start(bf16[256,192]{1,0:T(8,128)(2,1)S(1)} %get-tuple-element.148.refs_1_.refs_4_), channel_id=1, source_target_pairs={{0,2},{1,3},{2,0},{3,1},{4,6},{5,7},{6,4},{7,5},{8,10},{9,11},{10,... | collective-permute-start | bytes 294920 | tf_op jit(solution)/shard_map/ppermute | solution.py:147
  46.2 9.4 %collective-permute-start.6 = (bf16[256,192]{1,0:T(8,128)(2,1)S(1)}, bf16[256,192]{1,0:T(8,128)(2,1)S(1)}, u32[]{:S(2)}, u32[]{:S(2)}) collective-permute-start(bf16[256,192]{1,0:T(8,128)(2,1)S(1)} %get-tuple-element.148.refs_1_.refs_4_), channel_id=1, source_target_pairs={{0,3},{1,2},{2,1},{3,0},{4,7},{5,6},{6,5},{7,4},{8,11},{9,10},{10,... | collective-permute-start | bytes 294920 | tf_op jit(solution)/shard_map/ppermute | solution.py:147
  52.4 12.7 %collective-permute-start.16 = (s32[2,2,2,256]{3,2,1,0:T(2,128)S(1)}, s32[2,2,2,256]{3,2,1,0:T(2,128)S(1)}, u32[]{:S(2)}, u32[]{:S(2)}) collective-permute-start(s32[2,2,2,256]{3,2,1,0:T(2,128)S(1)} %get-tuple-element.158.refs_1_), channel_id=1, source_target_pairs={{0,4},{4,0},{8,12},{12,8},{1,5},{5,1},{9,13},{13,9},{2,6},{6,2},{1... | collective-permute-start | bytes 24584 | tf_op jit(solution)/shard_map/ppermute | solution.py:147
  54.0 13.4 %collective-permute-start.17 = (s32[2,2,2,256]{3,2,1,0:T(2,128)S(1)}, s32[2,2,2,256]{3,2,1,0:T(2,128)S(1)}, u32[]{:S(2)}, u32[]{:S(2)}) collective-permute-start(s32[2,2,2,256]{3,2,1,0:T(2,128)S(1)} %get-tuple-element.158.refs_1_), channel_id=1, source_target_pairs={{0,8},{4,12},{8,0},{12,4},{1,9},{5,13},{9,1},{13,5},{2,10},{6,14},... | collective-permute-start | bytes 24584 | tf_op jit(solution)/shard_map/ppermute | solution.py:147
  56.3 11.4 %collective-permute-start.18 = (s32[2,2,2,256]{3,2,1,0:T(2,128)S(1)}, s32[2,2,2,256]{3,2,1,0:T(2,128)S(1)}, u32[]{:S(2)}, u32[]{:S(2)}) collective-permute-start(s32[2,2,2,256]{3,2,1,0:T(2,128)S(1)} %get-tuple-element.158.refs_1_), channel_id=1, source_target_pairs={{0,12},{4,8},{8,4},{12,0},{1,13},{5,9},{9,5},{13,1},{2,14},{6,10},... | collective-permute-start | bytes 24584 | tf_op jit(solution)/shard_map/ppermute | solution.py:147
  65.1 6.1 %collective-permute-start.11 = (bf16[40,768]{1,0:T(8,128)(2,1)S(1)}, bf16[40,768]{1,0:T(8,128)(2,1)S(1)}, u32[]{:S(2)}, u32[]{:S(2)}) collective-permute-start(bf16[40,768]{1,0:T(8,128)(2,1)S(1)} %get-tuple-element.154), channel_id=1, source_target_pairs={{0,4},{4,0},{8,12},{12,8},{1,5},{5,1},{9,13},{13,9},{2,6},{6,2},{1... | collective-permute-start | bytes 184328 | tf_op jit(solution)/shard_map/ppermute | solution.py:147
  87.0 5.1 %collective-permute-start.19 = (bf16[160,768]{1,0:T(8,128)(2,1)S(1)}, bf16[160,768]{1,0:T(8,128)(2,1)S(1)}, u32[]{:S(2)}, u32[]{:S(2)}) collective-permute-start(bf16[160,768]{1,0:T(8,128)(2,1)S(1)} %get-tuple-element.161), channel_id=1, source_target_pairs={{0,1},{1,0},{2,3},{3,2},{4,5},{5,4},{6,7},{7,6},{8,9},{9,8},{10,11... | collective-permute-start | bytes 737288 | tf_op jit(solution)/shard_map/ppermute | solution.py:147
  88.2 7.7 %collective-permute-start.20 = (bf16[160,768]{1,0:T(8,128)(2,1)S(1)}, bf16[160,768]{1,0:T(8,128)(2,1)S(1)}, u32[]{:S(2)}, u32[]{:S(2)}) collective-permute-start(bf16[160,768]{1,0:T(8,128)(2,1)S(1)} %get-tuple-element.162), channel_id=1, source_target_pairs={{0,2},{1,3},{2,0},{3,1},{4,6},{5,7},{6,4},{7,5},{8,10},{9,11},{10,... | collective-permute-start | bytes 737288 | tf_op jit(solution)/shard_map/ppermute | solution.py:147
  88.5 7.4 %collective-permute-start.21 = (bf16[160,768]{1,0:T(8,128)(2,1)S(1)}, bf16[160,768]{1,0:T(8,128)(2,1)S(1)}, u32[]{:S(2)}, u32[]{:S(2)}) collective-permute-start(bf16[160,768]{1,0:T(8,128)(2,1)S(1)} %get-tuple-element.163), channel_id=1, source_target_pairs={{0,3},{1,2},{2,1},{3,0},{4,7},{5,6},{6,5},{7,4},{8,11},{9,10},{10,... | collective-permute-start | bytes 737288 | tf_op jit(solution)/shard_map/ppermute | solution.py:147
  96.0 10.3 %collective-permute-start.22 = (bf16[40,768]{1,0:T(8,128)(2,1)S(1)}, bf16[40,768]{1,0:T(8,128)(2,1)S(1)}, u32[]{:S(2)}, u32[]{:S(2)}) collective-permute-start(bf16[40,768]{1,0:T(8,128)(2,1)S(1)} %get-tuple-element.165), channel_id=1, source_target_pairs={{0,4},{4,0},{8,12},{12,8},{1,5},{5,1},{9,13},{13,9},{2,6},{6,2},{1... | collective-permute-start | bytes 184328 | tf_op jit(solution)/shard_map/ppermute | solution.py:147
  99.3 8.3 %collective-permute-start.23 = (bf16[40,768]{1,0:T(8,128)(2,1)S(1)}, bf16[40,768]{1,0:T(8,128)(2,1)S(1)}, u32[]{:S(2)}, u32[]{:S(2)}) collective-permute-start(bf16[40,768]{1,0:T(8,128)(2,1)S(1)} %get-tuple-element.166), channel_id=1, source_target_pairs={{0,8},{4,12},{8,0},{12,4},{1,9},{5,13},{9,1},{13,5},{2,10},{6,14},... | collective-permute-start | bytes 184328 | tf_op jit(solution)/shard_map/ppermute | solution.py:147
  99.3 8.3 %collective-permute-start.24 = (bf16[40,768]{1,0:T(8,128)(2,1)S(1)}, bf16[40,768]{1,0:T(8,128)(2,1)S(1)}, u32[]{:S(2)}, u32[]{:S(2)}) collective-permute-start(bf16[40,768]{1,0:T(8,128)(2,1)S(1)} %get-tuple-element.167), channel_id=1, source_target_pairs={{0,12},{4,8},{8,4},{12,0},{1,13},{5,9},{9,5},{13,1},{2,14},{6,10},... | collective-permute-start | bytes 184328 | tf_op jit(solution)/shard_map/ppermute | solution.py:147
  102.1 52.4 %collective-permute-start.25 = (bf16[160,768]{1,0:T(8,128)(2,1)S(1)}, bf16[160,768]{1,0:T(8,128)(2,1)S(1)}, u32[]{:S(2)}, u32[]{:S(2)}) collective-permute-start(bf16[160,768]{1,0:T(8,128)(2,1)S(1)} %get-tuple-element.175), channel_id=1, source_target_pairs={{0,4},{4,0},{8,12},{12,8},{1,5},{5,1},{9,13},{13,9},{2,6},{6,2},{1... | collective-permute-start | bytes 737288 | tf_op jit(solution)/shard_map/ppermute | solution.py:147
  104.4 50.8 %collective-permute-start.26 = (bf16[160,768]{1,0:T(8,128)(2,1)S(1)}, bf16[160,768]{1,0:T(8,128)(2,1)S(1)}, u32[]{:S(2)}, u32[]{:S(2)}) collective-permute-start(bf16[160,768]{1,0:T(8,128)(2,1)S(1)} %get-tuple-element.176), channel_id=1, source_target_pairs={{0,8},{4,12},{8,0},{12,4},{1,9},{5,13},{9,1},{13,5},{2,10},{6,14},... | collective-permute-start | bytes 737288 | tf_op jit(solution)/shard_map/ppermute | solution.py:147
  106.3 48.9 %collective-permute-start.27 = (bf16[160,768]{1,0:T(8,128)(2,1)S(1)}, bf16[160,768]{1,0:T(8,128)(2,1)S(1)}, u32[]{:S(2)}, u32[]{:S(2)}) collective-permute-start(bf16[160,768]{1,0:T(8,128)(2,1)S(1)} %get-tuple-element.177), channel_id=1, source_target_pairs={{0,12},{4,8},{8,4},{12,0},{1,13},{5,9},{9,5},{13,1},{2,14},{6,10},... | collective-permute-start | bytes 737288 | tf_op jit(solution)/shard_map/ppermute | solution.py:147
  141.3 5.3 %collective-permute-start.29 = (bf16[256,192]{1,0:T(8,128)(2,1)S(1)}, bf16[256,192]{1,0:T(8,128)(2,1)S(1)}, u32[]{:S(2)}, u32[]{:S(2)}) collective-permute-start(bf16[256,192]{1,0:T(8,128)(2,1)S(1)} %get-tuple-element.178.refs_1_.refs_4_), channel_id=1, source_target_pairs={{0,2},{1,3},{2,0},{3,1},{4,6},{5,7},{6,4},{7,5},{8,10},{9,11},{10,... | collective-permute-start | bytes 294920 | tf_op jit(solution)/shard_map/ppermute | solution.py:147
  145.4 4.7 %collective-permute-start.30 = (bf16[256,192]{1,0:T(8,128)(2,1)S(1)}, bf16[256,192]{1,0:T(8,128)(2,1)S(1)}, u32[]{:S(2)}, u32[]{:S(2)}) collective-permute-start(bf16[256,192]{1,0:T(8,128)(2,1)S(1)} %get-tuple-element.178.refs_1_.refs_4_), channel_id=1, source_target_pairs={{0,3},{1,2},{2,1},{3,0},{4,7},{5,6},{6,5},{7,4},{8,11},{9,10},{10,... | collective-permute-start | bytes 294920 | tf_op jit(solution)/shard_map/ppermute | solution.py:147
  176.2 8.0 %collective-permute-start.34 = (bf16[160,768]{1,0:T(8,128)(2,1)S(1)}, bf16[160,768]{1,0:T(8,128)(2,1)S(1)}, u32[]{:S(2)}, u32[]{:S(2)}) collective-permute-start(bf16[160,768]{1,0:T(8,128)(2,1)S(1)} %get-tuple-element.188), channel_id=1, source_target_pairs={{0,1},{1,0},{2,3},{3,2},{4,5},{5,4},{6,7},{7,6},{8,9},{9,8},{10,11... | collective-permute-start | bytes 737288 | tf_op jit(solution)/shard_map/ppermute | solution.py:147
  177.7 6.5 %collective-permute-start.35 = (bf16[160,768]{1,0:T(8,128)(2,1)S(1)}, bf16[160,768]{1,0:T(8,128)(2,1)S(1)}, u32[]{:S(2)}, u32[]{:S(2)}) collective-permute-start(bf16[160,768]{1,0:T(8,128)(2,1)S(1)} %get-tuple-element.189), channel_id=1, source_target_pairs={{0,2},{1,3},{2,0},{3,1},{4,6},{5,7},{6,4},{7,5},{8,10},{9,11},{10,... | collective-permute-start | bytes 737288 | tf_op jit(solution)/shard_map/ppermute | solution.py:147
  177.7 9.7 %collective-permute-start.36 = (bf16[160,768]{1,0:T(8,128)(2,1)S(1)}, bf16[160,768]{1,0:T(8,128)(2,1)S(1)}, u32[]{:S(2)}, u32[]{:S(2)}) collective-permute-start(bf16[160,768]{1,0:T(8,128)(2,1)S(1)} %get-tuple-element.190), channel_id=1, source_target_pairs={{0,3},{1,2},{2,1},{3,0},{4,7},{5,6},{6,5},{7,4},{8,11},{9,10},{10,... | collective-permute-start | bytes 737288 | tf_op jit(solution)/shard_map/ppermute | solution.py:147
  190.3 4.8 %collective-permute-start.39 = (bf16[40,768]{1,0:T(8,128)(2,1)S(1)}, bf16[40,768]{1,0:T(8,128)(2,1)S(1)}, u32[]{:S(2)}, u32[]{:S(2)}) collective-permute-start(bf16[40,768]{1,0:T(8,128)(2,1)S(1)} %get-tuple-element.194), channel_id=1, source_target_pairs={{0,12},{4,8},{8,4},{12,0},{1,13},{5,9},{9,5},{13,1},{2,14},{6,10},... | collective-permute-start | bytes 184328 | tf_op jit(solution)/shard_map/ppermute | solution.py:147
  214.3 5.3 %collective-permute-start.40 = (bf16[256,384]{1,0:T(8,128)(2,1)S(1)}, bf16[256,384]{1,0:T(8,128)(2,1)S(1)}, u32[]{:S(2)}, u32[]{:S(2)}) collective-permute-start(bf16[256,384]{1,0:T(8,128)(2,1)S(1)} %get-tuple-element.199), channel_id=1, source_target_pairs={{0,4},{4,0},{8,12},{12,8},{1,5},{5,1},{9,13},{13,9},{2,6},{6,2},{1... | collective-permute-start | bytes 589832 | tf_op jit(solution)/shard_map/ppermute | solution.py:147
  215.9 8.8 %collective-permute-start.41 = (bf16[256,384]{1,0:T(8,128)(2,1)S(1)}, bf16[256,384]{1,0:T(8,128)(2,1)S(1)}, u32[]{:S(2)}, u32[]{:S(2)}) collective-permute-start(bf16[256,384]{1,0:T(8,128)(2,1)S(1)} %get-tuple-element.200), channel_id=1, source_target_pairs={{0,8},{4,12},{8,0},{12,4},{1,9},{5,13},{9,1},{13,5},{2,10},{6,14},... | collective-permute-start | bytes 589832 | tf_op jit(solution)/shard_map/ppermute | solution.py:147
  217.8 9.9 %collective-permute-start.42 = (bf16[256,384]{1,0:T(8,128)(2,1)S(1)}, bf16[256,384]{1,0:T(8,128)(2,1)S(1)}, u32[]{:S(2)}, u32[]{:S(2)}) collective-permute-start(bf16[256,384]{1,0:T(8,128)(2,1)S(1)} %get-tuple-element.201), channel_id=1, source_target_pairs={{0,12},{4,8},{8,4},{12,0},{1,13},{5,9},{9,5},{13,1},{2,14},{6,10},... | collective-permute-start | bytes 589832 | tf_op jit(solution)/shard_map/ppermute | solution.py:147
  229.4 6.5 %collective-permute-start.43 = (bf16[64,768]{1,0:T(8,128)(2,1)S(1)}, bf16[64,768]{1,0:T(8,128)(2,1)S(1)}, u32[]{:S(2)}, u32[]{:S(2)}) collective-permute-start(bf16[64,768]{1,0:T(8,128)(2,1)S(1)} %get-tuple-element.203), channel_id=1, source_target_pairs={{0,1},{1,0},{2,3},{3,2},{4,5},{5,4},{6,7},{7,6},{8,9},{9,8},{10,11... | collective-permute-start | bytes 294920 | tf_op jit(solution)/shard_map/ppermute | solution.py:147
  230.4 5.5 %collective-permute-start.44 = (bf16[64,768]{1,0:T(8,128)(2,1)S(1)}, bf16[64,768]{1,0:T(8,128)(2,1)S(1)}, u32[]{:S(2)}, u32[]{:S(2)}) collective-permute-start(bf16[64,768]{1,0:T(8,128)(2,1)S(1)} %get-tuple-element.204), channel_id=1, source_target_pairs={{0,2},{1,3},{2,0},{3,1},{4,6},{5,7},{6,4},{7,5},{8,10},{9,11},{10,... | collective-permute-start | bytes 294920 | tf_op jit(solution)/shard_map/ppermute | solution.py:147
  230.9 5.0 %collective-permute-start.45 = (bf16[64,768]{1,0:T(8,128)(2,1)S(1)}, bf16[64,768]{1,0:T(8,128)(2,1)S(1)}, u32[]{:S(2)}, u32[]{:S(2)}) collective-permute-start(bf16[64,768]{1,0:T(8,128)(2,1)S(1)} %get-tuple-element.205), channel_id=1, source_target_pairs={{0,3},{1,2},{2,1},{3,0},{4,7},{5,6},{6,5},{7,4},{8,11},{9,10},{10,... | collective-permute-start | bytes 294920 | tf_op jit(solution)/shard_map/ppermute | solution.py:147
  234.9 16.1 %collective-permute-start.52 = (bf16[160,768]{1,0:T(8,128)(2,1)S(1)}, bf16[160,768]{1,0:T(8,128)(2,1)S(1)}, u32[]{:S(2)}, u32[]{:S(2)}) collective-permute-start(bf16[160,768]{1,0:T(8,128)(2,1)S(1)} %get-tuple-element.222), channel_id=1, source_target_pairs={{0,1},{1,0},{2,3},{3,2},{4,5},{5,4},{6,7},{7,6},{8,9},{9,8},{10,11... | collective-permute-start | bytes 737288 | tf_op jit(solution)/shard_map/ppermute | solution.py:147
  236.0 5.4 %collective-permute-start.46 = (bf16[64,768]{1,0:T(8,128)(2,1)S(1)}, bf16[64,768]{1,0:T(8,128)(2,1)S(1)}, u32[]{:S(2)}, u32[]{:S(2)}) collective-permute-start(bf16[64,768]{1,0:T(8,128)(2,1)S(1)} %shard_map.188.refs_1_), channel_id=1, source_target_pairs={{0,1},{1,0},{2,3},{3,2},{4,5},{5,4},{6,7},{7,6},{8,9},{9,8},{10,11... | collective-permute-start | bytes 294920 | tf_op jit(solution)/shard_map/ppermute | solution.py:147
  236.5 14.9 %collective-permute-start.53 = (bf16[160,768]{1,0:T(8,128)(2,1)S(1)}, bf16[160,768]{1,0:T(8,128)(2,1)S(1)}, u32[]{:S(2)}, u32[]{:S(2)}) collective-permute-start(bf16[160,768]{1,0:T(8,128)(2,1)S(1)} %get-tuple-element.223), channel_id=1, source_target_pairs={{0,2},{1,3},{2,0},{3,1},{4,6},{5,7},{6,4},{7,5},{8,10},{9,11},{10,... | collective-permute-start | bytes 737288 | tf_op jit(solution)/shard_map/ppermute | solution.py:147
  237.5 13.9 %collective-permute-start.54 = (bf16[160,768]{1,0:T(8,128)(2,1)S(1)}, bf16[160,768]{1,0:T(8,128)(2,1)S(1)}, u32[]{:S(2)}, u32[]{:S(2)}) collective-permute-start(bf16[160,768]{1,0:T(8,128)(2,1)S(1)} %get-tuple-element.224), channel_id=1, source_target_pairs={{0,3},{1,2},{2,1},{3,0},{4,7},{5,6},{6,5},{7,4},{8,11},{9,10},{10,... | collective-permute-start | bytes 737288 | tf_op jit(solution)/shard_map/ppermute | solution.py:147
  238.7 7.6 %collective-permute-start.47 = (bf16[64,768]{1,0:T(8,128)(2,1)S(1)}, bf16[64,768]{1,0:T(8,128)(2,1)S(1)}, u32[]{:S(2)}, u32[]{:S(2)}) collective-permute-start(bf16[64,768]{1,0:T(8,128)(2,1)S(1)} %shard_map.188.refs_1_), channel_id=1, source_target_pairs={{0,2},{1,3},{2,0},{3,1},{4,6},{5,7},{6,4},{7,5},{8,10},{9,11},{10,... | collective-permute-start | bytes 294920 | tf_op jit(solution)/shard_map/ppermute | solution.py:147
  241.3 5.0 %collective-permute-start.48 = (bf16[64,768]{1,0:T(8,128)(2,1)S(1)}, bf16[64,768]{1,0:T(8,128)(2,1)S(1)}, u32[]{:S(2)}, u32[]{:S(2)}) collective-permute-start(bf16[64,768]{1,0:T(8,128)(2,1)S(1)} %shard_map.188.refs_1_), channel_id=1, source_target_pairs={{0,3},{1,2},{2,1},{3,0},{4,7},{5,6},{6,5},{7,4},{8,11},{9,10},{10,... | collective-permute-start | bytes 294920 | tf_op jit(solution)/shard_map/ppermute | solution.py:147
  248.8 4.5 %collective-permute-start.50 = (bf16[40,768]{1,0:T(8,128)(2,1)S(1)}, bf16[40,768]{1,0:T(8,128)(2,1)S(1)}, u32[]{:S(2)}, u32[]{:S(2)}) collective-permute-start(bf16[40,768]{1,0:T(8,128)(2,1)S(1)} %get-tuple-element.214), channel_id=1, source_target_pairs={{0,8},{4,12},{8,0},{12,4},{1,9},{5,13},{9,1},{13,5},{2,10},{6,14},... | collective-permute-start | bytes 184328 | tf_op jit(solution)/shard_map/ppermute | solution.py:147
  278.0 11.2 %collective-permute-start.55 = (bf16[160,768]{1,0:T(8,128)(2,1)}, bf16[160,768]{1,0:T(8,128)(2,1)S(1)}, u32[]{:S(2)}, u32[]{:S(2)}) collective-permute-start(bf16[160,768]{1,0:T(8,128)(2,1)} %get-tuple-element.227), channel_id=1, source_target_pairs={{0,1},{1,0},{2,3},{3,2},{4,5},{5,4},{6,7},{7,6},{8,9},{9,8},{10,11... | collective-permute-start | bytes 737288 | tf_op jit(solution)/shard_map/ppermute | solution.py:147
  278.4 10.7 %collective-permute-start.56 = (bf16[160,768]{1,0:T(8,128)(2,1)}, bf16[160,768]{1,0:T(8,128)(2,1)S(1)}, u32[]{:S(2)}, u32[]{:S(2)}) collective-permute-start(bf16[160,768]{1,0:T(8,128)(2,1)} %get-tuple-element.228), channel_id=1, source_target_pairs={{0,2},{1,3},{2,0},{3,1},{4,6},{5,7},{6,4},{7,5},{8,10},{9,11},{10,... | collective-permute-start | bytes 737288 | tf_op jit(solution)/shard_map/ppermute | solution.py:147
  279.4 9.7 %collective-permute-start.57 = (bf16[160,768]{1,0:T(8,128)(2,1)}, bf16[160,768]{1,0:T(8,128)(2,1)S(1)}, u32[]{:S(2)}, u32[]{:S(2)}) collective-permute-start(bf16[160,768]{1,0:T(8,128)(2,1)} %get-tuple-element.229), channel_id=1, source_target_pairs={{0,3},{1,2},{2,1},{3,0},{4,7},{5,6},{6,5},{7,4},{8,11},{9,10},{10,... | collective-permute-start | bytes 737288 | tf_op jit(solution)/shard_map/ppermute | solution.py:147
  289.3 14.0 %collective-permute-start.58 = (bf16[40,768]{1,0:T(8,128)(2,1)S(1)}, bf16[40,768]{1,0:T(8,128)(2,1)S(1)}, u32[]{:S(2)}, u32[]{:S(2)}) collective-permute-start(bf16[40,768]{1,0:T(8,128)(2,1)S(1)} %get-tuple-element.236), channel_id=1, source_target_pairs={{0,4},{4,0},{8,12},{12,8},{1,5},{5,1},{9,13},{13,9},{2,6},{6,2},{1... | collective-permute-start | bytes 184328 | tf_op jit(solution)/shard_map/ppermute | solution.py:147
  294.0 9.3 %collective-permute-start.59 = (bf16[40,768]{1,0:T(8,128)(2,1)S(1)}, bf16[40,768]{1,0:T(8,128)(2,1)S(1)}, u32[]{:S(2)}, u32[]{:S(2)}) collective-permute-start(bf16[40,768]{1,0:T(8,128)(2,1)S(1)} %get-tuple-element.237), channel_id=1, source_target_pairs={{0,8},{4,12},{8,0},{12,4},{1,9},{5,13},{9,1},{13,5},{2,10},{6,14},... | collective-permute-start | bytes 184328 | tf_op jit(solution)/shard_map/ppermute | solution.py:147
  294.4 8.9 %collective-permute-start.60 = (bf16[40,768]{1,0:T(8,128)(2,1)S(1)}, bf16[40,768]{1,0:T(8,128)(2,1)S(1)}, u32[]{:S(2)}, u32[]{:S(2)}) collective-permute-start(bf16[40,768]{1,0:T(8,128)(2,1)S(1)} %get-tuple-element.238), channel_id=1, source_target_pairs={{0,12},{4,8},{8,4},{12,0},{1,13},{5,9},{9,5},{13,1},{2,14},{6,10},... | collective-permute-start | bytes 184328 | tf_op jit(solution)/shard_map/ppermute | solution.py:147
  323.5 8.0 %collective-permute-start.64 = (bf16[256,384]{1,0:T(8,128)(2,1)S(1)}, bf16[256,384]{1,0:T(8,128)(2,1)S(1)}, u32[]{:S(2)}, u32[]{:S(2)}) collective-permute-start(bf16[256,384]{1,0:T(8,128)(2,1)S(1)} %get-tuple-element.247), channel_id=1, source_target_pairs={{0,4},{4,0},{8,12},{12,8},{1,5},{5,1},{9,13},{13,9},{2,6},{6,2},{1... | collective-permute-start | bytes 589832 | tf_op jit(solution)/shard_map/ppermute | solution.py:147
  327.0 8.1 %collective-permute-start.65 = (bf16[256,384]{1,0:T(8,128)(2,1)S(1)}, bf16[256,384]{1,0:T(8,128)(2,1)S(1)}, u32[]{:S(2)}, u32[]{:S(2)}) collective-permute-start(bf16[256,384]{1,0:T(8,128)(2,1)S(1)} %get-tuple-element.248), channel_id=1, source_target_pairs={{0,8},{4,12},{8,0},{12,4},{1,9},{5,13},{9,1},{13,5},{2,10},{6,14},... | collective-permute-start | bytes 589832 | tf_op jit(solution)/shard_map/ppermute | solution.py:147
  328.2 9.9 %collective-permute-start.66 = (bf16[256,384]{1,0:T(8,128)(2,1)S(1)}, bf16[256,384]{1,0:T(8,128)(2,1)S(1)}, u32[]{:S(2)}, u32[]{:S(2)}) collective-permute-start(bf16[256,384]{1,0:T(8,128)(2,1)S(1)} %get-tuple-element.249), channel_id=1, source_target_pairs={{0,12},{4,8},{8,4},{12,0},{1,13},{5,9},{9,5},{13,1},{2,14},{6,10},... | collective-permute-start | bytes 589832 | tf_op jit(solution)/shard_map/ppermute | solution.py:147
  339.6 4.8 %collective-permute-start.67 = (bf16[64,768]{1,0:T(8,128)(2,1)S(1)}, bf16[64,768]{1,0:T(8,128)(2,1)S(1)}, u32[]{:S(2)}, u32[]{:S(2)}) collective-permute-start(bf16[64,768]{1,0:T(8,128)(2,1)S(1)} %get-tuple-element.251), channel_id=1, source_target_pairs={{0,1},{1,0},{2,3},{3,2},{4,5},{5,4},{6,7},{7,6},{8,9},{9,8},{10,11... | collective-permute-start | bytes 294920 | tf_op jit(solution)/shard_map/ppermute | solution.py:147
  340.5 5.3 %collective-permute-start.68 = (bf16[64,768]{1,0:T(8,128)(2,1)S(1)}, bf16[64,768]{1,0:T(8,128)(2,1)S(1)}, u32[]{:S(2)}, u32[]{:S(2)}) collective-permute-start(bf16[64,768]{1,0:T(8,128)(2,1)S(1)} %get-tuple-element.252), channel_id=1, source_target_pairs={{0,2},{1,3},{2,0},{3,1},{4,6},{5,7},{6,4},{7,5},{8,10},{9,11},{10,... | collective-permute-start | bytes 294920 | tf_op jit(solution)/shard_map/ppermute | solution.py:147
  341.1 5.4 %collective-permute-start.69 = (bf16[64,768]{1,0:T(8,128)(2,1)S(1)}, bf16[64,768]{1,0:T(8,128)(2,1)S(1)}, u32[]{:S(2)}, u32[]{:S(2)}) collective-permute-start(bf16[64,768]{1,0:T(8,128)(2,1)S(1)} %get-tuple-element.253), channel_id=1, source_target_pairs={{0,3},{1,2},{2,1},{3,0},{4,7},{5,6},{6,5},{7,4},{8,11},{9,10},{10,... | collective-permute-start | bytes 294920 | tf_op jit(solution)/shard_map/ppermute | solution.py:147
  346.6 5.2 %collective-permute-start.70 = (bf16[64,768]{1,0:T(8,128)(2,1)S(1)}, bf16[64,768]{1,0:T(8,128)(2,1)S(1)}, u32[]{:S(2)}, u32[]{:S(2)}) collective-permute-start(bf16[64,768]{1,0:T(8,128)(2,1)S(1)} %shard_map.202.refs_1_), channel_id=1, source_target_pairs={{0,1},{1,0},{2,3},{3,2},{4,5},{5,4},{6,7},{7,6},{8,9},{9,8},{10,11... | collective-permute-start | bytes 294920 | tf_op jit(solution)/shard_map/ppermute | solution.py:147
  356.4 35.4 %collective-permute-start.82 = (bf16[768,896]{1,0:T(8,128)(2,1)S(1)}, bf16[768,896]{1,0:T(8,128)(2,1)S(1)}, u32[]{:S(2)}, u32[]{:S(2)}) collective-permute-start(bf16[768,896]{1,0:T(8,128)(2,1)S(1)} %shard_map.211), channel_id=1, source_target_pairs={{0,16},{16,0},{1,17},{17,1},{2,18},{18,2},{3,19},{19,3},{4,20},{20... | collective-permute-start | bytes 4128776 | tf_op jit(solution)/shard_map/ppermute | solution.py:147
  387.8 29.6 %collective-permute-start.79 = (bf16[2,768,768]{2,1,0:T(8,128)(2,1)}, bf16[2,768,768]{2,1,0:T(8,128)(2,1)}, u32[]{:S(2)}, u32[]{:S(2)}) collective-permute-start(bf16[2,768,768]{2,1,0:T(8,128)(2,1)} %get-tuple-element.266), channel_id=1, source_target_pairs={{0,16},{16,0},{1,17},{17,1},{2,18},{18,2},{3,19},{19,3},{4,20},{20... | collective-permute-start | bytes 7077896 | tf_op jit(solution)/shard_map/ppermute | solution.py:147
  395.1 4.6 %collective-permute-start.74 = (bf16[40,768]{1,0:T(8,128)(2,1)S(1)}, bf16[40,768]{1,0:T(8,128)(2,1)S(1)}, u32[]{:S(2)}, u32[]{:S(2)}) collective-permute-start(bf16[40,768]{1,0:T(8,128)(2,1)S(1)} %copy-done.77), channel_id=1, source_target_pairs={{0,8},{4,12},{8,0},{12,4},{1,9},{5,13},{9,1},{13,5},{2,10},{6,14},... | collective-permute-start | bytes 184328 | tf_op jit(solution)/shard_map/ppermute | solution.py:147
  396.7 11.3 %collective-permute-start.75 = (bf16[40,768]{1,0:T(8,128)(2,1)S(1)}, bf16[40,768]{1,0:T(8,128)(2,1)S(1)}, u32[]{:S(2)}, u32[]{:S(2)}) collective-permute-start(bf16[40,768]{1,0:T(8,128)(2,1)S(1)} %copy-done.75), channel_id=1, source_target_pairs={{0,12},{4,8},{8,4},{12,0},{1,13},{5,9},{9,5},{13,1},{2,14},{6,10},... | collective-permute-start | bytes 184328 | tf_op jit(solution)/shard_map/ppermute | solution.py:147
  408.0 20.2 %collective-permute-start.76 = (bf16[160,768]{1,0:T(8,128)(2,1)S(1)}, bf16[160,768]{1,0:T(8,128)(2,1)S(1)}, u32[]{:S(2)}, u32[]{:S(2)}) collective-permute-start(bf16[160,768]{1,0:T(8,128)(2,1)S(1)} %shard_map.206.refs_2_), channel_id=1, source_target_pairs={{0,1},{1,0},{2,3},{3,2},{4,5},{5,4},{6,7},{7,6},{8,9},{9,8},{10,11... | collective-permute-start | bytes 737288 | tf_op jit(solution)/shard_map/ppermute | solution.py:147
  408.4 19.8 %collective-permute-start.77 = (bf16[160,768]{1,0:T(8,128)(2,1)S(1)}, bf16[160,768]{1,0:T(8,128)(2,1)S(1)}, u32[]{:S(2)}, u32[]{:S(2)}) collective-permute-start(bf16[160,768]{1,0:T(8,128)(2,1)S(1)} %shard_map.206.refs_2_), channel_id=1, source_target_pairs={{0,2},{1,3},{2,0},{3,1},{4,6},{5,7},{6,4},{7,5},{8,10},{9,11},{10,... | collective-permute-start | bytes 737288 | tf_op jit(solution)/shard_map/ppermute | solution.py:147
  408.5 19.6 %collective-permute-start.78 = (bf16[160,768]{1,0:T(8,128)(2,1)S(1)}, bf16[160,768]{1,0:T(8,128)(2,1)S(1)}, u32[]{:S(2)}, u32[]{:S(2)}) collective-permute-start(bf16[160,768]{1,0:T(8,128)(2,1)S(1)} %shard_map.206.refs_2_), channel_id=1, source_target_pairs={{0,3},{1,2},{2,1},{3,0},{4,7},{5,6},{6,5},{7,4},{8,11},{9,10},{10,... | collective-permute-start | bytes 737288 | tf_op jit(solution)/shard_map/ppermute | solution.py:147
  410.7 19.5 %collective-permute-start.81 = (f32[256,768]{1,0:T(8,128)}, f32[256,768]{1,0:T(8,128)S(1)}, u32[]{:S(2)}, u32[]{:S(2)}) collective-permute-start(f32[256,768]{1,0:T(8,128)} %copy-done.37), channel_id=1, source_target_pairs={{16,0},{17,1},{18,2},{19,3},{20,4},{21,5},{22,6},{23,7},{24,8},{25... | collective-permute-start | bytes 2359304 | tf_op jit(solution)/shard_map/ppermute | solution.py:151
  (104 other events, 1177.6 us)
Sparse Core Ops, SparseCore 0:
  11.4 40.7 all-gather.1
  394.4 32.7 reduce-scatter.1

commit v5 on v4

--- a/solution.py
+++ b/solution.py
@@ -206,21 +206,15 @@
     ]
 
 
-def load_keys(kv_refs, kv_ref):
-    rows = kv_refs[0].shape[0]
-    for r, ref in enumerate(kv_refs):
-        kv_ref[r * rows : (r + 1) * rows, :] = ref[...]
-
-
 def attend(place, q, kv_parts, table, n_ctx):
     rows, width = q.shape
     half, heads, keys = rows // 2, width // HD, rows * n_ctx
     ordered, count = len(kv_parts) == 1, len(kv_parts)
 
     def body(place_ref, q_ref, *refs):
-        kv_refs, (table_ref, mix_ref, lse_ref, scores_ref, kv_ref) = refs[:count], refs[count:]
+        kv_refs, (table_ref, mix_ref, lse_ref, scores_ref) = refs[:count], refs[count:]
         mine = place_ref[0]
-        load_keys(kv_refs, kv_ref)
+        kv_ref = kv_refs[0]
         for head in range(heads):
             cols = slice(head * HD, (head + 1) * HD)
             key_rows = kv_ref[:, cols]
@@ -243,7 +237,7 @@
         body,
         [like(rows, width), like(rows, heads, dtype=F32)],
         [place, q, *kv_parts, table],
-        [pltpu.VMEM((2, half, keys), F32), pltpu.VMEM((keys, 2 * width), BF16)],
+        [pltpu.VMEM((2, half, keys), F32)],
         flops=4 * rows * keys * width,
     )
 
@@ -256,9 +250,9 @@
     def body(place_ref, q_ref, *refs):
         kv_refs, refs = refs[:count], refs[count:]
         table_ref, lse_ref, dmix_ref, dq_ref, dtable_ref = refs[:5]
-        chunk_refs, (scores_ref, total_ref, kv_ref) = refs[5 : 5 + n_ctx], refs[5 + n_ctx :]
+        chunk_refs, (scores_ref, total_ref) = refs[5 : 5 + n_ctx], refs[5 + n_ctx :]
         mine = place_ref[0]
-        load_keys(kv_refs, kv_ref)
+        kv_ref = kv_refs[0]
         dtable_ref[...] = jnp.zeros(dtable_ref.shape, F32)
         for head in range(heads):
             cols = slice(head * HD, (head + 1) * HD)
@@ -301,7 +295,6 @@
         [
             pltpu.VMEM((2, half, keys), F32),
             pltpu.VMEM((keys, 2 * width), F32),
-            pltpu.VMEM((keys, 2 * width), BF16),
         ],
         flops=10 * rows * keys * width,
     )
@@ -568,7 +561,7 @@
     return kernel_call(body, [like(model, width + LANES)], [place, grad, *smalls, got])[0]
 
 
-def joint_split(total, width, n_experts):
+def joint_split(total, width, n_experts, bias_shape):
     share = total.shape[0]
 
     def body(total_ref, qkv_ref, out_ref, first_ref, second_ref, router_ref, bias_ref):
@@ -576,14 +569,31 @@
             qkv_ref[i] = total_ref[:, at * width : (at + 1) * width].astype(F32)
         out_ref[...] = total_ref[:, width : 2 * width].astype(F32).T
         small = total_ref[:, 4 * width :].astype(F32)
-        router_ref[...] = small[:, 2 : 2 + n_experts]
         rows = small.T
         first_ref[...] = rows[0:1]
         second_ref[...] = rows[1:2]
-        bias_ref[...] = rows[2 + n_experts : 3 + n_experts]
-
-    shapes = [(3, share, width), (width, share)] + [(1, share)] * 2 + [(share, n_experts), (1, share)]
+        router_ref[...] = rows[2 : 2 + n_experts]
+        column = small[:, 2 + n_experts : 3 + n_experts]
+        held = lax.broadcasted_iota(jnp.int32, (share, bias_shape[1]), 0)
+        bucket = lax.broadcasted_iota(jnp.int32, (share, bias_shape[1]), 1)
+        for head in range(bias_shape[0]):
+            hit = held == bucket * bias_shape[0] + head
+            picked = jnp.sum(jnp.where(hit, column, 0.0), axis=0, keepdims=True)
+            bias_ref[head : head + 1, :] = picked
+
+    shapes = [(3, share, width), (width, share)] + [(1, share)] * 2
+    shapes += [(n_experts, share), bias_shape]
     return kernel_call(body, [like(*shape, dtype=F32) for shape in shapes], [total])
+
+
+def joined(pair, after):
+    rows, model = pair[0].shape
+
+    def body(one_ref, two_ref, out_ref):
+        out_ref[:rows, :] = one_ref[...]
+        out_ref[rows:, :] = two_ref[...]
+
+    return kernel_call(body, [like(2 * rows, model)], list(pair), after=after)[0]
 
 
 def join_quarter(pieces, after):
@@ -1040,7 +1050,7 @@
     up = by_layer(*with_other(expert_up[0, 0]))
     down = by_layer(*with_other(expert_down[0, 0]))
     width = out_weight.shape[1]
-    out_gathered = gather_rows(jnp.concatenate(with_other(out_weight[0]), axis=0), "heads")
+    out_gathered = gather_rows(joined(with_other(out_weight[0]), [kv0]), "heads")
     out_full = [Rows(out_gathered, layer, width) for layer in range(2)]
     out_own = [Rows(out_gathered, layer, width, own=True) for layer in range(2)]
     mix0, lse0 = attend(place, q0, [kv_all0], bias0, n_ctx)
@@ -1111,8 +1121,8 @@
     )
     lists = [(arrived0, arrived1), (dpre0, dpre1), (kept0[1], hidden1), (dslots0, dslots1)]
     mine, theirs = [Pick(a, b) for a, b in lists], [Pick(b, a) for a, b in lists]
-    sends, sends_made = expert_grads(place, [theirs[:2], theirs[2:]])
-    back = heads_sum(chunks, n_ctx, [sends_made])
+    out_back = exchange(out_total, "ctx")
+    back = heads_sum(chunks, n_ctx, out_back[1:])
     returned = gather_rows(jnp.concatenate(exchange(back, "ctx"), axis=0), "heads")
     router_part = router_grads(
         place, [(dlogits0, arrived0), (dlogits1, arrived1)], n_experts, back[:1]
@@ -1133,7 +1143,9 @@
     )
     dq0, dtable0, dkv0 = attend_back(place, q0, [kv_all0], bias0, lse0, dmix0, n_ctx)
     lanes0 = table_back(dtable0)
-    dkv_sum0, chunks = project_back(place, dq0, exchange(dkv0, "ctx"), qkv[0], n_heads)
+    dkv_parts0 = exchange(dkv0, "ctx")
+    sends, made = expert_grads(place, [theirs[:2], theirs[2:]], after=dkv_parts0[1:2])
+    dkv_sum0, chunks = project_back(place, dq0, dkv_parts0, qkv[0], n_heads, [made])
     parts = exchange(chunks, "heads")
     total0 = share_sum(parts)
     dense0, made = dense_grad(
@@ -1157,26 +1169,23 @@
     got = swap(joint_send(place, Pick(dense1, dense0), smalls), "section")
     joint = joint_sum(place, Pick(dense0, dense1), smalls, got)
     joint = lax.psum_scatter(joint, "ctx", scatter_dimension=0, tiled=True)
-    out_back = exchange(out_total, "ctx")
     quarter = join_quarter(out_back, ())
     grad_up, grad_down, made = expert_grads(
         place, [mine[:2], mine[2:]], swap(sends, "section"), after=[dgain_first0]
     )
     out, _ = combine(middle1, exchange([quarter] * n_heads, "heads"), tokens_near, [made])
     grad_qkv, grad_out, grad_first, grad_second, grad_router, grad_bias = joint_split(
-        joint, width, n_experts
-    )
-    bias_share = BUCKETS // n_ctx
-    grad_bias = grad_bias[:, : bias_share * heads].reshape(1, bias_share, heads)
+        joint, width, n_experts, (heads, BUCKETS // n_ctx)
+    )
     boundary_out = assemble(place, dx0, one_way(out, 0), got_dx, out)
     return (
         boundary_out[None],
         grad_first,
         grad_qkv[None],
-        grad_bias,
+        grad_bias.T[None],
         grad_out[None],
         grad_second,
-        grad_router[None],
+        grad_router.T[None],
         grad_up[None, None],
         grad_down[None, None],
     )

time: 454 us -> 442 us (0.974)
  the two profiles are of different devices: /device:TPU:9 before, /device:TPU:0 now
where the time goes in v5:
time: 442 us; the launch traced here: 434 us
  blocking collectives  114 us (26%)
  starting transfers between devices  99.8 us (23%)
  Pallas kernels  95.3 us (22%)
  waiting for transfers between devices  85.3 us (19%)
  local copies, waits for them, and re-layouts  23.9 us (5%)
  between operations  15.6 us (4%)
    all_gather x8, blocking collectives, gather_rows(): return lax.all_gather(array, axis, axis=0, tiled=True)  114 us
    ppermute x81, starting transfers between devices, swap(): return lax.ppermute(array, axis, [(i, i ^ by) for i in range(devices)])  95.4 us
    pallas_call x44, Pallas kernels, kernel_call(): pl.pallas_call(wrapped, out_shape=outs, in_specs=in_specs, out_specs=[pl....  91.6 us
    ppermute x81, waiting for transfers between devices, swap(): return lax.ppermute(array, axis, [(i, i ^ by) for i in range(devices)])  76.4 us
    unnamed x131, local copies, waits for them, and re-layouts  20.5 us
  transfers between devices with their start and end apart: 85, of which 35 were waited for; matrix products, arithmetic and copies ran while one was open for 1% of the time, Pallas kernels for 12%

profile of v5, /device:TPU:0, one launch (start us, length us, event | category | flops | bytes accessed | tf_op | source)
XLA Modules:
  0.0 433.8 jit_solution(7454721120478232991)
XLA Ops:
  13.4 2.1 shard_map.169
  17.8 1.9 shard_map.172
  23.1 1.9 shard_map.170.refs_3_
  25.0 21.0 %all_gather.27.refs_2_ = bf16[1024,384]{1,0:T(8,128)(2,1)S(1)} all-gather(bf16[256,384]{1,0:T(8,128)(2,1)S(1)} %get-tuple-element.146.refs_0_.refs_2_), channel_id=1, replica_groups=mesh['section'=2,'ctx'=4,'heads'=4] {'ctx'}, dimensions={0}, use_global_device_ids=true | all-gather | bytes 983040 | tf_op jit(solution)/shard_map/all_gather | solution.py:159
  46.0 2.9 shard_map.171
  61.9 2.0 collective-permute-done.6.refs_4_
  64.5 2.2 collective-permute-start.18
  71.1 2.4 shard_map.175
  74.6 2.4 collective-permute-start.12
  78.6 2.5 shard_map.176
  83.0 13.4 %all_gather.29.refs_1_.refs_2_ = bf16[640,768]{1,0:T(8,128)(2,1)S(1)} all-gather(bf16[160,768]{1,0:T(8,128)(2,1)S(1)} %pad_maximum_fusion.1), channel_id=1, replica_groups=mesh['section'=2,'ctx'=4,'heads'=4] {'heads'}, dimensions={0}, use_global_device_ids=true | all-gather | bytes 1228800 | tf_op jit(solution)/shard_map/all_gather | solution.py:159
  96.4 4.5 %shard_map.177 = (bf16[160,768]{1,0:T(8,128)(2,1)S(1)}, bf16[160,768]{1,0:T(8,128)(2,1)S(1)}, bf16[160,768]{1,0:T(8,128)(2,1)S(1)}, bf16[160,768]{1,0:T(8,128)(2...) custom-call(s32[3]{0:T(128)S(1)} %pad_add_fusion.refs_0_.place_ref, ...), custom_call_target="tpu_custom_call" | custom-call | flops 1509949440 | bytes 7476236 | tf_op jit(solution)/shard_map/pallas_call | solution.py:118
  101.0 2.0 collective-permute-start.20
  104.5 2.7 collective-permute-done.19.refs_1_
  107.2 3.6 collective-permute-done.20.refs_2_
  113.2 2.2 collective-permute-start.24
  117.0 2.1 collective-permute-start.26
  119.1 1.9 shard_map.180.refs_3_
  121.0 2.3 collective-permute-start.27
  123.3 11.4 %all_gather.30.refs_2_ = bf16[640,768]{1,0:T(8,128)(2,1)S(1)} all-gather(bf16[160,768]{1,0:T(8,128)(2,1)S(1)} %pad_maximum_fusion.2), channel_id=1, replica_groups=mesh['section'=2,'ctx'=4,'heads'=4] {'heads'}, dimensions={0}, use_global_device_ids=true | all-gather | bytes 1228800 | tf_op jit(solution)/shard_map/all_gather | solution.py:159
  134.8 2.2 shard_map.179
  137.0 17.4 %all_gather.31.refs_2_ = bf16[1024,384]{1,0:T(8,128)(2,1)S(1)} all-gather(bf16[256,384]{1,0:T(8,128)(2,1)S(1)} %get-tuple-element.170), channel_id=1, replica_groups=mesh['section'=2,'ctx'=4,'heads'=4] {'ctx'}, dimensions={0}, use_global_device_ids=true | all-gather | bytes 983040 | tf_op jit(solution)/shard_map/all_gather | solution.py:159
  154.4 3.0 shard_map.181
  157.6 2.0 collective-permute-start.29
  159.6 2.8 collective-permute-done.28.refs_2_
  164.0 4.3 collective-permute-done.30.refs_4_
  168.3 2.4 shard_map.183
  170.8 2.1 collective-permute-start.32
  172.9 2.3 collective-permute-start.33
  176.0 2.9 collective-permute-done.33
  178.9 11.7 %all_gather.32.refs_2_.refs_4_.refs_1_ = bf16[640,768]{1,0:T(8,128)(2,1)S(1)} all-gather(bf16[160,768]{1,0:T(8,128)(2,1)S(1)} %pad_maximum_fusion.3), channel_id=1, replica_groups=mesh['section'=2,'ctx'=4,'heads'=4] {'heads'}, dimensions={0}, use_global_device_ids=true | all-gather | bytes 1228800 | tf_op jit(solution)/shard_map/all_gather | solution.py:159
  190.7 8.1 %shard_map.184 = (bf16[160,768]{1,0:T(8,128)(2,1)S(1)}, bf16[160,768]{1,0:T(8,128)(2,1)S(1)}, bf16[160,768]{1,0:T(8,128)(2,1)S(1)}, bf16[160,768]{1,0:T(8,128)(2...) custom-call(s32[3]{0:T(128)S(1)} %pad_add_fusion.refs_0_.place_ref, ...), custom_call_target="tpu_custom_call" | custom-call | flops 1509949440 | bytes 8623116 | tf_op jit(solution)/shard_map/pallas_call | solution.py:118
  202.4 2.7 collective-permute-done.34.refs_1_
  205.1 4.5 %collective-permute-done.35.refs_2_ = bf16[160,768]{1,0:T(8,128)(2,1)S(1)} collective-permute-done((bf16[160,768]{1,0:T(8,128)(2,1)S(1)}, bf16[160,768]{1,0:T(8,128)(2,1)S(1)}, u32[]{:S(2)}, u32[]{:S(2)}) %collective-permute-start.35) | collective-permute-done | bytes 245792 | tf_op jit(solution)/shard_map/ppermute | solution.py:147
  210.0 3.6 collective-permute-start.38
  215.8 3.8 collective-permute-done.39
  219.6 11.2 %all_gather.33.refs_1_ = bf16[640,768]{1,0:T(8,128)(2,1)S(1)} all-gather(bf16[160,768]{1,0:T(8,128)(2,1)S(1)} %pad_maximum_fusion.4), channel_id=1, replica_groups=mesh['section'=2,'ctx'=4,'heads'=4] {'heads'}, dimensions={0}, use_global_device_ids=true | all-gather | bytes 1228800 | tf_op jit(solution)/shard_map/all_gather | solution.py:159
  232.7 4.9 %shard_map.187 = (bf16[256,192]{1,0:T(8,128)(2,1)S(1)}, f32[3,4,128,128]{3,2,1,0:T(8,128)S(1)}, bf16[256,384]{1,0:T(8,128)(2,1)S(1)}, bf16[256,384]{1,0:T(8,128)...) custom-call(s32[3]{0:T(128)S(1)} %pad_add_fusion.refs_0_.place_ref, ...), custom_call_target="tpu_custom_call" | custom-call | flops 503316480 | bytes 3443724 | tf_op jit(solution)/shard_map/pallas_call | solution.py:118
  238.9 3.2 collective-permute-start.42
  242.0 2.7 collective-permute-done.40.refs_3_.refs_5_
  244.8 3.8 collective-permute-done.41.refs_4_
  253.8 2.8 shard_map.193
  267.8 3.6 collective-permute-done.47.refs_3_
  273.1 3.5 collective-permute-start.49
  276.7 2.4 collective-permute-start.51
  279.3 2.7 collective-permute-done.50
  282.8 14.6 %all_gather.34.refs_1_ = bf16[640,768]{1,0:T(8,128)(2,1)S(1)} all-gather(bf16[160,768]{1,0:T(8,128)(2,1)S(1)} %pad_maximum_fusion.5), channel_id=1, replica_groups=mesh['section'=2,'ctx'=4,'heads'=4] {'heads'}, dimensions={0}, use_global_device_ids=true | all-gather | bytes 1228800 | tf_op jit(solution)/shard_map/all_gather | solution.py:159
  297.4 6.8 %shard_map.195 = (bf16[160,768]{1,0:T(8,128)(2,1)S(1)}, bf16[160,768]{1,0:T(8,128)(2,1)S(1)}, bf16[160,768]{1,0:T(8,128)(2,1)S(1)}, bf16[160,768]{1,0:T(8,128)(2...) custom-call(s32[3]{0:T(128)S(1)} %pad_add_fusion.refs_0_.place_ref, ...), custom_call_target="tpu_custom_call" | custom-call | flops 1509949440 | bytes 9606156 | tf_op jit(solution)/shard_map/pallas_call | solution.py:118
  307.9 2.0 collective-permute-start.59
  309.9 2.1 collective-permute-done.58.refs_4_.refs_1_
  313.6 4.5 %collective-permute-done.60.refs_6_.refs_3_ = bf16[40,768]{1,0:T(8,128)(2,1)S(1)} collective-permute-done((bf16[40,768]{1,0:T(8,128)(2,1)S(1)}, bf16[40,768]{1,0:T(8,128)(2,1)S(1)}, u32[]{:S(2)}, u32[]{:S(2)}) %collective-permute-start.60) | collective-permute-done | bytes 61472 | tf_op jit(solution)/shard_map/ppermute | solution.py:147
  318.3 2.1 collective-permute-start.62
  320.4 2.3 collective-permute-start.63
  329.1 3.3 collective-permute-done.66.refs_7_
  333.1 12.8 %all_gather.35.refs_1_ = bf16[640,768]{1,0:T(8,128)(2,1)S(1)} all-gather(bf16[160,768]{1,0:T(8,128)(2,1)S(1)} %pad_maximum_fusion.6), channel_id=1, replica_groups=mesh['section'=2,'ctx'=4,'heads'=4] {'heads'}, dimensions={0}, use_global_device_ids=true | all-gather | bytes 1228800 | tf_op jit(solution)/shard_map/all_gather | solution.py:159
  347.8 4.9 %shard_map.200 = (bf16[256,192]{1,0:T(8,128)(2,1)S(1)}, f32[3,4,128,128]{3,2,1,0:T(8,128)S(1)}, bf16[256,384]{1,0:T(8,128)(2,1)S(1)}, bf16[256,384]{1,0:T(8,128)...) custom-call(s32[3]{0:T(128)S(1)} %pad_add_fusion.refs_0_.place_ref, ...), custom_call_target="tpu_custom_call" | custom-call | flops 503316480 | bytes 3443724 | tf_op jit(solution)/shard_map/pallas_call | solution.py:118
  352.8 2.6 collective-permute-start.68
  357.2 2.7 collective-permute-done.67.refs_9_.refs_3_
  359.9 5.9 %shard_map.201 = (bf16[2,768,768]{2,1,0:T(8,128)(2,1)}, f32[8,128]{1,0:T(8,128)S(1)}) custom-call(s32[3]{0:T(128)S(1)} %pad_add_fusion.refs_0_.place_ref, bf16[640,768]{1,0:T(8,128)(2,1)S(1)} %all_gather.32.refs_2_.refs_4_.refs_1_, bf16[640,768]{1,0:T(8,128)(2,1)S(1)} %all_gather.29.refs_1_.refs_2_, bf16[640,768]{1,0:T(8,128)(2,1)S(1)} %get-tuple-element.248.refs_3_.refs_4_, ...), custom_call_target="tpu_custom_call" | custom-call | flops 1509949440 | bytes 6295564 | tf_op jit(solution)/shard_map/pallas_call | solution.py:118
  386.2 3.8 collective-permute-done.82.refs_5_
  402.2 7.1 %shard_map.208 = (f32[768,768]{1,0:T(8,128)}, f32[768,768]{1,0:T(8,128)}, f32[8,128]{1,0:T(8,128)S(1)}) custom-call(s32[3]{0:T(128)S(1)} %pad_add_fusion.refs_0_.place_ref, bf16[640,768]{1,0:T(8,128)(2,1)S(1)} %all_gather.29.refs_1_.refs_2_, bf16[640,768]{1,0:T(8,128)(2,1)S(1)} %copy-done.3, bf16[640,768]{1,0:T(8,128)(2,1)S(1)} %copy-done.17, ...), custom_call_target="tpu_custom_call" | custom-call | flops 1509949440 | bytes 11014156 | tf_op jit(solution)/shard_map/pallas_call | solution.py:118
  410.0 3.1 collective-permute-start.80
  415.0 1.9 shard_map.210
  416.9 7.0 %reduce-scatter.2.cloned.1.call-done.refs_0_ = bf16[192,896]{1,0:T(8,128)(2,1)} async-done(((bf16[768,896]{1,0:T(8,128)(2,1)}), bf16[192,896]{1,0:T(8,128)(2,1)}) %reduce-scatter.2.cloned.1.call-update) | async-done | bytes 344080 | tf_op jit(solution)/shard_map/reduce_scatter | solution.py:1171
  (304 shorter events, 124.5 us)
Async XLA Ops:
  7.2 59.6 %all-gather.2.cloned.1.call-start = ((), (), s32[]{:S(2)}) async-start(), calls=%async_computation.1 | async-start | bytes 2949120 | tf_op jit(solution)/shard_map/all_gather | solution.py:159
  9.6 8.2 %collective-permute-start.7 = (bf16[192,768]{1,0:T(8,128)(2,1)}, bf16[192,768]{1,0:T(8,128)(2,1)}, u32[]{:S(2)}, u32[]{:S(2)}) collective-permute-start(bf16[192,768]{1,0:T(8,128)(2,1)} %bitcast.50), channel_id=1, source_target_pairs={{0,16},{16,0},{1,17},{17,1},{2,18},{18,2},{3,19},{19,3},{4,20},{20... | collective-permute-start | bytes 884744 | tf_op jit(solution)/shard_map/ppermute | solution.py:147
  19.7 404.2 %reduce-scatter.2.cloned.1.call-start = ((), (), s32[]{:S(2)}) async-start(), calls=%async_computation.2 | async-start | bytes 1720320 | tf_op jit(solution)/shard_map/reduce_scatter | solution.py:1171
  19.7 76.7 %collective-permute-start.15 = (bf16[768,768]{1,0:T(8,128)(2,1)}, bf16[768,768]{1,0:T(8,128)(2,1)}, u32[]{:S(2)}, u32[]{:S(2)}) collective-permute-start(bf16[768,768]{1,0:T(8,128)(2,1)} %bitcast.14.refs_4_.refs_6_.refs_7_), channel_id=1, source_target_pairs={{0,16},{16,0},{1,17},{17,1},{2,18},{18,2},{3,19},{19,3},{4,20},{20... | collective-permute-start | bytes 3538952 | tf_op jit(solution)/shard_map/ppermute | solution.py:147
  20.2 76.2 %collective-permute-start.14 = (bf16[768,768]{1,0:T(8,128)(2,1)}, bf16[768,768]{1,0:T(8,128)(2,1)}, u32[]{:S(2)}, u32[]{:S(2)}) collective-permute-start(bf16[768,768]{1,0:T(8,128)(2,1)} %bitcast.13.refs_2_.refs_4_.refs_5_), channel_id=1, source_target_pairs={{0,16},{16,0},{1,17},{17,1},{2,18},{18,2},{3,19},{19,3},{4,20},{20... | collective-permute-start | bytes 3538952 | tf_op jit(solution)/shard_map/ppermute | solution.py:147
  20.8 29.7 %collective-permute-start.10 = (s32[2,2,256]{2,1,0:T(2,128)S(1)}, s32[2,2,256]{2,1,0:T(2,128)S(1)}, u32[]{:S(2)}, u32[]{:S(2)}) collective-permute-start(s32[2,2,256]{2,1,0:T(2,128)S(1)} %bitcast.56), channel_id=1, source_target_pairs={{0,16},{16,0},{1,17},{17,1},{2,18},{18,2},{3,19},{19,3},{4,20},{20... | collective-permute-start | bytes 12296 | tf_op jit(solution)/shard_map/ppermute | solution.py:147
  21.1 31.0 %collective-permute-start.9 = (bf16[768,4]{1,0:T(8,128)(2,1)S(1)}, bf16[768,4]{1,0:T(8,128)(2,1)S(1)}, u32[]{:S(2)}, u32[]{:S(2)}) collective-permute-start(bf16[768,4]{1,0:T(8,128)(2,1)S(1)} %bitcast.48), channel_id=1, source_target_pairs={{0,16},{16,0},{1,17},{17,1},{2,18},{18,2},{3,19},{19,3},{4,20},{20... | collective-permute-start | bytes 18440 | tf_op jit(solution)/shard_map/ppermute | solution.py:147
  22.8 26.2 %collective-permute-start.8 = (bf16[1,768]{1,0:T(2,128)(2,1)S(1)}, bf16[1,768]{1,0:T(2,128)(2,1)S(1)}, u32[]{:S(2)}, u32[]{:S(2)}) collective-permute-start(bf16[1,768]{1,0:T(2,128)(2,1)S(1)} %copy-done.61), channel_id=1, source_target_pairs={{0,16},{16,0},{1,17},{17,1},{2,18},{18,2},{3,19},{19,3},{4,20},{20... | collective-permute-start | bytes 4616 | tf_op jit(solution)/shard_map/ppermute | solution.py:147
  49.0 9.2 %collective-permute-start.4 = (bf16[256,192]{1,0:T(8,128)(2,1)S(1)}, bf16[256,192]{1,0:T(8,128)(2,1)S(1)}, u32[]{:S(2)}, u32[]{:S(2)}) collective-permute-start(bf16[256,192]{1,0:T(8,128)(2,1)S(1)} %get-tuple-element.148.refs_1_.refs_4_), channel_id=1, source_target_pairs={{0,1},{1,0},{2,3},{3,2},{4,5},{5,4},{6,7},{7,6},{8,9},{9,8},{10,11... | collective-permute-start | bytes 294920 | tf_op jit(solution)/shard_map/ppermute | solution.py:147
  50.6 9.5 %collective-permute-start.5 = (bf16[256,192]{1,0:T(8,128)(2,1)S(1)}, bf16[256,192]{1,0:T(8,128)(2,1)S(1)}, u32[]{:S(2)}, u32[]{:S(2)}) collective-permute-start(bf16[256,192]{1,0:T(8,128)(2,1)S(1)} %get-tuple-element.148.refs_1_.refs_4_), channel_id=1, source_target_pairs={{0,2},{1,3},{2,0},{3,1},{4,6},{5,7},{6,4},{7,5},{8,10},{9,11},{10,... | collective-permute-start | bytes 294920 | tf_op jit(solution)/shard_map/ppermute | solution.py:147
  52.1 11.8 %collective-permute-start.6 = (bf16[256,192]{1,0:T(8,128)(2,1)S(1)}, bf16[256,192]{1,0:T(8,128)(2,1)S(1)}, u32[]{:S(2)}, u32[]{:S(2)}) collective-permute-start(bf16[256,192]{1,0:T(8,128)(2,1)S(1)} %get-tuple-element.148.refs_1_.refs_4_), channel_id=1, source_target_pairs={{0,3},{1,2},{2,1},{3,0},{4,7},{5,6},{6,5},{7,4},{8,11},{9,10},{10,... | collective-permute-start | bytes 294920 | tf_op jit(solution)/shard_map/ppermute | solution.py:147
  58.9 15.3 %collective-permute-start.16 = (s32[2,2,2,256]{3,2,1,0:T(2,128)S(1)}, s32[2,2,2,256]{3,2,1,0:T(2,128)S(1)}, u32[]{:S(2)}, u32[]{:S(2)}) collective-permute-start(s32[2,2,2,256]{3,2,1,0:T(2,128)S(1)} %get-tuple-element.158.refs_1_), channel_id=1, source_target_pairs={{0,4},{4,0},{8,12},{12,8},{1,5},{5,1},{9,13},{13,9},{2,6},{6,2},{1... | collective-permute-start | bytes 24584 | tf_op jit(solution)/shard_map/ppermute | solution.py:147
  60.7 13.9 %collective-permute-start.17 = (s32[2,2,2,256]{3,2,1,0:T(2,128)S(1)}, s32[2,2,2,256]{3,2,1,0:T(2,128)S(1)}, u32[]{:S(2)}, u32[]{:S(2)}) collective-permute-start(s32[2,2,2,256]{3,2,1,0:T(2,128)S(1)} %get-tuple-element.158.refs_1_), channel_id=1, source_target_pairs={{0,8},{4,12},{8,0},{12,4},{1,9},{5,13},{9,1},{13,5},{2,10},{6,14},... | collective-permute-start | bytes 24584 | tf_op jit(solution)/shard_map/ppermute | solution.py:147
  64.5 12.5 %collective-permute-start.18 = (s32[2,2,2,256]{3,2,1,0:T(2,128)S(1)}, s32[2,2,2,256]{3,2,1,0:T(2,128)S(1)}, u32[]{:S(2)}, u32[]{:S(2)}) collective-permute-start(s32[2,2,2,256]{3,2,1,0:T(2,128)S(1)} %get-tuple-element.158.refs_1_), channel_id=1, source_target_pairs={{0,12},{4,8},{8,4},{12,0},{1,13},{5,9},{9,5},{13,1},{2,14},{6,10},... | collective-permute-start | bytes 24584 | tf_op jit(solution)/shard_map/ppermute | solution.py:147
  74.2 6.9 %collective-permute-start.11 = (bf16[40,768]{1,0:T(8,128)(2,1)S(1)}, bf16[40,768]{1,0:T(8,128)(2,1)S(1)}, u32[]{:S(2)}, u32[]{:S(2)}) collective-permute-start(bf16[40,768]{1,0:T(8,128)(2,1)S(1)} %get-tuple-element.154), channel_id=1, source_target_pairs={{0,4},{4,0},{8,12},{12,8},{1,5},{5,1},{9,13},{13,9},{2,6},{6,2},{1... | collective-permute-start | bytes 184328 | tf_op jit(solution)/shard_map/ppermute | solution.py:147
  74.6 7.0 %collective-permute-start.12 = (bf16[40,768]{1,0:T(8,128)(2,1)S(1)}, bf16[40,768]{1,0:T(8,128)(2,1)S(1)}, u32[]{:S(2)}, u32[]{:S(2)}) collective-permute-start(bf16[40,768]{1,0:T(8,128)(2,1)S(1)} %get-tuple-element.155), channel_id=1, source_target_pairs={{0,8},{4,12},{8,0},{12,4},{1,9},{5,13},{9,1},{13,5},{2,10},{6,14},... | collective-permute-start | bytes 184328 | tf_op jit(solution)/shard_map/ppermute | solution.py:147
  77.0 6.0 %collective-permute-start.13 = (bf16[40,768]{1,0:T(8,128)(2,1)S(1)}, bf16[40,768]{1,0:T(8,128)(2,1)S(1)}, u32[]{:S(2)}, u32[]{:S(2)}) collective-permute-start(bf16[40,768]{1,0:T(8,128)(2,1)S(1)} %get-tuple-element.156), channel_id=1, source_target_pairs={{0,12},{4,8},{8,4},{12,0},{1,13},{5,9},{9,5},{13,1},{2,14},{6,10},... | collective-permute-start | bytes 184328 | tf_op jit(solution)/shard_map/ppermute | solution.py:147
  100.9 6.3 %collective-permute-start.19 = (bf16[160,768]{1,0:T(8,128)(2,1)S(1)}, bf16[160,768]{1,0:T(8,128)(2,1)S(1)}, u32[]{:S(2)}, u32[]{:S(2)}) collective-permute-start(bf16[160,768]{1,0:T(8,128)(2,1)S(1)} %get-tuple-element.161), channel_id=1, source_target_pairs={{0,1},{1,0},{2,3},{3,2},{4,5},{5,4},{6,7},{7,6},{8,9},{9,8},{10,11... | collective-permute-start | bytes 737288 | tf_op jit(solution)/shard_map/ppermute | solution.py:147
  101.0 9.8 %collective-permute-start.20 = (bf16[160,768]{1,0:T(8,128)(2,1)S(1)}, bf16[160,768]{1,0:T(8,128)(2,1)S(1)}, u32[]{:S(2)}, u32[]{:S(2)}) collective-permute-start(bf16[160,768]{1,0:T(8,128)(2,1)S(1)} %get-tuple-element.162), channel_id=1, source_target_pairs={{0,2},{1,3},{2,0},{3,1},{4,6},{5,7},{6,4},{7,5},{8,10},{9,11},{10,... | collective-permute-start | bytes 737288 | tf_op jit(solution)/shard_map/ppermute | solution.py:147
  103.0 7.8 %collective-permute-start.21 = (bf16[160,768]{1,0:T(8,128)(2,1)S(1)}, bf16[160,768]{1,0:T(8,128)(2,1)S(1)}, u32[]{:S(2)}, u32[]{:S(2)}) collective-permute-start(bf16[160,768]{1,0:T(8,128)(2,1)S(1)} %get-tuple-element.163), channel_id=1, source_target_pairs={{0,3},{1,2},{2,1},{3,0},{4,7},{5,6},{6,5},{7,4},{8,11},{9,10},{10,... | collective-permute-start | bytes 737288 | tf_op jit(solution)/shard_map/ppermute | solution.py:147
  110.9 10.0 %collective-permute-start.22 = (bf16[40,768]{1,0:T(8,128)(2,1)S(1)}, bf16[40,768]{1,0:T(8,128)(2,1)S(1)}, u32[]{:S(2)}, u32[]{:S(2)}) collective-permute-start(bf16[40,768]{1,0:T(8,128)(2,1)S(1)} %get-tuple-element.165), channel_id=1, source_target_pairs={{0,4},{4,0},{8,12},{12,8},{1,5},{5,1},{9,13},{13,9},{2,6},{6,2},{1... | collective-permute-start | bytes 184328 | tf_op jit(solution)/shard_map/ppermute | solution.py:147
  111.6 11.7 %collective-permute-start.23 = (bf16[40,768]{1,0:T(8,128)(2,1)S(1)}, bf16[40,768]{1,0:T(8,128)(2,1)S(1)}, u32[]{:S(2)}, u32[]{:S(2)}) collective-permute-start(bf16[40,768]{1,0:T(8,128)(2,1)S(1)} %get-tuple-element.166), channel_id=1, source_target_pairs={{0,8},{4,12},{8,0},{12,4},{1,9},{5,13},{9,1},{13,5},{2,10},{6,14},... | collective-permute-start | bytes 184328 | tf_op jit(solution)/shard_map/ppermute | solution.py:147
  113.2 10.2 %collective-permute-start.24 = (bf16[40,768]{1,0:T(8,128)(2,1)S(1)}, bf16[40,768]{1,0:T(8,128)(2,1)S(1)}, u32[]{:S(2)}, u32[]{:S(2)}) collective-permute-start(bf16[40,768]{1,0:T(8,128)(2,1)S(1)} %get-tuple-element.167), channel_id=1, source_target_pairs={{0,12},{4,8},{8,4},{12,0},{1,13},{5,9},{9,5},{13,1},{2,14},{6,10},... | collective-permute-start | bytes 184328 | tf_op jit(solution)/shard_map/ppermute | solution.py:147
  116.9 56.0 %collective-permute-start.25 = (bf16[160,768]{1,0:T(8,128)(2,1)S(1)}, bf16[160,768]{1,0:T(8,128)(2,1)S(1)}, u32[]{:S(2)}, u32[]{:S(2)}) collective-permute-start(bf16[160,768]{1,0:T(8,128)(2,1)S(1)} %get-tuple-element.175), channel_id=1, source_target_pairs={{0,4},{4,0},{8,12},{12,8},{1,5},{5,1},{9,13},{13,9},{2,6},{6,2},{1... | collective-permute-start | bytes 737288 | tf_op jit(solution)/shard_map/ppermute | solution.py:147
  117.0 58.2 %collective-permute-start.26 = (bf16[160,768]{1,0:T(8,128)(2,1)S(1)}, bf16[160,768]{1,0:T(8,128)(2,1)S(1)}, u32[]{:S(2)}, u32[]{:S(2)}) collective-permute-start(bf16[160,768]{1,0:T(8,128)(2,1)S(1)} %get-tuple-element.176), channel_id=1, source_target_pairs={{0,8},{4,12},{8,0},{12,4},{1,9},{5,13},{9,1},{13,5},{2,10},{6,14},... | collective-permute-start | bytes 737288 | tf_op jit(solution)/shard_map/ppermute | solution.py:147
  121.0 54.2 %collective-permute-start.27 = (bf16[160,768]{1,0:T(8,128)(2,1)S(1)}, bf16[160,768]{1,0:T(8,128)(2,1)S(1)}, u32[]{:S(2)}, u32[]{:S(2)}) collective-permute-start(bf16[160,768]{1,0:T(8,128)(2,1)S(1)} %get-tuple-element.177), channel_id=1, source_target_pairs={{0,12},{4,8},{8,4},{12,0},{1,13},{5,9},{9,5},{13,1},{2,14},{6,10},... | collective-permute-start | bytes 737288 | tf_op jit(solution)/shard_map/ppermute | solution.py:147
  157.6 6.4 %collective-permute-start.29 = (bf16[256,192]{1,0:T(8,128)(2,1)S(1)}, bf16[256,192]{1,0:T(8,128)(2,1)S(1)}, u32[]{:S(2)}, u32[]{:S(2)}) collective-permute-start(bf16[256,192]{1,0:T(8,128)(2,1)S(1)} %get-tuple-element.178.refs_1_.refs_4_), channel_id=1, source_target_pairs={{0,2},{1,3},{2,0},{3,1},{4,6},{5,7},{6,4},{7,5},{8,10},{9,11},{10,... | collective-permute-start | bytes 294920 | tf_op jit(solution)/shard_map/ppermute | solution.py:147
  162.4 5.9 %collective-permute-start.30 = (bf16[256,192]{1,0:T(8,128)(2,1)S(1)}, bf16[256,192]{1,0:T(8,128)(2,1)S(1)}, u32[]{:S(2)}, u32[]{:S(2)}) collective-permute-start(bf16[256,192]{1,0:T(8,128)(2,1)S(1)} %get-tuple-element.178.refs_1_.refs_4_), channel_id=1, source_target_pairs={{0,3},{1,2},{2,1},{3,0},{4,7},{5,6},{6,5},{7,4},{8,11},{9,10},{10,... | collective-permute-start | bytes 294920 | tf_op jit(solution)/shard_map/ppermute | solution.py:147
  172.9 6.0 %collective-permute-start.33 = (bf16[40,768]{1,0:T(8,128)(2,1)S(1)}, bf16[40,768]{1,0:T(8,128)(2,1)S(1)}, u32[]{:S(2)}, u32[]{:S(2)}) collective-permute-start(bf16[40,768]{1,0:T(8,128)(2,1)S(1)} %get-tuple-element.184), channel_id=1, source_target_pairs={{0,12},{4,8},{8,4},{12,0},{1,13},{5,9},{9,5},{13,1},{2,14},{6,10},... | collective-permute-start | bytes 184328 | tf_op jit(solution)/shard_map/ppermute | solution.py:147
  198.8 6.3 %collective-permute-start.34 = (bf16[160,768]{1,0:T(8,128)(2,1)S(1)}, bf16[160,768]{1,0:T(8,128)(2,1)S(1)}, u32[]{:S(2)}, u32[]{:S(2)}) collective-permute-start(bf16[160,768]{1,0:T(8,128)(2,1)S(1)} %get-tuple-element.188), channel_id=1, source_target_pairs={{0,1},{1,0},{2,3},{3,2},{4,5},{5,4},{6,7},{7,6},{8,9},{9,8},{10,11... | collective-permute-start | bytes 737288 | tf_op jit(solution)/shard_map/ppermute | solution.py:147
  200.4 9.2 %collective-permute-start.35 = (bf16[160,768]{1,0:T(8,128)(2,1)S(1)}, bf16[160,768]{1,0:T(8,128)(2,1)S(1)}, u32[]{:S(2)}, u32[]{:S(2)}) collective-permute-start(bf16[160,768]{1,0:T(8,128)(2,1)S(1)} %get-tuple-element.189), channel_id=1, source_target_pairs={{0,2},{1,3},{2,0},{3,1},{4,6},{5,7},{6,4},{7,5},{8,10},{9,11},{10,... | collective-permute-start | bytes 737288 | tf_op jit(solution)/shard_map/ppermute | solution.py:147
  200.9 8.8 %collective-permute-start.36 = (bf16[160,768]{1,0:T(8,128)(2,1)S(1)}, bf16[160,768]{1,0:T(8,128)(2,1)S(1)}, u32[]{:S(2)}, u32[]{:S(2)}) collective-permute-start(bf16[160,768]{1,0:T(8,128)(2,1)S(1)} %get-tuple-element.190), channel_id=1, source_target_pairs={{0,3},{1,2},{2,1},{3,0},{4,7},{5,6},{6,5},{7,4},{8,11},{9,10},{10,... | collective-permute-start | bytes 737288 | tf_op jit(solution)/shard_map/ppermute | solution.py:147
  210.0 5.8 %collective-permute-start.38 = (bf16[40,768]{1,0:T(8,128)(2,1)S(1)}, bf16[40,768]{1,0:T(8,128)(2,1)S(1)}, u32[]{:S(2)}, u32[]{:S(2)}) collective-permute-start(bf16[40,768]{1,0:T(8,128)(2,1)S(1)} %get-tuple-element.193), channel_id=1, source_target_pairs={{0,8},{4,12},{8,0},{12,4},{1,9},{5,13},{9,1},{13,5},{2,10},{6,14},... | collective-permute-start | bytes 184328 | tf_op jit(solution)/shard_map/ppermute | solution.py:147
  213.6 6.0 %collective-permute-start.39 = (bf16[40,768]{1,0:T(8,128)(2,1)S(1)}, bf16[40,768]{1,0:T(8,128)(2,1)S(1)}, u32[]{:S(2)}, u32[]{:S(2)}) collective-permute-start(bf16[40,768]{1,0:T(8,128)(2,1)S(1)} %get-tuple-element.194), channel_id=1, source_target_pairs={{0,12},{4,8},{8,4},{12,0},{1,13},{5,9},{9,5},{13,1},{2,14},{6,10},... | collective-permute-start | bytes 184328 | tf_op jit(solution)/shard_map/ppermute | solution.py:147
  237.6 7.2 %collective-permute-start.40 = (bf16[256,384]{1,0:T(8,128)(2,1)S(1)}, bf16[256,384]{1,0:T(8,128)(2,1)S(1)}, u32[]{:S(2)}, u32[]{:S(2)}) collective-permute-start(bf16[256,384]{1,0:T(8,128)(2,1)S(1)} %get-tuple-element.199), channel_id=1, source_target_pairs={{0,4},{4,0},{8,12},{12,8},{1,5},{5,1},{9,13},{13,9},{2,6},{6,2},{1... | collective-permute-start | bytes 589832 | tf_op jit(solution)/shard_map/ppermute | solution.py:147
  237.7 10.9 %collective-permute-start.41 = (bf16[256,384]{1,0:T(8,128)(2,1)S(1)}, bf16[256,384]{1,0:T(8,128)(2,1)S(1)}, u32[]{:S(2)}, u32[]{:S(2)}) collective-permute-start(bf16[256,384]{1,0:T(8,128)(2,1)S(1)} %get-tuple-element.200), channel_id=1, source_target_pairs={{0,8},{4,12},{8,0},{12,4},{1,9},{5,13},{9,1},{13,5},{2,10},{6,14},... | collective-permute-start | bytes 589832 | tf_op jit(solution)/shard_map/ppermute | solution.py:147
  238.9 9.7 %collective-permute-start.42 = (bf16[256,384]{1,0:T(8,128)(2,1)S(1)}, bf16[256,384]{1,0:T(8,128)(2,1)S(1)}, u32[]{:S(2)}, u32[]{:S(2)}) collective-permute-start(bf16[256,384]{1,0:T(8,128)(2,1)S(1)} %get-tuple-element.201), channel_id=1, source_target_pairs={{0,12},{4,8},{8,4},{12,0},{1,13},{5,9},{9,5},{13,1},{2,14},{6,10},... | collective-permute-start | bytes 589832 | tf_op jit(solution)/shard_map/ppermute | solution.py:147
  250.2 7.6 %collective-permute-start.43 = (bf16[64,768]{1,0:T(8,128)(2,1)S(1)}, bf16[64,768]{1,0:T(8,128)(2,1)S(1)}, u32[]{:S(2)}, u32[]{:S(2)}) collective-permute-start(bf16[64,768]{1,0:T(8,128)(2,1)S(1)} %get-tuple-element.203), channel_id=1, source_target_pairs={{0,1},{1,0},{2,3},{3,2},{4,5},{5,4},{6,7},{7,6},{8,9},{9,8},{10,11... | collective-permute-start | bytes 294920 | tf_op jit(solution)/shard_map/ppermute | solution.py:147
  251.5 6.4 %collective-permute-start.44 = (bf16[64,768]{1,0:T(8,128)(2,1)S(1)}, bf16[64,768]{1,0:T(8,128)(2,1)S(1)}, u32[]{:S(2)}, u32[]{:S(2)}) collective-permute-start(bf16[64,768]{1,0:T(8,128)(2,1)S(1)} %get-tuple-element.204), channel_id=1, source_target_pairs={{0,2},{1,3},{2,0},{3,1},{4,6},{5,7},{6,4},{7,5},{8,10},{9,11},{10,... | collective-permute-start | bytes 294920 | tf_op jit(solution)/shard_map/ppermute | solution.py:147
  256.6 20.1 %collective-permute-start.52 = (bf16[160,768]{1,0:T(8,128)(2,1)S(1)}, bf16[160,768]{1,0:T(8,128)(2,1)S(1)}, u32[]{:S(2)}, u32[]{:S(2)}) collective-permute-start(bf16[160,768]{1,0:T(8,128)(2,1)S(1)} %get-tuple-element.222), channel_id=1, source_target_pairs={{0,1},{1,0},{2,3},{3,2},{4,5},{5,4},{6,7},{7,6},{8,9},{9,8},{10,11... | collective-permute-start | bytes 737288 | tf_op jit(solution)/shard_map/ppermute | solution.py:147
  257.9 6.0 %collective-permute-start.46 = (bf16[64,768]{1,0:T(8,128)(2,1)S(1)}, bf16[64,768]{1,0:T(8,128)(2,1)S(1)}, u32[]{:S(2)}, u32[]{:S(2)}) collective-permute-start(bf16[64,768]{1,0:T(8,128)(2,1)S(1)} %shard_map.189.refs_1_), channel_id=1, source_target_pairs={{0,1},{1,0},{2,3},{3,2},{4,5},{5,4},{6,7},{7,6},{8,9},{9,8},{10,11... | collective-permute-start | bytes 294920 | tf_op jit(solution)/shard_map/ppermute | solution.py:147
  259.2 19.9 %collective-permute-start.53 = (bf16[160,768]{1,0:T(8,128)(2,1)S(1)}, bf16[160,768]{1,0:T(8,128)(2,1)S(1)}, u32[]{:S(2)}, u32[]{:S(2)}) collective-permute-start(bf16[160,768]{1,0:T(8,128)(2,1)S(1)} %get-tuple-element.223), channel_id=1, source_target_pairs={{0,2},{1,3},{2,0},{3,1},{4,6},{5,7},{6,4},{7,5},{8,10},{9,11},{10,... | collective-permute-start | bytes 737288 | tf_op jit(solution)/shard_map/ppermute | solution.py:147
  260.0 19.1 %collective-permute-start.54 = (bf16[160,768]{1,0:T(8,128)(2,1)S(1)}, bf16[160,768]{1,0:T(8,128)(2,1)S(1)}, u32[]{:S(2)}, u32[]{:S(2)}) collective-permute-start(bf16[160,768]{1,0:T(8,128)(2,1)S(1)} %get-tuple-element.224), channel_id=1, source_target_pairs={{0,3},{1,2},{2,1},{3,0},{4,7},{5,6},{6,5},{7,4},{8,11},{9,10},{10,... | collective-permute-start | bytes 737288 | tf_op jit(solution)/shard_map/ppermute | solution.py:147
  261.5 9.9 %collective-permute-start.47 = (bf16[64,768]{1,0:T(8,128)(2,1)S(1)}, bf16[64,768]{1,0:T(8,128)(2,1)S(1)}, u32[]{:S(2)}, u32[]{:S(2)}) collective-permute-start(bf16[64,768]{1,0:T(8,128)(2,1)S(1)} %shard_map.189.refs_1_), channel_id=1, source_target_pairs={{0,2},{1,3},{2,0},{3,1},{4,6},{5,7},{6,4},{7,5},{8,10},{9,11},{10,... | collective-permute-start | bytes 294920 | tf_op jit(solution)/shard_map/ppermute | solution.py:147
  263.9 7.5 %collective-permute-start.48 = (bf16[64,768]{1,0:T(8,128)(2,1)S(1)}, bf16[64,768]{1,0:T(8,128)(2,1)S(1)}, u32[]{:S(2)}, u32[]{:S(2)}) collective-permute-start(bf16[64,768]{1,0:T(8,128)(2,1)S(1)} %shard_map.189.refs_1_), channel_id=1, source_target_pairs={{0,3},{1,2},{2,1},{3,0},{4,7},{5,6},{6,5},{7,4},{8,11},{9,10},{10,... | collective-permute-start | bytes 294920 | tf_op jit(solution)/shard_map/ppermute | solution.py:147
  273.1 6.1 %collective-permute-start.49 = (bf16[40,768]{1,0:T(8,128)(2,1)S(1)}, bf16[40,768]{1,0:T(8,128)(2,1)S(1)}, u32[]{:S(2)}, u32[]{:S(2)}) collective-permute-start(bf16[40,768]{1,0:T(8,128)(2,1)S(1)} %get-tuple-element.213), channel_id=1, source_target_pairs={{0,4},{4,0},{8,12},{12,8},{1,5},{5,1},{9,13},{13,9},{2,6},{6,2},{1... | collective-permute-start | bytes 184328 | tf_op jit(solution)/shard_map/ppermute | solution.py:147
  276.7 6.1 %collective-permute-start.51 = (bf16[40,768]{1,0:T(8,128)(2,1)S(1)}, bf16[40,768]{1,0:T(8,128)(2,1)S(1)}, u32[]{:S(2)}, u32[]{:S(2)}) collective-permute-start(bf16[40,768]{1,0:T(8,128)(2,1)S(1)} %get-tuple-element.215), channel_id=1, source_target_pairs={{0,12},{4,8},{8,4},{12,0},{1,13},{5,9},{9,5},{13,1},{2,14},{6,10},... | collective-permute-start | bytes 184328 | tf_op jit(solution)/shard_map/ppermute | solution.py:147
  304.2 13.8 %collective-permute-start.55 = (bf16[160,768]{1,0:T(8,128)(2,1)S(1)}, bf16[160,768]{1,0:T(8,128)(2,1)S(1)}, u32[]{:S(2)}, u32[]{:S(2)}) collective-permute-start(bf16[160,768]{1,0:T(8,128)(2,1)S(1)} %get-tuple-element.227), channel_id=1, source_target_pairs={{0,1},{1,0},{2,3},{3,2},{4,5},{5,4},{6,7},{7,6},{8,9},{9,8},{10,11... | collective-permute-start | bytes 737288 | tf_op jit(solution)/shard_map/ppermute | solution.py:147
  304.9 13.2 %collective-permute-start.56 = (bf16[160,768]{1,0:T(8,128)(2,1)S(1)}, bf16[160,768]{1,0:T(8,128)(2,1)S(1)}, u32[]{:S(2)}, u32[]{:S(2)}) collective-permute-start(bf16[160,768]{1,0:T(8,128)(2,1)S(1)} %get-tuple-element.228), channel_id=1, source_target_pairs={{0,2},{1,3},{2,0},{3,1},{4,6},{5,7},{6,4},{7,5},{8,10},{9,11},{10,... | collective-permute-start | bytes 737288 | tf_op jit(solution)/shard_map/ppermute | solution.py:147
  306.3 11.7 %collective-permute-start.57 = (bf16[160,768]{1,0:T(8,128)(2,1)S(1)}, bf16[160,768]{1,0:T(8,128)(2,1)S(1)}, u32[]{:S(2)}, u32[]{:S(2)}) collective-permute-start(bf16[160,768]{1,0:T(8,128)(2,1)S(1)} %get-tuple-element.229), channel_id=1, source_target_pairs={{0,3},{1,2},{2,1},{3,0},{4,7},{5,6},{6,5},{7,4},{8,11},{9,10},{10,... | collective-permute-start | bytes 737288 | tf_op jit(solution)/shard_map/ppermute | solution.py:147
  307.9 5.7 %collective-permute-start.59 = (bf16[40,768]{1,0:T(8,128)(2,1)S(1)}, bf16[40,768]{1,0:T(8,128)(2,1)S(1)}, u32[]{:S(2)}, u32[]{:S(2)}) collective-permute-start(bf16[40,768]{1,0:T(8,128)(2,1)S(1)} %get-tuple-element.231), channel_id=1, source_target_pairs={{0,8},{4,12},{8,0},{12,4},{1,9},{5,13},{9,1},{13,5},{2,10},{6,14},... | collective-permute-start | bytes 184328 | tf_op jit(solution)/shard_map/ppermute | solution.py:147
  312.0 6.0 %collective-permute-start.60 = (bf16[40,768]{1,0:T(8,128)(2,1)S(1)}, bf16[40,768]{1,0:T(8,128)(2,1)S(1)}, u32[]{:S(2)}, u32[]{:S(2)}) collective-permute-start(bf16[40,768]{1,0:T(8,128)(2,1)S(1)} %get-tuple-element.232), channel_id=1, source_target_pairs={{0,12},{4,8},{8,4},{12,0},{1,13},{5,9},{9,5},{13,1},{2,14},{6,10},... | collective-permute-start | bytes 184328 | tf_op jit(solution)/shard_map/ppermute | solution.py:147
  318.2 14.8 %collective-permute-start.61 = (bf16[40,768]{1,0:T(8,128)(2,1)S(1)}, bf16[40,768]{1,0:T(8,128)(2,1)S(1)}, u32[]{:S(2)}, u32[]{:S(2)}) collective-permute-start(bf16[40,768]{1,0:T(8,128)(2,1)S(1)} %get-tuple-element.234), channel_id=1, source_target_pairs={{0,4},{4,0},{8,12},{12,8},{1,5},{5,1},{9,13},{13,9},{2,6},{6,2},{1... | collective-permute-start | bytes 184328 | tf_op jit(solution)/shard_map/ppermute | solution.py:147
  318.3 14.7 %collective-permute-start.62 = (bf16[40,768]{1,0:T(8,128)(2,1)S(1)}, bf16[40,768]{1,0:T(8,128)(2,1)S(1)}, u32[]{:S(2)}, u32[]{:S(2)}) collective-permute-start(bf16[40,768]{1,0:T(8,128)(2,1)S(1)} %get-tuple-element.235), channel_id=1, source_target_pairs={{0,8},{4,12},{8,0},{12,4},{1,9},{5,13},{9,1},{13,5},{2,10},{6,14},... | collective-permute-start | bytes 184328 | tf_op jit(solution)/shard_map/ppermute | solution.py:147
  320.4 12.7 %collective-permute-start.63 = (bf16[40,768]{1,0:T(8,128)(2,1)S(1)}, bf16[40,768]{1,0:T(8,128)(2,1)S(1)}, u32[]{:S(2)}, u32[]{:S(2)}) collective-permute-start(bf16[40,768]{1,0:T(8,128)(2,1)S(1)} %get-tuple-element.236), channel_id=1, source_target_pairs={{0,12},{4,8},{8,4},{12,0},{1,13},{5,9},{9,5},{13,1},{2,14},{6,10},... | collective-permute-start | bytes 184328 | tf_op jit(solution)/shard_map/ppermute | solution.py:147
  352.7 7.2 %collective-permute-start.67 = (bf16[256,384]{1,0:T(8,128)(2,1)S(1)}, bf16[256,384]{1,0:T(8,128)(2,1)S(1)}, u32[]{:S(2)}, u32[]{:S(2)}) collective-permute-start(bf16[256,384]{1,0:T(8,128)(2,1)S(1)} %get-tuple-element.245), channel_id=1, source_target_pairs={{0,4},{4,0},{8,12},{12,8},{1,5},{5,1},{9,13},{13,9},{2,6},{6,2},{1... | collective-permute-start | bytes 589832 | tf_op jit(solution)/shard_map/ppermute | solution.py:147
  352.8 13.0 %collective-permute-start.68 = (bf16[256,384]{1,0:T(8,128)(2,1)S(1)}, bf16[256,384]{1,0:T(8,128)(2,1)S(1)}, u32[]{:S(2)}, u32[]{:S(2)}) collective-permute-start(bf16[256,384]{1,0:T(8,128)(2,1)S(1)} %get-tuple-element.246), channel_id=1, source_target_pairs={{0,8},{4,12},{8,0},{12,4},{1,9},{5,13},{9,1},{13,5},{2,10},{6,14},... | collective-permute-start | bytes 589832 | tf_op jit(solution)/shard_map/ppermute | solution.py:147
  355.4 10.4 %collective-permute-start.69 = (bf16[256,384]{1,0:T(8,128)(2,1)S(1)}, bf16[256,384]{1,0:T(8,128)(2,1)S(1)}, u32[]{:S(2)}, u32[]{:S(2)}) collective-permute-start(bf16[256,384]{1,0:T(8,128)(2,1)S(1)} %get-tuple-element.247), channel_id=1, source_target_pairs={{0,12},{4,8},{8,4},{12,0},{1,13},{5,9},{9,5},{13,1},{2,14},{6,10},... | collective-permute-start | bytes 589832 | tf_op jit(solution)/shard_map/ppermute | solution.py:147
  375.0 6.0 %collective-permute-start.73 = (bf16[64,768]{1,0:T(8,128)(2,1)S(1)}, bf16[64,768]{1,0:T(8,128)(2,1)S(1)}, u32[]{:S(2)}, u32[]{:S(2)}) collective-permute-start(bf16[64,768]{1,0:T(8,128)(2,1)S(1)} %shard_map.203.refs_1_), channel_id=1, source_target_pairs={{0,1},{1,0},{2,3},{3,2},{4,5},{5,4},{6,7},{7,6},{8,9},{9,8},{10,11... | collective-permute-start | bytes 294920 | tf_op jit(solution)/shard_map/ppermute | solution.py:147
  385.7 12.8 %collective-permute-start.79 = (bf16[2,768,768]{2,1,0:T(8,128)(2,1)}, bf16[2,768,768]{2,1,0:T(8,128)(2,1)}, u32[]{:S(2)}, u32[]{:S(2)}) collective-permute-start(bf16[2,768,768]{2,1,0:T(8,128)(2,1)} %get-tuple-element.266), channel_id=1, source_target_pairs={{0,16},{16,0},{1,17},{17,1},{2,18},{18,2},{3,19},{19,3},{4,20},{20... | collective-permute-start | bytes 7077896 | tf_op jit(solution)/shard_map/ppermute | solution.py:147
  393.7 15.6 %collective-permute-start.76 = (bf16[160,768]{1,0:T(8,128)(2,1)S(1)}, bf16[160,768]{1,0:T(8,128)(2,1)S(1)}, u32[]{:S(2)}, u32[]{:S(2)}) collective-permute-start(bf16[160,768]{1,0:T(8,128)(2,1)S(1)} %shard_map.207.refs_2_), channel_id=1, source_target_pairs={{0,1},{1,0},{2,3},{3,2},{4,5},{5,4},{6,7},{7,6},{8,9},{9,8},{10,11... | collective-permute-start | bytes 737288 | tf_op jit(solution)/shard_map/ppermute | solution.py:147
  394.8 14.5 %collective-permute-start.77 = (bf16[160,768]{1,0:T(8,128)(2,1)S(1)}, bf16[160,768]{1,0:T(8,128)(2,1)S(1)}, u32[]{:S(2)}, u32[]{:S(2)}) collective-permute-start(bf16[160,768]{1,0:T(8,128)(2,1)S(1)} %shard_map.207.refs_2_), channel_id=1, source_target_pairs={{0,2},{1,3},{2,0},{3,1},{4,6},{5,7},{6,4},{7,5},{8,10},{9,11},{10,... | collective-permute-start | bytes 737288 | tf_op jit(solution)/shard_map/ppermute | solution.py:147
  395.8 13.5 %collective-permute-start.78 = (bf16[160,768]{1,0:T(8,128)(2,1)S(1)}, bf16[160,768]{1,0:T(8,128)(2,1)S(1)}, u32[]{:S(2)}, u32[]{:S(2)}) collective-permute-start(bf16[160,768]{1,0:T(8,128)(2,1)S(1)} %shard_map.207.refs_2_), channel_id=1, source_target_pairs={{0,3},{1,2},{2,1},{3,0},{4,7},{5,6},{6,5},{7,4},{8,11},{9,10},{10,... | collective-permute-start | bytes 737288 | tf_op jit(solution)/shard_map/ppermute | solution.py:147
  397.2 15.9 %collective-permute-start.81 = (f32[256,768]{1,0:T(8,128)}, f32[256,768]{1,0:T(8,128)S(1)}, u32[]{:S(2)}, u32[]{:S(2)}) collective-permute-start(f32[256,768]{1,0:T(8,128)} %copy-done.33), channel_id=1, source_target_pairs={{16,0},{17,1},{18,2},{19,3},{20,4},{21,5},{22,6},{23,7},{24,8},{25... | collective-permute-start | bytes 2359304 | tf_op jit(solution)/shard_map/ppermute | solution.py:151
  (85 other events, 1394.2 us)
Sparse Core Ops, SparseCore 0:
  19.8 45.7 all-gather.1
  392.9 30.9 reduce-scatter.1
